TPU v7x, 512 devices: a whole 4x4x16 slice. The times are simulated.
512 devices in a mesh: dp: 32 (over y, x, core), mp: 16 (over z).
Axes of the slice: x: 4, y: 4, z: 16, core: 2. Of those that a mesh axis runs over, the one named last changes fastest.
Arguments:
- activations: bfloat16 [4096, 8192], P('dp'), may hold values from -16 to 16
- out_grads: bfloat16 [4096, 16384], P('dp', 'mp'), may hold values from -1 to 1
- weight: float32 [8192, 16384], P('dp', 'mp'), may hold values from -16 to 16
- row_moment: float32 [8192], P('dp'), may hold values from 0.25 to 2
- col_moment: float32 [16384], P('mp'), may hold values from 0.25 to 2
Outputs:
- update: float32 [8192, 16384], P('dp', 'mp')
- new_rows: float32 [8192], P('dp')
- new_cols: float32 [16384], P('mp')
All inputs are finite; a program needn't handle non-finite values.
Results may differ from a plain program's by a relative error of at most 0.0003.
Values may be sent and summed in bfloat16 or wider, within the bound.
No kernel may reach another device: no remote copies, remote signals or barrier semaphores. Data moves between devices by JAX's collectives and lax.ppermute only.
A program may use at most 64 MiB of HBM per device.

v0:
```python
import jax
import jax.numpy as jnp
from jax import lax
from jax.sharding import PartitionSpec as P

D = 8192
FF = 16384


BETA_TWO = 0.8
CLIP_LEVEL = 0.25
WEIGHT_DECAY = 0.1
EPSILON = 1e-06


def shards(activations, out_grads, weight, row_moment, col_moment):
    feature_rows = lax.all_to_all(activations, "dp", split_axis=1, concat_axis=0, tiled=True)
    weight_grad = lax.dot_general(
        feature_rows,
        lax.all_gather(out_grads, "dp", axis=0, tiled=True),
        (((0,), (0,)), ((), ())),
        preferred_element_type=jnp.float32,
    )
    squares = weight_grad * weight_grad
    row_total = lax.psum(jnp.sum(squares, axis=1), "mp")
    col_total = lax.psum(jnp.sum(squares, axis=0), "dp")
    new_rows = BETA_TWO * row_moment + (1.0 - BETA_TWO) * (row_total / FF)
    new_cols = BETA_TWO * col_moment + (1.0 - BETA_TWO) * (col_total / D)
    scaled = weight_grad / jnp.sqrt(new_rows[:, None] * new_cols[None, :])
    local_scaled = jnp.sum(scaled * scaled)
    local_weight = jnp.sum(weight * weight)
    scaled_sum, weight_sum = lax.psum((local_scaled, local_weight), ("dp", "mp"))
    factor = 1.0 / jnp.maximum(1.0, jnp.sqrt(scaled_sum / (D * FF)) / CLIP_LEVEL)
    direction = factor * scaled + WEIGHT_DECAY * weight
    direction_sum = lax.psum(jnp.sum(direction * direction), ("dp", "mp"))
    trust_ratio = jnp.sqrt(weight_sum / (direction_sum + EPSILON))
    return (trust_ratio * direction, new_rows, new_cols)


def solution(mesh):
    placed = (P("dp", None), P("dp", "mp"), P("dp", "mp"), P("dp"), P("mp"))
    return jax.shard_map(
        shards,
        mesh=mesh,
        in_specs=placed,
        out_specs=(P("dp", "mp"), P("dp"), P("mp")),
        check_vma=False,
    )
```

profile of v0, /device:TPU:1, one launch (start us, length us, event | category | flops | bytes accessed | tf_op | source)
XLA Modules:
  0.0 408.2 jit_solution(12231303182900137489)
XLA Ops:
  7.2 0.0 all-gather.2.cloned.1.call-start
  7.2 0.7 all-gather.2.cloned.1.call-update
  7.9 3.2 copy.8
  11.1 41.7 %all_to_all.19 = bf16[128,32,256]{0,2,1:T(8,128)(2,1)} all-to-all(bf16[128,32,256]{0,2,1:T(8,128)(2,1)S(1)} %bitcast.7), channel_id=1, replica_groups=mesh['dp'=32,'mp'=16] {'dp'}, dimensions={1} | all-to-all | bytes 4194304 | tf_op jit(solution)/shard_map/all_to_all | solution.py:17
  52.8 3.3 copy.9
  56.1 37.2 %all-gather.2.cloned.1.call-done = bf16[4096,1024]{1,0:T(8,128)(2,1)} async-done(((bf16[128,1024]{1,0:T(8,128)(2,1)}), bf16[4096,1024]{1,0:T(8,128)(2,1)}) %all-gather.2.cloned.1.call-update) | async-done | bytes 8388624 | tf_op jit(solution)/shard_map/all_gather | solution.py:20
  93.3 0.0 copy-start.3
  93.3 0.0 copy-start.4
  93.3 5.8 %multiply_reduce_fusion.4 = (f32[256]{0:T(256)S(1)}, f32[1024]{0:T(1024)S(1)}, f32[256,1024]{1,0:T(8,128)S(1)}) fusion(bf16[4096,256]{1,0:T(8,128)(2,1)S(1)} %bitcast.5, bf16[4096,1024]{1,0:T(8,128)(2,1)} %all-gather.2.cloned.1.call-done), kind=kOutput, calls=%fused_computation.6 | convolution fusion | flops 2148268800 | bytes 11539456 | tf_op jit(solution)/shard_map/dot_general | solution.py:18
  99.1 0.0 copy-start
  99.2 62.4 %psum.37 = f32[1024]{0:T(1024)S(1)} all-reduce(f32[1024]{0:T(1024)S(1)} %get-tuple-element.6), channel_id=1, replica_groups=mesh['dp'=32,'mp'=16] {'dp'}, use_global_device_ids=true, to_apply=%region_5.0 | all-reduce | flops 1024 | bytes 8192 | tf_op jit(solution)/shard_map/psum | solution.py:26
  161.6 24.5 %psum.36 = f32[256]{0:T(256)S(1)} all-reduce(f32[256]{0:T(256)S(1)} %get-tuple-element.5), channel_id=1, replica_groups=mesh['dp'=32,'mp'=16] {'mp'}, use_global_device_ids=true, to_apply=%region_3.0 | all-reduce | flops 256 | bytes 2048 | tf_op jit(solution)/shard_map/psum | solution.py:25
  186.1 0.0 copy-done.3
  186.1 0.0 copy-done.4
  186.1 0.0 copy-start.1
  186.1 0.0 copy-start.2
  186.1 1.1 multiply_reduce_fusion.1
  187.2 107.7 %psum.38 = f32[]{:T(128)} all-reduce(f32[]{:T(128)} %multiply_reduce_fusion.1), channel_id=1, replica_groups=mesh['dp'=32,'mp'=16] {'dp','mp'}, use_global_device_ids=true, to_apply=%region_7.0 | all-reduce | flops 1 | bytes 8 | tf_op jit(solution)/shard_map/psum | solution.py:32
  295.6 2.4 multiply_reduce_fusion
  298.0 100.8 %all-reduce = (f32[]{:T(128)}, f32[]{:T(128)}) all-reduce(f32[]{:T(128)} %get-tuple-element.4, f32[]{:T(128)} %get-tuple-element.3), channel_id=1, replica_groups=mesh['dp'=32,'mp'=16] {'dp','mp'}, use_global_device_ids=true, to_apply=%region_1.0 | all-reduce | flops 2 | bytes 16 | tf_op jit(solution)/shard_map/psum | solution.py:32
  400.0 0.0 copy-done
  400.0 1.3 broadcast_multiply_fusion
  401.3 0.0 copy-done.1
  401.3 0.0 copy-done.2
  (2 shorter events, 0.0 us)
Async XLA Ops:
  7.2 86.1 %all-gather.2.cloned.1.call-start = ((), (), s32[]{:S(2)}) async-start(), calls=%async_computation.1 | async-start | bytes 8650752 | tf_op jit(solution)/shard_map/all_gather | solution.py:20
  93.3 92.8 %copy-start.3 = (f32[1024]{0:T(1024)S(1)}, f32[1024]{0:T(1024)}, u32[]{:S(2)}) copy-start(f32[1024]{0:T(1024)} %param.9) | copy-start | bytes 12292
  93.3 92.8 %copy-start.4 = (f32[256]{0:T(256)S(1)}, f32[256]{0:T(256)}, u32[]{:S(2)}) copy-start(f32[256]{0:T(256)} %param.8) | copy-start | bytes 3076
  99.1 300.9 %copy-start = (f32[256,1024]{1,0:T(8,128)S(1)}, f32[256,1024]{1,0:T(8,128)}, u32[]{:S(2)}) copy-start(f32[256,1024]{1,0:T(8,128)} %param.7) | copy-start | bytes 3145732
  186.1 215.3 %copy-start.1 = (f32[1024]{0:T(1024)}, f32[1024]{0:T(1024)S(1)}, u32[]{:S(2)}) copy-start(f32[1024]{0:T(1024)S(1)} %multiply_add_fusion.1) | copy-start | bytes 12292
  186.1 215.2 %copy-start.2 = (f32[256]{0:T(256)}, f32[256]{0:T(256)S(1)}, u32[]{:S(2)}) copy-start(f32[256]{0:T(256)S(1)} %multiply_add_fusion.2) | copy-start | bytes 3076
Sparse Core Ops, SparseCore 0:
  11.1 82.1 all-gather.1
where the time goes:
time: 409 us; the launch traced here: 408 us
  blocking collectives  337 us (82%)
  waiting for transfers between devices  37.9 us (9%)
  between operations  16.1 us (4%)
  local copies, waits for them, and re-layouts  6.52 us (2%)
  matrix products  5.85 us (1%)
  other arithmetic  4.81 us (1%)
    psum x2, blocking collectives, shards(): lax.psum((local_scaled, local_weight), ('dp', 'mp'))  208 us
    psum x1, blocking collectives, shards(): col_total = lax.psum(jnp.sum(squares, axis=0), 'dp')  62.4 us
    all_to_all x1, blocking collectives, shards(): lax.all_to_all(activations, 'dp', split_axis=1, concat_axis=0, tiled=True)  41.7 us
    all_gather x1, waiting for transfers between devices, shards(): lax.all_gather(out_grads, 'dp', axis=0, tiled=True)  37.2 us
    psum x1, blocking collectives, shards(): row_total = lax.psum(jnp.sum(squares, axis=1), 'mp')  24.5 us
  transfers between devices with their start and end apart: 1, of which 1 were waited for; matrix products, arithmetic and copies ran while one was open for 2% of the time, Pallas kernels for 0%

commit v1 on v0

v1 whole, which is shorter than its diff:
```python
import jax
import jax.numpy as jnp
from jax import lax
from jax.sharding import Mesh, PartitionSpec as P

D = 8192
FF = 16384


BETA_TWO = 0.8
CLIP_LEVEL = 0.25
WEIGHT_DECAY = 0.1
EPSILON = 1e-06

CHIPS = ("y", "x")
ROWS = ("y", "x", "core")
SIDE = 4


def total(value, axes, count):
    sent = jnp.broadcast_to(value, (count,) + value.shape)
    return jnp.sum(lax.all_to_all(sent, axes, 0, 0), axis=0)


def shards(activations, out_grads, weight, row_moment, col_moment):
    core = lax.axis_index("core")
    features = lax.all_to_all(activations, CHIPS, split_axis=1, concat_axis=0, tiled=True)
    grads = lax.all_gather(out_grads, CHIPS, axis=0, tiled=True)
    rows = features.shape[1] // 2

    def product(half):
        return lax.dot_general(
            lax.dynamic_slice_in_dim(features, half * rows, rows, 1),
            grads,
            (((0,), (0,)), ((), ())),
            preferred_element_type=jnp.float32,
        )

    received = lax.ppermute(product(1 - core), "core", [(0, 1), (1, 0)])
    weight_grad = product(core) + received
    squares = weight_grad * weight_grad
    col_total = total(jnp.sum(squares, axis=0).reshape(8, 128), ROWS, 32).reshape(-1)
    new_cols = BETA_TWO * col_moment + (1.0 - BETA_TWO) * (col_total / D)
    col_root = lax.rsqrt(new_cols)
    by_cols = weight_grad * col_root[None, :]
    row_parts = jnp.stack(
        [
            jnp.sum(squares, axis=1),
            jnp.sum(by_cols * by_cols, axis=1),
            jnp.sum(by_cols * weight, axis=1),
            jnp.sum(weight * weight, axis=1),
        ]
    )
    row_parts = total(row_parts.reshape(8, 128), "z", 16).reshape(4, rows)
    new_rows = BETA_TWO * row_moment + (1.0 - BETA_TWO) * (row_parts[0] / FF)
    row_root = lax.rsqrt(new_rows)
    sums = jnp.stack([row_parts[1] * row_root * row_root, row_parts[2] * row_root, row_parts[3], jnp.zeros_like(row_root)])
    sums = jnp.sum(total(sums.reshape(8, 128), ROWS, 32).reshape(4, rows), axis=1)
    scaled_sum, cross_sum, weight_sum = sums[0], sums[1], sums[2]
    factor = 1.0 / jnp.maximum(1.0, jnp.sqrt(scaled_sum / (D * FF)) / CLIP_LEVEL)
    direction_sum = (
        factor * factor * scaled_sum + 2.0 * WEIGHT_DECAY * factor * cross_sum + WEIGHT_DECAY * WEIGHT_DECAY * weight_sum
    )
    trust_ratio = jnp.sqrt(weight_sum / (jnp.maximum(direction_sum, 0.0) + EPSILON))
    update = by_cols * (trust_ratio * factor * row_root)[:, None] + (trust_ratio * WEIGHT_DECAY) * weight
    return (update, new_rows, new_cols)


def solution(mesh):
    mesh = Mesh(mesh.devices.reshape(SIDE, SIDE, 2, 16), ("y", "x", "core", "z"))
    placed = (P(ROWS, None), P(ROWS, "z"), P(ROWS, "z"), P(ROWS), P("z"))
    return jax.shard_map(
        shards,
        mesh=mesh,
        in_specs=placed,
        out_specs=(P(ROWS, "z"), P(ROWS), P("z")),
        check_vma=False,
    )
```

time: 409 us -> 170 us (0.42)
  blocking collectives: 337 us -> 26 us
  waiting for transfers between devices: 37.9 us -> 85.8 us
  starting transfers between devices: 0.04 us -> 22.2 us
    psum x4 -> x0, blocking collectives: 295 us -> none  [the longest x2 208 us: shards(): lax.psum((local_scaled, local_weight), ('dp', 'mp'))]
    all_to_all x0 -> x2, waiting for transfers between devices: none -> 38.5 us  [the longest x1 26.9 us: shards(): lax.all_to_all(activations, CHIPS, split_axis=1, concat_axis=0, tiled=True)]
    all_to_all x0 -> x2, starting transfers between devices: none -> 19.6 us  [the longest x1 12 us: total(): return jnp.sum(lax.all_to_all(sent, axes, 0, 0), axis=0)]
    all_to_all x1 -> x2, blocking collectives: 41.7 us -> 26 us  [total(): return jnp.sum(lax.all_to_all(sent, axes, 0, 0), axis=0)]
    all_gather x1, waiting for transfers between devices: 37.2 us -> 44.4 us  [shards(): grads = lax.all_gather(out_grads, CHIPS, axis=0, tiled=True)]
  transfers between devices with their start and end apart: 1 -> 4, of which waited for: 1 -> 4; matrix products, arithmetic and copies ran while one was open for 2% -> 4% of each run, Pallas kernels for 0% -> 0%
where the time goes in v1:
time: 170 us
  waiting for transfers between devices  85.8 us (50%)
  blocking collectives  26 us (15%)
  starting transfers between devices  22.2 us (13%)
  between operations  17.5 us (10%)
  local copies, waits for them, and re-layouts  8.16 us (5%)
  matrix products  7.6 us (4%)
  other arithmetic  2.62 us (2%)
    all_gather x1, waiting for transfers between devices, shards(): grads = lax.all_gather(out_grads, CHIPS, axis=0, tiled=True)  44.4 us
    all_to_all x1, waiting for transfers between devices, shards(): lax.all_to_all(activations, CHIPS, split_axis=1, concat_axis=0, tiled=True)  26.9 us
    all_to_all x2, blocking collectives, total(): return jnp.sum(lax.all_to_all(sent, axes, 0, 0), axis=0)  26 us
    all_to_all x1, starting transfers between devices, total(): return jnp.sum(lax.all_to_all(sent, axes, 0, 0), axis=0)  12 us
    all_to_all x1, waiting for transfers between devices, total(): return jnp.sum(lax.all_to_all(sent, axes, 0, 0), axis=0)  11.5 us
    dot_general x2, matrix products, product(): lax.dot_general(lax.dynamic_slice_in_dim(features, half * rows, rows, 1),...  7.6 us
    all_to_all x1, starting transfers between devices, shards(): lax.all_to_all(activations, CHIPS, split_axis=1, concat_axis=0, tiled=True)  7.58 us
    unnamed x9, local copies, waits for them, and re-layouts  4.12 us
  transfers between devices with their start and end apart: 4, of which 4 were waited for; matrix products, arithmetic and copies ran while one was open for 4% of the time, Pallas kernels for 0%

profile of v1, /device:TPU:1, one launch (start us, length us, event | category | flops | bytes accessed | tf_op | source)
XLA Modules:
  0.0 169.8 jit_solution(13523868068865285289)
XLA Ops:
  7.2 0.0 all-gather.2.cloned.1.call-start
  7.2 0.7 all-gather.2.cloned.1.call-update
  7.9 4.1 %copy.10 = bf16[128,8192]{0,1:T(8,128)(2,1)} copy(bf16[128,8192]{1,0:T(8,128)(2,1)} %param.5) | data formatting | bytes 4194304 | tf_op args[0]
  12.0 7.6 %all-to-all-start = ((bf16[128,16,512]{0,2,1:T(8,128)(2,1)}), bf16[128,16,512]{0,2,1:T(8,128)(2,1)S(1)}, u32[]{:S(2)}, u32[]{:S(2)}) async-start(bf16[128,16,512]{0,2,1:T(8,128)(2,1)} %bitcast.28), calls=%async_computation | async-start | bytes 4194304 | tf_op jit(solution)/shard_map/all_to_all | solution.py:27
  19.6 26.9 %all-to-all-done = bf16[128,16,512]{0,2,1:T(8,128)(2,1)S(1)} async-done(((bf16[128,16,512]{0,2,1:T(8,128)(2,1)}), bf16[128,16,512]{0,2,1:T(8,128)(2,1)S(1)}, u32[]{:S(2)}, u32[]{:S(2)}) %all-to-all-start) | async-done | bytes 2097184 | tf_op jit(solution)/shard_map/all_to_all | solution.py:27
  46.5 2.6 %copy.11 = bf16[16,128,512]{2,1,0:T(8,128)(2,1)} copy(bf16[16,128,512]{1,2,0:T(8,128)(2,1)S(1)} %bitcast.27) | data formatting | bytes 4194304 | tf_op jit(solution)/shard_map/all_to_all | solution.py:27
  49.1 44.4 %all-gather.2.cloned.1.call-done = bf16[2048,1024]{1,0:T(8,128)(2,1)} async-done(((bf16[128,1024]{1,0:T(8,128)(2,1)}), bf16[2048,1024]{1,0:T(8,128)(2,1)}) %all-gather.2.cloned.1.call-update) | async-done | bytes 4194320 | tf_op jit(solution)/shard_map/all_gather | solution.py:28
  93.5 3.8 %fusion = f32[256,1024]{1,0:T(8,128)S(1)} fusion(bf16[2048,1024]{1,0:T(8,128)(2,1)} %all-gather.2.cloned.1.call-done, bf16[2048,512]{1,0:T(8,128)(2,1)} %bitcast.29, s32[]{:T(128)S(6)} %select_n.7), kind=kOutput, calls=%fused_computation.5 | convolution fusion | flops 1073741824 | bytes 6291460 | tf_op jit(solution)/shard_map/dot_general | solution.py:32
  97.3 2.6 %collective-permute-start = (f32[256,1024]{1,0:T(8,128)S(1)}, f32[256,1024]{1,0:T(8,128)S(1)}, u32[]{:S(2)}, u32[]{:S(2)}) collective-permute-start(f32[256,1024]{1,0:T(8,128)S(1)} %fusion), channel_id=1, source_target_pairs={{0,16},{16,0},{1,17},{17,1},{2,18},{18,2},{3,19},{19,3},{4,20},{20... | collective-permute-start | bytes 3145736 | tf_op jit(solution)/shard_map/ppermute | solution.py:39
  99.9 0.0 copy-start.2
  99.9 0.0 copy-start
  100.0 2.2 %collective-permute-done = f32[256,1024]{1,0:T(8,128)S(1)} collective-permute-done((f32[256,1024]{1,0:T(8,128)S(1)}, f32[256,1024]{1,0:T(8,128)S(1)}, u32[]{:S(2)}, u32[]{:S(2)}) %collective-permute-start) | collective-permute-done | bytes 1048608 | tf_op jit(solution)/shard_map/ppermute | solution.py:39
  102.2 3.8 %multiply_reduce_fusion.4 = (f32[1024]{0:T(1024)S(1)}, f32[256,1024]{1,0:T(8,128)S(1)}) fusion(f32[256,1024]{1,0:T(8,128)S(1)} %collective-permute-done, bf16[2048,1024]{1,0:T(8,128)(2,1)} %all-gather.2.cloned.1.call-done, bf16[2048,512]{1,0:T(8,128)(2,1)} %bitcast.30, s32[]{:T(128)S(6)} %select_n.6), kind=kOutput, calls=%fused_computation.9 | convolution fusion | flops 1074527232 | bytes 7344132 | tf_op jit(solution)/shard_map/dot_general | solution.py:32
  106.0 0.0 copy-start.3
  106.0 13.1 %all_to_all.34 = f32[32,8,128]{2,1,0:T(8,128)S(1)} all-to-all(f32[32,8,128]{2,1,0:T(8,128)S(1)} %broadcast_in_dim.11), channel_id=1, replica_groups=mesh['y'=4,'x'=4,'core'=2,'z'=16] {'y','x','core'}, dimensions={0} | all-to-all | bytes 262144 | tf_op jit(solution)/shard_map/all_to_all | solution.py:22
  119.2 0.0 copy-done.2
  119.2 0.6 fusion.5
  119.8 0.0 copy-done
  119.8 0.4 multiply_reduce_fusion.2
  120.2 0.6 broadcast_in_dim.12
  120.9 12.0 %all-to-all-start.2 = ((f32[16,8,128]{2,1,0:T(8,128)}), f32[16,8,128]{2,1,0:T(8,128)S(1)}, u32[]{:S(2)}, u32[]{:S(2)}) async-start(f32[16,8,128]{2,1,0:T(8,128)} %broadcast_in_dim.12), calls=%async_computation.2 | async-start | bytes 131072 | tf_op jit(solution)/shard_map/all_to_all | solution.py:22
  132.9 0.1 pad.3.clone
  132.9 11.5 %all-to-all-done.2 = f32[16,8,128]{2,1,0:T(8,128)S(1)} async-done(((f32[16,8,128]{2,1,0:T(8,128)}), f32[16,8,128]{2,1,0:T(8,128)S(1)}, u32[]{:S(2)}, u32[]{:S(2)}) %all-to-all-start.2) | async-done | bytes 65568 | tf_op jit(solution)/shard_map/all_to_all | solution.py:22
  144.5 0.0 copy-done.3
  144.5 0.0 copy-start.1
  144.5 0.1 maximum_maximum_fusion
  144.6 12.8 %all_to_all.35 = f32[32,8,128]{2,1,0:T(8,128)S(1)} all-to-all(f32[32,8,128]{2,1,0:T(8,128)S(1)} %broadcast_in_dim.13), channel_id=1, replica_groups=mesh['y'=4,'x'=4,'core'=2,'z'=16] {'y','x','core'}, dimensions={0} | all-to-all | bytes 262144 | tf_op jit(solution)/shard_map/all_to_all | solution.py:22
  157.5 0.1 reduce_sum.90
  157.6 0.1 reduce_sum.91
  157.7 0.1 reduce_sum.92
  157.8 0.6 fusion.6
  161.7 1.2 multiply_add_fusion
  (12 shorter events, 0.1 us)
Async XLA Ops:
  7.2 86.4 %all-gather.2.cloned.1.call-start = ((), (), s32[]{:S(2)}) async-start(), calls=%async_computation.4 | async-start | bytes 4456448 | tf_op jit(solution)/shard_map/all_gather | solution.py:28
  12.0 34.5 %all-to-all-start = ((bf16[128,16,512]{0,2,1:T(8,128)(2,1)}), bf16[128,16,512]{0,2,1:T(8,128)(2,1)S(1)}, u32[]{:S(2)}, u32[]{:S(2)}) async-start(bf16[128,16,512]{0,2,1:T(8,128)(2,1)} %bitcast.28), calls=%async_computation | async-start | bytes 4194304 | tf_op jit(solution)/shard_map/all_to_all | solution.py:27
  97.3 4.8 %collective-permute-start = (f32[256,1024]{1,0:T(8,128)S(1)}, f32[256,1024]{1,0:T(8,128)S(1)}, u32[]{:S(2)}, u32[]{:S(2)}) collective-permute-start(f32[256,1024]{1,0:T(8,128)S(1)} %fusion), channel_id=1, source_target_pairs={{0,16},{16,0},{1,17},{17,1},{2,18},{18,2},{3,19},{19,3},{4,20},{20... | collective-permute-start | bytes 3145736 | tf_op jit(solution)/shard_map/ppermute | solution.py:39
  99.9 19.2 %copy-start.2 = (f32[1024]{0:T(1024)S(1)}, f32[1024]{0:T(1024)}, u32[]{:S(2)}) copy-start(f32[1024]{0:T(1024)} %param.9) | copy-start | bytes 12292
  99.9 19.8 %copy-start = (f32[256,1024]{1,0:T(8,128)S(1)}, f32[256,1024]{1,0:T(8,128)}, u32[]{:S(2)}) copy-start(f32[256,1024]{1,0:T(8,128)} %param.7) | copy-start | bytes 3145732
  106.0 38.5 %copy-start.3 = (f32[256]{0:T(256)S(1)}, f32[256]{0:T(256)}, u32[]{:S(2)}) copy-start(f32[256]{0:T(256)} %param.8) | copy-start | bytes 3076
  120.9 23.6 %all-to-all-start.2 = ((f32[16,8,128]{2,1,0:T(8,128)}), f32[16,8,128]{2,1,0:T(8,128)S(1)}, u32[]{:S(2)}, u32[]{:S(2)}) async-start(f32[16,8,128]{2,1,0:T(8,128)} %broadcast_in_dim.12), calls=%async_computation.2 | async-start | bytes 131072 | tf_op jit(solution)/shard_map/all_to_all | solution.py:22
  144.5 18.4 %copy-start.1 = (f32[256]{0:T(256)}, f32[256]{0:T(256)S(1)}, u32[]{:S(2)}) copy-start(f32[256]{0:T(256)S(1)} %get-tuple-element.8) | copy-start | bytes 3076
Sparse Core Ops, SparseCore 0:
  11.0 82.4 all-gather.1

commit v2 on v1

--- a/solution.py
+++ b/solution.py
@@ -1,6 +1,10 @@
+import functools
+
 import jax
 import jax.numpy as jnp
 from jax import lax
+from jax.experimental import pallas as pl
+from jax.experimental.pallas import tpu as pltpu
 from jax.sharding import Mesh, PartitionSpec as P
 
 D = 8192
@@ -15,6 +19,9 @@
 CHIPS = ("y", "x")
 ROWS = ("y", "x", "core")
 SIDE = 4
+LAYERS = 16
+TOKENS = 128
+ROW_BLOCK = 256
 
 
 def total(value, axes, count):
@@ -22,22 +29,100 @@
     return jnp.sum(lax.all_to_all(sent, axes, 0, 0), axis=0)
 
 
+def device(y, x, core):
+    return ((y % SIDE) * SIDE + x % SIDE) * 2 + core
+
+
+def along(value, step, stage):
+    pairs = []
+    for y in range(SIDE):
+        for x in range(SIDE):
+            for core in range(2):
+                on_x = core == stage
+                to = device(y, x + step, core) if on_x else device(y + step, x, core)
+                pairs.append((device(y, x, core), to))
+    return lax.ppermute(value, ROWS, pairs)
+
+
+def next_layer(value):
+    pairs = [(i, (i + 1) % LAYERS) for i in range(LAYERS)]
+    pairs += [(LAYERS + i, LAYERS + (i - 1) % LAYERS) for i in range(LAYERS)]
+    return lax.ppermute(value, ("core", "z"), pairs)
+
+
+def product_kernel(place, first, second, *refs):
+    count = SIDE * SIDE
+    grads, (out, first_buf, second_buf, grad_buf, turned, sems) = refs[:-6], refs[-6:]
+    copies = [pltpu.make_async_copy(first, first_buf, sems.at[0]), pltpu.make_async_copy(second, second_buf, sems.at[1])]
+    row = 0
+    for i, grad in enumerate(grads):
+        copies.append(pltpu.make_async_copy(grad, grad_buf.at[pl.ds(row, grad.shape[0])], sems.at[2 + i]))
+        row += grad.shape[0]
+    for copy in copies:
+        copy.start()
+    half = TOKENS // 2
+    y, x, core, flipped = place[0], place[1], place[2], place[3] == 1
+    column = pl.multiple_of(place[4], ROW_BLOCK)
+    copies[0].wait()
+    copies[1].wait()
+    for i in range(count):
+        j, k = i // SIDE, i % SIDE
+        dx, dy = jnp.where(core == 0, k, j), jnp.where(core == 0, j, k)
+        chip = ((y - dy) & (SIDE - 1)) * SIDE + ((x - dx) & (SIDE - 1))
+        mine = first_buf[chip, :, pl.ds(column, ROW_BLOCK)]
+        other = second_buf[chip, :, pl.ds(column, ROW_BLOCK)]
+        low = jnp.where(flipped, other, mine)
+        high = jnp.where(flipped, mine, other)
+        turned[:, i * TOKENS : (i + 1) * TOKENS] = jnp.concatenate([low, high], axis=0).T
+    for copy in copies[2:]:
+        copy.wait()
+
+    @pl.loop(0, out.shape[1] // 256)
+    def _(n):
+        columns = pl.ds(pl.multiple_of(n * 256, 256), 256)
+        out[:, columns] = jnp.dot(turned[...], grad_buf[:, columns], preferred_element_type=jnp.float32)
+
+
+def product(place, first, second, grads):
+    depth = sum(g.shape[0] for g in grads)
+    width = grads[0].shape[1]
+    anywhere = pl.BlockSpec(memory_space=pl.ANY)
+    return pl.pallas_call(
+        product_kernel,
+        out_shape=jax.ShapeDtypeStruct((ROW_BLOCK, width), jnp.float32),
+        in_specs=[pl.BlockSpec(memory_space=pltpu.SMEM)] + [anywhere] * (2 + len(grads)),
+        out_specs=pl.BlockSpec(memory_space=pltpu.VMEM),
+        scratch_shapes=[
+            pltpu.VMEM(first.shape, jnp.bfloat16),
+            pltpu.VMEM(first.shape, jnp.bfloat16),
+            pltpu.VMEM((depth, width), jnp.bfloat16),
+            pltpu.VMEM((ROW_BLOCK, depth), jnp.bfloat16),
+            pltpu.SemaphoreType.DMA((2 + len(grads),)),
+        ],
+        compiler_params=pltpu.CompilerParams(vmem_limit_bytes=24 * 2**20),
+        cost_estimate=pl.CostEstimate(
+            flops=2 * ROW_BLOCK * depth * width, bytes_accessed=8 * 2**20, transcendentals=0
+        ),
+    )(place, first, second, *grads)
+
+
 def shards(activations, out_grads, weight, row_moment, col_moment):
-    core = lax.axis_index("core")
-    features = lax.all_to_all(activations, CHIPS, split_axis=1, concat_axis=0, tiled=True)
-    grads = lax.all_gather(out_grads, CHIPS, axis=0, tiled=True)
-    rows = features.shape[1] // 2
-
-    def product(half):
-        return lax.dot_general(
-            lax.dynamic_slice_in_dim(features, half * rows, rows, 1),
-            grads,
-            (((0,), (0,)), ((), ())),
-            preferred_element_type=jnp.float32,
-        )
-
-    received = lax.ppermute(product(1 - core), "core", [(0, 1), (1, 0)])
-    weight_grad = product(core) + received
+    y, x, core, layer = (lax.axis_index(name) for name in ("y", "x", "core", "z"))
+    half = layer % 2
+    sent = lax.dynamic_slice_in_dim(activations, half * (TOKENS // 2), TOKENS // 2, 0)
+    sent = sent.reshape(TOKENS // 2, SIDE * SIDE, 2 * ROW_BLOCK)
+    first = lax.all_to_all(sent, CHIPS, split_axis=1, concat_axis=0, tiled=True)
+    first = first.reshape(SIDE * SIDE, TOKENS // 2, 2 * ROW_BLOCK)
+    second = next_layer(first)
+    line = [out_grads] + [along(out_grads, k, 0) for k in range(1, SIDE)]
+    line = jnp.concatenate(line, axis=0)
+    grads = [line] + [along(line, j, 1) for j in range(1, SIDE)]
+    place = lambda which: jnp.stack([y, x, core, half, which * ROW_BLOCK])
+    theirs = product(place(1 - core), first, second, grads)
+    received = lax.ppermute(theirs, "core", [(0, 1), (1, 0)])
+    mine = product(place(core), first, second, grads)
+    weight_grad = mine + received
+    rows = ROW_BLOCK
     squares = weight_grad * weight_grad
     col_total = total(jnp.sum(squares, axis=0).reshape(8, 128), ROWS, 32).reshape(-1)
     new_cols = BETA_TWO * col_moment + (1.0 - BETA_TWO) * (col_total / D)
@@ -67,7 +152,7 @@
 
 
 def solution(mesh):
-    mesh = Mesh(mesh.devices.reshape(SIDE, SIDE, 2, 16), ("y", "x", "core", "z"))
+    mesh = Mesh(mesh.devices.reshape(SIDE, SIDE, 2, LAYERS), ("y", "x", "core", "z"))
     placed = (P(ROWS, None), P(ROWS, "z"), P(ROWS, "z"), P(ROWS), P("z"))
     return jax.shard_map(
         shards,

time: 170 us -> 144 us (0.85)
  waiting for transfers between devices: 85.8 us -> 32.6 us
  starting transfers between devices: 22.2 us -> 58 us
  between operations: 17.5 us -> 4.17 us
  Pallas kernels: 0 us -> 11 us
  matrix products: 7.6 us -> 0 us
  other arithmetic: 2.62 us -> 6.5 us
  blocking collectives: 26 us -> 23.9 us
    all_gather x1 -> x0, waiting for transfers between devices: 44.4 us -> none  [shards(): grads = lax.all_gather(out_grads, CHIPS, axis=0, tiled=True)]
    ppermute x1 -> x8, starting transfers between devices: 2.58 us -> 36.5 us  [the longest x6 20.4 us: along(): return lax.ppermute(value, ROWS, pairs)]
    all_to_all x1, waiting for transfers between devices: 26.9 us -> 0.01 us  [shards(): first = lax.all_to_all(sent, CHIPS, split_axis=1, concat_axis=0, tiled=True)]
    ppermute x1 -> x8, waiting for transfers between devices: 2.24 us -> 21.1 us  [the longest x6 19.5 us: along(): return lax.ppermute(value, ROWS, pairs)]
    pallas_call x0 -> x2, Pallas kernels: none -> 11 us  [product(): pl.pallas_call(product_kernel, out_shape=jax.ShapeDtypeStruct((ROW_BLOCK,...]
    dot_general x2 -> x0, matrix products: 7.6 us -> none  [product(): lax.dot_general(lax.dynamic_slice_in_dim(features, half * rows, rows, 1),...]
    all_to_all x1 -> x0, local copies, waits for them, and re-layouts: 2.6 us -> none  [shards(): lax.all_to_all(activations, CHIPS, split_axis=1, concat_axis=0, tiled=True)]
    all_to_all x2, blocking collectives: 26 us -> 23.9 us  [total(): return jnp.sum(lax.all_to_all(sent, axes, 0, 0), axis=0)]
  transfers between devices with their start and end apart: 4 -> 10, of which waited for: 4 -> 6; matrix products, arithmetic and copies ran while one was open for 4% -> 2% of each run, Pallas kernels for 0% -> 3%
where the time goes in v2:
time: 144 us; the launch traced here: 143 us
  starting transfers between devices  58 us (40%)
  waiting for transfers between devices  32.6 us (23%)
  blocking collectives  23.9 us (17%)
  Pallas kernels  11 us (8%)
  local copies, waits for them, and re-layouts  7.28 us (5%)
  other arithmetic  6.5 us (5%)
  between operations  4.17 us (3%)
    all_to_all x2, blocking collectives, total(): return jnp.sum(lax.all_to_all(sent, axes, 0, 0), axis=0)  23.9 us
    ppermute x6, starting transfers between devices, along(): return lax.ppermute(value, ROWS, pairs)  20.4 us
    ppermute x6, waiting for transfers between devices, along(): return lax.ppermute(value, ROWS, pairs)  19.5 us
    all_to_all x1, starting transfers between devices, total(): return jnp.sum(lax.all_to_all(sent, axes, 0, 0), axis=0)  14 us
    all_to_all x1, waiting for transfers between devices, total(): return jnp.sum(lax.all_to_all(sent, axes, 0, 0), axis=0)  11.5 us
    ppermute x1, starting transfers between devices, next_layer(): return lax.ppermute(value, ('core', 'z'), pairs)  11.1 us
    pallas_call x2, Pallas kernels, product(): pl.pallas_call(product_kernel, out_shape=jax.ShapeDtypeStruct((ROW_BLOCK,...  11 us
    all_to_all x1, starting transfers between devices, shards(): first = lax.all_to_all(sent, CHIPS, split_axis=1, concat_axis=0, tiled=True)  7.58 us
  transfers between devices with their start and end apart: 10, of which 6 were waited for; matrix products, arithmetic and copies ran while one was open for 2% of the time, Pallas kernels for 3%

profile of v2, /device:TPU:1, one launch (start us, length us, event | category | flops | bytes accessed | tf_op | source)
XLA Modules:
  0.0 143.4 jit_solution(617953835712205662)
XLA Ops:
  0.7 1.6 %copy-done = bf16[128,8192]{1,0:T(8,128)(2,1)S(1)} copy-done((bf16[128,8192]{1,0:T(8,128)(2,1)S(1)}, bf16[128,8192]{1,0:T(8,128)(2,1)}, u32[]{:S(2)}) %copy-start) | copy-done | bytes 2097176
  2.3 1.1 copy.12
  3.4 7.6 %all-to-all-start = ((bf16[64,16,512]{2,0,1:T(8,128)(2,1)}), bf16[64,16,512]{2,0,1:T(8,128)(2,1)S(1)}, u32[]{:S(2)}, u32[]{:S(2)}) async-start(bf16[64,16,512]{2,0,1:T(8,128)(2,1)} %bitcast.41), calls=%async_computation | async-start | bytes 2097152 | tf_op jit(solution)/shard_map/all_to_all | solution.py:114
  11.0 3.3 %collective-permute-start.1 = (bf16[128,1024]{1,0:T(8,128)(2,1)S(1)}, bf16[128,1024]{1,0:T(8,128)(2,1)S(1)}, u32[]{:S(2)}, u32[]{:S(2)}) collective-permute-start(bf16[128,1024]{1,0:T(8,128)(2,1)S(1)} %copy-done.1), channel_id=1, source_target_pairs={{0,32},{16,144},{32,64},{48,176},{64,96},{80,208},{96,0},{112,240}... | collective-permute-start | bytes 786440 | tf_op jit(solution)/shard_map/ppermute | solution.py:44
  14.3 4.3 %collective-permute-start.2 = (bf16[128,1024]{1,0:T(8,128)(2,1)S(1)}, bf16[128,1024]{1,0:T(8,128)(2,1)S(1)}, u32[]{:S(2)}, u32[]{:S(2)}) collective-permute-start(bf16[128,1024]{1,0:T(8,128)(2,1)S(1)} %copy-done.1), channel_id=1, source_target_pairs={{0,64},{16,272},{32,96},{48,304},{64,0},{80,336},{96,32},{112,368}... | collective-permute-start | bytes 786440 | tf_op jit(solution)/shard_map/ppermute | solution.py:44
  18.6 3.1 %collective-permute-start.3 = (bf16[128,1024]{1,0:T(8,128)(2,1)S(1)}, bf16[128,1024]{1,0:T(8,128)(2,1)S(1)}, u32[]{:S(2)}, u32[]{:S(2)}) collective-permute-start(bf16[128,1024]{1,0:T(8,128)(2,1)S(1)} %copy-done.1), channel_id=1, source_target_pairs={{0,96},{16,400},{32,0},{48,432},{64,32},{80,464},{96,64},{112,496}... | collective-permute-start | bytes 786440 | tf_op jit(solution)/shard_map/ppermute | solution.py:44
  21.7 0.7 constant_dynamic-update-slice_fusion.3
  22.4 6.7 %collective-permute-done.1 = bf16[128,1024]{1,0:T(8,128)(2,1)S(1)} collective-permute-done((bf16[128,1024]{1,0:T(8,128)(2,1)S(1)}, bf16[128,1024]{1,0:T(8,128)(2,1)S(1)}, u32[]{:S(2)}, u32[]{:S(2)}) %collective-permute-start.1) | collective-permute-done | bytes 262176 | tf_op jit(solution)/shard_map/ppermute | solution.py:44
  29.2 0.7 constant_dynamic-update-slice_fusion.2
  29.9 2.7 %collective-permute-done.2 = bf16[128,1024]{1,0:T(8,128)(2,1)S(1)} collective-permute-done((bf16[128,1024]{1,0:T(8,128)(2,1)S(1)}, bf16[128,1024]{1,0:T(8,128)(2,1)S(1)}, u32[]{:S(2)}, u32[]{:S(2)}) %collective-permute-start.2) | collective-permute-done | bytes 262176 | tf_op jit(solution)/shard_map/ppermute | solution.py:44
  32.6 0.7 constant_dynamic-update-slice_fusion.1
  33.3 0.7 constant_dynamic-update-slice_fusion.refs_0_
  34.0 2.4 %collective-permute-start.4 = (bf16[512,1024]{1,0:T(8,128)(2,1)}, bf16[512,1024]{1,0:T(8,128)(2,1)}, u32[]{:S(2)}, u32[]{:S(2)}) collective-permute-start(bf16[512,1024]{1,0:T(8,128)(2,1)} %constant_dynamic-update-slice_fusion.refs_0_), channel_id=1, source_target_pairs={{0,128},{16,48},{32,160},{48,80},{64,192},{80,112},{96,224},{112,1... | collective-permute-start | bytes 3145736 | tf_op jit(solution)/shard_map/ppermute | solution.py:44
  36.5 4.3 %collective-permute-start.5 = (bf16[512,1024]{1,0:T(8,128)(2,1)}, bf16[512,1024]{1,0:T(8,128)(2,1)}, u32[]{:S(2)}, u32[]{:S(2)}) collective-permute-start(bf16[512,1024]{1,0:T(8,128)(2,1)} %constant_dynamic-update-slice_fusion.refs_0_), channel_id=1, source_target_pairs={{0,256},{16,80},{32,288},{48,112},{64,320},{80,16},{96,352},{112,4... | collective-permute-start | bytes 3145736 | tf_op jit(solution)/shard_map/ppermute | solution.py:44
  40.8 3.0 %collective-permute-start.6 = (bf16[512,1024]{1,0:T(8,128)(2,1)}, bf16[512,1024]{1,0:T(8,128)(2,1)}, u32[]{:S(2)}, u32[]{:S(2)}) collective-permute-start(bf16[512,1024]{1,0:T(8,128)(2,1)} %constant_dynamic-update-slice_fusion.refs_0_), channel_id=1, source_target_pairs={{0,384},{16,112},{32,416},{48,16},{64,448},{80,48},{96,480},{112,8... | collective-permute-start | bytes 3145736 | tf_op jit(solution)/shard_map/ppermute | solution.py:44
  43.8 11.1 %collective-permute-start = (bf16[16,64,512]{2,1,0:T(8,128)(2,1)S(1)}, bf16[16,64,512]{2,1,0:T(8,128)(2,1)}, u32[]{:S(2)}, u32[]{:S(2)}) collective-permute-start(bf16[16,64,512]{2,1,0:T(8,128)(2,1)S(1)} %bitcast.37), channel_id=1, source_target_pairs={{0,1},{1,2},{2,3},{3,4},{4,5},{5,6},{6,7},{7,8},{8,9},{9,10},{10,1... | collective-permute-start | bytes 3145736 | tf_op jit(solution)/shard_map/ppermute | solution.py:50
  55.1 7.8 %collective-permute-done.5.refs_2_ = bf16[512,1024]{1,0:T(8,128)(2,1)} collective-permute-done((bf16[512,1024]{1,0:T(8,128)(2,1)}, bf16[512,1024]{1,0:T(8,128)(2,1)}, u32[]{:S(2)}, u32[]{:S(2)}) %collective-permute-start.5) | collective-permute-done | bytes 1048608 | tf_op jit(solution)/shard_map/ppermute | solution.py:44
  62.9 2.3 %collective-permute-done.6.refs_3_ = bf16[512,1024]{1,0:T(8,128)(2,1)} collective-permute-done((bf16[512,1024]{1,0:T(8,128)(2,1)}, bf16[512,1024]{1,0:T(8,128)(2,1)}, u32[]{:S(2)}, u32[]{:S(2)}) %collective-permute-start.6) | collective-permute-done | bytes 1048608 | tf_op jit(solution)/shard_map/ppermute | solution.py:44
  65.2 1.5 %collective-permute-done.second = bf16[16,64,512]{2,1,0:T(8,128)(2,1)} collective-permute-done((bf16[16,64,512]{2,1,0:T(8,128)(2,1)S(1)}, bf16[16,64,512]{2,1,0:T(8,128)(2,1)}, u32[]{:S(2)}, u32[]{:S(2)}) %collective-permute-start) | collective-permute-done | bytes 1048608 | tf_op jit(solution)/shard_map/ppermute | solution.py:50
  66.7 6.0 %shard_map.77 = f32[256,1024]{1,0:T(8,128)} custom-call(s32[5]{0:T(128)S(1)} %stack.59.place, bf16[16,64,512]{2,1,0:T(8,128)(2,1)S(1)} %bitcast.38, bf16[16,64,512]{2,1,0:T(8,128)(2,1)} %collective-permute-done.second, bf16[512,1024]{1,0:T(8,128)(2,1)} %constant_dynamic-update-slice_fusion.refs_0_, bf16[512,1024]{1,0:T(8,128)(2,1)} %collective-permute-done.4.refs_1_, ...), custom_call_target="tpu_custom_call" | custom-call | flops 1073741824 | bytes 8388608 | tf_op jit(solution)/shard_map/pallas_call | solution.py:90
  72.7 4.9 %collective-permute-start.7 = (f32[256,1024]{1,0:T(8,128)}, f32[256,1024]{1,0:T(8,128)}, u32[]{:S(2)}, u32[]{:S(2)}) collective-permute-start(f32[256,1024]{1,0:T(8,128)} %shard_map.77), channel_id=1, source_target_pairs={{0,16},{16,0},{1,17},{17,1},{2,18},{18,2},{3,19},{19,3},{4,20},{20... | collective-permute-start | bytes 3145736 | tf_op jit(solution)/shard_map/ppermute | solution.py:122
  77.7 5.0 %shard_map.76 = f32[256,1024]{1,0:T(8,128)S(1)} custom-call(s32[5]{0:T(128)S(1)} %stack.57.place, bf16[16,64,512]{2,1,0:T(8,128)(2,1)S(1)} %bitcast.39, bf16[16,64,512]{2,1,0:T(8,128)(2,1)} %collective-permute-done.second, bf16[512,1024]{1,0:T(8,128)(2,1)} %constant_dynamic-update-slice_fusion.refs_0_, bf16[512,1024]{1,0:T(8,128)(2,1)} %collective-permute-done.4.refs_1_, ...), custom_call_target="tpu_custom_call" | custom-call | flops 1073741824 | bytes 8388608 | tf_op jit(solution)/shard_map/pallas_call | solution.py:90
  82.8 1.4 multiply_reduce_fusion.4
  84.2 11.0 %all_to_all.30 = f32[32,8,128]{2,1,0:T(8,128)S(1)} all-to-all(f32[32,8,128]{2,1,0:T(8,128)S(1)} %broadcast_in_dim.11), channel_id=1, replica_groups=mesh['y'=4,'x'=4,'core'=2,'z'=16] {'y','x','core'}, dimensions={0} | all-to-all | bytes 262144 | tf_op jit(solution)/shard_map/all_to_all | solution.py:29
  95.3 0.6 fusion
  95.9 1.6 %multiply_reduce_fusion.2 = (f32[256]{0:T(256)S(1)}, f32[256]{0:T(256)S(1)}, f32[256]{0:T(256)S(1)}, f32[256]{0:T(256)S(1)}) fusion(f32[256,1024]{1,0:T(8,128)S(1)} %get-tuple-element.12, f32[1024]{0:T(1024)S(1)} %get-tuple-element.9, f32[256,1024]{1,0:T(8,128)} %param.7), kind=kLoop, calls=%fused_computation.4 | loop fusion | flops 2358272 | bytes 2105344 | tf_op jit(solution)/shard_map/reduce_sum | solution.py:134
  97.5 0.6 broadcast_in_dim.12
  98.2 14.0 %all-to-all-start.2 = ((f32[16,8,128]{2,1,0:T(8,128)}), f32[16,8,128]{2,1,0:T(8,128)S(1)}, u32[]{:S(2)}, u32[]{:S(2)}) async-start(f32[16,8,128]{2,1,0:T(8,128)} %broadcast_in_dim.12), calls=%async_computation.2 | async-start | bytes 131072 | tf_op jit(solution)/shard_map/all_to_all | solution.py:29
  112.2 11.5 %all-to-all-done.2 = f32[16,8,128]{2,1,0:T(8,128)S(1)} async-done(((f32[16,8,128]{2,1,0:T(8,128)}), f32[16,8,128]{2,1,0:T(8,128)S(1)}, u32[]{:S(2)}, u32[]{:S(2)}) %all-to-all-start.2) | async-done | bytes 65568 | tf_op jit(solution)/shard_map/all_to_all | solution.py:29
  123.9 12.8 %all_to_all.31 = f32[32,8,128]{2,1,0:T(8,128)S(1)} all-to-all(f32[32,8,128]{2,1,0:T(8,128)S(1)} %broadcast_in_dim.13), channel_id=1, replica_groups=mesh['y'=4,'x'=4,'core'=2,'z'=16] {'y','x','core'}, dimensions={0} | all-to-all | bytes 262144 | tf_op jit(solution)/shard_map/all_to_all | solution.py:29
  137.1 0.6 fusion.1
  141.0 2.4 %multiply_add_fusion = f32[256,1024]{1,0:T(8,128)} fusion(f32[256,1024]{1,0:T(8,128)} %param.7, f32[256,1024]{1,0:T(8,128)S(1)} %get-tuple-element.12, f32[]{:T(128)S(6)} %mul.137, f32[256]{0:T(256)S(1)} %rsqrt_multiply_fusion, f32[1024]{0:T(1024)S(1)} %get-tuple-element.9), kind=kLoop, calls=%fused_computation.1 | loop fusion | flops 1048576 | bytes 3150852 | tf_op jit(solution)/shard_map/add | solution.py:150
  (32 shorter events, 0.9 us)
Async XLA Ops:
  0.6 1.6 %copy-start = (bf16[128,8192]{1,0:T(8,128)(2,1)S(1)}, bf16[128,8192]{1,0:T(8,128)(2,1)}, u32[]{:S(2)}) copy-start(bf16[128,8192]{1,0:T(8,128)(2,1)} %param.5) | copy-start | bytes 6291460
  2.3 8.7 %copy-start.1 = (bf16[128,1024]{1,0:T(8,128)(2,1)S(1)}, bf16[128,1024]{1,0:T(8,128)(2,1)}, u32[]{:S(2)}) copy-start(bf16[128,1024]{1,0:T(8,128)(2,1)} %param.6) | copy-start | bytes 786436
  3.4 40.4 %all-to-all-start = ((bf16[64,16,512]{2,0,1:T(8,128)(2,1)}), bf16[64,16,512]{2,0,1:T(8,128)(2,1)S(1)}, u32[]{:S(2)}, u32[]{:S(2)}) async-start(bf16[64,16,512]{2,0,1:T(8,128)(2,1)} %bitcast.41), calls=%async_computation | async-start | bytes 2097152 | tf_op jit(solution)/shard_map/all_to_all | solution.py:114
  11.0 18.2 %collective-permute-start.1 = (bf16[128,1024]{1,0:T(8,128)(2,1)S(1)}, bf16[128,1024]{1,0:T(8,128)(2,1)S(1)}, u32[]{:S(2)}, u32[]{:S(2)}) collective-permute-start(bf16[128,1024]{1,0:T(8,128)(2,1)S(1)} %copy-done.1), channel_id=1, source_target_pairs={{0,32},{16,144},{32,64},{48,176},{64,96},{80,208},{96,0},{112,240}... | collective-permute-start | bytes 786440 | tf_op jit(solution)/shard_map/ppermute | solution.py:44
  14.3 18.3 %collective-permute-start.2 = (bf16[128,1024]{1,0:T(8,128)(2,1)S(1)}, bf16[128,1024]{1,0:T(8,128)(2,1)S(1)}, u32[]{:S(2)}, u32[]{:S(2)}) collective-permute-start(bf16[128,1024]{1,0:T(8,128)(2,1)S(1)} %copy-done.1), channel_id=1, source_target_pairs={{0,64},{16,272},{32,96},{48,304},{64,0},{80,336},{96,32},{112,368}... | collective-permute-start | bytes 786440 | tf_op jit(solution)/shard_map/ppermute | solution.py:44
  18.6 14.7 %collective-permute-start.3 = (bf16[128,1024]{1,0:T(8,128)(2,1)S(1)}, bf16[128,1024]{1,0:T(8,128)(2,1)S(1)}, u32[]{:S(2)}, u32[]{:S(2)}) collective-permute-start(bf16[128,1024]{1,0:T(8,128)(2,1)S(1)} %copy-done.1), channel_id=1, source_target_pairs={{0,96},{16,400},{32,0},{48,432},{64,32},{80,464},{96,64},{112,496}... | collective-permute-start | bytes 786440 | tf_op jit(solution)/shard_map/ppermute | solution.py:44
  34.0 21.0 %collective-permute-start.4 = (bf16[512,1024]{1,0:T(8,128)(2,1)}, bf16[512,1024]{1,0:T(8,128)(2,1)}, u32[]{:S(2)}, u32[]{:S(2)}) collective-permute-start(bf16[512,1024]{1,0:T(8,128)(2,1)} %constant_dynamic-update-slice_fusion.refs_0_), channel_id=1, source_target_pairs={{0,128},{16,48},{32,160},{48,80},{64,192},{80,112},{96,224},{112,1... | collective-permute-start | bytes 3145736 | tf_op jit(solution)/shard_map/ppermute | solution.py:44
  36.5 26.4 %collective-permute-start.5 = (bf16[512,1024]{1,0:T(8,128)(2,1)}, bf16[512,1024]{1,0:T(8,128)(2,1)}, u32[]{:S(2)}, u32[]{:S(2)}) collective-permute-start(bf16[512,1024]{1,0:T(8,128)(2,1)} %constant_dynamic-update-slice_fusion.refs_0_), channel_id=1, source_target_pairs={{0,256},{16,80},{32,288},{48,112},{64,320},{80,16},{96,352},{112,4... | collective-permute-start | bytes 3145736 | tf_op jit(solution)/shard_map/ppermute | solution.py:44
  40.8 24.4 %collective-permute-start.6 = (bf16[512,1024]{1,0:T(8,128)(2,1)}, bf16[512,1024]{1,0:T(8,128)(2,1)}, u32[]{:S(2)}, u32[]{:S(2)}) collective-permute-start(bf16[512,1024]{1,0:T(8,128)(2,1)} %constant_dynamic-update-slice_fusion.refs_0_), channel_id=1, source_target_pairs={{0,384},{16,112},{32,416},{48,16},{64,448},{80,48},{96,480},{112,8... | collective-permute-start | bytes 3145736 | tf_op jit(solution)/shard_map/ppermute | solution.py:44
  43.8 22.9 %collective-permute-start = (bf16[16,64,512]{2,1,0:T(8,128)(2,1)S(1)}, bf16[16,64,512]{2,1,0:T(8,128)(2,1)}, u32[]{:S(2)}, u32[]{:S(2)}) collective-permute-start(bf16[16,64,512]{2,1,0:T(8,128)(2,1)S(1)} %bitcast.37), channel_id=1, source_target_pairs={{0,1},{1,2},{2,3},{3,4},{4,5},{5,6},{6,7},{7,8},{8,9},{9,10},{10,1... | collective-permute-start | bytes 3145736 | tf_op jit(solution)/shard_map/ppermute | solution.py:50
  72.7 10.1 %collective-permute-start.7 = (f32[256,1024]{1,0:T(8,128)}, f32[256,1024]{1,0:T(8,128)}, u32[]{:S(2)}, u32[]{:S(2)}) collective-permute-start(f32[256,1024]{1,0:T(8,128)} %shard_map.77), channel_id=1, source_target_pairs={{0,16},{16,0},{1,17},{17,1},{2,18},{18,2},{3,19},{19,3},{4,20},{20... | collective-permute-start | bytes 3145736 | tf_op jit(solution)/shard_map/ppermute | solution.py:122
  82.7 12.5 %copy-start.3 = (f32[1024]{0:T(1024)S(1)}, f32[1024]{0:T(1024)}, u32[]{:S(2)}) copy-start(f32[1024]{0:T(1024)} %param.9) | copy-start | bytes 12292
  84.2 39.6 %copy-start.4 = (f32[256]{0:T(256)S(1)}, f32[256]{0:T(256)}, u32[]{:S(2)}) copy-start(f32[256]{0:T(256)} %param.8) | copy-start | bytes 3076
  98.2 25.6 %all-to-all-start.2 = ((f32[16,8,128]{2,1,0:T(8,128)}), f32[16,8,128]{2,1,0:T(8,128)S(1)}, u32[]{:S(2)}, u32[]{:S(2)}) async-start(f32[16,8,128]{2,1,0:T(8,128)} %broadcast_in_dim.12), calls=%async_computation.2 | async-start | bytes 131072 | tf_op jit(solution)/shard_map/all_to_all | solution.py:29
  123.8 19.6 %copy-start.2 = (f32[256]{0:T(256)}, f32[256]{0:T(256)S(1)}, u32[]{:S(2)}) copy-start(f32[256]{0:T(256)S(1)} %get-tuple-element.8) | copy-start | bytes 3076

commit v3 on v0

v3 whole, which is shorter than its diff:
```python
import functools

import jax
import jax.numpy as jnp
from jax import lax
from jax.experimental import pallas as pl
from jax.experimental.pallas import tpu as pltpu
from jax.sharding import Mesh, PartitionSpec as P

D = 8192
FF = 16384


BETA_TWO = 0.8
CLIP_LEVEL = 0.25
WEIGHT_DECAY = 0.1
EPSILON = 1e-06

CHIPS = ("y", "x")
ROWS = ("y", "x", "core")
SIDE = 4
COUNT = SIDE * SIDE
LAYERS = 16
DEVICES = 2 * COUNT
TOKENS = 128
HALF = TOKENS // 2
GROUP = SIDE * TOKENS
ROW_BLOCK = 256
WIDTH = 1024
LANES = 128
TILE = (8, LANES)

ANYWHERE = pl.BlockSpec(memory_space=pl.ANY)
WHOLE = pl.BlockSpec(memory_space=pltpu.VMEM)
SCALARS = pl.BlockSpec(memory_space=pltpu.SMEM)
PARAMS = pltpu.CompilerParams(vmem_limit_bytes=16 * 2**20)


def shape(*dims, dtype=jnp.float32):
    return jax.ShapeDtypeStruct(dims, dtype)


def cost(flops, bytes_accessed):
    return pl.CostEstimate(flops=flops, bytes_accessed=bytes_accessed, transcendentals=0)


def device(y, x, core):
    return ((y % SIDE) * SIDE + x % SIDE) * 2 + core


def along(value, step, stage):
    pairs = []
    for y in range(SIDE):
        for x in range(SIDE):
            for core in range(2):
                on_x = core == stage
                to = device(y, x + step, core) if on_x else device(y + step, x, core)
                pairs.append((device(y, x, core), to))
    return lax.ppermute(value, ROWS, pairs)


def next_layer(value):
    pairs = [(i, (i + 1) % LAYERS) for i in range(LAYERS)]
    pairs += [(LAYERS + i, LAYERS + (i - 1) % LAYERS) for i in range(LAYERS)]
    return lax.ppermute(value, ("core", "z"), pairs)


def exchange(tiles, axes):
    return lax.all_to_all(tiles, axes, 0, 0)


def pack_kernel(place, source, out, sems):
    rows = pl.ds(pl.multiple_of(place[3] * HALF, HALF), HALF)
    copies = [
        pltpu.make_async_copy(source.at[rows, pl.ds(i * 2 * ROW_BLOCK, 2 * ROW_BLOCK)], out.at[i], sems.at[i])
        for i in range(COUNT)
    ]
    for copy in copies:
        copy.start()
    for copy in copies:
        copy.wait()


def pack(place, activations):
    return pl.pallas_call(
        pack_kernel,
        out_shape=shape(COUNT, HALF, 2 * ROW_BLOCK, dtype=jnp.bfloat16),
        in_specs=[SCALARS, ANYWHERE],
        out_specs=ANYWHERE,
        scratch_shapes=[pltpu.SemaphoreType.DMA((COUNT,))],
        compiler_params=PARAMS,
        cost_estimate=cost(0, 2**21),
    )(place, activations)


def join_kernel(*refs):
    blocks, out, sems = refs[:-2], refs[-2], refs[-1]
    copies = [
        pltpu.make_async_copy(block, out.at[pl.ds(i * TOKENS, TOKENS)], sems.at[i]) for i, block in enumerate(blocks)
    ]
    for copy in copies:
        copy.start()
    for copy in copies:
        copy.wait()


def join(blocks):
    return pl.pallas_call(
        join_kernel,
        out_shape=shape(GROUP, WIDTH, dtype=jnp.bfloat16),
        in_specs=[ANYWHERE] * len(blocks),
        out_specs=ANYWHERE,
        scratch_shapes=[pltpu.SemaphoreType.DMA((len(blocks),))],
        compiler_params=PARAMS,
        cost_estimate=cost(0, 2**21),
    )(*blocks)


def turn_kernel(place, part, out):
    y, x, core = place[0], place[1], place[2]

    def block(i):
        j, k = i // SIDE, i % SIDE
        dx, dy = jnp.where(core == 0, k, j), jnp.where(core == 0, j, k)
        return part[((y - dy) & (SIDE - 1)) * SIDE + ((x - dx) & (SIDE - 1))]

    for i in range(0, COUNT, 2):
        out[:, i * HALF : (i + 2) * HALF] = jnp.concatenate([block(i), block(i + 1)], axis=0).T


def turn(place, part):
    return pl.pallas_call(
        turn_kernel,
        out_shape=shape(2 * ROW_BLOCK, COUNT * HALF, dtype=jnp.bfloat16),
        in_specs=[SCALARS, WHOLE],
        out_specs=WHOLE,
        compiler_params=PARAMS,
        cost_estimate=cost(0, 2**21),
    )(place, part)


def product_kernel(place, first, second, grads, *refs):
    total, out = refs if len(refs) == 2 else (None, refs[0])
    start = place[3] * HALF

    def rows(offset):
        offset = pl.multiple_of(offset, HALF)
        return jnp.concatenate([grads[pl.ds(i * TOKENS + offset, HALF), :] for i in range(SIDE)], axis=0)

    value = jnp.dot(first[...], rows(start), preferred_element_type=jnp.float32)
    value += jnp.dot(second[...], rows(HALF - start), preferred_element_type=jnp.float32)
    out[...] = value if total is None else value + total[...]


def product(place, first, second, grads, total, group, which=None):
    block = WIDTH // 4
    count = 2 * ROW_BLOCK if which is None else ROW_BLOCK
    row = (lambda place: 0) if which is None else (lambda place: which(place[2]))
    turned = pl.BlockSpec((count, SIDE * HALF), lambda n, place: (row(place), group))
    totals = pl.BlockSpec((count, block), lambda n, place: (row(place), n))
    return pl.pallas_call(
        product_kernel,
        out_shape=shape(count, WIDTH),
        grid_spec=pltpu.PrefetchScalarGridSpec(
            num_scalar_prefetch=1,
            grid=(WIDTH // block,),
            in_specs=[turned, turned, pl.BlockSpec((GROUP, block), lambda n, place: (0, n))]
            + ([] if total is None else [totals]),
            out_specs=pl.BlockSpec((count, block), lambda n, place: (0, n)),
        ),
        compiler_params=PARAMS,
        cost_estimate=cost(2 * count * GROUP * WIDTH, 6 * 2**20),
    )(place, first, second, grads, *([] if total is None else [total]))


def columns_kernel(mine, theirs, grad, sent):
    value = mine[...] + theirs[...]
    grad[...] = value
    sums = jnp.sum(value * value, axis=0, keepdims=True)
    tile = jnp.concatenate([sums[:, i * LANES : (i + 1) * LANES] for i in range(8)], axis=0)
    for i in range(DEVICES):
        sent[i] = tile


def columns(mine, theirs):
    return pl.pallas_call(
        columns_kernel,
        out_shape=(shape(ROW_BLOCK, WIDTH), shape(DEVICES, *TILE)),
        in_specs=[WHOLE] * 2,
        out_specs=(WHOLE, WHOLE),
        compiler_params=PARAMS,
        cost_estimate=cost(2**20, 3 * 2**20),
    )(mine, theirs)


def rows_kernel(received, moment, grad, weight, cols, sent):
    new = BETA_TWO * moment[...] + (1.0 - BETA_TWO) * (jnp.sum(received[...], axis=0) / D)
    cols[...] = new
    root = lax.rsqrt(new)
    sums = [jnp.zeros((ROW_BLOCK, LANES), jnp.float32)] * 4
    for i in range(WIDTH // LANES):
        lanes = slice(i * LANES, (i + 1) * LANES)
        value, held = grad[:, lanes], weight[:, lanes]
        by_cols = value * root[i : i + 1, :]
        terms = (value * value, by_cols * by_cols, by_cols * held, held * held)
        sums = [a + b for a, b in zip(sums, terms)]
    parts = []
    for value in sums:
        for row in range(0, ROW_BLOCK, LANES):
            parts.append(jnp.sum(value[row : row + LANES, :].T, axis=0, keepdims=True))
    tile = jnp.concatenate(parts, axis=0)
    for i in range(LAYERS):
        sent[i] = tile


def rows(received, moment, grad, weight):
    return pl.pallas_call(
        rows_kernel,
        out_shape=(shape(*TILE), shape(LAYERS, *TILE)),
        in_specs=[WHOLE] * 4,
        out_specs=(WHOLE, WHOLE),
        compiler_params=PARAMS,
        cost_estimate=cost(2**21, 2**21),
    )(received, moment, grad, weight)


def scalars_kernel(received, moment, rows_out, sent):
    parts = jnp.sum(received[...], axis=0)
    new = BETA_TWO * moment[...] + (1.0 - BETA_TWO) * (parts[0:2] / FF)
    rows_out[...] = new
    root = lax.rsqrt(new)
    tile = jnp.concatenate([parts[2:4] * root * root, parts[4:6] * root, parts[6:8], jnp.zeros_like(root)], axis=0)
    for i in range(DEVICES):
        sent[i] = tile


def scalars(received, moment):
    return pl.pallas_call(
        scalars_kernel,
        out_shape=(shape(2, LANES), shape(DEVICES, *TILE)),
        in_specs=[WHOLE] * 2,
        out_specs=(WHOLE, WHOLE),
        compiler_params=PARAMS,
        cost_estimate=cost(2**14, 2**18),
    )(received, moment)


def update_kernel(received, new_rows, new_cols, grad, weight, out):
    parts = jnp.sum(received[...], axis=0)
    scaled_sum, cross_sum, weight_sum = (jnp.sum(parts[i : i + 2], keepdims=True) for i in (0, 2, 4))
    factor = 1.0 / jnp.maximum(1.0, jnp.sqrt(scaled_sum / (D * FF)) / CLIP_LEVEL)
    direction_sum = (
        factor * factor * scaled_sum + 2.0 * WEIGHT_DECAY * factor * cross_sum + WEIGHT_DECAY * WEIGHT_DECAY * weight_sum
    )
    trust_ratio = jnp.sqrt(weight_sum / (jnp.maximum(direction_sum, 0.0) + EPSILON))
    by_row = lax.rsqrt(new_rows[...]) * (trust_ratio * factor)
    by_col = lax.rsqrt(new_cols[...])
    decay = trust_ratio * WEIGHT_DECAY
    for half in range(2):
        here = slice(half * LANES, (half + 1) * LANES)
        scale = jnp.broadcast_to(by_row[half : half + 1, :], (LANES, LANES)).T
        for i in range(WIDTH // LANES):
            lanes = slice(i * LANES, (i + 1) * LANES)
            out[here, lanes] = grad[here, lanes] * by_col[i : i + 1, :] * scale + decay * weight[here, lanes]


def update(received, new_rows, new_cols, grad, weight):
    return pl.pallas_call(
        update_kernel,
        out_shape=shape(ROW_BLOCK, WIDTH),
        in_specs=[WHOLE] * 5,
        out_specs=WHOLE,
        compiler_params=PARAMS,
        cost_estimate=cost(2**20, 3 * 2**20),
    )(received, new_rows, new_cols, grad, weight)


def shards(activations, out_grads, weight, row_moment, col_moment):
    y, x, core, layer = (lax.axis_index(name) for name in ("y", "x", "core", "z"))
    place = jnp.stack([y, x, core, layer & 1])
    line = [out_grads] + [along(out_grads, k, 0) for k in range(1, SIDE)]
    packed = pack(place, activations)
    packed, line[1] = lax.optimization_barrier((packed, line[1]))
    first = lax.all_to_all(packed, CHIPS, 0, 0)
    second = next_layer(first)
    line = join(line)
    grads = [line] + [along(line, j, 1) for j in range(1, SIDE)]
    first, second = turn(place, first), turn(place, second)
    total = None
    for j in range(SIDE - 1):
        total = product(place, first, second, grads[j], total, j)
    theirs = product(place, first, second, grads[-1], total, SIDE - 1, lambda core: 1 - core)
    received = lax.ppermute(theirs, "core", [(0, 1), (1, 0)])
    mine = product(place, first, second, grads[-1], total, SIDE - 1, lambda core: core)
    weight_grad, tiles = columns(mine, received)
    new_cols, tiles = rows(exchange(tiles, ROWS), col_moment.reshape(TILE), weight_grad, weight)
    new_rows, tiles = scalars(exchange(tiles, "z"), row_moment.reshape(2, LANES))
    out = update(exchange(tiles, ROWS), new_rows, new_cols, weight_grad, weight)
    return (out, new_rows.reshape(-1), new_cols.reshape(-1))


def solution(mesh):
    mesh = Mesh(mesh.devices.reshape(SIDE, SIDE, 2, LAYERS), ("y", "x", "core", "z"))
    placed = (P(ROWS, None), P(ROWS, "z"), P(ROWS, "z"), P(ROWS), P("z"))
    return jax.shard_map(
        shards,
        mesh=mesh,
        in_specs=placed,
        out_specs=(P(ROWS, "z"), P(ROWS), P("z")),
        check_vma=False,
    )
```

time: 409 us -> 133 us (0.33)
  blocking collectives: 337 us -> 46.2 us
  starting transfers between devices: 0.04 us -> 42 us
  Pallas kernels: 0 us -> 17.3 us
  between operations: 16.1 us -> 0.86 us
  waiting for transfers between devices: 37.9 us -> 22.7 us
  matrix products: 5.85 us -> 0 us
  other arithmetic: 4.81 us -> 0.08 us
    psum x4 -> x0, blocking collectives: 295 us -> none  [the longest x2 208 us: shards(): lax.psum((local_scaled, local_weight), ('dp', 'mp'))]
    all_gather x1 -> x0, waiting for transfers between devices: 37.2 us -> none  [shards(): lax.all_gather(out_grads, 'dp', axis=0, tiled=True)]
    ppermute x0 -> x8, starting transfers between devices: none -> 36.2 us  [the longest x6 21.3 us: along(): return lax.ppermute(value, ROWS, pairs)]
    pallas_call x0 -> x13, Pallas kernels: none -> 17.3 us  [the longest x5 10.7 us: product(): pl.pallas_call(product_kernel, out_shape=shape(count, WIDTH), grid_spec=p...]
    ppermute x0 -> x8, waiting for transfers between devices: none -> 17 us  [the longest x6 15.4 us: along(): return lax.ppermute(value, ROWS, pairs)]
    dot_general x1 -> x0, matrix products: 5.85 us -> none  [shards(): lax.dot_general(feature_rows, lax.all_gather(out_grads, 'dp', axis=0, til...]
    all_to_all x0 -> x1, starting transfers between devices: none -> 5.77 us  [shards(): first = lax.all_to_all(packed, CHIPS, 0, 0)]
    all_to_all x0 -> x1, waiting for transfers between devices: none -> 5.64 us  [shards(): first = lax.all_to_all(packed, CHIPS, 0, 0)]
  transfers between devices with their start and end apart: 1 -> 9, of which waited for: 1 -> 5; matrix products, arithmetic and copies ran while one was open for 2% -> 0% of each run, Pallas kernels for 0% -> 9%
where the time goes in v3:
time: 133 us; the launch traced here: 132 us
  blocking collectives  46.2 us (35%)
  starting transfers between devices  42 us (32%)
  waiting for transfers between devices  22.7 us (17%)
  Pallas kernels  17.3 us (13%)
  local copies, waits for them, and re-layouts  2.98 us (2%)
    all_to_all x3, blocking collectives, exchange(): return lax.all_to_all(tiles, axes, 0, 0)  46.2 us
    ppermute x6, starting transfers between devices, along(): return lax.ppermute(value, ROWS, pairs)  21.3 us
    ppermute x6, waiting for transfers between devices, along(): return lax.ppermute(value, ROWS, pairs)  15.4 us
    ppermute x1, starting transfers between devices, next_layer(): return lax.ppermute(value, ('core', 'z'), pairs)  13 us
    pallas_call x5, Pallas kernels, product(): pl.pallas_call(product_kernel, out_shape=shape(count, WIDTH), grid_spec=p...  10.7 us
    all_to_all x1, starting transfers between devices, shards(): first = lax.all_to_all(packed, CHIPS, 0, 0)  5.77 us
    all_to_all x1, waiting for transfers between devices, shards(): first = lax.all_to_all(packed, CHIPS, 0, 0)  5.64 us
    unnamed x14, local copies, waits for them, and re-layouts  2.98 us
  transfers between devices with their start and end apart: 9, of which 5 were waited for; matrix products, arithmetic and copies ran while one was open for 0% of the time, Pallas kernels for 9%

profile of v3, /device:TPU:1, one launch (start us, length us, event | category | flops | bytes accessed | tf_op | source)
XLA Modules:
  0.0 132.1 jit_solution(13920812113446160645)
XLA Ops:
  0.6 4.0 %collective-permute-start = (bf16[128,1024]{1,0:T(8,128)(2,1)}, bf16[128,1024]{1,0:T(8,128)(2,1)S(1)}, u32[]{:S(2)}, u32[]{:S(2)}) collective-permute-start(bf16[128,1024]{1,0:T(8,128)(2,1)} %refs_0_.1), channel_id=1, source_target_pairs={{0,32},{16,144},{32,64},{48,176},{64,96},{80,208},{96,0},{112,240}... | collective-permute-start | bytes 786440 | tf_op jit(solution)/shard_map/ppermute | solution.py:59
  4.8 1.6 %copy-done.1 = bf16[128,8192]{1,0:T(8,128)(2,1)S(1)} copy-done((bf16[128,8192]{1,0:T(8,128)(2,1)S(1)}, bf16[128,8192]{1,0:T(8,128)(2,1)}, u32[]{:S(2)}) %copy-start.1) | copy-done | bytes 2097176
  6.4 1.6 %shard_map.76 = bf16[16,64,512]{2,1,0:T(8,128)(2,1)} custom-call(s32[4]{0:T(128)S(1)} %pad_add_fusion.place, bf16[128,8192]{1,0:T(8,128)(2,1)S(1)} %copy-done.1), custom_call_target="tpu_custom_call" | custom-call | bytes 2097152 | tf_op jit(solution)/shard_map/pallas_call | solution.py:85
  8.0 2.1 %collective-permute-done.refs_1_ = bf16[128,1024]{1,0:T(8,128)(2,1)S(1)} collective-permute-done((bf16[128,1024]{1,0:T(8,128)(2,1)}, bf16[128,1024]{1,0:T(8,128)(2,1)S(1)}, u32[]{:S(2)}, u32[]{:S(2)}) %collective-permute-start) | collective-permute-done | bytes 262176 | tf_op jit(solution)/shard_map/ppermute | solution.py:59
  10.1 5.8 %all-to-all-start = ((bf16[16,64,512]{2,1,0:T(8,128)(2,1)}), bf16[16,64,512]{2,1,0:T(8,128)(2,1)S(1)}, u32[]{:S(2)}, u32[]{:S(2)}) async-start(bf16[16,64,512]{2,1,0:T(8,128)(2,1)} %shard_map.76), calls=%async_computation | async-start | bytes 2097152 | tf_op jit(solution)/shard_map/all_to_all | solution.py:284
  15.9 4.8 %collective-permute-start.2 = (bf16[128,1024]{1,0:T(8,128)(2,1)S(1)}, bf16[128,1024]{1,0:T(8,128)(2,1)S(1)}, u32[]{:S(2)}, u32[]{:S(2)}) collective-permute-start(bf16[128,1024]{1,0:T(8,128)(2,1)S(1)} %copy-done.2), channel_id=1, source_target_pairs={{0,64},{16,272},{32,96},{48,304},{64,0},{80,336},{96,32},{112,368}... | collective-permute-start | bytes 786440 | tf_op jit(solution)/shard_map/ppermute | solution.py:59
  20.6 2.8 %collective-permute-start.3 = (bf16[128,1024]{1,0:T(8,128)(2,1)S(1)}, bf16[128,1024]{1,0:T(8,128)(2,1)S(1)}, u32[]{:S(2)}, u32[]{:S(2)}) collective-permute-start(bf16[128,1024]{1,0:T(8,128)(2,1)S(1)} %copy-done.2), channel_id=1, source_target_pairs={{0,96},{16,400},{32,0},{48,432},{64,32},{80,464},{96,64},{112,496}... | collective-permute-start | bytes 786440 | tf_op jit(solution)/shard_map/ppermute | solution.py:59
  23.4 5.6 %all-to-all-done.part = bf16[16,64,512]{2,1,0:T(8,128)(2,1)S(1)} async-done(((bf16[16,64,512]{2,1,0:T(8,128)(2,1)}), bf16[16,64,512]{2,1,0:T(8,128)(2,1)S(1)}, u32[]{:S(2)}, u32[]{:S(2)}) %all-to-all-start) | async-done | bytes 1048608 | tf_op jit(solution)/shard_map/all_to_all | solution.py:284
  29.1 13.0 %collective-permute-start.1 = (bf16[16,64,512]{2,1,0:T(8,128)(2,1)S(1)}, bf16[16,64,512]{2,1,0:T(8,128)(2,1)S(1)}, u32[]{:S(2)}, u32[]{:S(2)}) collective-permute-start(bf16[16,64,512]{2,1,0:T(8,128)(2,1)S(1)} %all-to-all-done.part), channel_id=1, source_target_pairs={{0,1},{1,2},{2,3},{3,4},{4,5},{5,6},{6,7},{7,8},{8,9},{9,10},{10,1... | collective-permute-start | bytes 3145736 | tf_op jit(solution)/shard_map/ppermute | solution.py:65
  42.2 2.6 %collective-permute-start.6 = (bf16[512,1024]{1,0:T(8,128)(2,1)S(1)}, bf16[512,1024]{1,0:T(8,128)(2,1)S(1)}, u32[]{:S(2)}, u32[]{:S(2)}) collective-permute-start(bf16[512,1024]{1,0:T(8,128)(2,1)S(1)} %shard_map.79.grads), channel_id=1, source_target_pairs={{0,128},{16,48},{32,160},{48,80},{64,192},{80,112},{96,224},{112,1... | collective-permute-start | bytes 3145736 | tf_op jit(solution)/shard_map/ppermute | solution.py:59
  44.8 3.2 %collective-permute-start.5 = (bf16[512,1024]{1,0:T(8,128)(2,1)S(1)}, bf16[512,1024]{1,0:T(8,128)(2,1)S(1)}, u32[]{:S(2)}, u32[]{:S(2)}) collective-permute-start(bf16[512,1024]{1,0:T(8,128)(2,1)S(1)} %shard_map.79.grads), channel_id=1, source_target_pairs={{0,256},{16,80},{32,288},{48,112},{64,320},{80,16},{96,352},{112,4... | collective-permute-start | bytes 3145736 | tf_op jit(solution)/shard_map/ppermute | solution.py:59
  48.0 4.0 %collective-permute-start.4 = (bf16[512,1024]{1,0:T(8,128)(2,1)S(1)}, bf16[512,1024]{1,0:T(8,128)(2,1)S(1)}, u32[]{:S(2)}, u32[]{:S(2)}) collective-permute-start(bf16[512,1024]{1,0:T(8,128)(2,1)S(1)} %shard_map.79.grads), channel_id=1, source_target_pairs={{0,384},{16,112},{32,416},{48,16},{64,448},{80,48},{96,480},{112,8... | collective-permute-start | bytes 3145736 | tf_op jit(solution)/shard_map/ppermute | solution.py:59
  52.0 0.9 shard_map.77.first
  52.9 0.9 collective-permute-done.1.part
  53.8 0.9 shard_map.78.second
  54.7 2.2 %shard_map.80.refs_0_ = f32[512,1024]{1,0:T(8,128)S(1)} custom-call(s32[4]{0:T(128)S(1)} %pad_add_fusion.place, bf16[512,1024]{1,0:T(8,128)(2,1)S(1)} %shard_map.77.first, bf16[512,1024]{1,0:T(8,128)(2,1)S(1)} %shard_map.78.second, bf16[512,1024]{1,0:T(8,128)(2,1)S(1)} %shard_map.79.grads), custom_call_target="tpu_custom_call" | custom-call | flops 536870912 | bytes 6291456 | tf_op jit(solution)/shard_map/pallas_call | solution.py:161
  56.9 13.3 %collective-permute-done.6.grads = bf16[512,1024]{1,0:T(8,128)(2,1)S(1)} collective-permute-done((bf16[512,1024]{1,0:T(8,128)(2,1)S(1)}, bf16[512,1024]{1,0:T(8,128)(2,1)S(1)}, u32[]{:S(2)}, u32[]{:S(2)}) %collective-permute-start.6) | collective-permute-done | bytes 1048608 | tf_op jit(solution)/shard_map/ppermute | solution.py:59
  70.2 2.3 %shard_map.81.refs_0_ = f32[512,1024]{1,0:T(8,128)S(1)} custom-call(s32[4]{0:T(128)S(1)} %pad_add_fusion.place, bf16[512,1024]{1,0:T(8,128)(2,1)S(1)} %shard_map.77.first, bf16[512,1024]{1,0:T(8,128)(2,1)S(1)} %shard_map.78.second, bf16[512,1024]{1,0:T(8,128)(2,1)S(1)} %collective-permute-done.6.grads, f32[512,1024]{1,0:T(8,128)S(1)} %shard_map.80.refs_0_), custom_call_target="tpu_custom_call" | custom-call | flops 536870912 | bytes 6291456 | tf_op jit(solution)/shard_map/pallas_call | solution.py:161
  72.6 2.3 %shard_map.82.refs_0_ = f32[512,1024]{1,0:T(8,128)S(1)} custom-call(s32[4]{0:T(128)S(1)} %pad_add_fusion.place, bf16[512,1024]{1,0:T(8,128)(2,1)S(1)} %shard_map.77.first, bf16[512,1024]{1,0:T(8,128)(2,1)S(1)} %shard_map.78.second, bf16[512,1024]{1,0:T(8,128)(2,1)S(1)} %collective-permute-done.5.grads, f32[512,1024]{1,0:T(8,128)S(1)} %shard_map.81.refs_0_), custom_call_target="tpu_custom_call" | custom-call | flops 536870912 | bytes 6291456 | tf_op jit(solution)/shard_map/pallas_call | solution.py:161
  74.9 1.9 %shard_map.84 = f32[256,1024]{1,0:T(8,128)S(1)} custom-call(s32[4]{0:T(128)S(1)} %pad_add_fusion.place, bf16[512,1024]{1,0:T(8,128)(2,1)S(1)} %shard_map.77.first, bf16[512,1024]{1,0:T(8,128)(2,1)S(1)} %shard_map.78.second, bf16[512,1024]{1,0:T(8,128)(2,1)S(1)} %collective-permute-done.4.grads, f32[512,1024]{1,0:T(8,128)S(1)} %shard_map.82.refs_0_), custom_call_target="tpu_custom_call" | custom-call | flops 268435456 | bytes 6291456 | tf_op jit(solution)/shard_map/pallas_call | solution.py:161
  76.9 1.9 %collective-permute-start.7 = (f32[256,1024]{1,0:T(8,128)S(1)}, f32[256,1024]{1,0:T(8,128)S(1)}, u32[]{:S(2)}, u32[]{:S(2)}) collective-permute-start(f32[256,1024]{1,0:T(8,128)S(1)} %shard_map.84), channel_id=1, source_target_pairs={{0,16},{16,0},{1,17},{17,1},{2,18},{18,2},{3,19},{19,3},{4,20},{20... | collective-permute-start | bytes 3145736 | tf_op jit(solution)/shard_map/ppermute | solution.py:293
  78.8 1.9 %shard_map.83.mine = f32[256,1024]{1,0:T(8,128)S(1)} custom-call(s32[4]{0:T(128)S(1)} %pad_add_fusion.place, bf16[512,1024]{1,0:T(8,128)(2,1)S(1)} %shard_map.77.first, bf16[512,1024]{1,0:T(8,128)(2,1)S(1)} %shard_map.78.second, bf16[512,1024]{1,0:T(8,128)(2,1)S(1)} %collective-permute-done.4.grads, f32[512,1024]{1,0:T(8,128)S(1)} %shard_map.82.refs_0_), custom_call_target="tpu_custom_call" | custom-call | flops 268435456 | bytes 6291456 | tf_op jit(solution)/shard_map/pallas_call | solution.py:161
  80.8 0.7 collective-permute-done.7.theirs
  81.4 0.1 shard_map.85
  81.6 12.1 %all_to_all.20.received = f32[32,8,128]{2,1,0:T(8,128)S(1)} all-to-all(f32[32,8,128]{2,1,0:T(8,128)S(1)} %get-tuple-element.13), channel_id=1, replica_groups=mesh['y'=4,'x'=4,'core'=2,'z'=16] {'y','x','core'}, dimensions={0} | all-to-all | bytes 262144 | tf_op jit(solution)/shard_map/all_to_all | solution.py:69
  93.7 0.9 shard_map.86
  94.6 21.3 %all_to_all.21.received = f32[16,8,128]{2,1,0:T(8,128)S(1)} all-to-all(f32[16,8,128]{2,1,0:T(8,128)S(1)} %get-tuple-element.15), channel_id=1, replica_groups=mesh['y'=4,'x'=4,'core'=2,'z'=16] {'z'}, dimensions={0} | all-to-all | bytes 131072 | tf_op jit(solution)/shard_map/all_to_all | solution.py:69
  115.9 0.6 shard_map.87
  116.5 12.8 %all_to_all.22.received = f32[32,8,128]{2,1,0:T(8,128)S(1)} all-to-all(f32[32,8,128]{2,1,0:T(8,128)S(1)} %get-tuple-element.16), channel_id=1, replica_groups=mesh['y'=4,'x'=4,'core'=2,'z'=16] {'y','x','core'}, dimensions={0} | all-to-all | bytes 262144 | tf_op jit(solution)/shard_map/all_to_all | solution.py:69
  129.3 0.7 copy-done.4
  130.0 0.7 copy-done.6
  130.7 1.4 %shard_map.88 = f32[256,1024]{1,0:T(8,128)} custom-call(f32[32,8,128]{2,1,0:T(8,128)S(1)} %all_to_all.22.received, f32[2,128]{1,0:T(2,128)S(1)} %copy-done.6, f32[8,128]{1,0:T(8,128)S(1)} %copy-done.4, f32[256,1024]{1,0:T(8,128)S(1)} %get-tuple-element.14.grad, f32[256,1024]{1,0:T(8,128)S(1)} %copy-done), custom_call_target="tpu_custom_call" | custom-call | flops 1048576 | bytes 3145728 | tf_op jit(solution)/shard_map/pallas_call | solution.py:268
  (17 shorter events, 0.2 us)
Async XLA Ops:
  0.6 9.4 %collective-permute-start = (bf16[128,1024]{1,0:T(8,128)(2,1)}, bf16[128,1024]{1,0:T(8,128)(2,1)S(1)}, u32[]{:S(2)}, u32[]{:S(2)}) collective-permute-start(bf16[128,1024]{1,0:T(8,128)(2,1)} %refs_0_.1), channel_id=1, source_target_pairs={{0,32},{16,144},{32,64},{48,176},{64,96},{80,208},{96,0},{112,240}... | collective-permute-start | bytes 786440 | tf_op jit(solution)/shard_map/ppermute | solution.py:59
  4.8 1.6 %copy-start.1 = (bf16[128,8192]{1,0:T(8,128)(2,1)S(1)}, bf16[128,8192]{1,0:T(8,128)(2,1)}, u32[]{:S(2)}) copy-start(bf16[128,8192]{1,0:T(8,128)(2,1)} %source.1) | copy-start | bytes 6291460
  6.4 9.5 %copy-start.2 = (bf16[128,1024]{1,0:T(8,128)(2,1)S(1)}, bf16[128,1024]{1,0:T(8,128)(2,1)}, u32[]{:S(2)}) copy-start(bf16[128,1024]{1,0:T(8,128)(2,1)} %refs_0_.1) | copy-start | bytes 786436
  10.1 19.0 %all-to-all-start = ((bf16[16,64,512]{2,1,0:T(8,128)(2,1)}), bf16[16,64,512]{2,1,0:T(8,128)(2,1)S(1)}, u32[]{:S(2)}, u32[]{:S(2)}) async-start(bf16[16,64,512]{2,1,0:T(8,128)(2,1)} %shard_map.76), calls=%async_computation | async-start | bytes 2097152 | tf_op jit(solution)/shard_map/all_to_all | solution.py:284
  15.9 26.2 %collective-permute-start.2 = (bf16[128,1024]{1,0:T(8,128)(2,1)S(1)}, bf16[128,1024]{1,0:T(8,128)(2,1)S(1)}, u32[]{:S(2)}, u32[]{:S(2)}) collective-permute-start(bf16[128,1024]{1,0:T(8,128)(2,1)S(1)} %copy-done.2), channel_id=1, source_target_pairs={{0,64},{16,272},{32,96},{48,304},{64,0},{80,336},{96,32},{112,368}... | collective-permute-start | bytes 786440 | tf_op jit(solution)/shard_map/ppermute | solution.py:59
  20.6 21.5 %collective-permute-start.3 = (bf16[128,1024]{1,0:T(8,128)(2,1)S(1)}, bf16[128,1024]{1,0:T(8,128)(2,1)S(1)}, u32[]{:S(2)}, u32[]{:S(2)}) collective-permute-start(bf16[128,1024]{1,0:T(8,128)(2,1)S(1)} %copy-done.2), channel_id=1, source_target_pairs={{0,96},{16,400},{32,0},{48,432},{64,32},{80,464},{96,64},{112,496}... | collective-permute-start | bytes 786440 | tf_op jit(solution)/shard_map/ppermute | solution.py:59
  29.1 24.7 %collective-permute-start.1 = (bf16[16,64,512]{2,1,0:T(8,128)(2,1)S(1)}, bf16[16,64,512]{2,1,0:T(8,128)(2,1)S(1)}, u32[]{:S(2)}, u32[]{:S(2)}) collective-permute-start(bf16[16,64,512]{2,1,0:T(8,128)(2,1)S(1)} %all-to-all-done.part), channel_id=1, source_target_pairs={{0,1},{1,2},{2,3},{3,4},{4,5},{5,6},{6,7},{7,8},{8,9},{9,10},{10,1... | collective-permute-start | bytes 3145736 | tf_op jit(solution)/shard_map/ppermute | solution.py:65
  42.2 28.0 %collective-permute-start.6 = (bf16[512,1024]{1,0:T(8,128)(2,1)S(1)}, bf16[512,1024]{1,0:T(8,128)(2,1)S(1)}, u32[]{:S(2)}, u32[]{:S(2)}) collective-permute-start(bf16[512,1024]{1,0:T(8,128)(2,1)S(1)} %shard_map.79.grads), channel_id=1, source_target_pairs={{0,128},{16,48},{32,160},{48,80},{64,192},{80,112},{96,224},{112,1... | collective-permute-start | bytes 3145736 | tf_op jit(solution)/shard_map/ppermute | solution.py:59
  44.8 27.8 %collective-permute-start.5 = (bf16[512,1024]{1,0:T(8,128)(2,1)S(1)}, bf16[512,1024]{1,0:T(8,128)(2,1)S(1)}, u32[]{:S(2)}, u32[]{:S(2)}) collective-permute-start(bf16[512,1024]{1,0:T(8,128)(2,1)S(1)} %shard_map.79.grads), channel_id=1, source_target_pairs={{0,256},{16,80},{32,288},{48,112},{64,320},{80,16},{96,352},{112,4... | collective-permute-start | bytes 3145736 | tf_op jit(solution)/shard_map/ppermute | solution.py:59
  48.0 27.0 %collective-permute-start.4 = (bf16[512,1024]{1,0:T(8,128)(2,1)S(1)}, bf16[512,1024]{1,0:T(8,128)(2,1)S(1)}, u32[]{:S(2)}, u32[]{:S(2)}) collective-permute-start(bf16[512,1024]{1,0:T(8,128)(2,1)S(1)} %shard_map.79.grads), channel_id=1, source_target_pairs={{0,384},{16,112},{32,416},{48,16},{64,448},{80,48},{96,480},{112,8... | collective-permute-start | bytes 3145736 | tf_op jit(solution)/shard_map/ppermute | solution.py:59
  76.9 4.6 %collective-permute-start.7 = (f32[256,1024]{1,0:T(8,128)S(1)}, f32[256,1024]{1,0:T(8,128)S(1)}, u32[]{:S(2)}, u32[]{:S(2)}) collective-permute-start(f32[256,1024]{1,0:T(8,128)S(1)} %shard_map.84), channel_id=1, source_target_pairs={{0,16},{16,0},{1,17},{17,1},{2,18},{18,2},{3,19},{19,3},{4,20},{20... | collective-permute-start | bytes 3145736 | tf_op jit(solution)/shard_map/ppermute | solution.py:293
  80.7 12.9 %copy-start = (f32[256,1024]{1,0:T(8,128)S(1)}, f32[256,1024]{1,0:T(8,128)}, u32[]{:S(2)}) copy-start(f32[256,1024]{1,0:T(8,128)} %weight.3) | copy-start | bytes 3145732
  80.8 12.9 %copy-start.3 = (f32[1024]{0:T(1024)S(1)}, f32[1024]{0:T(1024)}, u32[]{:S(2)}) copy-start(f32[1024]{0:T(1024)} %param.9) | copy-start | bytes 12292
  80.8 35.1 %copy-start.5 = (f32[256]{0:T(256)S(1)}, f32[256]{0:T(256)}, u32[]{:S(2)}) copy-start(f32[256]{0:T(256)} %param.8) | copy-start | bytes 3076
  129.3 0.7 copy-start.4
  130.0 0.7 copy-start.6

commit v4 on v3

--- a/solution.py
+++ b/solution.py
@@ -28,6 +28,7 @@
 ROW_BLOCK = 256
 WIDTH = 1024
 LANES = 128
+COLUMNS = 256
 TILE = (8, LANES)
 
 ANYWHERE = pl.BlockSpec(memory_space=pl.ANY)
@@ -85,7 +86,7 @@
     return pl.pallas_call(
         pack_kernel,
         out_shape=shape(COUNT, HALF, 2 * ROW_BLOCK, dtype=jnp.bfloat16),
-        in_specs=[SCALARS, ANYWHERE],
+        in_specs=[SCALARS, pl.BlockSpec(memory_space=pltpu.HBM)],
         out_specs=ANYWHERE,
         scratch_shapes=[pltpu.SemaphoreType.DMA((COUNT,))],
         compiler_params=PARAMS,
@@ -139,38 +140,36 @@
     )(place, part)
 
 
-def product_kernel(place, first, second, grads, *refs):
+def product_kernel(group, which, place, first, second, grads, *refs):
     total, out = refs if len(refs) == 2 else (None, refs[0])
     start = place[3] * HALF
-
-    def rows(offset):
-        offset = pl.multiple_of(offset, HALF)
-        return jnp.concatenate([grads[pl.ds(i * TOKENS + offset, HALF), :] for i in range(SIDE)], axis=0)
-
-    value = jnp.dot(first[...], rows(start), preferred_element_type=jnp.float32)
-    value += jnp.dot(second[...], rows(HALF - start), preferred_element_type=jnp.float32)
-    out[...] = value if total is None else value + total[...]
+    rows = pl.ds(0 if which is None else pl.multiple_of(which(place[2]) * ROW_BLOCK, ROW_BLOCK), out.shape[0])
+    depth = slice(group * SIDE * HALF, (group + 1) * SIDE * HALF)
+
+    @pl.loop(0, WIDTH // COLUMNS)
+    def _(n):
+        columns = pl.ds(pl.multiple_of(n * COLUMNS, COLUMNS), COLUMNS)
+
+        def tokens(offset):
+            offset = pl.multiple_of(offset, HALF)
+            return jnp.concatenate([grads[pl.ds(i * TOKENS + offset, HALF), columns] for i in range(SIDE)], axis=0)
+
+        value = jnp.dot(first[rows, depth], tokens(start), preferred_element_type=jnp.float32)
+        value += jnp.dot(second[rows, depth], tokens(HALF - start), preferred_element_type=jnp.float32)
+        out[:, columns] = value if total is None else value + total[rows, columns]
 
 
 def product(place, first, second, grads, total, group, which=None):
-    block = WIDTH // 4
     count = 2 * ROW_BLOCK if which is None else ROW_BLOCK
-    row = (lambda place: 0) if which is None else (lambda place: which(place[2]))
-    turned = pl.BlockSpec((count, SIDE * HALF), lambda n, place: (row(place), group))
-    totals = pl.BlockSpec((count, block), lambda n, place: (row(place), n))
-    return pl.pallas_call(
-        product_kernel,
+    operands = [first, second, grads] + ([] if total is None else [total])
+    return pl.pallas_call(
+        functools.partial(product_kernel, group, which),
         out_shape=shape(count, WIDTH),
-        grid_spec=pltpu.PrefetchScalarGridSpec(
-            num_scalar_prefetch=1,
-            grid=(WIDTH // block,),
-            in_specs=[turned, turned, pl.BlockSpec((GROUP, block), lambda n, place: (0, n))]
-            + ([] if total is None else [totals]),
-            out_specs=pl.BlockSpec((count, block), lambda n, place: (0, n)),
-        ),
-        compiler_params=PARAMS,
-        cost_estimate=cost(2 * count * GROUP * WIDTH, 6 * 2**20),
-    )(place, first, second, grads, *([] if total is None else [total]))
+        in_specs=[SCALARS] + [WHOLE] * len(operands),
+        out_specs=WHOLE,
+        compiler_params=PARAMS,
+        cost_estimate=cost(2 * count * GROUP * WIDTH, 2**20),
+    )(place, *operands)
 
 
 def columns_kernel(mine, theirs, grad, sent):
@@ -193,10 +192,11 @@
     )(mine, theirs)
 
 
-def rows_kernel(received, moment, grad, weight, cols, sent):
+def rows_kernel(received, moment, grad, weight, cols, col_root, sent):
     new = BETA_TWO * moment[...] + (1.0 - BETA_TWO) * (jnp.sum(received[...], axis=0) / D)
     cols[...] = new
     root = lax.rsqrt(new)
+    col_root[...] = root
     sums = [jnp.zeros((ROW_BLOCK, LANES), jnp.float32)] * 4
     for i in range(WIDTH // LANES):
         lanes = slice(i * LANES, (i + 1) * LANES)
@@ -216,20 +216,22 @@
 def rows(received, moment, grad, weight):
     return pl.pallas_call(
         rows_kernel,
-        out_shape=(shape(*TILE), shape(LAYERS, *TILE)),
+        out_shape=(shape(*TILE), shape(*TILE), shape(LAYERS, *TILE)),
         in_specs=[WHOLE] * 4,
-        out_specs=(WHOLE, WHOLE),
+        out_specs=(WHOLE, WHOLE, WHOLE),
         compiler_params=PARAMS,
         cost_estimate=cost(2**21, 2**21),
     )(received, moment, grad, weight)
 
 
-def scalars_kernel(received, moment, rows_out, sent):
+def scalars_kernel(received, moment, rows_out, row_root, sent):
     parts = jnp.sum(received[...], axis=0)
     new = BETA_TWO * moment[...] + (1.0 - BETA_TWO) * (parts[0:2] / FF)
     rows_out[...] = new
     root = lax.rsqrt(new)
-    tile = jnp.concatenate([parts[2:4] * root * root, parts[4:6] * root, parts[6:8], jnp.zeros_like(root)], axis=0)
+    row_root[...] = root
+    sums = [jnp.sum(part, axis=0, keepdims=True) for part in (parts[2:4] * root * root, parts[4:6] * root, parts[6:8])]
+    tile = jnp.concatenate(sums + [jnp.zeros_like(sums[0])], axis=0)
     for i in range(DEVICES):
         sent[i] = tile
 
@@ -237,42 +239,48 @@
 def scalars(received, moment):
     return pl.pallas_call(
         scalars_kernel,
-        out_shape=(shape(2, LANES), shape(DEVICES, *TILE)),
+        out_shape=(shape(2, LANES), shape(2, LANES), shape(DEVICES, 4, LANES)),
         in_specs=[WHOLE] * 2,
-        out_specs=(WHOLE, WHOLE),
+        out_specs=(WHOLE, WHOLE, WHOLE),
         compiler_params=PARAMS,
         cost_estimate=cost(2**14, 2**18),
     )(received, moment)
 
 
-def update_kernel(received, new_rows, new_cols, grad, weight, out):
+def update_kernel(received, row_root, col_root, grad, weight, out, done, sems):
     parts = jnp.sum(received[...], axis=0)
-    scaled_sum, cross_sum, weight_sum = (jnp.sum(parts[i : i + 2], keepdims=True) for i in (0, 2, 4))
+    scaled_sum, cross_sum, weight_sum = (jnp.sum(parts[i : i + 1], keepdims=True) for i in range(3))
     factor = 1.0 / jnp.maximum(1.0, jnp.sqrt(scaled_sum / (D * FF)) / CLIP_LEVEL)
     direction_sum = (
         factor * factor * scaled_sum + 2.0 * WEIGHT_DECAY * factor * cross_sum + WEIGHT_DECAY * WEIGHT_DECAY * weight_sum
     )
     trust_ratio = jnp.sqrt(weight_sum / (jnp.maximum(direction_sum, 0.0) + EPSILON))
-    by_row = lax.rsqrt(new_rows[...]) * (trust_ratio * factor)
-    by_col = lax.rsqrt(new_cols[...])
+    by_row = row_root[...] * (trust_ratio * factor)
+    by_col = col_root[...]
     decay = trust_ratio * WEIGHT_DECAY
+    copies = []
     for half in range(2):
         here = slice(half * LANES, (half + 1) * LANES)
         scale = jnp.broadcast_to(by_row[half : half + 1, :], (LANES, LANES)).T
         for i in range(WIDTH // LANES):
             lanes = slice(i * LANES, (i + 1) * LANES)
-            out[here, lanes] = grad[here, lanes] * by_col[i : i + 1, :] * scale + decay * weight[here, lanes]
-
-
-def update(received, new_rows, new_cols, grad, weight):
+            done[here, lanes] = grad[here, lanes] * by_col[i : i + 1, :] * scale + decay * weight[here, lanes]
+        copies.append(pltpu.make_async_copy(done.at[here], out.at[here], sems.at[half]))
+        copies[-1].start()
+    for copy in copies:
+        copy.wait()
+
+
+def update(received, row_root, col_root, grad, weight):
     return pl.pallas_call(
         update_kernel,
         out_shape=shape(ROW_BLOCK, WIDTH),
         in_specs=[WHOLE] * 5,
-        out_specs=WHOLE,
+        out_specs=ANYWHERE,
+        scratch_shapes=[pltpu.VMEM((ROW_BLOCK, WIDTH), jnp.float32), pltpu.SemaphoreType.DMA((2,))],
         compiler_params=PARAMS,
         cost_estimate=cost(2**20, 3 * 2**20),
-    )(received, new_rows, new_cols, grad, weight)
+    )(received, row_root, col_root, grad, weight)
 
 
 def shards(activations, out_grads, weight, row_moment, col_moment):
@@ -280,7 +288,7 @@
     place = jnp.stack([y, x, core, layer & 1])
     line = [out_grads] + [along(out_grads, k, 0) for k in range(1, SIDE)]
     packed = pack(place, activations)
-    packed, line[1] = lax.optimization_barrier((packed, line[1]))
+    packed, *line[1:] = lax.optimization_barrier((packed, *line[1:]))
     first = lax.all_to_all(packed, CHIPS, 0, 0)
     second = next_layer(first)
     line = join(line)
@@ -293,9 +301,9 @@
     received = lax.ppermute(theirs, "core", [(0, 1), (1, 0)])
     mine = product(place, first, second, grads[-1], total, SIDE - 1, lambda core: core)
     weight_grad, tiles = columns(mine, received)
-    new_cols, tiles = rows(exchange(tiles, ROWS), col_moment.reshape(TILE), weight_grad, weight)
-    new_rows, tiles = scalars(exchange(tiles, "z"), row_moment.reshape(2, LANES))
-    out = update(exchange(tiles, ROWS), new_rows, new_cols, weight_grad, weight)
+    new_cols, col_root, tiles = rows(exchange(tiles, ROWS), col_moment.reshape(TILE), weight_grad, weight)
+    new_rows, row_root, tiles = scalars(exchange(tiles, "z"), row_moment.reshape(2, LANES))
+    out = update(exchange(tiles, ROWS), row_root, col_root, weight_grad, weight)
     return (out, new_rows.reshape(-1), new_cols.reshape(-1))
 
 

time: 133 us -> 136 us (1.023)
  blocking collectives: 46.2 us -> 65.1 us
  starting transfers between devices: 42 us -> 34.5 us
  waiting for transfers between devices: 22.7 us -> 19 us
  Pallas kernels: 17.3 us -> 14.3 us
    all_to_all x0 -> x1, blocking collectives: none -> 18.8 us  [shards(): first = lax.all_to_all(packed, CHIPS, 0, 0)]
    all_to_all x1 -> x0, starting transfers between devices: 5.77 us -> none  [shards(): first = lax.all_to_all(packed, CHIPS, 0, 0)]
    all_to_all x1 -> x0, waiting for transfers between devices: 5.64 us -> none  [shards(): first = lax.all_to_all(packed, CHIPS, 0, 0)]
    pallas_call x7, Pallas kernels: 12.2 us -> 9.92 us  [the longest x5 8.38 us: product(): pl.pallas_call(functools.partial(product_kernel, group, which), out_shape...]
    unnamed x14 -> x10, local copies, waits for them, and re-layouts: 2.98 us -> 1.62 us
  transfers between devices with their start and end apart: 9 -> 8, of which waited for: 5 -> 4; matrix products, arithmetic and copies ran while one was open for 0% -> 0% of each run, Pallas kernels for 9% -> 7%
where the time goes in v4:
time: 136 us; the launch traced here: 135 us
  blocking collectives  65.1 us (48%)
  starting transfers between devices  34.5 us (25%)
  waiting for transfers between devices  19 us (14%)
  Pallas kernels  14.3 us (11%)
  local copies, waits for them, and re-layouts  1.62 us (1%)
    all_to_all x3, blocking collectives, exchange(): return lax.all_to_all(tiles, axes, 0, 0)  46.3 us
    ppermute x6, starting transfers between devices, along(): return lax.ppermute(value, ROWS, pairs)  20 us
    all_to_all x1, blocking collectives, shards(): first = lax.all_to_all(packed, CHIPS, 0, 0)  18.8 us
    ppermute x6, waiting for transfers between devices, along(): return lax.ppermute(value, ROWS, pairs)  15.7 us
    ppermute x1, starting transfers between devices, next_layer(): return lax.ppermute(value, ('core', 'z'), pairs)  12.6 us
    pallas_call x5, Pallas kernels, product(): pl.pallas_call(functools.partial(product_kernel, group, which), out_shape...  8.38 us
  transfers between devices with their start and end apart: 8, of which 4 were waited for; matrix products, arithmetic and copies ran while one was open for 0% of the time, Pallas kernels for 7%

profile of v4, /device:TPU:1, one launch (start us, length us, event | category | flops | bytes accessed | tf_op | source)
XLA Modules:
  0.0 135.4 jit_solution(15209316810148868030)
XLA Ops:
  0.6 4.0 %collective-permute-start = (bf16[128,1024]{1,0:T(8,128)(2,1)}, bf16[128,1024]{1,0:T(8,128)(2,1)S(1)}, u32[]{:S(2)}, u32[]{:S(2)}) collective-permute-start(bf16[128,1024]{1,0:T(8,128)(2,1)} %refs_0_.1), channel_id=1, source_target_pairs={{0,32},{16,144},{32,64},{48,176},{64,96},{80,208},{96,0},{112,240}... | collective-permute-start | bytes 786440 | tf_op jit(solution)/shard_map/ppermute | solution.py:60
  4.7 4.5 %collective-permute-start.1 = (bf16[128,1024]{1,0:T(8,128)(2,1)}, bf16[128,1024]{1,0:T(8,128)(2,1)S(1)}, u32[]{:S(2)}, u32[]{:S(2)}) collective-permute-start(bf16[128,1024]{1,0:T(8,128)(2,1)} %refs_0_.1), channel_id=1, source_target_pairs={{0,64},{16,272},{32,96},{48,304},{64,0},{80,336},{96,32},{112,368}... | collective-permute-start | bytes 786440 | tf_op jit(solution)/shard_map/ppermute | solution.py:60
  9.2 3.0 %collective-permute-start.2 = (bf16[128,1024]{1,0:T(8,128)(2,1)}, bf16[128,1024]{1,0:T(8,128)(2,1)S(1)}, u32[]{:S(2)}, u32[]{:S(2)}) collective-permute-start(bf16[128,1024]{1,0:T(8,128)(2,1)} %refs_0_.1), channel_id=1, source_target_pairs={{0,96},{16,400},{32,0},{48,432},{64,32},{80,464},{96,64},{112,496}... | collective-permute-start | bytes 786440 | tf_op jit(solution)/shard_map/ppermute | solution.py:60
  12.2 0.1 pad_add_fusion.place
  12.3 1.6 %copy-done.1 = bf16[128,8192]{1,0:T(8,128)(2,1)S(1)} copy-done((bf16[128,8192]{1,0:T(8,128)(2,1)S(1)}, bf16[128,8192]{1,0:T(8,128)(2,1)}, u32[]{:S(2)}) %copy-start.1) | copy-done | bytes 2097176
  13.9 0.9 shard_map.76
  14.8 2.0 %collective-permute-done.2.refs_3_ = bf16[128,1024]{1,0:T(8,128)(2,1)S(1)} collective-permute-done((bf16[128,1024]{1,0:T(8,128)(2,1)}, bf16[128,1024]{1,0:T(8,128)(2,1)S(1)}, u32[]{:S(2)}, u32[]{:S(2)}) %collective-permute-start.2) | collective-permute-done | bytes 262176 | tf_op jit(solution)/shard_map/ppermute | solution.py:60
  16.8 18.8 %all_to_all.20.part = bf16[16,64,512]{2,1,0:T(8,128)(2,1)S(1)} all-to-all(bf16[16,64,512]{2,1,0:T(8,128)(2,1)S(1)} %shard_map.76), channel_id=1, replica_groups=mesh['y'=4,'x'=4,'core'=2,'z'=16] {'y','x'}, dimensions={0} | all-to-all | bytes 2097152 | tf_op jit(solution)/shard_map/all_to_all | solution.py:292
  35.6 12.6 %collective-permute-start.3 = (bf16[16,64,512]{2,1,0:T(8,128)(2,1)S(1)}, bf16[16,64,512]{2,1,0:T(8,128)(2,1)S(1)}, u32[]{:S(2)}, u32[]{:S(2)}) collective-permute-start(bf16[16,64,512]{2,1,0:T(8,128)(2,1)S(1)} %all_to_all.20.part), channel_id=1, source_target_pairs={{0,1},{1,2},{2,3},{3,4},{4,5},{5,6},{6,7},{7,8},{8,9},{9,10},{10,1... | collective-permute-start | bytes 3145736 | tf_op jit(solution)/shard_map/ppermute | solution.py:66
  48.2 0.1 shard_map.79.grads
  48.4 2.2 %collective-permute-start.6 = (bf16[512,1024]{1,0:T(8,128)(2,1)S(1)}, bf16[512,1024]{1,0:T(8,128)(2,1)S(1)}, u32[]{:S(2)}, u32[]{:S(2)}) collective-permute-start(bf16[512,1024]{1,0:T(8,128)(2,1)S(1)} %shard_map.79.grads), channel_id=1, source_target_pairs={{0,128},{16,48},{32,160},{48,80},{64,192},{80,112},{96,224},{112,1... | collective-permute-start | bytes 3145736 | tf_op jit(solution)/shard_map/ppermute | solution.py:60
  50.6 3.8 %collective-permute-start.5 = (bf16[512,1024]{1,0:T(8,128)(2,1)S(1)}, bf16[512,1024]{1,0:T(8,128)(2,1)S(1)}, u32[]{:S(2)}, u32[]{:S(2)}) collective-permute-start(bf16[512,1024]{1,0:T(8,128)(2,1)S(1)} %shard_map.79.grads), channel_id=1, source_target_pairs={{0,256},{16,80},{32,288},{48,112},{64,320},{80,16},{96,352},{112,4... | collective-permute-start | bytes 3145736 | tf_op jit(solution)/shard_map/ppermute | solution.py:60
  54.4 2.4 %collective-permute-start.4 = (bf16[512,1024]{1,0:T(8,128)(2,1)S(1)}, bf16[512,1024]{1,0:T(8,128)(2,1)S(1)}, u32[]{:S(2)}, u32[]{:S(2)}) collective-permute-start(bf16[512,1024]{1,0:T(8,128)(2,1)S(1)} %shard_map.79.grads), channel_id=1, source_target_pairs={{0,384},{16,112},{32,416},{48,16},{64,448},{80,48},{96,480},{112,8... | collective-permute-start | bytes 3145736 | tf_op jit(solution)/shard_map/ppermute | solution.py:60
  56.8 0.9 shard_map.77.first
  57.7 2.2 %collective-permute-done.3.part = bf16[16,64,512]{2,1,0:T(8,128)(2,1)S(1)} collective-permute-done((bf16[16,64,512]{2,1,0:T(8,128)(2,1)S(1)}, bf16[16,64,512]{2,1,0:T(8,128)(2,1)S(1)}, u32[]{:S(2)}, u32[]{:S(2)}) %collective-permute-start.3) | collective-permute-done | bytes 1048608 | tf_op jit(solution)/shard_map/ppermute | solution.py:66
  60.0 0.9 shard_map.78.second
  60.9 1.8 %shard_map.80.refs_0_ = f32[512,1024]{1,0:T(8,128)S(1)} custom-call(s32[4]{0:T(128)S(1)} %pad_add_fusion.place, bf16[512,1024]{1,0:T(8,128)(2,1)S(1)} %shard_map.77.first, bf16[512,1024]{1,0:T(8,128)(2,1)S(1)} %shard_map.78.second, bf16[512,1024]{1,0:T(8,128)(2,1)S(1)} %shard_map.79.grads), custom_call_target="tpu_custom_call" | custom-call | flops 536870912 | bytes 1048576 | tf_op jit(solution)/shard_map/pallas_call | solution.py:165
  62.7 13.7 %collective-permute-done.6.grads = bf16[512,1024]{1,0:T(8,128)(2,1)S(1)} collective-permute-done((bf16[512,1024]{1,0:T(8,128)(2,1)S(1)}, bf16[512,1024]{1,0:T(8,128)(2,1)S(1)}, u32[]{:S(2)}, u32[]{:S(2)}) %collective-permute-start.6) | collective-permute-done | bytes 1048608 | tf_op jit(solution)/shard_map/ppermute | solution.py:60
  76.4 1.8 %shard_map.81.refs_0_ = f32[512,1024]{1,0:T(8,128)S(1)} custom-call(s32[4]{0:T(128)S(1)} %pad_add_fusion.place, bf16[512,1024]{1,0:T(8,128)(2,1)S(1)} %shard_map.77.first, bf16[512,1024]{1,0:T(8,128)(2,1)S(1)} %shard_map.78.second, bf16[512,1024]{1,0:T(8,128)(2,1)S(1)} %collective-permute-done.6.grads, f32[512,1024]{1,0:T(8,128)S(1)} %shard_map.80.refs_0_), custom_call_target="tpu_custom_call" | custom-call | flops 536870912 | bytes 1048576 | tf_op jit(solution)/shard_map/pallas_call | solution.py:165
  78.2 1.8 %shard_map.82.refs_0_ = f32[512,1024]{1,0:T(8,128)S(1)} custom-call(s32[4]{0:T(128)S(1)} %pad_add_fusion.place, bf16[512,1024]{1,0:T(8,128)(2,1)S(1)} %shard_map.77.first, bf16[512,1024]{1,0:T(8,128)(2,1)S(1)} %shard_map.78.second, bf16[512,1024]{1,0:T(8,128)(2,1)S(1)} %collective-permute-done.5.grads, f32[512,1024]{1,0:T(8,128)S(1)} %shard_map.81.refs_0_), custom_call_target="tpu_custom_call" | custom-call | flops 536870912 | bytes 1048576 | tf_op jit(solution)/shard_map/pallas_call | solution.py:165
  80.0 1.5 %shard_map.84 = f32[256,1024]{1,0:T(8,128)S(1)} custom-call(s32[4]{0:T(128)S(1)} %pad_add_fusion.place, bf16[512,1024]{1,0:T(8,128)(2,1)S(1)} %shard_map.77.first, bf16[512,1024]{1,0:T(8,128)(2,1)S(1)} %shard_map.78.second, bf16[512,1024]{1,0:T(8,128)(2,1)S(1)} %collective-permute-done.4.grads, f32[512,1024]{1,0:T(8,128)S(1)} %shard_map.82.refs_0_), custom_call_target="tpu_custom_call" | custom-call | flops 268435456 | bytes 1048576 | tf_op jit(solution)/shard_map/pallas_call | solution.py:165
  81.5 1.9 %collective-permute-start.7 = (f32[256,1024]{1,0:T(8,128)S(1)}, f32[256,1024]{1,0:T(8,128)S(1)}, u32[]{:S(2)}, u32[]{:S(2)}) collective-permute-start(f32[256,1024]{1,0:T(8,128)S(1)} %shard_map.84), channel_id=1, source_target_pairs={{0,16},{16,0},{1,17},{17,1},{2,18},{18,2},{3,19},{19,3},{4,20},{20... | collective-permute-start | bytes 3145736 | tf_op jit(solution)/shard_map/ppermute | solution.py:301
  83.4 1.5 %shard_map.83.mine = f32[256,1024]{1,0:T(8,128)S(1)} custom-call(s32[4]{0:T(128)S(1)} %pad_add_fusion.place, bf16[512,1024]{1,0:T(8,128)(2,1)S(1)} %shard_map.77.first, bf16[512,1024]{1,0:T(8,128)(2,1)S(1)} %shard_map.78.second, bf16[512,1024]{1,0:T(8,128)(2,1)S(1)} %collective-permute-done.4.grads, f32[512,1024]{1,0:T(8,128)S(1)} %shard_map.82.refs_0_), custom_call_target="tpu_custom_call" | custom-call | flops 268435456 | bytes 1048576 | tf_op jit(solution)/shard_map/pallas_call | solution.py:165
  84.9 0.0 copy-start.4
  85.0 1.1 collective-permute-done.7.theirs
  86.0 0.1 shard_map.85
  86.2 10.9 %all_to_all.21.received = f32[32,8,128]{2,1,0:T(8,128)S(1)} all-to-all(f32[32,8,128]{2,1,0:T(8,128)S(1)} %get-tuple-element.19), channel_id=1, replica_groups=mesh['y'=4,'x'=4,'core'=2,'z'=16] {'y','x','core'}, dimensions={0} | all-to-all | bytes 262144 | tf_op jit(solution)/shard_map/all_to_all | solution.py:70
  97.0 1.0 shard_map.86
  98.0 22.9 %all_to_all.22.received = f32[16,8,128]{2,1,0:T(8,128)S(1)} all-to-all(f32[16,8,128]{2,1,0:T(8,128)S(1)} %get-tuple-element.21), channel_id=1, replica_groups=mesh['y'=4,'x'=4,'core'=2,'z'=16] {'z'}, dimensions={0} | all-to-all | bytes 131072 | tf_op jit(solution)/shard_map/all_to_all | solution.py:70
  120.9 0.6 shard_map.87
  121.5 12.5 %all_to_all.23.received = f32[32,4,128]{2,1,0:T(4,128)S(1)} all-to-all(f32[32,4,128]{2,1,0:T(4,128)S(1)} %get-tuple-element.22), channel_id=1, replica_groups=mesh['y'=4,'x'=4,'core'=2,'z'=16] {'y','x','core'}, dimensions={0} | all-to-all | bytes 131072 | tf_op jit(solution)/shard_map/all_to_all | solution.py:70
  134.0 1.4 %shard_map.88 = f32[256,1024]{1,0:T(8,128)} custom-call(f32[32,4,128]{2,1,0:T(4,128)S(1)} %all_to_all.23.received, f32[2,128]{1,0:T(2,128)S(1)} %get-tuple-element.23.row_root, f32[8,128]{1,0:T(8,128)S(1)} %get-tuple-element.24.col_root, f32[256,1024]{1,0:T(8,128)S(1)} %get-tuple-element.20.grad, f32[256,1024]{1,0:T(8,128)S(1)} %copy-done), custom_call_target="tpu_custom_call" | custom-call | flops 1048576 | bytes 3145728 | tf_op jit(solution)/shard_map/pallas_call | solution.py:275
  (12 shorter events, 0.0 us)
Async XLA Ops:
  0.6 14.2 %collective-permute-start = (bf16[128,1024]{1,0:T(8,128)(2,1)}, bf16[128,1024]{1,0:T(8,128)(2,1)S(1)}, u32[]{:S(2)}, u32[]{:S(2)}) collective-permute-start(bf16[128,1024]{1,0:T(8,128)(2,1)} %refs_0_.1), channel_id=1, source_target_pairs={{0,32},{16,144},{32,64},{48,176},{64,96},{80,208},{96,0},{112,240}... | collective-permute-start | bytes 786440 | tf_op jit(solution)/shard_map/ppermute | solution.py:60
  4.7 10.1 %collective-permute-start.1 = (bf16[128,1024]{1,0:T(8,128)(2,1)}, bf16[128,1024]{1,0:T(8,128)(2,1)S(1)}, u32[]{:S(2)}, u32[]{:S(2)}) collective-permute-start(bf16[128,1024]{1,0:T(8,128)(2,1)} %refs_0_.1), channel_id=1, source_target_pairs={{0,64},{16,272},{32,96},{48,304},{64,0},{80,336},{96,32},{112,368}... | collective-permute-start | bytes 786440 | tf_op jit(solution)/shard_map/ppermute | solution.py:60
  9.2 7.6 %collective-permute-start.2 = (bf16[128,1024]{1,0:T(8,128)(2,1)}, bf16[128,1024]{1,0:T(8,128)(2,1)S(1)}, u32[]{:S(2)}, u32[]{:S(2)}) collective-permute-start(bf16[128,1024]{1,0:T(8,128)(2,1)} %refs_0_.1), channel_id=1, source_target_pairs={{0,96},{16,400},{32,0},{48,432},{64,32},{80,464},{96,64},{112,496}... | collective-permute-start | bytes 786440 | tf_op jit(solution)/shard_map/ppermute | solution.py:60
  12.3 1.6 %copy-start.1 = (bf16[128,8192]{1,0:T(8,128)(2,1)S(1)}, bf16[128,8192]{1,0:T(8,128)(2,1)}, u32[]{:S(2)}) copy-start(bf16[128,8192]{1,0:T(8,128)(2,1)} %source.1) | copy-start | bytes 6291460
  13.9 34.4 %copy-start.2 = (bf16[128,1024]{1,0:T(8,128)(2,1)S(1)}, bf16[128,1024]{1,0:T(8,128)(2,1)}, u32[]{:S(2)}) copy-start(bf16[128,1024]{1,0:T(8,128)(2,1)} %refs_0_.1) | copy-start | bytes 786436
  35.6 24.3 %collective-permute-start.3 = (bf16[16,64,512]{2,1,0:T(8,128)(2,1)S(1)}, bf16[16,64,512]{2,1,0:T(8,128)(2,1)S(1)}, u32[]{:S(2)}, u32[]{:S(2)}) collective-permute-start(bf16[16,64,512]{2,1,0:T(8,128)(2,1)S(1)} %all_to_all.20.part), channel_id=1, source_target_pairs={{0,1},{1,2},{2,3},{3,4},{4,5},{5,6},{6,7},{7,8},{8,9},{9,10},{10,1... | collective-permute-start | bytes 3145736 | tf_op jit(solution)/shard_map/ppermute | solution.py:66
  48.4 28.0 %collective-permute-start.6 = (bf16[512,1024]{1,0:T(8,128)(2,1)S(1)}, bf16[512,1024]{1,0:T(8,128)(2,1)S(1)}, u32[]{:S(2)}, u32[]{:S(2)}) collective-permute-start(bf16[512,1024]{1,0:T(8,128)(2,1)S(1)} %shard_map.79.grads), channel_id=1, source_target_pairs={{0,128},{16,48},{32,160},{48,80},{64,192},{80,112},{96,224},{112,1... | collective-permute-start | bytes 3145736 | tf_op jit(solution)/shard_map/ppermute | solution.py:60
  50.6 27.6 %collective-permute-start.5 = (bf16[512,1024]{1,0:T(8,128)(2,1)S(1)}, bf16[512,1024]{1,0:T(8,128)(2,1)S(1)}, u32[]{:S(2)}, u32[]{:S(2)}) collective-permute-start(bf16[512,1024]{1,0:T(8,128)(2,1)S(1)} %shard_map.79.grads), channel_id=1, source_target_pairs={{0,256},{16,80},{32,288},{48,112},{64,320},{80,16},{96,352},{112,4... | collective-permute-start | bytes 3145736 | tf_op jit(solution)/shard_map/ppermute | solution.py:60
  54.4 25.6 %collective-permute-start.4 = (bf16[512,1024]{1,0:T(8,128)(2,1)S(1)}, bf16[512,1024]{1,0:T(8,128)(2,1)S(1)}, u32[]{:S(2)}, u32[]{:S(2)}) collective-permute-start(bf16[512,1024]{1,0:T(8,128)(2,1)S(1)} %shard_map.79.grads), channel_id=1, source_target_pairs={{0,384},{16,112},{32,416},{48,16},{64,448},{80,48},{96,480},{112,8... | collective-permute-start | bytes 3145736 | tf_op jit(solution)/shard_map/ppermute | solution.py:60
  81.5 4.6 %collective-permute-start.7 = (f32[256,1024]{1,0:T(8,128)S(1)}, f32[256,1024]{1,0:T(8,128)S(1)}, u32[]{:S(2)}, u32[]{:S(2)}) collective-permute-start(f32[256,1024]{1,0:T(8,128)S(1)} %shard_map.84), channel_id=1, source_target_pairs={{0,16},{16,0},{1,17},{17,1},{2,18},{18,2},{3,19},{19,3},{4,20},{20... | collective-permute-start | bytes 3145736 | tf_op jit(solution)/shard_map/ppermute | solution.py:301
  84.9 12.1 %copy-start = (f32[256,1024]{1,0:T(8,128)S(1)}, f32[256,1024]{1,0:T(8,128)}, u32[]{:S(2)}) copy-start(f32[256,1024]{1,0:T(8,128)} %weight.3) | copy-start | bytes 3145732
  84.9 12.1 %copy-start.3 = (f32[1024]{0:T(1024)S(1)}, f32[1024]{0:T(1024)}, u32[]{:S(2)}) copy-start(f32[1024]{0:T(1024)} %param.9) | copy-start | bytes 12292
  84.9 36.0 %copy-start.4 = (f32[256]{0:T(256)S(1)}, f32[256]{0:T(256)}, u32[]{:S(2)}) copy-start(f32[256]{0:T(256)} %param.8) | copy-start | bytes 3076

commit v5 on v4

--- a/solution.py
+++ b/solution.py
@@ -140,35 +140,35 @@
     )(place, part)
 
 
-def product_kernel(group, which, place, first, second, grads, *refs):
-    total, out = refs if len(refs) == 2 else (None, refs[0])
+def product_kernel(parts, which, place, *refs):
+    operands, out = refs[:-1], refs[-1]
+    total = None if len(operands) == 1 + max(max(part[:2]) for part in parts) else operands[-1]
     start = place[3] * HALF
     rows = pl.ds(0 if which is None else pl.multiple_of(which(place[2]) * ROW_BLOCK, ROW_BLOCK), out.shape[0])
-    depth = slice(group * SIDE * HALF, (group + 1) * SIDE * HALF)
 
     @pl.loop(0, WIDTH // COLUMNS)
     def _(n):
         columns = pl.ds(pl.multiple_of(n * COLUMNS, COLUMNS), COLUMNS)
-
-        def tokens(offset):
-            offset = pl.multiple_of(offset, HALF)
-            return jnp.concatenate([grads[pl.ds(i * TOKENS + offset, HALF), columns] for i in range(SIDE)], axis=0)
-
-        value = jnp.dot(first[rows, depth], tokens(start), preferred_element_type=jnp.float32)
-        value += jnp.dot(second[rows, depth], tokens(HALF - start), preferred_element_type=jnp.float32)
-        out[:, columns] = value if total is None else value + total[rows, columns]
-
-
-def product(place, first, second, grads, total, group, which=None):
+        value = None if total is None else total[rows, columns]
+        for turned, grads, group, exchanged in parts:
+            offset = pl.multiple_of(start if exchanged else HALF - start, HALF)
+            blocks = [operands[grads][pl.ds(i * TOKENS + offset, HALF), columns] for i in range(SIDE)]
+            features = operands[turned][rows, group * SIDE * HALF : (group + 1) * SIDE * HALF]
+            term = jnp.dot(features, jnp.concatenate(blocks, axis=0), preferred_element_type=jnp.float32)
+            value = term if value is None else value + term
+        out[:, columns] = value
+
+
+def product(place, operands, parts, total=None, which=None):
     count = 2 * ROW_BLOCK if which is None else ROW_BLOCK
-    operands = [first, second, grads] + ([] if total is None else [total])
-    return pl.pallas_call(
-        functools.partial(product_kernel, group, which),
+    operands = operands + ([] if total is None else [total])
+    return pl.pallas_call(
+        functools.partial(product_kernel, parts, which),
         out_shape=shape(count, WIDTH),
         in_specs=[SCALARS] + [WHOLE] * len(operands),
         out_specs=WHOLE,
         compiler_params=PARAMS,
-        cost_estimate=cost(2 * count * GROUP * WIDTH, 2**20),
+        cost_estimate=cost(2 * count * SIDE * HALF * WIDTH * len(parts), 2**20),
     )(place, *operands)
 
 
@@ -293,13 +293,16 @@
     second = next_layer(first)
     line = join(line)
     grads = [line] + [along(line, j, 1) for j in range(1, SIDE)]
-    first, second = turn(place, first), turn(place, second)
+    first = turn(place, first)
     total = None
     for j in range(SIDE - 1):
-        total = product(place, first, second, grads[j], total, j)
-    theirs = product(place, first, second, grads[-1], total, SIDE - 1, lambda core: 1 - core)
+        total = product(place, [first, grads[j]], [(0, 1, j, True)], total)
+    second, *grads = lax.optimization_barrier((second, *grads))
+    operands = [first, turn(place, second)] + grads
+    parts = [(0, 1 + SIDE, SIDE - 1, True)] + [(1, 2 + j, j, False) for j in range(SIDE)]
+    theirs = product(place, operands, parts, total, lambda core: 1 - core)
     received = lax.ppermute(theirs, "core", [(0, 1), (1, 0)])
-    mine = product(place, first, second, grads[-1], total, SIDE - 1, lambda core: core)
+    mine = product(place, operands, parts, total, lambda core: core)
     weight_grad, tiles = columns(mine, received)
     new_cols, col_root, tiles = rows(exchange(tiles, ROWS), col_moment.reshape(TILE), weight_grad, weight)
     new_rows, row_root, tiles = scalars(exchange(tiles, "z"), row_moment.reshape(2, LANES))

time: 136 us -> 132 us (0.971)
  starting transfers between devices: 34.5 us -> 48.9 us
  blocking collectives: 65.1 us -> 51 us
  waiting for transfers between devices: 19 us -> 11.8 us
  Pallas kernels: 14.3 us -> 17.1 us
    all_to_all x1 -> x0, blocking collectives: 18.8 us -> none  [shards(): first = lax.all_to_all(packed, CHIPS, 0, 0)]
    ppermute x6, waiting for transfers between devices: 15.7 us -> 7.93 us  [along(): return lax.ppermute(value, ROWS, pairs)]
    all_to_all x0 -> x1, starting transfers between devices: none -> 6.93 us  [shards(): first = lax.all_to_all(packed, CHIPS, 0, 0)]
    ppermute x1, starting transfers between devices: 1.92 us -> 8.05 us  [shards(): received = lax.ppermute(theirs, 'core', [(0, 1), (1, 0)])]
    all_to_all x3, blocking collectives: 46.3 us -> 51 us  [exchange(): return lax.all_to_all(tiles, axes, 0, 0)]
    all_to_all x0 -> x1, waiting for transfers between devices: none -> 3.87 us  [shards(): first = lax.all_to_all(packed, CHIPS, 0, 0)]
    ppermute x6, starting transfers between devices: 20 us -> 22.8 us  [along(): return lax.ppermute(value, ROWS, pairs)]
    ppermute x1, waiting for transfers between devices: 2.23 us -> 0.01 us  [next_layer(): return lax.ppermute(value, ('core', 'z'), pairs)]
  transfers between devices with their start and end apart: 8 -> 9, of which waited for: 4 -> 3; matrix products, arithmetic and copies ran while one was open for 0% -> 0% of each run, Pallas kernels for 7% -> 8%
where the time goes in v5:
time: 132 us; the launch traced here: 131 us
  blocking collectives  51 us (39%)
  starting transfers between devices  48.9 us (37%)
  Pallas kernels  17.1 us (13%)
  waiting for transfers between devices  11.8 us (9%)
  local copies, waits for them, and re-layouts  1.62 us (1%)
    all_to_all x3, blocking collectives, exchange(): return lax.all_to_all(tiles, axes, 0, 0)  51 us
    ppermute x6, starting transfers between devices, along(): return lax.ppermute(value, ROWS, pairs)  22.8 us
    ppermute x1, starting transfers between devices, next_layer(): return lax.ppermute(value, ('core', 'z'), pairs)  11.1 us
    pallas_call x5, Pallas kernels, product(): pl.pallas_call(functools.partial(product_kernel, parts, which), out_shape...  9.74 us
    ppermute x1, starting transfers between devices, shards(): received = lax.ppermute(theirs, 'core', [(0, 1), (1, 0)])  8.05 us
    ppermute x6, waiting for transfers between devices, along(): return lax.ppermute(value, ROWS, pairs)  7.93 us
    all_to_all x1, starting transfers between devices, shards(): first = lax.all_to_all(packed, CHIPS, 0, 0)  6.93 us
    all_to_all x1, waiting for transfers between devices, shards(): first = lax.all_to_all(packed, CHIPS, 0, 0)  3.87 us
  transfers between devices with their start and end apart: 9, of which 3 were waited for; matrix products, arithmetic and copies ran while one was open for 0% of the time, Pallas kernels for 8%

profile of v5, /device:TPU:1, one launch (start us, length us, event | category | flops | bytes accessed | tf_op | source)
XLA Modules:
  0.0 131.4 jit_solution(18423816721374909556)
XLA Ops:
  0.6 5.7 %collective-permute-start.1 = (bf16[128,1024]{1,0:T(8,128)(2,1)}, bf16[128,1024]{1,0:T(8,128)(2,1)S(1)}, u32[]{:S(2)}, u32[]{:S(2)}) collective-permute-start(bf16[128,1024]{1,0:T(8,128)(2,1)} %refs_0_.1), channel_id=1, source_target_pairs={{0,64},{16,272},{32,96},{48,304},{64,0},{80,336},{96,32},{112,368}... | collective-permute-start | bytes 786440 | tf_op jit(solution)/shard_map/ppermute | solution.py:60
  6.3 2.3 %collective-permute-start = (bf16[128,1024]{1,0:T(8,128)(2,1)}, bf16[128,1024]{1,0:T(8,128)(2,1)S(1)}, u32[]{:S(2)}, u32[]{:S(2)}) collective-permute-start(bf16[128,1024]{1,0:T(8,128)(2,1)} %refs_0_.1), channel_id=1, source_target_pairs={{0,32},{16,144},{32,64},{48,176},{64,96},{80,208},{96,0},{112,240}... | collective-permute-start | bytes 786440 | tf_op jit(solution)/shard_map/ppermute | solution.py:60
  8.6 4.2 %collective-permute-start.2 = (bf16[128,1024]{1,0:T(8,128)(2,1)}, bf16[128,1024]{1,0:T(8,128)(2,1)S(1)}, u32[]{:S(2)}, u32[]{:S(2)}) collective-permute-start(bf16[128,1024]{1,0:T(8,128)(2,1)} %refs_0_.1), channel_id=1, source_target_pairs={{0,96},{16,400},{32,0},{48,432},{64,32},{80,464},{96,64},{112,496}... | collective-permute-start | bytes 786440 | tf_op jit(solution)/shard_map/ppermute | solution.py:60
  12.8 0.1 pad_add_fusion.place
  12.9 1.6 %copy-done.1 = bf16[128,8192]{1,0:T(8,128)(2,1)S(1)} copy-done((bf16[128,8192]{1,0:T(8,128)(2,1)S(1)}, bf16[128,8192]{1,0:T(8,128)(2,1)}, u32[]{:S(2)}) %copy-start.1) | copy-done | bytes 2097176
  14.5 1.6 %shard_map.76 = bf16[16,64,512]{2,1,0:T(8,128)(2,1)} custom-call(s32[4]{0:T(128)S(1)} %pad_add_fusion.place, bf16[128,8192]{1,0:T(8,128)(2,1)S(1)} %copy-done.1), custom_call_target="tpu_custom_call" | custom-call | bytes 2097152 | tf_op jit(solution)/shard_map/pallas_call | solution.py:86
  16.1 0.3 collective-permute-done.2.refs_3_
  16.4 6.9 %all-to-all-start = ((bf16[16,64,512]{2,1,0:T(8,128)(2,1)}), bf16[16,64,512]{2,1,0:T(8,128)(2,1)}, u32[]{:S(2)}, u32[]{:S(2)}) async-start(bf16[16,64,512]{2,1,0:T(8,128)(2,1)} %shard_map.76), calls=%async_computation | async-start | bytes 2097152 | tf_op jit(solution)/shard_map/all_to_all | solution.py:292
  23.4 0.1 shard_map.78.refs_1_.refs_2_
  23.5 3.2 %collective-permute-start.4 = (bf16[512,1024]{1,0:T(8,128)(2,1)S(1)}, bf16[512,1024]{1,0:T(8,128)(2,1)S(1)}, u32[]{:S(2)}, u32[]{:S(2)}) collective-permute-start(bf16[512,1024]{1,0:T(8,128)(2,1)S(1)} %shard_map.78.refs_1_.refs_2_), channel_id=1, source_target_pairs={{0,128},{16,48},{32,160},{48,80},{64,192},{80,112},{96,224},{112,1... | collective-permute-start | bytes 3145736 | tf_op jit(solution)/shard_map/ppermute | solution.py:60
  26.7 4.3 %collective-permute-start.5 = (bf16[512,1024]{1,0:T(8,128)(2,1)S(1)}, bf16[512,1024]{1,0:T(8,128)(2,1)S(1)}, u32[]{:S(2)}, u32[]{:S(2)}) collective-permute-start(bf16[512,1024]{1,0:T(8,128)(2,1)S(1)} %shard_map.78.refs_1_.refs_2_), channel_id=1, source_target_pairs={{0,256},{16,80},{32,288},{48,112},{64,320},{80,16},{96,352},{112,4... | collective-permute-start | bytes 3145736 | tf_op jit(solution)/shard_map/ppermute | solution.py:60
  31.0 3.1 %collective-permute-start.6 = (bf16[512,1024]{1,0:T(8,128)(2,1)S(1)}, bf16[512,1024]{1,0:T(8,128)(2,1)}, u32[]{:S(2)}, u32[]{:S(2)}) collective-permute-start(bf16[512,1024]{1,0:T(8,128)(2,1)S(1)} %shard_map.78.refs_1_.refs_2_), channel_id=1, source_target_pairs={{0,384},{16,112},{32,416},{48,16},{64,448},{80,48},{96,480},{112,8... | collective-permute-start | bytes 3145736 | tf_op jit(solution)/shard_map/ppermute | solution.py:60
  34.1 3.9 %all-to-all-done.part = bf16[16,64,512]{2,1,0:T(8,128)(2,1)} async-done(((bf16[16,64,512]{2,1,0:T(8,128)(2,1)}), bf16[16,64,512]{2,1,0:T(8,128)(2,1)}, u32[]{:S(2)}, u32[]{:S(2)}) %all-to-all-start) | async-done | bytes 1048608 | tf_op jit(solution)/shard_map/all_to_all | solution.py:292
  38.0 11.1 %collective-permute-start.3 = (bf16[16,64,512]{2,1,0:T(8,128)(2,1)}, bf16[16,64,512]{2,1,0:T(8,128)(2,1)S(1)}, u32[]{:S(2)}, u32[]{:S(2)}) collective-permute-start(bf16[16,64,512]{2,1,0:T(8,128)(2,1)} %all-to-all-done.part), channel_id=1, source_target_pairs={{0,1},{1,2},{2,3},{3,4},{4,5},{5,6},{6,7},{7,8},{8,9},{9,10},{10,1... | collective-permute-start | bytes 3145736 | tf_op jit(solution)/shard_map/ppermute | solution.py:66
  49.1 1.6 %shard_map.77.refs_0_ = bf16[512,1024]{1,0:T(8,128)(2,1)S(1)} custom-call(s32[4]{0:T(128)S(1)} %pad_add_fusion.place, bf16[16,64,512]{2,1,0:T(8,128)(2,1)} %all-to-all-done.part), custom_call_target="tpu_custom_call" | custom-call | bytes 2097152 | tf_op jit(solution)/shard_map/pallas_call | solution.py:133
  50.7 1.5 %shard_map.80.refs_2_ = f32[512,1024]{1,0:T(8,128)S(1)} custom-call(s32[4]{0:T(128)S(1)} %pad_add_fusion.place, bf16[512,1024]{1,0:T(8,128)(2,1)S(1)} %shard_map.77.refs_0_, bf16[512,1024]{1,0:T(8,128)(2,1)S(1)} %shard_map.78.refs_1_.refs_2_), custom_call_target="tpu_custom_call" | custom-call | flops 268435456 | bytes 1048576 | tf_op jit(solution)/shard_map/pallas_call | solution.py:165
  52.2 1.5 %shard_map.81.refs_2_ = f32[512,1024]{1,0:T(8,128)S(1)} custom-call(s32[4]{0:T(128)S(1)} %pad_add_fusion.place, bf16[512,1024]{1,0:T(8,128)(2,1)S(1)} %shard_map.77.refs_0_, bf16[512,1024]{1,0:T(8,128)(2,1)S(1)} %collective-permute-done.4.refs_1_.refs_3_, f32[512,1024]{1,0:T(8,128)S(1)} %shard_map.80.refs_2_), custom_call_target="tpu_custom_call" | custom-call | flops 268435456 | bytes 1048576 | tf_op jit(solution)/shard_map/pallas_call | solution.py:165
  53.7 7.7 %collective-permute-done.5.refs_1_.refs_4_ = bf16[512,1024]{1,0:T(8,128)(2,1)S(1)} collective-permute-done((bf16[512,1024]{1,0:T(8,128)(2,1)S(1)}, bf16[512,1024]{1,0:T(8,128)(2,1)S(1)}, u32[]{:S(2)}, u32[]{:S(2)}) %collective-permute-start.5) | collective-permute-done | bytes 1048608 | tf_op jit(solution)/shard_map/ppermute | solution.py:60
  61.4 1.5 %shard_map.82.refs_6_ = f32[512,1024]{1,0:T(8,128)S(1)} custom-call(s32[4]{0:T(128)S(1)} %pad_add_fusion.place, bf16[512,1024]{1,0:T(8,128)(2,1)S(1)} %shard_map.77.refs_0_, bf16[512,1024]{1,0:T(8,128)(2,1)S(1)} %collective-permute-done.5.refs_1_.refs_4_, f32[512,1024]{1,0:T(8,128)S(1)} %shard_map.81.refs_2_), custom_call_target="tpu_custom_call" | custom-call | flops 268435456 | bytes 1048576 | tf_op jit(solution)/shard_map/pallas_call | solution.py:165
  62.9 0.9 shard_map.79.refs_1_
  63.8 2.7 %shard_map.84 = f32[256,1024]{1,0:T(8,128)S(1)} custom-call(s32[4]{0:T(128)S(1)} %pad_add_fusion.place, bf16[512,1024]{1,0:T(8,128)(2,1)S(1)} %shard_map.77.refs_0_, bf16[512,1024]{1,0:T(8,128)(2,1)S(1)} %shard_map.79.refs_1_, bf16[512,1024]{1,0:T(8,128)(2,1)S(1)} %shard_map.78.refs_1_.refs_2_, bf16[512,1024]{1,0:T(8,128)(2,1)S(1)} %collective-permute-done.4.refs_1_.refs_3_, ...), custom_call_target="tpu_custom_call" | custom-call | flops 671088640 | bytes 1048576 | tf_op jit(solution)/shard_map/pallas_call | solution.py:165
  66.4 8.0 %collective-permute-start.7 = (f32[256,1024]{1,0:T(8,128)S(1)}, f32[256,1024]{1,0:T(8,128)S(1)}, u32[]{:S(2)}, u32[]{:S(2)}) collective-permute-start(f32[256,1024]{1,0:T(8,128)S(1)} %shard_map.84), channel_id=1, source_target_pairs={{0,16},{16,0},{1,17},{17,1},{2,18},{18,2},{3,19},{19,3},{4,20},{20... | collective-permute-start | bytes 3145736 | tf_op jit(solution)/shard_map/ppermute | solution.py:304
  74.5 2.7 %shard_map.83.mine = f32[256,1024]{1,0:T(8,128)S(1)} custom-call(s32[4]{0:T(128)S(1)} %pad_add_fusion.place, bf16[512,1024]{1,0:T(8,128)(2,1)S(1)} %shard_map.77.refs_0_, bf16[512,1024]{1,0:T(8,128)(2,1)S(1)} %shard_map.79.refs_1_, bf16[512,1024]{1,0:T(8,128)(2,1)S(1)} %shard_map.78.refs_1_.refs_2_, ...), custom_call_target="tpu_custom_call" | custom-call | flops 671088640 | bytes 1048576 | tf_op jit(solution)/shard_map/pallas_call | solution.py:165
  77.2 0.0 copy-start
  77.2 0.0 copy-start.3
  77.2 0.1 shard_map.85
  77.4 18.5 %all_to_all.20.received = f32[32,8,128]{2,1,0:T(8,128)S(1)} all-to-all(f32[32,8,128]{2,1,0:T(8,128)S(1)} %get-tuple-element.29), channel_id=1, replica_groups=mesh['y'=4,'x'=4,'core'=2,'z'=16] {'y','x','core'}, dimensions={0} | all-to-all | bytes 262144 | tf_op jit(solution)/shard_map/all_to_all | solution.py:70
  95.9 1.0 shard_map.86
  96.8 20.0 %all_to_all.21.received = f32[16,8,128]{2,1,0:T(8,128)S(1)} all-to-all(f32[16,8,128]{2,1,0:T(8,128)S(1)} %get-tuple-element.31), channel_id=1, replica_groups=mesh['y'=4,'x'=4,'core'=2,'z'=16] {'z'}, dimensions={0} | all-to-all | bytes 131072 | tf_op jit(solution)/shard_map/all_to_all | solution.py:70
  116.8 0.6 shard_map.87
  117.4 12.5 %all_to_all.22.received = f32[32,4,128]{2,1,0:T(4,128)S(1)} all-to-all(f32[32,4,128]{2,1,0:T(4,128)S(1)} %get-tuple-element.32), channel_id=1, replica_groups=mesh['y'=4,'x'=4,'core'=2,'z'=16] {'y','x','core'}, dimensions={0} | all-to-all | bytes 131072 | tf_op jit(solution)/shard_map/all_to_all | solution.py:70
  129.9 1.4 %shard_map.88 = f32[256,1024]{1,0:T(8,128)} custom-call(f32[32,4,128]{2,1,0:T(4,128)S(1)} %all_to_all.22.received, f32[2,128]{1,0:T(2,128)S(1)} %get-tuple-element.33.row_root, f32[8,128]{1,0:T(8,128)S(1)} %get-tuple-element.34.col_root, f32[256,1024]{1,0:T(8,128)S(1)} %get-tuple-element.30.grad, f32[256,1024]{1,0:T(8,128)S(1)} %copy-done), custom_call_target="tpu_custom_call" | custom-call | flops 1048576 | bytes 3145728 | tf_op jit(solution)/shard_map/pallas_call | solution.py:275
  (13 shorter events, 0.0 us)
Async XLA Ops:
  0.6 15.5 %collective-permute-start.1 = (bf16[128,1024]{1,0:T(8,128)(2,1)}, bf16[128,1024]{1,0:T(8,128)(2,1)S(1)}, u32[]{:S(2)}, u32[]{:S(2)}) collective-permute-start(bf16[128,1024]{1,0:T(8,128)(2,1)} %refs_0_.1), channel_id=1, source_target_pairs={{0,64},{16,272},{32,96},{48,304},{64,0},{80,336},{96,32},{112,368}... | collective-permute-start | bytes 786440 | tf_op jit(solution)/shard_map/ppermute | solution.py:60
  6.3 9.8 %collective-permute-start = (bf16[128,1024]{1,0:T(8,128)(2,1)}, bf16[128,1024]{1,0:T(8,128)(2,1)S(1)}, u32[]{:S(2)}, u32[]{:S(2)}) collective-permute-start(bf16[128,1024]{1,0:T(8,128)(2,1)} %refs_0_.1), channel_id=1, source_target_pairs={{0,32},{16,144},{32,64},{48,176},{64,96},{80,208},{96,0},{112,240}... | collective-permute-start | bytes 786440 | tf_op jit(solution)/shard_map/ppermute | solution.py:60
  8.6 7.8 %collective-permute-start.2 = (bf16[128,1024]{1,0:T(8,128)(2,1)}, bf16[128,1024]{1,0:T(8,128)(2,1)S(1)}, u32[]{:S(2)}, u32[]{:S(2)}) collective-permute-start(bf16[128,1024]{1,0:T(8,128)(2,1)} %refs_0_.1), channel_id=1, source_target_pairs={{0,96},{16,400},{32,0},{48,432},{64,32},{80,464},{96,64},{112,496}... | collective-permute-start | bytes 786440 | tf_op jit(solution)/shard_map/ppermute | solution.py:60
  12.9 1.6 %copy-start.1 = (bf16[128,8192]{1,0:T(8,128)(2,1)S(1)}, bf16[128,8192]{1,0:T(8,128)(2,1)}, u32[]{:S(2)}) copy-start(bf16[128,8192]{1,0:T(8,128)(2,1)} %source.1) | copy-start | bytes 6291460
  14.5 8.9 %copy-start.2 = (bf16[128,1024]{1,0:T(8,128)(2,1)S(1)}, bf16[128,1024]{1,0:T(8,128)(2,1)}, u32[]{:S(2)}) copy-start(bf16[128,1024]{1,0:T(8,128)(2,1)} %refs_0_.1) | copy-start | bytes 786436
  16.4 21.6 %all-to-all-start = ((bf16[16,64,512]{2,1,0:T(8,128)(2,1)}), bf16[16,64,512]{2,1,0:T(8,128)(2,1)}, u32[]{:S(2)}, u32[]{:S(2)}) async-start(bf16[16,64,512]{2,1,0:T(8,128)(2,1)} %shard_map.76), calls=%async_computation | async-start | bytes 2097152 | tf_op jit(solution)/shard_map/all_to_all | solution.py:292
  23.5 28.7 %collective-permute-start.4 = (bf16[512,1024]{1,0:T(8,128)(2,1)S(1)}, bf16[512,1024]{1,0:T(8,128)(2,1)S(1)}, u32[]{:S(2)}, u32[]{:S(2)}) collective-permute-start(bf16[512,1024]{1,0:T(8,128)(2,1)S(1)} %shard_map.78.refs_1_.refs_2_), channel_id=1, source_target_pairs={{0,128},{16,48},{32,160},{48,80},{64,192},{80,112},{96,224},{112,1... | collective-permute-start | bytes 3145736 | tf_op jit(solution)/shard_map/ppermute | solution.py:60
  26.7 34.7 %collective-permute-start.5 = (bf16[512,1024]{1,0:T(8,128)(2,1)S(1)}, bf16[512,1024]{1,0:T(8,128)(2,1)S(1)}, u32[]{:S(2)}, u32[]{:S(2)}) collective-permute-start(bf16[512,1024]{1,0:T(8,128)(2,1)S(1)} %shard_map.78.refs_1_.refs_2_), channel_id=1, source_target_pairs={{0,256},{16,80},{32,288},{48,112},{64,320},{80,16},{96,352},{112,4... | collective-permute-start | bytes 3145736 | tf_op jit(solution)/shard_map/ppermute | solution.py:60
  31.0 31.8 %collective-permute-start.6 = (bf16[512,1024]{1,0:T(8,128)(2,1)S(1)}, bf16[512,1024]{1,0:T(8,128)(2,1)}, u32[]{:S(2)}, u32[]{:S(2)}) collective-permute-start(bf16[512,1024]{1,0:T(8,128)(2,1)S(1)} %shard_map.78.refs_1_.refs_2_), channel_id=1, source_target_pairs={{0,384},{16,112},{32,416},{48,16},{64,448},{80,48},{96,480},{112,8... | collective-permute-start | bytes 3145736 | tf_op jit(solution)/shard_map/ppermute | solution.py:60
  38.0 24.9 %collective-permute-start.3 = (bf16[16,64,512]{2,1,0:T(8,128)(2,1)}, bf16[16,64,512]{2,1,0:T(8,128)(2,1)S(1)}, u32[]{:S(2)}, u32[]{:S(2)}) collective-permute-start(bf16[16,64,512]{2,1,0:T(8,128)(2,1)} %all-to-all-done.part), channel_id=1, source_target_pairs={{0,1},{1,2},{2,3},{3,4},{4,5},{5,6},{6,7},{7,8},{8,9},{9,10},{10,1... | collective-permute-start | bytes 3145736 | tf_op jit(solution)/shard_map/ppermute | solution.py:66
  66.4 10.8 %collective-permute-start.7 = (f32[256,1024]{1,0:T(8,128)S(1)}, f32[256,1024]{1,0:T(8,128)S(1)}, u32[]{:S(2)}, u32[]{:S(2)}) collective-permute-start(f32[256,1024]{1,0:T(8,128)S(1)} %shard_map.84), channel_id=1, source_target_pairs={{0,16},{16,0},{1,17},{17,1},{2,18},{18,2},{3,19},{19,3},{4,20},{20... | collective-permute-start | bytes 3145736 | tf_op jit(solution)/shard_map/ppermute | solution.py:304
  77.2 18.7 %copy-start = (f32[256,1024]{1,0:T(8,128)S(1)}, f32[256,1024]{1,0:T(8,128)}, u32[]{:S(2)}) copy-start(f32[256,1024]{1,0:T(8,128)} %weight.3) | copy-start | bytes 3145732
  77.2 18.7 %copy-start.3 = (f32[1024]{0:T(1024)S(1)}, f32[1024]{0:T(1024)}, u32[]{:S(2)}) copy-start(f32[1024]{0:T(1024)} %param.9) | copy-start | bytes 12292
  77.2 39.6 %copy-start.4 = (f32[256]{0:T(256)S(1)}, f32[256]{0:T(256)}, u32[]{:S(2)}) copy-start(f32[256]{0:T(256)} %param.8) | copy-start | bytes 3076

commit v6 on v5

--- a/solution.py
+++ b/solution.py
@@ -24,7 +24,6 @@
 DEVICES = 2 * COUNT
 TOKENS = 128
 HALF = TOKENS // 2
-GROUP = SIDE * TOKENS
 ROW_BLOCK = 256
 WIDTH = 1024
 LANES = 128
@@ -86,12 +85,12 @@
     return pl.pallas_call(
         pack_kernel,
         out_shape=shape(COUNT, HALF, 2 * ROW_BLOCK, dtype=jnp.bfloat16),
-        in_specs=[SCALARS, pl.BlockSpec(memory_space=pltpu.HBM)],
+        in_specs=[SCALARS, ANYWHERE],
         out_specs=ANYWHERE,
         scratch_shapes=[pltpu.SemaphoreType.DMA((COUNT,))],
         compiler_params=PARAMS,
         cost_estimate=cost(0, 2**21),
-    )(place, activations)
+    )(place, pltpu.with_memory_space_constraint(activations, pltpu.HBM))
 
 
 def join_kernel(*refs):
@@ -108,7 +107,7 @@
 def join(blocks):
     return pl.pallas_call(
         join_kernel,
-        out_shape=shape(GROUP, WIDTH, dtype=jnp.bfloat16),
+        out_shape=shape(len(blocks) * TOKENS, WIDTH, dtype=jnp.bfloat16),
         in_specs=[ANYWHERE] * len(blocks),
         out_specs=ANYWHERE,
         scratch_shapes=[pltpu.SemaphoreType.DMA((len(blocks),))],
@@ -142,7 +141,7 @@
 
 def product_kernel(parts, which, place, *refs):
     operands, out = refs[:-1], refs[-1]
-    total = None if len(operands) == 1 + max(max(part[:2]) for part in parts) else operands[-1]
+    total = None if len(operands) == 2 + max(part[1] for part in parts) else operands[-1]
     start = place[3] * HALF
     rows = pl.ds(0 if which is None else pl.multiple_of(which(place[2]) * ROW_BLOCK, ROW_BLOCK), out.shape[0])
 
@@ -152,7 +151,8 @@
         value = None if total is None else total[rows, columns]
         for turned, grads, group, exchanged in parts:
             offset = pl.multiple_of(start if exchanged else HALF - start, HALF)
-            blocks = [operands[grads][pl.ds(i * TOKENS + offset, HALF), columns] for i in range(SIDE)]
+            blocks = [operands[grads][pl.ds(offset, HALF), columns]]
+            blocks += [operands[grads + 1][pl.ds(i * TOKENS + offset, HALF), columns] for i in range(SIDE - 1)]
             features = operands[turned][rows, group * SIDE * HALF : (group + 1) * SIDE * HALF]
             term = jnp.dot(features, jnp.concatenate(blocks, axis=0), preferred_element_type=jnp.float32)
             value = term if value is None else value + term
@@ -286,20 +286,20 @@
 def shards(activations, out_grads, weight, row_moment, col_moment):
     y, x, core, layer = (lax.axis_index(name) for name in ("y", "x", "core", "z"))
     place = jnp.stack([y, x, core, layer & 1])
-    line = [out_grads] + [along(out_grads, k, 0) for k in range(1, SIDE)]
-    packed = pack(place, activations)
-    packed, *line[1:] = lax.optimization_barrier((packed, *line[1:]))
-    first = lax.all_to_all(packed, CHIPS, 0, 0)
+    first = exchange(pack(place, activations), CHIPS)
     second = next_layer(first)
+    line = [along(out_grads, k, 0) for k in range(1, SIDE)]
+    grads = [out_grads] + [along(out_grads, j, 1) for j in range(1, SIDE)]
+    line, grads[1:] = lax.optimization_barrier((line, grads[1:]))
     line = join(line)
-    grads = [line] + [along(line, j, 1) for j in range(1, SIDE)]
+    lines = [line] + [along(line, j, 1) for j in range(1, SIDE)]
     first = turn(place, first)
     total = None
     for j in range(SIDE - 1):
-        total = product(place, [first, grads[j]], [(0, 1, j, True)], total)
-    second, *grads = lax.optimization_barrier((second, *grads))
-    operands = [first, turn(place, second)] + grads
-    parts = [(0, 1 + SIDE, SIDE - 1, True)] + [(1, 2 + j, j, False) for j in range(SIDE)]
+        total = product(place, [first, grads[j], lines[j]], [(0, 1, j, True)], total)
+    second, *lines = lax.optimization_barrier((second, *lines))
+    operands = [first, turn(place, second)] + [block for pair in zip(grads, lines) for block in pair]
+    parts = [(0, 2 * SIDE, SIDE - 1, True)] + [(1, 2 + 2 * j, j, False) for j in range(SIDE)]
     theirs = product(place, operands, parts, total, lambda core: 1 - core)
     received = lax.ppermute(theirs, "core", [(0, 1), (1, 0)])
     mine = product(place, operands, parts, total, lambda core: core)

time: 132 us -> 160 us (1.21)
  Pallas kernels: 17.1 us -> 46.9 us
  starting transfers between devices: 48.9 us -> 52.2 us
  blocking collectives: 51 us -> 48.3 us
  local copies, waits for them, and re-layouts: 1.62 us -> 0.02 us
    pallas_call x1, Pallas kernels: 1.63 us -> 33.6 us  [pack(): pl.pallas_call(pack_kernel, out_shape=shape(COUNT, HALF, 2 * ROW_BLOCK, d...]
    ppermute x6 -> x9, starting transfers between devices: 22.8 us -> 31.1 us  [along(): return lax.ppermute(value, ROWS, pairs)]
    ppermute x1, starting transfers between devices: 8.05 us -> 1.92 us  [shards(): received = lax.ppermute(theirs, 'core', [(0, 1), (1, 0)])]
    all_to_all x1, waiting for transfers between devices: 3.87 us -> 0.01 us  [exchange(): return lax.all_to_all(tiles, axes, 0, 0)]
    all_to_all x3, blocking collectives: 51 us -> 48.3 us  [exchange(): return lax.all_to_all(tiles, axes, 0, 0)]
    ppermute x6 -> x9, waiting for transfers between devices: 7.93 us -> 10.4 us  [along(): return lax.ppermute(value, ROWS, pairs)]
  transfers between devices with their start and end apart: 9 -> 12, of which waited for: 3 -> 4; matrix products, arithmetic and copies ran while one was open for 0% -> 0% of each run, Pallas kernels for 8% -> 5%
where the time goes in v6:
time: 160 us
  starting transfers between devices  52.2 us (33%)
  blocking collectives  48.3 us (30%)
  Pallas kernels  46.9 us (29%)
  waiting for transfers between devices  11.1 us (7%)
    all_to_all x3, blocking collectives, exchange(): return lax.all_to_all(tiles, axes, 0, 0)  48.3 us
    pallas_call x1, Pallas kernels, pack(): pl.pallas_call(pack_kernel, out_shape=shape(COUNT, HALF, 2 * ROW_BLOCK, d...  33.6 us
    ppermute x9, starting transfers between devices, along(): return lax.ppermute(value, ROWS, pairs)  31.1 us
    ppermute x1, starting transfers between devices, next_layer(): return lax.ppermute(value, ('core', 'z'), pairs)  11.6 us
    ppermute x9, waiting for transfers between devices, along(): return lax.ppermute(value, ROWS, pairs)  10.4 us
    pallas_call x5, Pallas kernels, product(): pl.pallas_call(functools.partial(product_kernel, parts, which), out_shape...  8.35 us
    all_to_all x1, starting transfers between devices, exchange(): return lax.all_to_all(tiles, axes, 0, 0)  7.6 us
  transfers between devices with their start and end apart: 12, of which 4 were waited for; matrix products, arithmetic and copies ran while one was open for 0% of the time, Pallas kernels for 5%

profile of v6, /device:TPU:1, one launch (start us, length us, event | category | flops | bytes accessed | tf_op | source)
XLA Modules:
  0.0 159.5 jit_solution(11441778416715536191)
XLA Ops:
  0.7 33.6 %shard_map.76 = bf16[16,64,512]{2,1,0:T(8,128)(2,1)} custom-call(s32[4]{0:T(128)S(1)} %pad_add_fusion.place, bf16[128,8192]{1,0:T(8,128)(2,1)} %source.1), custom_call_target="tpu_custom_call" | custom-call | bytes 2097152 | tf_op jit(solution)/shard_map/pallas_call | solution.py:85
  34.3 7.6 %all-to-all-start = ((bf16[16,64,512]{2,1,0:T(8,128)(2,1)}), bf16[16,64,512]{2,1,0:T(8,128)(2,1)S(1)}, u32[]{:S(2)}, u32[]{:S(2)}) async-start(bf16[16,64,512]{2,1,0:T(8,128)(2,1)} %shard_map.76), calls=%async_computation | async-start | bytes 2097152 | tf_op jit(solution)/shard_map/all_to_all | solution.py:69
  41.9 4.5 %collective-permute-start.6 = (bf16[128,1024]{1,0:T(8,128)(2,1)S(1)}, bf16[128,1024]{1,0:T(8,128)(2,1)S(1)}, u32[]{:S(2)}, u32[]{:S(2)}) collective-permute-start(bf16[128,1024]{1,0:T(8,128)(2,1)S(1)} %copy-done.1), channel_id=1, source_target_pairs={{0,384},{16,112},{32,416},{48,16},{64,448},{80,48},{96,480},{112,8... | collective-permute-start | bytes 786440 | tf_op jit(solution)/shard_map/ppermute | solution.py:59
  46.4 2.5 %collective-permute-start.5 = (bf16[128,1024]{1,0:T(8,128)(2,1)S(1)}, bf16[128,1024]{1,0:T(8,128)(2,1)S(1)}, u32[]{:S(2)}, u32[]{:S(2)}) collective-permute-start(bf16[128,1024]{1,0:T(8,128)(2,1)S(1)} %copy-done.1), channel_id=1, source_target_pairs={{0,256},{16,80},{32,288},{48,112},{64,320},{80,16},{96,352},{112,4... | collective-permute-start | bytes 786440 | tf_op jit(solution)/shard_map/ppermute | solution.py:59
  48.9 2.5 %collective-permute-start.4 = (bf16[128,1024]{1,0:T(8,128)(2,1)S(1)}, bf16[128,1024]{1,0:T(8,128)(2,1)S(1)}, u32[]{:S(2)}, u32[]{:S(2)}) collective-permute-start(bf16[128,1024]{1,0:T(8,128)(2,1)S(1)} %copy-done.1), channel_id=1, source_target_pairs={{0,128},{16,48},{32,160},{48,80},{64,192},{80,112},{96,224},{112,1... | collective-permute-start | bytes 786440 | tf_op jit(solution)/shard_map/ppermute | solution.py:59
  51.4 4.3 %collective-permute-start.3 = (bf16[128,1024]{1,0:T(8,128)(2,1)S(1)}, bf16[128,1024]{1,0:T(8,128)(2,1)S(1)}, u32[]{:S(2)}, u32[]{:S(2)}) collective-permute-start(bf16[128,1024]{1,0:T(8,128)(2,1)S(1)} %copy-done.1), channel_id=1, source_target_pairs={{0,96},{16,400},{32,0},{48,432},{64,32},{80,464},{96,64},{112,496}... | collective-permute-start | bytes 786440 | tf_op jit(solution)/shard_map/ppermute | solution.py:59
  55.7 2.5 %collective-permute-start.2 = (bf16[128,1024]{1,0:T(8,128)(2,1)S(1)}, bf16[128,1024]{1,0:T(8,128)(2,1)S(1)}, u32[]{:S(2)}, u32[]{:S(2)}) collective-permute-start(bf16[128,1024]{1,0:T(8,128)(2,1)S(1)} %copy-done.1), channel_id=1, source_target_pairs={{0,64},{16,272},{32,96},{48,304},{64,0},{80,336},{96,32},{112,368}... | collective-permute-start | bytes 786440 | tf_op jit(solution)/shard_map/ppermute | solution.py:59
  58.2 0.4 collective-permute-done.6.refs_8_
  58.5 2.8 %collective-permute-start.1 = (bf16[128,1024]{1,0:T(8,128)(2,1)S(1)}, bf16[128,1024]{1,0:T(8,128)(2,1)S(1)}, u32[]{:S(2)}, u32[]{:S(2)}) collective-permute-start(bf16[128,1024]{1,0:T(8,128)(2,1)S(1)} %copy-done.1), channel_id=1, source_target_pairs={{0,32},{16,144},{32,64},{48,176},{64,96},{80,208},{96,0},{112,240}... | collective-permute-start | bytes 786440 | tf_op jit(solution)/shard_map/ppermute | solution.py:59
  61.4 11.6 %collective-permute-start = (bf16[16,64,512]{2,1,0:T(8,128)(2,1)S(1)}, bf16[16,64,512]{2,1,0:T(8,128)(2,1)S(1)}, u32[]{:S(2)}, u32[]{:S(2)}) collective-permute-start(bf16[16,64,512]{2,1,0:T(8,128)(2,1)S(1)} %all-to-all-done.part), channel_id=1, source_target_pairs={{0,1},{1,2},{2,3},{3,4},{4,5},{5,6},{6,7},{7,8},{8,9},{9,10},{10,1... | collective-permute-start | bytes 3145736 | tf_op jit(solution)/shard_map/ppermute | solution.py:65
  73.1 0.1 shard_map.78.refs_2_.refs_3_
  73.2 5.8 %collective-permute-start.7 = (bf16[384,1024]{1,0:T(8,128)(2,1)S(1)}, bf16[384,1024]{1,0:T(8,128)(2,1)S(1)}, u32[]{:S(2)}, u32[]{:S(2)}) collective-permute-start(bf16[384,1024]{1,0:T(8,128)(2,1)S(1)} %shard_map.78.refs_2_.refs_3_), channel_id=1, source_target_pairs={{0,128},{16,48},{32,160},{48,80},{64,192},{80,112},{96,224},{112,1... | collective-permute-start | bytes 2359304 | tf_op jit(solution)/shard_map/ppermute | solution.py:59
  79.0 4.3 %collective-permute-start.8 = (bf16[384,1024]{1,0:T(8,128)(2,1)S(1)}, bf16[384,1024]{1,0:T(8,128)(2,1)S(1)}, u32[]{:S(2)}, u32[]{:S(2)}) collective-permute-start(bf16[384,1024]{1,0:T(8,128)(2,1)S(1)} %shard_map.78.refs_2_.refs_3_), channel_id=1, source_target_pairs={{0,256},{16,80},{32,288},{48,112},{64,320},{80,16},{96,352},{112,4... | collective-permute-start | bytes 2359304 | tf_op jit(solution)/shard_map/ppermute | solution.py:59
  83.3 1.9 %collective-permute-start.9 = (bf16[384,1024]{1,0:T(8,128)(2,1)S(1)}, bf16[384,1024]{1,0:T(8,128)(2,1)S(1)}, u32[]{:S(2)}, u32[]{:S(2)}) collective-permute-start(bf16[384,1024]{1,0:T(8,128)(2,1)S(1)} %shard_map.78.refs_2_.refs_3_), channel_id=1, source_target_pairs={{0,384},{16,112},{32,416},{48,16},{64,448},{80,48},{96,480},{112,8... | collective-permute-start | bytes 2359304 | tf_op jit(solution)/shard_map/ppermute | solution.py:59
  85.2 0.9 shard_map.77.refs_0_
  86.1 1.5 shard_map.80.refs_3_
  87.6 2.2 %collective-permute-done.7.refs_2_.refs_5_ = bf16[384,1024]{1,0:T(8,128)(2,1)S(1)} collective-permute-done((bf16[384,1024]{1,0:T(8,128)(2,1)S(1)}, bf16[384,1024]{1,0:T(8,128)(2,1)S(1)}, u32[]{:S(2)}, u32[]{:S(2)}) %collective-permute-start.7) | collective-permute-done | bytes 786464 | tf_op jit(solution)/shard_map/ppermute | solution.py:59
  89.8 1.5 shard_map.81.refs_3_
  91.3 7.8 %collective-permute-done.8.refs_2_.refs_7_ = bf16[384,1024]{1,0:T(8,128)(2,1)S(1)} collective-permute-done((bf16[384,1024]{1,0:T(8,128)(2,1)S(1)}, bf16[384,1024]{1,0:T(8,128)(2,1)S(1)}, u32[]{:S(2)}, u32[]{:S(2)}) %collective-permute-start.8) | collective-permute-done | bytes 786464 | tf_op jit(solution)/shard_map/ppermute | solution.py:59
  99.1 1.5 shard_map.82.refs_10_
  100.7 0.9 shard_map.79.refs_1_
  101.6 1.9 %shard_map.84 = f32[256,1024]{1,0:T(8,128)S(1)} custom-call(s32[4]{0:T(128)S(1)} %pad_add_fusion.place, bf16[512,1024]{1,0:T(8,128)(2,1)S(1)} %shard_map.77.refs_0_, bf16[512,1024]{1,0:T(8,128)(2,1)S(1)} %shard_map.79.refs_1_, bf16[128,1024]{1,0:T(8,128)(2,1)S(1)} %copy-done.1, bf16[384,1024]{1,0:T(8,128)(2,1)S(1)} %shard_map.78.refs_2_.refs_3_, ...), custom_call_target="tpu_custom_call" | custom-call | flops 671088640 | bytes 1048576 | tf_op jit(solution)/shard_map/pallas_call | solution.py:165
  103.5 1.9 %collective-permute-start.10 = (f32[256,1024]{1,0:T(8,128)S(1)}, f32[256,1024]{1,0:T(8,128)S(1)}, u32[]{:S(2)}, u32[]{:S(2)}) collective-permute-start(f32[256,1024]{1,0:T(8,128)S(1)} %shard_map.84), channel_id=1, source_target_pairs={{0,16},{16,0},{1,17},{17,1},{2,18},{18,2},{3,19},{19,3},{4,20},{20... | collective-permute-start | bytes 3145736 | tf_op jit(solution)/shard_map/ppermute | solution.py:304
  105.5 1.9 %shard_map.83.mine = f32[256,1024]{1,0:T(8,128)S(1)} custom-call(s32[4]{0:T(128)S(1)} %pad_add_fusion.place, bf16[512,1024]{1,0:T(8,128)(2,1)S(1)} %shard_map.77.refs_0_, bf16[512,1024]{1,0:T(8,128)(2,1)S(1)} %shard_map.79.refs_1_, bf16[128,1024]{1,0:T(8,128)(2,1)S(1)} %copy-done.1, bf16[384,1024]{1,0:T(8,128)(2,1)S(1)} %shard_map.78.refs_2_.refs_3_, ...), custom_call_target="tpu_custom_call" | custom-call | flops 671088640 | bytes 1048576 | tf_op jit(solution)/shard_map/pallas_call | solution.py:165
  107.4 0.6 collective-permute-done.10.theirs
  108.1 0.1 shard_map.85
  108.2 15.1 %all_to_all.20.received = f32[32,8,128]{2,1,0:T(8,128)S(1)} all-to-all(f32[32,8,128]{2,1,0:T(8,128)S(1)} %get-tuple-element.33), channel_id=1, replica_groups=mesh['y'=4,'x'=4,'core'=2,'z'=16] {'y','x','core'}, dimensions={0} | all-to-all | bytes 262144 | tf_op jit(solution)/shard_map/all_to_all | solution.py:69
  123.3 1.0 shard_map.86
  124.2 20.7 %all_to_all.21.received = f32[16,8,128]{2,1,0:T(8,128)S(1)} all-to-all(f32[16,8,128]{2,1,0:T(8,128)S(1)} %get-tuple-element.35), channel_id=1, replica_groups=mesh['y'=4,'x'=4,'core'=2,'z'=16] {'z'}, dimensions={0} | all-to-all | bytes 131072 | tf_op jit(solution)/shard_map/all_to_all | solution.py:69
  145.0 0.6 shard_map.87
  145.5 12.5 %all_to_all.22.received = f32[32,4,128]{2,1,0:T(4,128)S(1)} all-to-all(f32[32,4,128]{2,1,0:T(4,128)S(1)} %get-tuple-element.36), channel_id=1, replica_groups=mesh['y'=4,'x'=4,'core'=2,'z'=16] {'y','x','core'}, dimensions={0} | all-to-all | bytes 131072 | tf_op jit(solution)/shard_map/all_to_all | solution.py:69
  158.1 1.4 shard_map.88
  (17 shorter events, 0.1 us)
Async XLA Ops:
  0.7 41.2 %copy-start.1 = (bf16[128,1024]{1,0:T(8,128)(2,1)S(1)}, bf16[128,1024]{1,0:T(8,128)(2,1)}, u32[]{:S(2)}) copy-start(bf16[128,1024]{1,0:T(8,128)(2,1)} %refs_2_.3) | copy-start | bytes 786436
  34.3 27.1 %all-to-all-start = ((bf16[16,64,512]{2,1,0:T(8,128)(2,1)}), bf16[16,64,512]{2,1,0:T(8,128)(2,1)S(1)}, u32[]{:S(2)}, u32[]{:S(2)}) async-start(bf16[16,64,512]{2,1,0:T(8,128)(2,1)} %shard_map.76), calls=%async_computation | async-start | bytes 2097152 | tf_op jit(solution)/shard_map/all_to_all | solution.py:69
  41.9 16.7 %collective-permute-start.6 = (bf16[128,1024]{1,0:T(8,128)(2,1)S(1)}, bf16[128,1024]{1,0:T(8,128)(2,1)S(1)}, u32[]{:S(2)}, u32[]{:S(2)}) collective-permute-start(bf16[128,1024]{1,0:T(8,128)(2,1)S(1)} %copy-done.1), channel_id=1, source_target_pairs={{0,384},{16,112},{32,416},{48,16},{64,448},{80,48},{96,480},{112,8... | collective-permute-start | bytes 786440 | tf_op jit(solution)/shard_map/ppermute | solution.py:59
  46.4 15.0 %collective-permute-start.5 = (bf16[128,1024]{1,0:T(8,128)(2,1)S(1)}, bf16[128,1024]{1,0:T(8,128)(2,1)S(1)}, u32[]{:S(2)}, u32[]{:S(2)}) collective-permute-start(bf16[128,1024]{1,0:T(8,128)(2,1)S(1)} %copy-done.1), channel_id=1, source_target_pairs={{0,256},{16,80},{32,288},{48,112},{64,320},{80,16},{96,352},{112,4... | collective-permute-start | bytes 786440 | tf_op jit(solution)/shard_map/ppermute | solution.py:59
  48.9 24.2 %collective-permute-start.4 = (bf16[128,1024]{1,0:T(8,128)(2,1)S(1)}, bf16[128,1024]{1,0:T(8,128)(2,1)S(1)}, u32[]{:S(2)}, u32[]{:S(2)}) collective-permute-start(bf16[128,1024]{1,0:T(8,128)(2,1)S(1)} %copy-done.1), channel_id=1, source_target_pairs={{0,128},{16,48},{32,160},{48,80},{64,192},{80,112},{96,224},{112,1... | collective-permute-start | bytes 786440 | tf_op jit(solution)/shard_map/ppermute | solution.py:59
  51.4 21.7 %collective-permute-start.3 = (bf16[128,1024]{1,0:T(8,128)(2,1)S(1)}, bf16[128,1024]{1,0:T(8,128)(2,1)S(1)}, u32[]{:S(2)}, u32[]{:S(2)}) collective-permute-start(bf16[128,1024]{1,0:T(8,128)(2,1)S(1)} %copy-done.1), channel_id=1, source_target_pairs={{0,96},{16,400},{32,0},{48,432},{64,32},{80,464},{96,64},{112,496}... | collective-permute-start | bytes 786440 | tf_op jit(solution)/shard_map/ppermute | solution.py:59
  55.7 17.4 %collective-permute-start.2 = (bf16[128,1024]{1,0:T(8,128)(2,1)S(1)}, bf16[128,1024]{1,0:T(8,128)(2,1)S(1)}, u32[]{:S(2)}, u32[]{:S(2)}) collective-permute-start(bf16[128,1024]{1,0:T(8,128)(2,1)S(1)} %copy-done.1), channel_id=1, source_target_pairs={{0,64},{16,272},{32,96},{48,304},{64,0},{80,336},{96,32},{112,368}... | collective-permute-start | bytes 786440 | tf_op jit(solution)/shard_map/ppermute | solution.py:59
  58.5 14.5 %collective-permute-start.1 = (bf16[128,1024]{1,0:T(8,128)(2,1)S(1)}, bf16[128,1024]{1,0:T(8,128)(2,1)S(1)}, u32[]{:S(2)}, u32[]{:S(2)}) collective-permute-start(bf16[128,1024]{1,0:T(8,128)(2,1)S(1)} %copy-done.1), channel_id=1, source_target_pairs={{0,32},{16,144},{32,64},{48,176},{64,96},{80,208},{96,0},{112,240}... | collective-permute-start | bytes 786440 | tf_op jit(solution)/shard_map/ppermute | solution.py:59
  61.4 39.2 %collective-permute-start = (bf16[16,64,512]{2,1,0:T(8,128)(2,1)S(1)}, bf16[16,64,512]{2,1,0:T(8,128)(2,1)S(1)}, u32[]{:S(2)}, u32[]{:S(2)}) collective-permute-start(bf16[16,64,512]{2,1,0:T(8,128)(2,1)S(1)} %all-to-all-done.part), channel_id=1, source_target_pairs={{0,1},{1,2},{2,3},{3,4},{4,5},{5,6},{6,7},{7,8},{8,9},{9,10},{10,1... | collective-permute-start | bytes 3145736 | tf_op jit(solution)/shard_map/ppermute | solution.py:65
  73.2 16.7 %collective-permute-start.7 = (bf16[384,1024]{1,0:T(8,128)(2,1)S(1)}, bf16[384,1024]{1,0:T(8,128)(2,1)S(1)}, u32[]{:S(2)}, u32[]{:S(2)}) collective-permute-start(bf16[384,1024]{1,0:T(8,128)(2,1)S(1)} %shard_map.78.refs_2_.refs_3_), channel_id=1, source_target_pairs={{0,128},{16,48},{32,160},{48,80},{64,192},{80,112},{96,224},{112,1... | collective-permute-start | bytes 2359304 | tf_op jit(solution)/shard_map/ppermute | solution.py:59
  79.0 20.2 %collective-permute-start.8 = (bf16[384,1024]{1,0:T(8,128)(2,1)S(1)}, bf16[384,1024]{1,0:T(8,128)(2,1)S(1)}, u32[]{:S(2)}, u32[]{:S(2)}) collective-permute-start(bf16[384,1024]{1,0:T(8,128)(2,1)S(1)} %shard_map.78.refs_2_.refs_3_), channel_id=1, source_target_pairs={{0,256},{16,80},{32,288},{48,112},{64,320},{80,16},{96,352},{112,4... | collective-permute-start | bytes 2359304 | tf_op jit(solution)/shard_map/ppermute | solution.py:59
  83.3 17.4 %collective-permute-start.9 = (bf16[384,1024]{1,0:T(8,128)(2,1)S(1)}, bf16[384,1024]{1,0:T(8,128)(2,1)S(1)}, u32[]{:S(2)}, u32[]{:S(2)}) collective-permute-start(bf16[384,1024]{1,0:T(8,128)(2,1)S(1)} %shard_map.78.refs_2_.refs_3_), channel_id=1, source_target_pairs={{0,384},{16,112},{32,416},{48,16},{64,448},{80,48},{96,480},{112,8... | collective-permute-start | bytes 2359304 | tf_op jit(solution)/shard_map/ppermute | solution.py:59
  103.5 4.6 %collective-permute-start.10 = (f32[256,1024]{1,0:T(8,128)S(1)}, f32[256,1024]{1,0:T(8,128)S(1)}, u32[]{:S(2)}, u32[]{:S(2)}) collective-permute-start(f32[256,1024]{1,0:T(8,128)S(1)} %shard_map.84), channel_id=1, source_target_pairs={{0,16},{16,0},{1,17},{17,1},{2,18},{18,2},{3,19},{19,3},{4,20},{20... | collective-permute-start | bytes 3145736 | tf_op jit(solution)/shard_map/ppermute | solution.py:304
  107.4 15.9 %copy-start = (f32[256,1024]{1,0:T(8,128)S(1)}, f32[256,1024]{1,0:T(8,128)}, u32[]{:S(2)}) copy-start(f32[256,1024]{1,0:T(8,128)} %weight.3) | copy-start | bytes 3145732
  107.4 15.9 %copy-start.2 = (f32[1024]{0:T(1024)S(1)}, f32[1024]{0:T(1024)}, u32[]{:S(2)}) copy-start(f32[1024]{0:T(1024)} %param.9) | copy-start | bytes 12292
  107.4 37.5 %copy-start.3 = (f32[256]{0:T(256)S(1)}, f32[256]{0:T(256)}, u32[]{:S(2)}) copy-start(f32[256]{0:T(256)} %param.8) | copy-start | bytes 3076

commit v7 on v6

--- a/solution.py
+++ b/solution.py
@@ -86,7 +86,7 @@
         pack_kernel,
         out_shape=shape(COUNT, HALF, 2 * ROW_BLOCK, dtype=jnp.bfloat16),
         in_specs=[SCALARS, ANYWHERE],
-        out_specs=ANYWHERE,
+        out_specs=WHOLE,
         scratch_shapes=[pltpu.SemaphoreType.DMA((COUNT,))],
         compiler_params=PARAMS,
         cost_estimate=cost(0, 2**21),

time: 160 us -> 129 us (0.81)
  Pallas kernels: 46.9 us -> 16.2 us
    pallas_call x1, Pallas kernels: 33.6 us -> 2.9 us  [pack(): pl.pallas_call(pack_kernel, out_shape=shape(COUNT, HALF, 2 * ROW_BLOCK, d...]
  transfers between devices with their start and end apart: 12 -> 12, of which waited for: 4 -> 4; matrix products, arithmetic and copies ran while one was open for 0% -> 0% of each run, Pallas kernels for 5% -> 6%
where the time goes in v7:
time: 129 us
  starting transfers between devices  52.2 us (40%)
  blocking collectives  48.3 us (37%)
  Pallas kernels  16.2 us (13%)
  waiting for transfers between devices  11.1 us (9%)
    all_to_all x3, blocking collectives, exchange(): return lax.all_to_all(tiles, axes, 0, 0)  48.3 us
    ppermute x9, starting transfers between devices, along(): return lax.ppermute(value, ROWS, pairs)  31.1 us
    ppermute x1, starting transfers between devices, next_layer(): return lax.ppermute(value, ('core', 'z'), pairs)  11.6 us
    ppermute x9, waiting for transfers between devices, along(): return lax.ppermute(value, ROWS, pairs)  10.4 us
    pallas_call x5, Pallas kernels, product(): pl.pallas_call(functools.partial(product_kernel, parts, which), out_shape...  8.33 us
    all_to_all x1, starting transfers between devices, exchange(): return lax.all_to_all(tiles, axes, 0, 0)  7.6 us
    pallas_call x1, Pallas kernels, pack(): pl.pallas_call(pack_kernel, out_shape=shape(COUNT, HALF, 2 * ROW_BLOCK, d...  2.9 us
  transfers between devices with their start and end apart: 12, of which 4 were waited for; matrix products, arithmetic and copies ran while one was open for 0% of the time, Pallas kernels for 6%

profile of v7, /device:TPU:1, one launch (start us, length us, event | category | flops | bytes accessed | tf_op | source)
XLA Modules:
  0.0 128.8 jit_solution(4664955812181479822)
XLA Ops:
  0.7 2.9 %shard_map.76 = bf16[16,64,512]{2,1,0:T(8,128)(2,1)} custom-call(s32[4]{0:T(128)S(1)} %pad_add_fusion.place, bf16[128,8192]{1,0:T(8,128)(2,1)} %source.1), custom_call_target="tpu_custom_call" | custom-call | bytes 2097152 | tf_op jit(solution)/shard_map/pallas_call | solution.py:85
  3.6 7.6 %all-to-all-start = ((bf16[16,64,512]{2,1,0:T(8,128)(2,1)}), bf16[16,64,512]{2,1,0:T(8,128)(2,1)S(1)}, u32[]{:S(2)}, u32[]{:S(2)}) async-start(bf16[16,64,512]{2,1,0:T(8,128)(2,1)} %shard_map.76), calls=%async_computation | async-start | bytes 2097152 | tf_op jit(solution)/shard_map/all_to_all | solution.py:69
  11.2 4.5 %collective-permute-start.6 = (bf16[128,1024]{1,0:T(8,128)(2,1)S(1)}, bf16[128,1024]{1,0:T(8,128)(2,1)S(1)}, u32[]{:S(2)}, u32[]{:S(2)}) collective-permute-start(bf16[128,1024]{1,0:T(8,128)(2,1)S(1)} %copy-done.1), channel_id=1, source_target_pairs={{0,384},{16,112},{32,416},{48,16},{64,448},{80,48},{96,480},{112,8... | collective-permute-start | bytes 786440 | tf_op jit(solution)/shard_map/ppermute | solution.py:59
  15.7 2.5 %collective-permute-start.5 = (bf16[128,1024]{1,0:T(8,128)(2,1)S(1)}, bf16[128,1024]{1,0:T(8,128)(2,1)S(1)}, u32[]{:S(2)}, u32[]{:S(2)}) collective-permute-start(bf16[128,1024]{1,0:T(8,128)(2,1)S(1)} %copy-done.1), channel_id=1, source_target_pairs={{0,256},{16,80},{32,288},{48,112},{64,320},{80,16},{96,352},{112,4... | collective-permute-start | bytes 786440 | tf_op jit(solution)/shard_map/ppermute | solution.py:59
  18.2 2.5 %collective-permute-start.4 = (bf16[128,1024]{1,0:T(8,128)(2,1)S(1)}, bf16[128,1024]{1,0:T(8,128)(2,1)S(1)}, u32[]{:S(2)}, u32[]{:S(2)}) collective-permute-start(bf16[128,1024]{1,0:T(8,128)(2,1)S(1)} %copy-done.1), channel_id=1, source_target_pairs={{0,128},{16,48},{32,160},{48,80},{64,192},{80,112},{96,224},{112,1... | collective-permute-start | bytes 786440 | tf_op jit(solution)/shard_map/ppermute | solution.py:59
  20.7 4.3 %collective-permute-start.3 = (bf16[128,1024]{1,0:T(8,128)(2,1)S(1)}, bf16[128,1024]{1,0:T(8,128)(2,1)S(1)}, u32[]{:S(2)}, u32[]{:S(2)}) collective-permute-start(bf16[128,1024]{1,0:T(8,128)(2,1)S(1)} %copy-done.1), channel_id=1, source_target_pairs={{0,96},{16,400},{32,0},{48,432},{64,32},{80,464},{96,64},{112,496}... | collective-permute-start | bytes 786440 | tf_op jit(solution)/shard_map/ppermute | solution.py:59
  25.0 2.5 %collective-permute-start.2 = (bf16[128,1024]{1,0:T(8,128)(2,1)S(1)}, bf16[128,1024]{1,0:T(8,128)(2,1)S(1)}, u32[]{:S(2)}, u32[]{:S(2)}) collective-permute-start(bf16[128,1024]{1,0:T(8,128)(2,1)S(1)} %copy-done.1), channel_id=1, source_target_pairs={{0,64},{16,272},{32,96},{48,304},{64,0},{80,336},{96,32},{112,368}... | collective-permute-start | bytes 786440 | tf_op jit(solution)/shard_map/ppermute | solution.py:59
  27.5 0.4 collective-permute-done.6.refs_8_
  27.9 2.8 %collective-permute-start.1 = (bf16[128,1024]{1,0:T(8,128)(2,1)S(1)}, bf16[128,1024]{1,0:T(8,128)(2,1)S(1)}, u32[]{:S(2)}, u32[]{:S(2)}) collective-permute-start(bf16[128,1024]{1,0:T(8,128)(2,1)S(1)} %copy-done.1), channel_id=1, source_target_pairs={{0,32},{16,144},{32,64},{48,176},{64,96},{80,208},{96,0},{112,240}... | collective-permute-start | bytes 786440 | tf_op jit(solution)/shard_map/ppermute | solution.py:59
  30.8 11.6 %collective-permute-start = (bf16[16,64,512]{2,1,0:T(8,128)(2,1)S(1)}, bf16[16,64,512]{2,1,0:T(8,128)(2,1)S(1)}, u32[]{:S(2)}, u32[]{:S(2)}) collective-permute-start(bf16[16,64,512]{2,1,0:T(8,128)(2,1)S(1)} %all-to-all-done.part), channel_id=1, source_target_pairs={{0,1},{1,2},{2,3},{3,4},{4,5},{5,6},{6,7},{7,8},{8,9},{9,10},{10,1... | collective-permute-start | bytes 3145736 | tf_op jit(solution)/shard_map/ppermute | solution.py:65
  42.4 0.1 shard_map.78.refs_2_.refs_3_
  42.5 5.8 %collective-permute-start.7 = (bf16[384,1024]{1,0:T(8,128)(2,1)S(1)}, bf16[384,1024]{1,0:T(8,128)(2,1)S(1)}, u32[]{:S(2)}, u32[]{:S(2)}) collective-permute-start(bf16[384,1024]{1,0:T(8,128)(2,1)S(1)} %shard_map.78.refs_2_.refs_3_), channel_id=1, source_target_pairs={{0,128},{16,48},{32,160},{48,80},{64,192},{80,112},{96,224},{112,1... | collective-permute-start | bytes 2359304 | tf_op jit(solution)/shard_map/ppermute | solution.py:59
  48.3 4.3 %collective-permute-start.8 = (bf16[384,1024]{1,0:T(8,128)(2,1)S(1)}, bf16[384,1024]{1,0:T(8,128)(2,1)S(1)}, u32[]{:S(2)}, u32[]{:S(2)}) collective-permute-start(bf16[384,1024]{1,0:T(8,128)(2,1)S(1)} %shard_map.78.refs_2_.refs_3_), channel_id=1, source_target_pairs={{0,256},{16,80},{32,288},{48,112},{64,320},{80,16},{96,352},{112,4... | collective-permute-start | bytes 2359304 | tf_op jit(solution)/shard_map/ppermute | solution.py:59
  52.6 1.9 %collective-permute-start.9 = (bf16[384,1024]{1,0:T(8,128)(2,1)S(1)}, bf16[384,1024]{1,0:T(8,128)(2,1)S(1)}, u32[]{:S(2)}, u32[]{:S(2)}) collective-permute-start(bf16[384,1024]{1,0:T(8,128)(2,1)S(1)} %shard_map.78.refs_2_.refs_3_), channel_id=1, source_target_pairs={{0,384},{16,112},{32,416},{48,16},{64,448},{80,48},{96,480},{112,8... | collective-permute-start | bytes 2359304 | tf_op jit(solution)/shard_map/ppermute | solution.py:59
  54.6 0.9 shard_map.77.refs_0_
  55.5 1.5 %shard_map.80.refs_3_ = f32[512,1024]{1,0:T(8,128)S(1)} custom-call(s32[4]{0:T(128)S(1)} %pad_add_fusion.place, bf16[512,1024]{1,0:T(8,128)(2,1)S(1)} %shard_map.77.refs_0_, bf16[128,1024]{1,0:T(8,128)(2,1)S(1)} %copy-done.1, bf16[384,1024]{1,0:T(8,128)(2,1)S(1)} %shard_map.78.refs_2_.refs_3_), custom_call_target="tpu_custom_call" | custom-call | flops 268435456 | bytes 1048576 | tf_op jit(solution)/shard_map/pallas_call | solution.py:165
  57.0 2.2 %collective-permute-done.7.refs_2_.refs_5_ = bf16[384,1024]{1,0:T(8,128)(2,1)S(1)} collective-permute-done((bf16[384,1024]{1,0:T(8,128)(2,1)S(1)}, bf16[384,1024]{1,0:T(8,128)(2,1)S(1)}, u32[]{:S(2)}, u32[]{:S(2)}) %collective-permute-start.7) | collective-permute-done | bytes 786464 | tf_op jit(solution)/shard_map/ppermute | solution.py:59
  59.2 1.5 %shard_map.81.refs_3_ = f32[512,1024]{1,0:T(8,128)S(1)} custom-call(s32[4]{0:T(128)S(1)} %pad_add_fusion.place, bf16[512,1024]{1,0:T(8,128)(2,1)S(1)} %shard_map.77.refs_0_, bf16[128,1024]{1,0:T(8,128)(2,1)S(1)} %collective-permute-done.4.refs_1_.refs_4_, bf16[384,1024]{1,0:T(8,128)(2,1)S(1)} %collective-permute-done.7.refs_2_.refs_5_, ...), custom_call_target="tpu_custom_call" | custom-call | flops 268435456 | bytes 1048576 | tf_op jit(solution)/shard_map/pallas_call | solution.py:165
  60.7 7.8 %collective-permute-done.8.refs_2_.refs_7_ = bf16[384,1024]{1,0:T(8,128)(2,1)S(1)} collective-permute-done((bf16[384,1024]{1,0:T(8,128)(2,1)S(1)}, bf16[384,1024]{1,0:T(8,128)(2,1)S(1)}, u32[]{:S(2)}, u32[]{:S(2)}) %collective-permute-start.8) | collective-permute-done | bytes 786464 | tf_op jit(solution)/shard_map/ppermute | solution.py:59
  68.5 1.5 %shard_map.82.refs_10_ = f32[512,1024]{1,0:T(8,128)S(1)} custom-call(s32[4]{0:T(128)S(1)} %pad_add_fusion.place, bf16[512,1024]{1,0:T(8,128)(2,1)S(1)} %shard_map.77.refs_0_, bf16[128,1024]{1,0:T(8,128)(2,1)S(1)} %collective-permute-done.5.refs_1_.refs_6_, bf16[384,1024]{1,0:T(8,128)(2,1)S(1)} %collective-permute-done.8.refs_2_.refs_7_, ...), custom_call_target="tpu_custom_call" | custom-call | flops 268435456 | bytes 1048576 | tf_op jit(solution)/shard_map/pallas_call | solution.py:165
  70.0 0.9 shard_map.79.refs_1_
  70.9 1.9 %shard_map.84 = f32[256,1024]{1,0:T(8,128)S(1)} custom-call(s32[4]{0:T(128)S(1)} %pad_add_fusion.place, bf16[512,1024]{1,0:T(8,128)(2,1)S(1)} %shard_map.77.refs_0_, bf16[512,1024]{1,0:T(8,128)(2,1)S(1)} %shard_map.79.refs_1_, bf16[128,1024]{1,0:T(8,128)(2,1)S(1)} %copy-done.1, bf16[384,1024]{1,0:T(8,128)(2,1)S(1)} %shard_map.78.refs_2_.refs_3_, ...), custom_call_target="tpu_custom_call" | custom-call | flops 671088640 | bytes 1048576 | tf_op jit(solution)/shard_map/pallas_call | solution.py:165
  72.9 1.9 %collective-permute-start.10 = (f32[256,1024]{1,0:T(8,128)S(1)}, f32[256,1024]{1,0:T(8,128)S(1)}, u32[]{:S(2)}, u32[]{:S(2)}) collective-permute-start(f32[256,1024]{1,0:T(8,128)S(1)} %shard_map.84), channel_id=1, source_target_pairs={{0,16},{16,0},{1,17},{17,1},{2,18},{18,2},{3,19},{19,3},{4,20},{20... | collective-permute-start | bytes 3145736 | tf_op jit(solution)/shard_map/ppermute | solution.py:304
  74.8 2.0 %shard_map.83.mine = f32[256,1024]{1,0:T(8,128)S(1)} custom-call(s32[4]{0:T(128)S(1)} %pad_add_fusion.place, bf16[512,1024]{1,0:T(8,128)(2,1)S(1)} %shard_map.77.refs_0_, bf16[512,1024]{1,0:T(8,128)(2,1)S(1)} %shard_map.79.refs_1_, bf16[128,1024]{1,0:T(8,128)(2,1)S(1)} %copy-done.1, bf16[384,1024]{1,0:T(8,128)(2,1)S(1)} %shard_map.78.refs_2_.refs_3_, ...), custom_call_target="tpu_custom_call" | custom-call | flops 671088640 | bytes 1048576 | tf_op jit(solution)/shard_map/pallas_call | solution.py:165
  76.8 0.6 collective-permute-done.10.theirs
  77.4 0.1 shard_map.85
  77.5 15.1 %all_to_all.20.received = f32[32,8,128]{2,1,0:T(8,128)S(1)} all-to-all(f32[32,8,128]{2,1,0:T(8,128)S(1)} %get-tuple-element.33), channel_id=1, replica_groups=mesh['y'=4,'x'=4,'core'=2,'z'=16] {'y','x','core'}, dimensions={0} | all-to-all | bytes 262144 | tf_op jit(solution)/shard_map/all_to_all | solution.py:69
  92.6 1.0 shard_map.86
  93.6 20.7 %all_to_all.21.received = f32[16,8,128]{2,1,0:T(8,128)S(1)} all-to-all(f32[16,8,128]{2,1,0:T(8,128)S(1)} %get-tuple-element.35), channel_id=1, replica_groups=mesh['y'=4,'x'=4,'core'=2,'z'=16] {'z'}, dimensions={0} | all-to-all | bytes 131072 | tf_op jit(solution)/shard_map/all_to_all | solution.py:69
  114.3 0.6 shard_map.87
  114.9 12.5 %all_to_all.22.received = f32[32,4,128]{2,1,0:T(4,128)S(1)} all-to-all(f32[32,4,128]{2,1,0:T(4,128)S(1)} %get-tuple-element.36), channel_id=1, replica_groups=mesh['y'=4,'x'=4,'core'=2,'z'=16] {'y','x','core'}, dimensions={0} | all-to-all | bytes 131072 | tf_op jit(solution)/shard_map/all_to_all | solution.py:69
  127.4 1.4 %shard_map.88 = f32[256,1024]{1,0:T(8,128)} custom-call(f32[32,4,128]{2,1,0:T(4,128)S(1)} %all_to_all.22.received, f32[2,128]{1,0:T(2,128)S(1)} %get-tuple-element.37.row_root, f32[8,128]{1,0:T(8,128)S(1)} %get-tuple-element.38.col_root, f32[256,1024]{1,0:T(8,128)S(1)} %get-tuple-element.34.grad, f32[256,1024]{1,0:T(8,128)S(1)} %copy-done), custom_call_target="tpu_custom_call" | custom-call | flops 1048576 | bytes 3145728 | tf_op jit(solution)/shard_map/pallas_call | solution.py:275
  (17 shorter events, 0.1 us)
Async XLA Ops:
  0.7 10.5 %copy-start.1 = (bf16[128,1024]{1,0:T(8,128)(2,1)S(1)}, bf16[128,1024]{1,0:T(8,128)(2,1)}, u32[]{:S(2)}) copy-start(bf16[128,1024]{1,0:T(8,128)(2,1)} %refs_2_.3) | copy-start | bytes 786436
  3.6 27.1 %all-to-all-start = ((bf16[16,64,512]{2,1,0:T(8,128)(2,1)}), bf16[16,64,512]{2,1,0:T(8,128)(2,1)S(1)}, u32[]{:S(2)}, u32[]{:S(2)}) async-start(bf16[16,64,512]{2,1,0:T(8,128)(2,1)} %shard_map.76), calls=%async_computation | async-start | bytes 2097152 | tf_op jit(solution)/shard_map/all_to_all | solution.py:69
  11.2 16.7 %collective-permute-start.6 = (bf16[128,1024]{1,0:T(8,128)(2,1)S(1)}, bf16[128,1024]{1,0:T(8,128)(2,1)S(1)}, u32[]{:S(2)}, u32[]{:S(2)}) collective-permute-start(bf16[128,1024]{1,0:T(8,128)(2,1)S(1)} %copy-done.1), channel_id=1, source_target_pairs={{0,384},{16,112},{32,416},{48,16},{64,448},{80,48},{96,480},{112,8... | collective-permute-start | bytes 786440 | tf_op jit(solution)/shard_map/ppermute | solution.py:59
  15.7 15.0 %collective-permute-start.5 = (bf16[128,1024]{1,0:T(8,128)(2,1)S(1)}, bf16[128,1024]{1,0:T(8,128)(2,1)S(1)}, u32[]{:S(2)}, u32[]{:S(2)}) collective-permute-start(bf16[128,1024]{1,0:T(8,128)(2,1)S(1)} %copy-done.1), channel_id=1, source_target_pairs={{0,256},{16,80},{32,288},{48,112},{64,320},{80,16},{96,352},{112,4... | collective-permute-start | bytes 786440 | tf_op jit(solution)/shard_map/ppermute | solution.py:59
  18.2 24.2 %collective-permute-start.4 = (bf16[128,1024]{1,0:T(8,128)(2,1)S(1)}, bf16[128,1024]{1,0:T(8,128)(2,1)S(1)}, u32[]{:S(2)}, u32[]{:S(2)}) collective-permute-start(bf16[128,1024]{1,0:T(8,128)(2,1)S(1)} %copy-done.1), channel_id=1, source_target_pairs={{0,128},{16,48},{32,160},{48,80},{64,192},{80,112},{96,224},{112,1... | collective-permute-start | bytes 786440 | tf_op jit(solution)/shard_map/ppermute | solution.py:59
  20.7 21.7 %collective-permute-start.3 = (bf16[128,1024]{1,0:T(8,128)(2,1)S(1)}, bf16[128,1024]{1,0:T(8,128)(2,1)S(1)}, u32[]{:S(2)}, u32[]{:S(2)}) collective-permute-start(bf16[128,1024]{1,0:T(8,128)(2,1)S(1)} %copy-done.1), channel_id=1, source_target_pairs={{0,96},{16,400},{32,0},{48,432},{64,32},{80,464},{96,64},{112,496}... | collective-permute-start | bytes 786440 | tf_op jit(solution)/shard_map/ppermute | solution.py:59
  25.0 17.4 %collective-permute-start.2 = (bf16[128,1024]{1,0:T(8,128)(2,1)S(1)}, bf16[128,1024]{1,0:T(8,128)(2,1)S(1)}, u32[]{:S(2)}, u32[]{:S(2)}) collective-permute-start(bf16[128,1024]{1,0:T(8,128)(2,1)S(1)} %copy-done.1), channel_id=1, source_target_pairs={{0,64},{16,272},{32,96},{48,304},{64,0},{80,336},{96,32},{112,368}... | collective-permute-start | bytes 786440 | tf_op jit(solution)/shard_map/ppermute | solution.py:59
  27.9 14.5 %collective-permute-start.1 = (bf16[128,1024]{1,0:T(8,128)(2,1)S(1)}, bf16[128,1024]{1,0:T(8,128)(2,1)S(1)}, u32[]{:S(2)}, u32[]{:S(2)}) collective-permute-start(bf16[128,1024]{1,0:T(8,128)(2,1)S(1)} %copy-done.1), channel_id=1, source_target_pairs={{0,32},{16,144},{32,64},{48,176},{64,96},{80,208},{96,0},{112,240}... | collective-permute-start | bytes 786440 | tf_op jit(solution)/shard_map/ppermute | solution.py:59
  30.8 39.2 %collective-permute-start = (bf16[16,64,512]{2,1,0:T(8,128)(2,1)S(1)}, bf16[16,64,512]{2,1,0:T(8,128)(2,1)S(1)}, u32[]{:S(2)}, u32[]{:S(2)}) collective-permute-start(bf16[16,64,512]{2,1,0:T(8,128)(2,1)S(1)} %all-to-all-done.part), channel_id=1, source_target_pairs={{0,1},{1,2},{2,3},{3,4},{4,5},{5,6},{6,7},{7,8},{8,9},{9,10},{10,1... | collective-permute-start | bytes 3145736 | tf_op jit(solution)/shard_map/ppermute | solution.py:65
  42.5 16.7 %collective-permute-start.7 = (bf16[384,1024]{1,0:T(8,128)(2,1)S(1)}, bf16[384,1024]{1,0:T(8,128)(2,1)S(1)}, u32[]{:S(2)}, u32[]{:S(2)}) collective-permute-start(bf16[384,1024]{1,0:T(8,128)(2,1)S(1)} %shard_map.78.refs_2_.refs_3_), channel_id=1, source_target_pairs={{0,128},{16,48},{32,160},{48,80},{64,192},{80,112},{96,224},{112,1... | collective-permute-start | bytes 2359304 | tf_op jit(solution)/shard_map/ppermute | solution.py:59
  48.3 20.2 %collective-permute-start.8 = (bf16[384,1024]{1,0:T(8,128)(2,1)S(1)}, bf16[384,1024]{1,0:T(8,128)(2,1)S(1)}, u32[]{:S(2)}, u32[]{:S(2)}) collective-permute-start(bf16[384,1024]{1,0:T(8,128)(2,1)S(1)} %shard_map.78.refs_2_.refs_3_), channel_id=1, source_target_pairs={{0,256},{16,80},{32,288},{48,112},{64,320},{80,16},{96,352},{112,4... | collective-permute-start | bytes 2359304 | tf_op jit(solution)/shard_map/ppermute | solution.py:59
  52.6 17.3 %collective-permute-start.9 = (bf16[384,1024]{1,0:T(8,128)(2,1)S(1)}, bf16[384,1024]{1,0:T(8,128)(2,1)S(1)}, u32[]{:S(2)}, u32[]{:S(2)}) collective-permute-start(bf16[384,1024]{1,0:T(8,128)(2,1)S(1)} %shard_map.78.refs_2_.refs_3_), channel_id=1, source_target_pairs={{0,384},{16,112},{32,416},{48,16},{64,448},{80,48},{96,480},{112,8... | collective-permute-start | bytes 2359304 | tf_op jit(solution)/shard_map/ppermute | solution.py:59
  72.9 4.6 %collective-permute-start.10 = (f32[256,1024]{1,0:T(8,128)S(1)}, f32[256,1024]{1,0:T(8,128)S(1)}, u32[]{:S(2)}, u32[]{:S(2)}) collective-permute-start(f32[256,1024]{1,0:T(8,128)S(1)} %shard_map.84), channel_id=1, source_target_pairs={{0,16},{16,0},{1,17},{17,1},{2,18},{18,2},{3,19},{19,3},{4,20},{20... | collective-permute-start | bytes 3145736 | tf_op jit(solution)/shard_map/ppermute | solution.py:304
  76.7 15.9 %copy-start = (f32[256,1024]{1,0:T(8,128)S(1)}, f32[256,1024]{1,0:T(8,128)}, u32[]{:S(2)}) copy-start(f32[256,1024]{1,0:T(8,128)} %weight.3) | copy-start | bytes 3145732
  76.8 15.9 %copy-start.2 = (f32[1024]{0:T(1024)S(1)}, f32[1024]{0:T(1024)}, u32[]{:S(2)}) copy-start(f32[1024]{0:T(1024)} %param.9) | copy-start | bytes 12292
  76.8 37.5 %copy-start.3 = (f32[256]{0:T(256)S(1)}, f32[256]{0:T(256)}, u32[]{:S(2)}) copy-start(f32[256]{0:T(256)} %param.8) | copy-start | bytes 3076

commit v8 on v7

--- a/solution.py
+++ b/solution.py
@@ -33,7 +33,7 @@
 ANYWHERE = pl.BlockSpec(memory_space=pl.ANY)
 WHOLE = pl.BlockSpec(memory_space=pltpu.VMEM)
 SCALARS = pl.BlockSpec(memory_space=pltpu.SMEM)
-PARAMS = pltpu.CompilerParams(vmem_limit_bytes=16 * 2**20)
+PARAMS = pltpu.CompilerParams(vmem_limit_bytes=12 * 2**20)
 
 
 def shape(*dims, dtype=jnp.float32):
@@ -116,7 +116,7 @@
     )(*blocks)
 
 
-def turn_kernel(place, part, out):
+def turn_kernel(place, part, *outs):
     y, x, core = place[0], place[1], place[2]
 
     def block(i):
@@ -125,15 +125,16 @@
         return part[((y - dy) & (SIDE - 1)) * SIDE + ((x - dx) & (SIDE - 1))]
 
     for i in range(0, COUNT, 2):
-        out[:, i * HALF : (i + 2) * HALF] = jnp.concatenate([block(i), block(i + 1)], axis=0).T
+        first = i % (2 * SIDE) * HALF
+        outs[i // (2 * SIDE)][:, first : first + 2 * HALF] = jnp.concatenate([block(i), block(i + 1)], axis=0).T
 
 
 def turn(place, part):
     return pl.pallas_call(
         turn_kernel,
-        out_shape=shape(2 * ROW_BLOCK, COUNT * HALF, dtype=jnp.bfloat16),
+        out_shape=(shape(2 * ROW_BLOCK, 2 * SIDE * HALF, dtype=jnp.bfloat16),) * 2,
         in_specs=[SCALARS, WHOLE],
-        out_specs=WHOLE,
+        out_specs=(WHOLE, WHOLE),
         compiler_params=PARAMS,
         cost_estimate=cost(0, 2**21),
     )(place, part)
@@ -153,7 +154,8 @@
             offset = pl.multiple_of(start if exchanged else HALF - start, HALF)
             blocks = [operands[grads][pl.ds(offset, HALF), columns]]
             blocks += [operands[grads + 1][pl.ds(i * TOKENS + offset, HALF), columns] for i in range(SIDE - 1)]
-            features = operands[turned][rows, group * SIDE * HALF : (group + 1) * SIDE * HALF]
+            lanes = group % 2 * SIDE * HALF
+            features = operands[turned][rows, lanes : lanes + SIDE * HALF]
             term = jnp.dot(features, jnp.concatenate(blocks, axis=0), preferred_element_type=jnp.float32)
             value = term if value is None else value + term
         out[:, columns] = value
@@ -286,20 +288,20 @@
 def shards(activations, out_grads, weight, row_moment, col_moment):
     y, x, core, layer = (lax.axis_index(name) for name in ("y", "x", "core", "z"))
     place = jnp.stack([y, x, core, layer & 1])
-    first = exchange(pack(place, activations), CHIPS)
-    second = next_layer(first)
+    packed = pack(place, activations)
     line = [along(out_grads, k, 0) for k in range(1, SIDE)]
     grads = [out_grads] + [along(out_grads, j, 1) for j in range(1, SIDE)]
-    line, grads[1:] = lax.optimization_barrier((line, grads[1:]))
+    packed, line, grads[1] = lax.optimization_barrier((packed, line, grads[1]))
+    line, grads[2:] = lax.optimization_barrier((line, grads[2:]))
+    first = turn(place, exchange(packed, CHIPS))
+    second = [next_layer(part) for part in first]
     line = join(line)
     lines = [line] + [along(line, j, 1) for j in range(1, SIDE)]
-    first = turn(place, first)
     total = None
     for j in range(SIDE - 1):
-        total = product(place, [first, grads[j], lines[j]], [(0, 1, j, True)], total)
-    second, *lines = lax.optimization_barrier((second, *lines))
-    operands = [first, turn(place, second)] + [block for pair in zip(grads, lines) for block in pair]
-    parts = [(0, 2 * SIDE, SIDE - 1, True)] + [(1, 2 + 2 * j, j, False) for j in range(SIDE)]
+        total = product(place, [first[j // 2], grads[j], lines[j]], [(0, 1, j, True)], total)
+    operands = [first[1]] + second + [block for pair in zip(grads, lines) for block in pair]
+    parts = [(0, 1 + 2 * SIDE, SIDE - 1, True)] + [(1 + j // 2, 3 + 2 * j, j, False) for j in range(SIDE)]
     theirs = product(place, operands, parts, total, lambda core: 1 - core)
     received = lax.ppermute(theirs, "core", [(0, 1), (1, 0)])
     mine = product(place, operands, parts, total, lambda core: core)

time: 129 us -> 138 us (1.070)
  waiting for transfers between devices: 11.1 us -> 19 us
  blocking collectives: 48.3 us -> 43.9 us
  local copies, waits for them, and re-layouts: 0.02 us -> 2.4 us
  starting transfers between devices: 52.2 us -> 54.2 us
    ppermute x9, waiting for transfers between devices: 10.4 us -> 15.3 us  [along(): return lax.ppermute(value, ROWS, pairs)]
    all_to_all x3, blocking collectives: 48.3 us -> 43.9 us  [exchange(): return lax.all_to_all(tiles, axes, 0, 0)]
    all_to_all x1, starting transfers between devices: 7.6 us -> 3.66 us  [exchange(): return lax.all_to_all(tiles, axes, 0, 0)]
    ppermute x1, starting transfers between devices: 1.92 us -> 5.55 us  [shards(): received = lax.ppermute(theirs, 'core', [(0, 1), (1, 0)])]
    ppermute x1 -> x2, waiting for transfers between devices: 0.01 us -> 3.6 us  [next_layer(): return lax.ppermute(value, ('core', 'z'), pairs)]
    unnamed x8 -> x22, local copies, waits for them, and re-layouts: 0.02 us -> 2.4 us
    ppermute x9, starting transfers between devices: 31.1 us -> 32.6 us  [along(): return lax.ppermute(value, ROWS, pairs)]
    ppermute x1 -> x2, starting transfers between devices: 11.6 us -> 12.4 us  [next_layer(): return lax.ppermute(value, ('core', 'z'), pairs)]
  transfers between devices with their start and end apart: 12 -> 13, of which waited for: 4 -> 4; matrix products, arithmetic and copies ran while one was open for 0% -> 0% of each run, Pallas kernels for 6% -> 8%
where the time goes in v8:
time: 138 us; the launch traced here: 137 us
  starting transfers between devices  54.2 us (39%)
  blocking collectives  43.9 us (32%)
  waiting for transfers between devices  19 us (14%)
  Pallas kernels  16.5 us (12%)
  local copies, waits for them, and re-layouts  2.4 us (2%)
    all_to_all x3, blocking collectives, exchange(): return lax.all_to_all(tiles, axes, 0, 0)  43.9 us
    ppermute x9, starting transfers between devices, along(): return lax.ppermute(value, ROWS, pairs)  32.6 us
    ppermute x9, waiting for transfers between devices, along(): return lax.ppermute(value, ROWS, pairs)  15.3 us
    ppermute x2, starting transfers between devices, next_layer(): return lax.ppermute(value, ('core', 'z'), pairs)  12.4 us
    pallas_call x5, Pallas kernels, product(): pl.pallas_call(functools.partial(product_kernel, parts, which), out_shape...  9.53 us
    ppermute x1, starting transfers between devices, shards(): received = lax.ppermute(theirs, 'core', [(0, 1), (1, 0)])  5.55 us
    all_to_all x1, starting transfers between devices, exchange(): return lax.all_to_all(tiles, axes, 0, 0)  3.66 us
    ppermute x2, waiting for transfers between devices, next_layer(): return lax.ppermute(value, ('core', 'z'), pairs)  3.6 us
  transfers between devices with their start and end apart: 13, of which 4 were waited for; matrix products, arithmetic and copies ran while one was open for 0% of the time, Pallas kernels for 8%

profile of v8, /device:TPU:1, one launch (start us, length us, event | category | flops | bytes accessed | tf_op | source)
XLA Modules:
  0.0 137.0 jit_solution(12664472245024334964)
XLA Ops:
  0.6 4.0 %collective-permute-start = (bf16[128,1024]{1,0:T(8,128)(2,1)}, bf16[128,1024]{1,0:T(8,128)(2,1)S(1)}, u32[]{:S(2)}, u32[]{:S(2)}) collective-permute-start(bf16[128,1024]{1,0:T(8,128)(2,1)} %refs_3_.3), channel_id=1, source_target_pairs={{0,32},{16,144},{32,64},{48,176},{64,96},{80,208},{96,0},{112,240}... | collective-permute-start | bytes 786440 | tf_op jit(solution)/shard_map/ppermute | solution.py:59
  4.7 4.5 %collective-permute-start.1 = (bf16[128,1024]{1,0:T(8,128)(2,1)}, bf16[128,1024]{1,0:T(8,128)(2,1)S(1)}, u32[]{:S(2)}, u32[]{:S(2)}) collective-permute-start(bf16[128,1024]{1,0:T(8,128)(2,1)} %refs_3_.3), channel_id=1, source_target_pairs={{0,64},{16,272},{32,96},{48,304},{64,0},{80,336},{96,32},{112,368}... | collective-permute-start | bytes 786440 | tf_op jit(solution)/shard_map/ppermute | solution.py:59
  9.2 3.0 %collective-permute-start.2 = (bf16[128,1024]{1,0:T(8,128)(2,1)}, bf16[128,1024]{1,0:T(8,128)(2,1)S(1)}, u32[]{:S(2)}, u32[]{:S(2)}) collective-permute-start(bf16[128,1024]{1,0:T(8,128)(2,1)} %refs_3_.3), channel_id=1, source_target_pairs={{0,96},{16,400},{32,0},{48,432},{64,32},{80,464},{96,64},{112,496}... | collective-permute-start | bytes 786440 | tf_op jit(solution)/shard_map/ppermute | solution.py:59
  12.2 3.1 %collective-permute-start.3 = (bf16[128,1024]{1,0:T(8,128)(2,1)}, bf16[128,1024]{1,0:T(8,128)(2,1)S(1)}, u32[]{:S(2)}, u32[]{:S(2)}) collective-permute-start(bf16[128,1024]{1,0:T(8,128)(2,1)} %refs_3_.3), channel_id=1, source_target_pairs={{0,128},{16,48},{32,160},{48,80},{64,192},{80,112},{96,224},{112,1... | collective-permute-start | bytes 786440 | tf_op jit(solution)/shard_map/ppermute | solution.py:59
  15.4 2.9 %shard_map.76 = bf16[16,64,512]{2,1,0:T(8,128)(2,1)} custom-call(s32[4]{0:T(128)S(1)} %pad_add_fusion.place, bf16[128,8192]{1,0:T(8,128)(2,1)} %source.1), custom_call_target="tpu_custom_call" | custom-call | bytes 2097152 | tf_op jit(solution)/shard_map/pallas_call | solution.py:85
  18.4 3.8 %collective-permute-done.3.refs_1_.refs_5_ = bf16[128,1024]{1,0:T(8,128)(2,1)S(1)} collective-permute-done((bf16[128,1024]{1,0:T(8,128)(2,1)}, bf16[128,1024]{1,0:T(8,128)(2,1)S(1)}, u32[]{:S(2)}, u32[]{:S(2)}) %collective-permute-start.3) | collective-permute-done | bytes 262176 | tf_op jit(solution)/shard_map/ppermute | solution.py:59
  22.1 3.7 %all-to-all-start = ((bf16[16,64,512]{2,1,0:T(8,128)(2,1)}), bf16[16,64,512]{2,1,0:T(8,128)(2,1)S(1)}, u32[]{:S(2)}, u32[]{:S(2)}) async-start(bf16[16,64,512]{2,1,0:T(8,128)(2,1)} %shard_map.76), calls=%async_computation | async-start | bytes 2097152 | tf_op jit(solution)/shard_map/all_to_all | solution.py:69
  25.8 4.7 %collective-permute-start.6 = (bf16[128,1024]{1,0:T(8,128)(2,1)S(1)}, bf16[128,1024]{1,0:T(8,128)(2,1)S(1)}, u32[]{:S(2)}, u32[]{:S(2)}) collective-permute-start(bf16[128,1024]{1,0:T(8,128)(2,1)S(1)} %copy-done.5), channel_id=1, source_target_pairs={{0,256},{16,80},{32,288},{48,112},{64,320},{80,16},{96,352},{112,4... | collective-permute-start | bytes 786440 | tf_op jit(solution)/shard_map/ppermute | solution.py:59
  30.5 2.8 %collective-permute-start.7 = (bf16[128,1024]{1,0:T(8,128)(2,1)S(1)}, bf16[128,1024]{1,0:T(8,128)(2,1)S(1)}, u32[]{:S(2)}, u32[]{:S(2)}) collective-permute-start(bf16[128,1024]{1,0:T(8,128)(2,1)S(1)} %copy-done.5), channel_id=1, source_target_pairs={{0,384},{16,112},{32,416},{48,16},{64,448},{80,48},{96,480},{112,8... | collective-permute-start | bytes 786440 | tf_op jit(solution)/shard_map/ppermute | solution.py:59
  33.3 9.3 %collective-permute-done.6.refs_1_.refs_7_ = bf16[128,1024]{1,0:T(8,128)(2,1)S(1)} collective-permute-done((bf16[128,1024]{1,0:T(8,128)(2,1)S(1)}, bf16[128,1024]{1,0:T(8,128)(2,1)S(1)}, u32[]{:S(2)}, u32[]{:S(2)}) %collective-permute-start.6) | collective-permute-done | bytes 262176 | tf_op jit(solution)/shard_map/ppermute | solution.py:59
  42.6 0.7 copy-done.3
  43.3 2.2 %collective-permute-done.7.refs_9_ = bf16[128,1024]{1,0:T(8,128)(2,1)S(1)} collective-permute-done((bf16[128,1024]{1,0:T(8,128)(2,1)S(1)}, bf16[128,1024]{1,0:T(8,128)(2,1)S(1)}, u32[]{:S(2)}, u32[]{:S(2)}) %collective-permute-start.7) | collective-permute-done | bytes 262176 | tf_op jit(solution)/shard_map/ppermute | solution.py:59
  45.5 0.7 copy-done.7
  46.3 3.3 %collective-permute-start.8 = (bf16[384,1024]{1,0:T(8,128)(2,1)S(1)}, bf16[384,1024]{1,0:T(8,128)(2,1)S(1)}, u32[]{:S(2)}, u32[]{:S(2)}) collective-permute-start(bf16[384,1024]{1,0:T(8,128)(2,1)S(1)} %shard_map.78.refs_2_.refs_4_), channel_id=1, source_target_pairs={{0,128},{16,48},{32,160},{48,80},{64,192},{80,112},{96,224},{112,1... | collective-permute-start | bytes 2359304 | tf_op jit(solution)/shard_map/ppermute | solution.py:59
  49.6 3.3 %collective-permute-start.9 = (bf16[384,1024]{1,0:T(8,128)(2,1)S(1)}, bf16[384,1024]{1,0:T(8,128)(2,1)S(1)}, u32[]{:S(2)}, u32[]{:S(2)}) collective-permute-start(bf16[384,1024]{1,0:T(8,128)(2,1)S(1)} %shard_map.78.refs_2_.refs_4_), channel_id=1, source_target_pairs={{0,256},{16,80},{32,288},{48,112},{64,320},{80,16},{96,352},{112,4... | collective-permute-start | bytes 2359304 | tf_op jit(solution)/shard_map/ppermute | solution.py:59
  52.9 4.0 %collective-permute-start.10 = (bf16[384,1024]{1,0:T(8,128)(2,1)S(1)}, bf16[384,1024]{1,0:T(8,128)(2,1)}, u32[]{:S(2)}, u32[]{:S(2)}) collective-permute-start(bf16[384,1024]{1,0:T(8,128)(2,1)S(1)} %shard_map.78.refs_2_.refs_4_), channel_id=1, source_target_pairs={{0,384},{16,112},{32,416},{48,16},{64,448},{80,48},{96,480},{112,8... | collective-permute-start | bytes 2359304 | tf_op jit(solution)/shard_map/ppermute | solution.py:59
  56.9 0.9 shard_map.77
  57.7 9.8 %collective-permute-start.5 = (bf16[512,512]{1,0:T(8,128)(2,1)S(1)}, bf16[512,512]{1,0:T(8,128)(2,1)S(1)}, u32[]{:S(2)}, u32[]{:S(2)}) collective-permute-start(bf16[512,512]{1,0:T(8,128)(2,1)S(1)} %get-tuple-element.24.refs_0_), channel_id=1, source_target_pairs={{0,1},{1,2},{2,3},{3,4},{4,5},{5,6},{6,7},{7,8},{8,9},{9,10},{10,1... | collective-permute-start | bytes 1572872 | tf_op jit(solution)/shard_map/ppermute | solution.py:65
  67.5 2.6 %collective-permute-start.4 = (bf16[512,512]{1,0:T(8,128)(2,1)S(1)}, bf16[512,512]{1,0:T(8,128)(2,1)S(1)}, u32[]{:S(2)}, u32[]{:S(2)}) collective-permute-start(bf16[512,512]{1,0:T(8,128)(2,1)S(1)} %get-tuple-element.25.refs_0_), channel_id=1, source_target_pairs={{0,1},{1,2},{2,3},{3,4},{4,5},{5,6},{6,7},{7,8},{8,9},{9,10},{10,1... | collective-permute-start | bytes 1572872 | tf_op jit(solution)/shard_map/ppermute | solution.py:65
  70.2 0.9 copy-done.6
  71.1 1.5 %shard_map.79.refs_3_ = f32[512,1024]{1,0:T(8,128)S(1)} custom-call(s32[4]{0:T(128)S(1)} %pad_add_fusion.place, bf16[512,512]{1,0:T(8,128)(2,1)S(1)} %get-tuple-element.25.refs_0_, bf16[128,1024]{1,0:T(8,128)(2,1)S(1)} %copy-done.6, bf16[384,1024]{1,0:T(8,128)(2,1)S(1)} %shard_map.78.refs_2_.refs_4_), custom_call_target="tpu_custom_call" | custom-call | flops 268435456 | bytes 1048576 | tf_op jit(solution)/shard_map/pallas_call | solution.py:167
  72.6 1.5 %shard_map.80.refs_3_ = f32[512,1024]{1,0:T(8,128)S(1)} custom-call(s32[4]{0:T(128)S(1)} %pad_add_fusion.place, bf16[512,512]{1,0:T(8,128)(2,1)S(1)} %get-tuple-element.25.refs_0_, bf16[128,1024]{1,0:T(8,128)(2,1)S(1)} %copy-done.2, bf16[384,1024]{1,0:T(8,128)(2,1)S(1)} %collective-permute-done.8.refs_2_.refs_6_, f32[512,1024]{1,0:T(8,128)S(1)} %shard_map.79.refs_3_), custom_call_target="tpu_custom_call" | custom-call | flops 268435456 | bytes 1048576 | tf_op jit(solution)/shard_map/pallas_call | solution.py:167
  74.2 1.5 %shard_map.81.refs_11_ = f32[512,1024]{1,0:T(8,128)S(1)} custom-call(s32[4]{0:T(128)S(1)} %pad_add_fusion.place, bf16[512,512]{1,0:T(8,128)(2,1)S(1)} %get-tuple-element.24.refs_0_, bf16[128,1024]{1,0:T(8,128)(2,1)S(1)} %copy-done.4, bf16[384,1024]{1,0:T(8,128)(2,1)S(1)} %collective-permute-done.9.refs_2_.refs_8_, f32[512,1024]{1,0:T(8,128)S(1)} %shard_map.80.refs_3_), custom_call_target="tpu_custom_call" | custom-call | flops 268435456 | bytes 1048576 | tf_op jit(solution)/shard_map/pallas_call | solution.py:167
  75.6 3.6 %collective-permute-done.4.refs_1_ = bf16[512,512]{1,0:T(8,128)(2,1)S(1)} collective-permute-done((bf16[512,512]{1,0:T(8,128)(2,1)S(1)}, bf16[512,512]{1,0:T(8,128)(2,1)S(1)}, u32[]{:S(2)}, u32[]{:S(2)}) %collective-permute-start.4) | collective-permute-done | bytes 524320 | tf_op jit(solution)/shard_map/ppermute | solution.py:65
  79.2 2.6 %shard_map.83 = f32[256,1024]{1,0:T(8,128)S(1)} custom-call(s32[4]{0:T(128)S(1)} %pad_add_fusion.place, bf16[512,512]{1,0:T(8,128)(2,1)S(1)} %get-tuple-element.24.refs_0_, bf16[512,512]{1,0:T(8,128)(2,1)S(1)} %collective-permute-done.4.refs_1_, bf16[512,512]{1,0:T(8,128)(2,1)S(1)} %collective-permute-done.5.refs_2_, bf16[128,1024]{1,0:T(8,128)(2,1)S(1)} %copy-done.6, ...), custom_call_target="tpu_custom_call" | custom-call | flops 671088640 | bytes 1048576 | tf_op jit(solution)/shard_map/pallas_call | solution.py:167
  81.8 5.6 %collective-permute-start.11 = (f32[256,1024]{1,0:T(8,128)S(1)}, f32[256,1024]{1,0:T(8,128)S(1)}, u32[]{:S(2)}, u32[]{:S(2)}) collective-permute-start(f32[256,1024]{1,0:T(8,128)S(1)} %shard_map.83), channel_id=1, source_target_pairs={{0,16},{16,0},{1,17},{17,1},{2,18},{18,2},{3,19},{19,3},{4,20},{20... | collective-permute-start | bytes 3145736 | tf_op jit(solution)/shard_map/ppermute | solution.py:306
  87.4 2.6 %shard_map.82.mine = f32[256,1024]{1,0:T(8,128)S(1)} custom-call(s32[4]{0:T(128)S(1)} %pad_add_fusion.place, bf16[512,512]{1,0:T(8,128)(2,1)S(1)} %get-tuple-element.24.refs_0_, bf16[512,512]{1,0:T(8,128)(2,1)S(1)} %collective-permute-done.4.refs_1_, bf16[512,512]{1,0:T(8,128)(2,1)S(1)} %collective-permute-done.5.refs_2_, bf16[128,1024]{1,0:T(8,128)(2,1)S(1)} %copy-done.6, ...), custom_call_target="tpu_custom_call" | custom-call | flops 671088640 | bytes 1048576 | tf_op jit(solution)/shard_map/pallas_call | solution.py:167
  90.1 11.4 %all_to_all.20.received = f32[32,8,128]{2,1,0:T(8,128)S(1)} all-to-all(f32[32,8,128]{2,1,0:T(8,128)S(1)} %get-tuple-element.35), channel_id=1, replica_groups=mesh['y'=4,'x'=4,'core'=2,'z'=16] {'y','x','core'}, dimensions={0} | all-to-all | bytes 262144 | tf_op jit(solution)/shard_map/all_to_all | solution.py:69
  101.5 1.0 shard_map.85
  102.5 20.0 %all_to_all.21.received = f32[16,8,128]{2,1,0:T(8,128)S(1)} all-to-all(f32[16,8,128]{2,1,0:T(8,128)S(1)} %get-tuple-element.37), channel_id=1, replica_groups=mesh['y'=4,'x'=4,'core'=2,'z'=16] {'z'}, dimensions={0} | all-to-all | bytes 131072 | tf_op jit(solution)/shard_map/all_to_all | solution.py:69
  123.1 12.5 %all_to_all.22.received = f32[32,4,128]{2,1,0:T(4,128)S(1)} all-to-all(f32[32,4,128]{2,1,0:T(4,128)S(1)} %get-tuple-element.38), channel_id=1, replica_groups=mesh['y'=4,'x'=4,'core'=2,'z'=16] {'y','x','core'}, dimensions={0} | all-to-all | bytes 131072 | tf_op jit(solution)/shard_map/all_to_all | solution.py:69
  135.6 1.4 %shard_map.87 = f32[256,1024]{1,0:T(8,128)} custom-call(f32[32,4,128]{2,1,0:T(4,128)S(1)} %all_to_all.22.received, f32[2,128]{1,0:T(2,128)S(1)} %get-tuple-element.39.row_root, f32[8,128]{1,0:T(8,128)S(1)} %get-tuple-element.40.col_root, f32[256,1024]{1,0:T(8,128)S(1)} %get-tuple-element.36.grad, f32[256,1024]{1,0:T(8,128)S(1)} %copy-done), custom_call_target="tpu_custom_call" | custom-call | flops 1048576 | bytes 3145728 | tf_op jit(solution)/shard_map/pallas_call | solution.py:277
  (32 shorter events, 1.0 us)
Async XLA Ops:
  0.6 17.7 %collective-permute-start = (bf16[128,1024]{1,0:T(8,128)(2,1)}, bf16[128,1024]{1,0:T(8,128)(2,1)S(1)}, u32[]{:S(2)}, u32[]{:S(2)}) collective-permute-start(bf16[128,1024]{1,0:T(8,128)(2,1)} %refs_3_.3), channel_id=1, source_target_pairs={{0,32},{16,144},{32,64},{48,176},{64,96},{80,208},{96,0},{112,240}... | collective-permute-start | bytes 786440 | tf_op jit(solution)/shard_map/ppermute | solution.py:59
  4.7 13.7 %collective-permute-start.1 = (bf16[128,1024]{1,0:T(8,128)(2,1)}, bf16[128,1024]{1,0:T(8,128)(2,1)S(1)}, u32[]{:S(2)}, u32[]{:S(2)}) collective-permute-start(bf16[128,1024]{1,0:T(8,128)(2,1)} %refs_3_.3), channel_id=1, source_target_pairs={{0,64},{16,272},{32,96},{48,304},{64,0},{80,336},{96,32},{112,368}... | collective-permute-start | bytes 786440 | tf_op jit(solution)/shard_map/ppermute | solution.py:59
  9.2 9.1 %collective-permute-start.2 = (bf16[128,1024]{1,0:T(8,128)(2,1)}, bf16[128,1024]{1,0:T(8,128)(2,1)S(1)}, u32[]{:S(2)}, u32[]{:S(2)}) collective-permute-start(bf16[128,1024]{1,0:T(8,128)(2,1)} %refs_3_.3), channel_id=1, source_target_pairs={{0,96},{16,400},{32,0},{48,432},{64,32},{80,464},{96,64},{112,496}... | collective-permute-start | bytes 786440 | tf_op jit(solution)/shard_map/ppermute | solution.py:59
  12.2 9.9 %collective-permute-start.3 = (bf16[128,1024]{1,0:T(8,128)(2,1)}, bf16[128,1024]{1,0:T(8,128)(2,1)S(1)}, u32[]{:S(2)}, u32[]{:S(2)}) collective-permute-start(bf16[128,1024]{1,0:T(8,128)(2,1)} %refs_3_.3), channel_id=1, source_target_pairs={{0,128},{16,48},{32,160},{48,80},{64,192},{80,112},{96,224},{112,1... | collective-permute-start | bytes 786440 | tf_op jit(solution)/shard_map/ppermute | solution.py:59
  15.4 10.4 %copy-start.5 = (bf16[128,1024]{1,0:T(8,128)(2,1)S(1)}, bf16[128,1024]{1,0:T(8,128)(2,1)}, u32[]{:S(2)}) copy-start(bf16[128,1024]{1,0:T(8,128)(2,1)} %refs_3_.3) | copy-start | bytes 786436
  22.1 20.5 %copy-start.1 = (bf16[128,1024]{1,0:T(8,128)(2,1)}, bf16[128,1024]{1,0:T(8,128)(2,1)S(1)}, u32[]{:S(2)}) copy-start(bf16[128,1024]{1,0:T(8,128)(2,1)S(1)} %collective-permute-done.3.refs_1_.refs_5_) | copy-start | bytes 786436
  22.1 34.7 %all-to-all-start = ((bf16[16,64,512]{2,1,0:T(8,128)(2,1)}), bf16[16,64,512]{2,1,0:T(8,128)(2,1)S(1)}, u32[]{:S(2)}, u32[]{:S(2)}) async-start(bf16[16,64,512]{2,1,0:T(8,128)(2,1)} %shard_map.76), calls=%async_computation | async-start | bytes 2097152 | tf_op jit(solution)/shard_map/all_to_all | solution.py:69
  25.8 16.8 %collective-permute-start.6 = (bf16[128,1024]{1,0:T(8,128)(2,1)S(1)}, bf16[128,1024]{1,0:T(8,128)(2,1)S(1)}, u32[]{:S(2)}, u32[]{:S(2)}) collective-permute-start(bf16[128,1024]{1,0:T(8,128)(2,1)S(1)} %copy-done.5), channel_id=1, source_target_pairs={{0,256},{16,80},{32,288},{48,112},{64,320},{80,16},{96,352},{112,4... | collective-permute-start | bytes 786440 | tf_op jit(solution)/shard_map/ppermute | solution.py:59
  30.5 15.1 %collective-permute-start.7 = (bf16[128,1024]{1,0:T(8,128)(2,1)S(1)}, bf16[128,1024]{1,0:T(8,128)(2,1)S(1)}, u32[]{:S(2)}, u32[]{:S(2)}) collective-permute-start(bf16[128,1024]{1,0:T(8,128)(2,1)S(1)} %copy-done.5), channel_id=1, source_target_pairs={{0,384},{16,112},{32,416},{48,16},{64,448},{80,48},{96,480},{112,8... | collective-permute-start | bytes 786440 | tf_op jit(solution)/shard_map/ppermute | solution.py:59
  42.6 0.7 copy-start.3
  45.5 0.7 copy-start.7
  46.3 26.3 %collective-permute-start.8 = (bf16[384,1024]{1,0:T(8,128)(2,1)S(1)}, bf16[384,1024]{1,0:T(8,128)(2,1)S(1)}, u32[]{:S(2)}, u32[]{:S(2)}) collective-permute-start(bf16[384,1024]{1,0:T(8,128)(2,1)S(1)} %shard_map.78.refs_2_.refs_4_), channel_id=1, source_target_pairs={{0,128},{16,48},{32,160},{48,80},{64,192},{80,112},{96,224},{112,1... | collective-permute-start | bytes 2359304 | tf_op jit(solution)/shard_map/ppermute | solution.py:59
  49.6 24.5 %collective-permute-start.9 = (bf16[384,1024]{1,0:T(8,128)(2,1)S(1)}, bf16[384,1024]{1,0:T(8,128)(2,1)S(1)}, u32[]{:S(2)}, u32[]{:S(2)}) collective-permute-start(bf16[384,1024]{1,0:T(8,128)(2,1)S(1)} %shard_map.78.refs_2_.refs_4_), channel_id=1, source_target_pairs={{0,256},{16,80},{32,288},{48,112},{64,320},{80,16},{96,352},{112,4... | collective-permute-start | bytes 2359304 | tf_op jit(solution)/shard_map/ppermute | solution.py:59
  52.9 22.7 %collective-permute-start.10 = (bf16[384,1024]{1,0:T(8,128)(2,1)S(1)}, bf16[384,1024]{1,0:T(8,128)(2,1)}, u32[]{:S(2)}, u32[]{:S(2)}) collective-permute-start(bf16[384,1024]{1,0:T(8,128)(2,1)S(1)} %shard_map.78.refs_2_.refs_4_), channel_id=1, source_target_pairs={{0,384},{16,112},{32,416},{48,16},{64,448},{80,48},{96,480},{112,8... | collective-permute-start | bytes 2359304 | tf_op jit(solution)/shard_map/ppermute | solution.py:59
  57.7 14.9 %copy-start.2 = (bf16[128,1024]{1,0:T(8,128)(2,1)S(1)}, bf16[128,1024]{1,0:T(8,128)(2,1)}, u32[]{:S(2)}) copy-start(bf16[128,1024]{1,0:T(8,128)(2,1)} %copy-done.1) | copy-start | bytes 786436
  57.7 17.9 %collective-permute-start.5 = (bf16[512,512]{1,0:T(8,128)(2,1)S(1)}, bf16[512,512]{1,0:T(8,128)(2,1)S(1)}, u32[]{:S(2)}, u32[]{:S(2)}) collective-permute-start(bf16[512,512]{1,0:T(8,128)(2,1)S(1)} %get-tuple-element.24.refs_0_), channel_id=1, source_target_pairs={{0,1},{1,2},{2,3},{3,4},{4,5},{5,6},{6,7},{7,8},{8,9},{9,10},{10,1... | collective-permute-start | bytes 1572872 | tf_op jit(solution)/shard_map/ppermute | solution.py:65
  67.5 11.7 %collective-permute-start.4 = (bf16[512,512]{1,0:T(8,128)(2,1)S(1)}, bf16[512,512]{1,0:T(8,128)(2,1)S(1)}, u32[]{:S(2)}, u32[]{:S(2)}) collective-permute-start(bf16[512,512]{1,0:T(8,128)(2,1)S(1)} %get-tuple-element.25.refs_0_), channel_id=1, source_target_pairs={{0,1},{1,2},{2,3},{3,4},{4,5},{5,6},{6,7},{7,8},{8,9},{9,10},{10,1... | collective-permute-start | bytes 1572872 | tf_op jit(solution)/shard_map/ppermute | solution.py:65
  70.2 1.0 copy-start.6
  72.6 1.6 %copy-start.4 = (bf16[128,1024]{1,0:T(8,128)(2,1)S(1)}, bf16[128,1024]{1,0:T(8,128)(2,1)}, u32[]{:S(2)}) copy-start(bf16[128,1024]{1,0:T(8,128)(2,1)} %copy-done.3) | copy-start | bytes 786436
  74.1 5.1 %copy-start.8 = (bf16[128,1024]{1,0:T(8,128)(2,1)S(1)}, bf16[128,1024]{1,0:T(8,128)(2,1)}, u32[]{:S(2)}) copy-start(bf16[128,1024]{1,0:T(8,128)(2,1)} %copy-done.7) | copy-start | bytes 786436
  81.8 8.2 %collective-permute-start.11 = (f32[256,1024]{1,0:T(8,128)S(1)}, f32[256,1024]{1,0:T(8,128)S(1)}, u32[]{:S(2)}, u32[]{:S(2)}) collective-permute-start(f32[256,1024]{1,0:T(8,128)S(1)} %shard_map.83), channel_id=1, source_target_pairs={{0,16},{16,0},{1,17},{17,1},{2,18},{18,2},{3,19},{19,3},{4,20},{20... | collective-permute-start | bytes 3145736 | tf_op jit(solution)/shard_map/ppermute | solution.py:306
  89.9 11.6 %copy-start = (f32[256,1024]{1,0:T(8,128)S(1)}, f32[256,1024]{1,0:T(8,128)}, u32[]{:S(2)}) copy-start(f32[256,1024]{1,0:T(8,128)} %weight.3) | copy-start | bytes 3145732
  89.9 11.6 %copy-start.9 = (f32[1024]{0:T(1024)S(1)}, f32[1024]{0:T(1024)}, u32[]{:S(2)}) copy-start(f32[1024]{0:T(1024)} %param.9) | copy-start | bytes 12292
  90.0 32.5 %copy-start.10 = (f32[256]{0:T(256)S(1)}, f32[256]{0:T(256)}, u32[]{:S(2)}) copy-start(f32[256]{0:T(256)} %param.8) | copy-start | bytes 3076

commit v9 on v7

--- a/solution.py
+++ b/solution.py
@@ -139,9 +139,9 @@
     )(place, part)
 
 
-def product_kernel(parts, which, place, *refs):
+def product_kernel(parts, which, place, first, second, *refs):
     operands, out = refs[:-1], refs[-1]
-    total = None if len(operands) == 2 + max(part[1] for part in parts) else operands[-1]
+    total = operands[-1] if len(operands) > 1 + max(index for *_, blocks in parts for index, _ in blocks) else None
     start = place[3] * HALF
     rows = pl.ds(0 if which is None else pl.multiple_of(which(place[2]) * ROW_BLOCK, ROW_BLOCK), out.shape[0])
 
@@ -149,19 +149,19 @@
     def _(n):
         columns = pl.ds(pl.multiple_of(n * COLUMNS, COLUMNS), COLUMNS)
         value = None if total is None else total[rows, columns]
-        for turned, grads, group, exchanged in parts:
-            offset = pl.multiple_of(start if exchanged else HALF - start, HALF)
-            blocks = [operands[grads][pl.ds(offset, HALF), columns]]
-            blocks += [operands[grads + 1][pl.ds(i * TOKENS + offset, HALF), columns] for i in range(SIDE - 1)]
-            features = operands[turned][rows, group * SIDE * HALF : (group + 1) * SIDE * HALF]
-            term = jnp.dot(features, jnp.concatenate(blocks, axis=0), preferred_element_type=jnp.float32)
+        for group, exchanged, blocks in parts:
+            depth = slice(group * SIDE * HALF, (group + 1) * SIDE * HALF)
+            features, offset = (first, start) if exchanged else (second, HALF - start)
+            offset = pl.multiple_of(offset, HALF)
+            grads = [operands[index][pl.ds(i * TOKENS + offset, HALF), columns] for index, i in blocks]
+            term = jnp.dot(features[rows, depth], jnp.concatenate(grads, axis=0), preferred_element_type=jnp.float32)
             value = term if value is None else value + term
         out[:, columns] = value
 
 
-def product(place, operands, parts, total=None, which=None):
+def product(place, features, operands, parts, total=None, which=None):
     count = 2 * ROW_BLOCK if which is None else ROW_BLOCK
-    operands = operands + ([] if total is None else [total])
+    operands = [*features, *operands] + ([] if total is None else [total])
     return pl.pallas_call(
         functools.partial(product_kernel, parts, which),
         out_shape=shape(count, WIDTH),
@@ -286,23 +286,22 @@
 def shards(activations, out_grads, weight, row_moment, col_moment):
     y, x, core, layer = (lax.axis_index(name) for name in ("y", "x", "core", "z"))
     place = jnp.stack([y, x, core, layer & 1])
-    first = exchange(pack(place, activations), CHIPS)
+    first = turn(place, exchange(pack(place, activations), CHIPS))
     second = next_layer(first)
-    line = [along(out_grads, k, 0) for k in range(1, SIDE)]
-    grads = [out_grads] + [along(out_grads, j, 1) for j in range(1, SIDE)]
-    line, grads[1:] = lax.optimization_barrier((line, grads[1:]))
-    line = join(line)
-    lines = [line] + [along(line, j, 1) for j in range(1, SIDE)]
-    first = turn(place, first)
+    line = join([out_grads] + [along(out_grads, k, 0) for k in range(1, SIDE)])
+    back, ahead = along(line, 1, 1), along(line, SIDE - 1, 1)
+    middle = 2 * TOKENS
+    far = [along(back[:middle], 1, 1), along(ahead[middle:], SIDE - 1, 1)]
+    whole = lambda operand: [(operand, i) for i in range(SIDE)]
     total = None
-    for j in range(SIDE - 1):
-        total = product(place, [first, grads[j], lines[j]], [(0, 1, j, True)], total)
-    second, *lines = lax.optimization_barrier((second, *lines))
-    operands = [first, turn(place, second)] + [block for pair in zip(grads, lines) for block in pair]
-    parts = [(0, 2 * SIDE, SIDE - 1, True)] + [(1, 2 + 2 * j, j, False) for j in range(SIDE)]
-    theirs = product(place, operands, parts, total, lambda core: 1 - core)
+    for group, lines in ((0, line), (1, back), (3, ahead)):
+        total = product(place, (first, first), [lines], [(group, True, whole(0))], total)
+    operands = [line, back, ahead] + far
+    parts = [(2, True, [(3, 0), (3, 1), (4, 0), (4, 1)]), (2, False, [(3, 0), (3, 1), (4, 0), (4, 1)])]
+    parts += [(group, False, whole(i)) for i, group in enumerate((0, 1, 3))]
+    theirs = product(place, (first, second), operands, parts, total, lambda core: 1 - core)
     received = lax.ppermute(theirs, "core", [(0, 1), (1, 0)])
-    mine = product(place, operands, parts, total, lambda core: core)
+    mine = product(place, (first, second), operands, parts, total, lambda core: core)
     weight_grad, tiles = columns(mine, received)
     new_cols, col_root, tiles = rows(exchange(tiles, ROWS), col_moment.reshape(TILE), weight_grad, weight)
     new_rows, row_root, tiles = scalars(exchange(tiles, "z"), row_moment.reshape(2, LANES))

time: 129 us -> 127 us (0.984)
  starting transfers between devices: 52.2 us -> 44.8 us
  waiting for transfers between devices: 11.1 us -> 15.4 us
    ppermute x9 -> x7, starting transfers between devices: 31.1 us -> 23.4 us  [along(): return lax.ppermute(value, ROWS, pairs)]
    ppermute x9 -> x7, waiting for transfers between devices: 10.4 us -> 15.1 us  [along(): return lax.ppermute(value, ROWS, pairs)]
  transfers between devices with their start and end apart: 12 -> 10, of which waited for: 4 -> 4; matrix products, arithmetic and copies ran while one was open for 0% -> 0% of each run, Pallas kernels for 6% -> 6%
where the time goes in v9:
time: 127 us; the launch traced here: 126 us
  blocking collectives  49 us (39%)
  starting transfers between devices  44.8 us (35%)
  Pallas kernels  16.1 us (13%)
  waiting for transfers between devices  15.4 us (12%)
    all_to_all x3, blocking collectives, exchange(): return lax.all_to_all(tiles, axes, 0, 0)  49 us
    ppermute x7, starting transfers between devices, along(): return lax.ppermute(value, ROWS, pairs)  23.4 us
    ppermute x7, waiting for transfers between devices, along(): return lax.ppermute(value, ROWS, pairs)  15.1 us
    ppermute x1, starting transfers between devices, next_layer(): return lax.ppermute(value, ('core', 'z'), pairs)  10.8 us
    pallas_call x5, Pallas kernels, product(): pl.pallas_call(functools.partial(product_kernel, parts, which), out_shape...  8.37 us
    all_to_all x1, starting transfers between devices, exchange(): return lax.all_to_all(tiles, axes, 0, 0)  7.65 us
    ppermute x1, starting transfers between devices, shards(): received = lax.ppermute(theirs, 'core', [(0, 1), (1, 0)])  2.96 us
    pallas_call x1, Pallas kernels, pack(): pl.pallas_call(pack_kernel, out_shape=shape(COUNT, HALF, 2 * ROW_BLOCK, d...  2.9 us
  transfers between devices with their start and end apart: 10, of which 4 were waited for; matrix products, arithmetic and copies ran while one was open for 0% of the time, Pallas kernels for 6%

profile of v9, /device:TPU:1, one launch (start us, length us, event | category | flops | bytes accessed | tf_op | source)
XLA Modules:
  0.0 126.4 jit_solution(15732351665224292565)
XLA Ops:
  0.6 0.1 pad_add_fusion.place
  0.7 2.9 %shard_map.76 = bf16[16,64,512]{2,1,0:T(8,128)(2,1)} custom-call(s32[4]{0:T(128)S(1)} %pad_add_fusion.place, bf16[128,8192]{1,0:T(8,128)(2,1)} %source.1), custom_call_target="tpu_custom_call" | custom-call | bytes 2097152 | tf_op jit(solution)/shard_map/pallas_call | solution.py:85
  3.6 7.6 %all-to-all-start = ((bf16[16,64,512]{2,1,0:T(8,128)(2,1)}), bf16[16,64,512]{2,1,0:T(8,128)(2,1)}, u32[]{:S(2)}, u32[]{:S(2)}) async-start(bf16[16,64,512]{2,1,0:T(8,128)(2,1)} %shard_map.76), calls=%async_computation | async-start | bytes 2097152 | tf_op jit(solution)/shard_map/all_to_all | solution.py:69
  11.3 4.7 %collective-permute-start.2 = (bf16[128,1024]{1,0:T(8,128)(2,1)S(1)}, bf16[128,1024]{1,0:T(8,128)(2,1)S(1)}, u32[]{:S(2)}, u32[]{:S(2)}) collective-permute-start(bf16[128,1024]{1,0:T(8,128)(2,1)S(1)} %copy-done.1), channel_id=1, source_target_pairs={{0,64},{16,272},{32,96},{48,304},{64,0},{80,336},{96,32},{112,368}... | collective-permute-start | bytes 786440 | tf_op jit(solution)/shard_map/ppermute | solution.py:59
  16.0 2.2 %collective-permute-start.1 = (bf16[128,1024]{1,0:T(8,128)(2,1)S(1)}, bf16[128,1024]{1,0:T(8,128)(2,1)S(1)}, u32[]{:S(2)}, u32[]{:S(2)}) collective-permute-start(bf16[128,1024]{1,0:T(8,128)(2,1)S(1)} %copy-done.1), channel_id=1, source_target_pairs={{0,32},{16,144},{32,64},{48,176},{64,96},{80,208},{96,0},{112,240}... | collective-permute-start | bytes 786440 | tf_op jit(solution)/shard_map/ppermute | solution.py:59
  18.2 4.3 %collective-permute-start.3 = (bf16[128,1024]{1,0:T(8,128)(2,1)S(1)}, bf16[128,1024]{1,0:T(8,128)(2,1)S(1)}, u32[]{:S(2)}, u32[]{:S(2)}) collective-permute-start(bf16[128,1024]{1,0:T(8,128)(2,1)S(1)} %copy-done.1), channel_id=1, source_target_pairs={{0,96},{16,400},{32,0},{48,432},{64,32},{80,464},{96,64},{112,496}... | collective-permute-start | bytes 786440 | tf_op jit(solution)/shard_map/ppermute | solution.py:59
  22.5 7.2 %collective-permute-done.2.refs_2_ = bf16[128,1024]{1,0:T(8,128)(2,1)S(1)} collective-permute-done((bf16[128,1024]{1,0:T(8,128)(2,1)S(1)}, bf16[128,1024]{1,0:T(8,128)(2,1)S(1)}, u32[]{:S(2)}, u32[]{:S(2)}) %collective-permute-start.2) | collective-permute-done | bytes 262176 | tf_op jit(solution)/shard_map/ppermute | solution.py:59
  29.7 2.9 %collective-permute-done.1.refs_1_ = bf16[128,1024]{1,0:T(8,128)(2,1)S(1)} collective-permute-done((bf16[128,1024]{1,0:T(8,128)(2,1)S(1)}, bf16[128,1024]{1,0:T(8,128)(2,1)S(1)}, u32[]{:S(2)}, u32[]{:S(2)}) %collective-permute-start.1) | collective-permute-done | bytes 262176 | tf_op jit(solution)/shard_map/ppermute | solution.py:59
  32.6 0.1 shard_map.78.refs_0_
  32.8 3.8 %collective-permute-start.5 = (bf16[512,1024]{1,0:T(8,128)(2,1)S(1)}, bf16[512,1024]{1,0:T(8,128)(2,1)S(1)}, u32[]{:S(2)}, u32[]{:S(2)}) collective-permute-start(bf16[512,1024]{1,0:T(8,128)(2,1)S(1)} %shard_map.78.refs_0_), channel_id=1, source_target_pairs={{0,384},{16,112},{32,416},{48,16},{64,448},{80,48},{96,480},{112,8... | collective-permute-start | bytes 3145736 | tf_op jit(solution)/shard_map/ppermute | solution.py:59
  36.5 1.9 %collective-permute-start.4 = (bf16[512,1024]{1,0:T(8,128)(2,1)S(1)}, bf16[512,1024]{1,0:T(8,128)(2,1)S(1)}, u32[]{:S(2)}, u32[]{:S(2)}) collective-permute-start(bf16[512,1024]{1,0:T(8,128)(2,1)S(1)} %shard_map.78.refs_0_), channel_id=1, source_target_pairs={{0,128},{16,48},{32,160},{48,80},{64,192},{80,112},{96,224},{112,1... | collective-permute-start | bytes 3145736 | tf_op jit(solution)/shard_map/ppermute | solution.py:59
  38.5 1.6 %shard_map.77.first.second = bf16[512,1024]{1,0:T(8,128)(2,1)S(1)} custom-call(s32[4]{0:T(128)S(1)} %pad_add_fusion.place, bf16[16,64,512]{2,1,0:T(8,128)(2,1)} %all-to-all-done.part), custom_call_target="tpu_custom_call" | custom-call | bytes 2097152 | tf_op jit(solution)/shard_map/pallas_call | solution.py:132
  40.1 10.8 %collective-permute-start = (bf16[512,1024]{1,0:T(8,128)(2,1)S(1)}, bf16[512,1024]{1,0:T(8,128)(2,1)S(1)}, u32[]{:S(2)}, u32[]{:S(2)}) collective-permute-start(bf16[512,1024]{1,0:T(8,128)(2,1)S(1)} %shard_map.77.first.second), channel_id=1, source_target_pairs={{0,1},{1,2},{2,3},{3,4},{4,5},{5,6},{6,7},{7,8},{8,9},{9,10},{10,1... | collective-permute-start | bytes 3145736 | tf_op jit(solution)/shard_map/ppermute | solution.py:65
  51.0 4.6 %collective-permute-start.7 = (bf16[256,1024]{1,0:T(8,128)(2,1)S(1)}, bf16[256,1024]{1,0:T(8,128)(2,1)S(1)}, u32[]{:S(2)}, u32[]{:S(2)}) collective-permute-start(bf16[256,1024]{1,0:T(8,128)(2,1)S(1)} %slice.9), channel_id=1, source_target_pairs={{0,384},{16,112},{32,416},{48,16},{64,448},{80,48},{96,480},{112,8... | collective-permute-start | bytes 1572872 | tf_op jit(solution)/shard_map/ppermute | solution.py:59
  55.6 1.9 %collective-permute-start.6 = (bf16[256,1024]{1,0:T(8,128)(2,1)S(1)}, bf16[256,1024]{1,0:T(8,128)(2,1)S(1)}, u32[]{:S(2)}, u32[]{:S(2)}) collective-permute-start(bf16[256,1024]{1,0:T(8,128)(2,1)S(1)} %slice.8), channel_id=1, source_target_pairs={{0,128},{16,48},{32,160},{48,80},{64,192},{80,112},{96,224},{112,1... | collective-permute-start | bytes 1572872 | tf_op jit(solution)/shard_map/ppermute | solution.py:59
  57.5 1.5 %shard_map.79.refs_1_ = f32[512,1024]{1,0:T(8,128)S(1)} custom-call(s32[4]{0:T(128)S(1)} %pad_add_fusion.place, bf16[512,1024]{1,0:T(8,128)(2,1)S(1)} %shard_map.77.first.second, bf16[512,1024]{1,0:T(8,128)(2,1)S(1)} %shard_map.77.first.second, bf16[512,1024]{1,0:T(8,128)(2,1)S(1)} %shard_map.78.refs_0_), custom_call_target="tpu_custom_call" | custom-call | flops 268435456 | bytes 1048576 | tf_op jit(solution)/shard_map/pallas_call | solution.py:165
  59.0 1.5 %shard_map.80.refs_1_ = f32[512,1024]{1,0:T(8,128)S(1)} custom-call(s32[4]{0:T(128)S(1)} %pad_add_fusion.place, bf16[512,1024]{1,0:T(8,128)(2,1)S(1)} %shard_map.77.first.second, bf16[512,1024]{1,0:T(8,128)(2,1)S(1)} %shard_map.77.first.second, bf16[512,1024]{1,0:T(8,128)(2,1)S(1)} %collective-permute-done.4.refs_0_.refs_1_, f32[512,1024]{1,0:T(8,128)S(1)} %shard_map.79.refs_1_), custom_call_target="tpu_custom_call" | custom-call | flops 268435456 | bytes 1048576 | tf_op jit(solution)/shard_map/pallas_call | solution.py:165
  60.5 1.5 %shard_map.81.refs_5_ = f32[512,1024]{1,0:T(8,128)S(1)} custom-call(s32[4]{0:T(128)S(1)} %pad_add_fusion.place, bf16[512,1024]{1,0:T(8,128)(2,1)S(1)} %shard_map.77.first.second, bf16[512,1024]{1,0:T(8,128)(2,1)S(1)} %shard_map.77.first.second, bf16[512,1024]{1,0:T(8,128)(2,1)S(1)} %collective-permute-done.5.refs_0_.refs_2_, f32[512,1024]{1,0:T(8,128)S(1)} %shard_map.80.refs_1_), custom_call_target="tpu_custom_call" | custom-call | flops 268435456 | bytes 1048576 | tf_op jit(solution)/shard_map/pallas_call | solution.py:165
  62.0 5.0 %collective-permute-done.6.refs_3_ = bf16[256,1024]{1,0:T(8,128)(2,1)S(1)} collective-permute-done((bf16[256,1024]{1,0:T(8,128)(2,1)S(1)}, bf16[256,1024]{1,0:T(8,128)(2,1)S(1)}, u32[]{:S(2)}, u32[]{:S(2)}) %collective-permute-start.6) | collective-permute-done | bytes 524320 | tf_op jit(solution)/shard_map/ppermute | solution.py:59
  67.1 2.0 %shard_map.83 = f32[256,1024]{1,0:T(8,128)S(1)} custom-call(s32[4]{0:T(128)S(1)} %pad_add_fusion.place, bf16[512,1024]{1,0:T(8,128)(2,1)S(1)} %shard_map.77.first.second, bf16[512,1024]{1,0:T(8,128)(2,1)S(1)} %collective-permute-done.second, bf16[512,1024]{1,0:T(8,128)(2,1)S(1)} %shard_map.78.refs_0_, ...), custom_call_target="tpu_custom_call" | custom-call | flops 671088640 | bytes 1048576 | tf_op jit(solution)/shard_map/pallas_call | solution.py:165
  69.0 3.0 %collective-permute-start.8 = (f32[256,1024]{1,0:T(8,128)S(1)}, f32[256,1024]{1,0:T(8,128)S(1)}, u32[]{:S(2)}, u32[]{:S(2)}) collective-permute-start(f32[256,1024]{1,0:T(8,128)S(1)} %shard_map.83), channel_id=1, source_target_pairs={{0,16},{16,0},{1,17},{17,1},{2,18},{18,2},{3,19},{19,3},{4,20},{20... | collective-permute-start | bytes 3145736 | tf_op jit(solution)/shard_map/ppermute | solution.py:303
  72.0 2.0 %shard_map.82.mine = f32[256,1024]{1,0:T(8,128)S(1)} custom-call(s32[4]{0:T(128)S(1)} %pad_add_fusion.place, bf16[512,1024]{1,0:T(8,128)(2,1)S(1)} %shard_map.77.first.second, bf16[512,1024]{1,0:T(8,128)(2,1)S(1)} %collective-permute-done.second, bf16[512,1024]{1,0:T(8,128)(2,1)S(1)} %shard_map.78.refs_0_, ...), custom_call_target="tpu_custom_call" | custom-call | flops 671088640 | bytes 1048576 | tf_op jit(solution)/shard_map/pallas_call | solution.py:165
  73.9 0.0 copy-start
  74.0 0.0 copy-start.2
  74.0 0.3 collective-permute-done.8.theirs
  74.3 0.1 shard_map.84
  74.4 10.9 %all_to_all.20.received = f32[32,8,128]{2,1,0:T(8,128)S(1)} all-to-all(f32[32,8,128]{2,1,0:T(8,128)S(1)} %get-tuple-element.11), channel_id=1, replica_groups=mesh['y'=4,'x'=4,'core'=2,'z'=16] {'y','x','core'}, dimensions={0} | all-to-all | bytes 262144 | tf_op jit(solution)/shard_map/all_to_all | solution.py:69
  85.3 1.0 shard_map.85
  86.3 25.5 %all_to_all.21.received = f32[16,8,128]{2,1,0:T(8,128)S(1)} all-to-all(f32[16,8,128]{2,1,0:T(8,128)S(1)} %get-tuple-element.13), channel_id=1, replica_groups=mesh['y'=4,'x'=4,'core'=2,'z'=16] {'z'}, dimensions={0} | all-to-all | bytes 131072 | tf_op jit(solution)/shard_map/all_to_all | solution.py:69
  111.8 0.6 shard_map.86
  112.4 12.5 %all_to_all.22.received = f32[32,4,128]{2,1,0:T(4,128)S(1)} all-to-all(f32[32,4,128]{2,1,0:T(4,128)S(1)} %get-tuple-element.14), channel_id=1, replica_groups=mesh['y'=4,'x'=4,'core'=2,'z'=16] {'y','x','core'}, dimensions={0} | all-to-all | bytes 131072 | tf_op jit(solution)/shard_map/all_to_all | solution.py:69
  125.0 1.4 %shard_map.87 = f32[256,1024]{1,0:T(8,128)} custom-call(f32[32,4,128]{2,1,0:T(4,128)S(1)} %all_to_all.22.received, f32[2,128]{1,0:T(2,128)S(1)} %get-tuple-element.15.row_root, f32[8,128]{1,0:T(8,128)S(1)} %get-tuple-element.16.col_root, f32[256,1024]{1,0:T(8,128)S(1)} %get-tuple-element.12.grad, f32[256,1024]{1,0:T(8,128)S(1)} %copy-done), custom_call_target="tpu_custom_call" | custom-call | flops 1048576 | bytes 3145728 | tf_op jit(solution)/shard_map/pallas_call | solution.py:275
  (14 shorter events, 0.1 us)
Async XLA Ops:
  0.7 10.6 %copy-start.1 = (bf16[128,1024]{1,0:T(8,128)(2,1)S(1)}, bf16[128,1024]{1,0:T(8,128)(2,1)}, u32[]{:S(2)}) copy-start(bf16[128,1024]{1,0:T(8,128)(2,1)} %refs_0_.1) | copy-start | bytes 786436
  3.6 34.9 %all-to-all-start = ((bf16[16,64,512]{2,1,0:T(8,128)(2,1)}), bf16[16,64,512]{2,1,0:T(8,128)(2,1)}, u32[]{:S(2)}, u32[]{:S(2)}) async-start(bf16[16,64,512]{2,1,0:T(8,128)(2,1)} %shard_map.76), calls=%async_computation | async-start | bytes 2097152 | tf_op jit(solution)/shard_map/all_to_all | solution.py:69
  11.3 18.4 %collective-permute-start.2 = (bf16[128,1024]{1,0:T(8,128)(2,1)S(1)}, bf16[128,1024]{1,0:T(8,128)(2,1)S(1)}, u32[]{:S(2)}, u32[]{:S(2)}) collective-permute-start(bf16[128,1024]{1,0:T(8,128)(2,1)S(1)} %copy-done.1), channel_id=1, source_target_pairs={{0,64},{16,272},{32,96},{48,304},{64,0},{80,336},{96,32},{112,368}... | collective-permute-start | bytes 786440 | tf_op jit(solution)/shard_map/ppermute | solution.py:59
  16.0 16.6 %collective-permute-start.1 = (bf16[128,1024]{1,0:T(8,128)(2,1)S(1)}, bf16[128,1024]{1,0:T(8,128)(2,1)S(1)}, u32[]{:S(2)}, u32[]{:S(2)}) collective-permute-start(bf16[128,1024]{1,0:T(8,128)(2,1)S(1)} %copy-done.1), channel_id=1, source_target_pairs={{0,32},{16,144},{32,64},{48,176},{64,96},{80,208},{96,0},{112,240}... | collective-permute-start | bytes 786440 | tf_op jit(solution)/shard_map/ppermute | solution.py:59
  18.2 14.4 %collective-permute-start.3 = (bf16[128,1024]{1,0:T(8,128)(2,1)S(1)}, bf16[128,1024]{1,0:T(8,128)(2,1)S(1)}, u32[]{:S(2)}, u32[]{:S(2)}) collective-permute-start(bf16[128,1024]{1,0:T(8,128)(2,1)S(1)} %copy-done.1), channel_id=1, source_target_pairs={{0,96},{16,400},{32,0},{48,432},{64,32},{80,464},{96,64},{112,496}... | collective-permute-start | bytes 786440 | tf_op jit(solution)/shard_map/ppermute | solution.py:59
  32.8 18.2 %collective-permute-start.5 = (bf16[512,1024]{1,0:T(8,128)(2,1)S(1)}, bf16[512,1024]{1,0:T(8,128)(2,1)S(1)}, u32[]{:S(2)}, u32[]{:S(2)}) collective-permute-start(bf16[512,1024]{1,0:T(8,128)(2,1)S(1)} %shard_map.78.refs_0_), channel_id=1, source_target_pairs={{0,384},{16,112},{32,416},{48,16},{64,448},{80,48},{96,480},{112,8... | collective-permute-start | bytes 3145736 | tf_op jit(solution)/shard_map/ppermute | solution.py:59
  36.5 19.0 %collective-permute-start.4 = (bf16[512,1024]{1,0:T(8,128)(2,1)S(1)}, bf16[512,1024]{1,0:T(8,128)(2,1)S(1)}, u32[]{:S(2)}, u32[]{:S(2)}) collective-permute-start(bf16[512,1024]{1,0:T(8,128)(2,1)S(1)} %shard_map.78.refs_0_), channel_id=1, source_target_pairs={{0,128},{16,48},{32,160},{48,80},{64,192},{80,112},{96,224},{112,1... | collective-permute-start | bytes 3145736 | tf_op jit(solution)/shard_map/ppermute | solution.py:59
  40.1 27.0 %collective-permute-start = (bf16[512,1024]{1,0:T(8,128)(2,1)S(1)}, bf16[512,1024]{1,0:T(8,128)(2,1)S(1)}, u32[]{:S(2)}, u32[]{:S(2)}) collective-permute-start(bf16[512,1024]{1,0:T(8,128)(2,1)S(1)} %shard_map.77.first.second), channel_id=1, source_target_pairs={{0,1},{1,2},{2,3},{3,4},{4,5},{5,6},{6,7},{7,8},{8,9},{9,10},{10,1... | collective-permute-start | bytes 3145736 | tf_op jit(solution)/shard_map/ppermute | solution.py:65
  51.0 11.0 %collective-permute-start.7 = (bf16[256,1024]{1,0:T(8,128)(2,1)S(1)}, bf16[256,1024]{1,0:T(8,128)(2,1)S(1)}, u32[]{:S(2)}, u32[]{:S(2)}) collective-permute-start(bf16[256,1024]{1,0:T(8,128)(2,1)S(1)} %slice.9), channel_id=1, source_target_pairs={{0,384},{16,112},{32,416},{48,16},{64,448},{80,48},{96,480},{112,8... | collective-permute-start | bytes 1572872 | tf_op jit(solution)/shard_map/ppermute | solution.py:59
  55.6 11.4 %collective-permute-start.6 = (bf16[256,1024]{1,0:T(8,128)(2,1)S(1)}, bf16[256,1024]{1,0:T(8,128)(2,1)S(1)}, u32[]{:S(2)}, u32[]{:S(2)}) collective-permute-start(bf16[256,1024]{1,0:T(8,128)(2,1)S(1)} %slice.8), channel_id=1, source_target_pairs={{0,128},{16,48},{32,160},{48,80},{64,192},{80,112},{96,224},{112,1... | collective-permute-start | bytes 1572872 | tf_op jit(solution)/shard_map/ppermute | solution.py:59
  69.0 5.2 %collective-permute-start.8 = (f32[256,1024]{1,0:T(8,128)S(1)}, f32[256,1024]{1,0:T(8,128)S(1)}, u32[]{:S(2)}, u32[]{:S(2)}) collective-permute-start(f32[256,1024]{1,0:T(8,128)S(1)} %shard_map.83), channel_id=1, source_target_pairs={{0,16},{16,0},{1,17},{17,1},{2,18},{18,2},{3,19},{19,3},{4,20},{20... | collective-permute-start | bytes 3145736 | tf_op jit(solution)/shard_map/ppermute | solution.py:303
  73.9 11.4 %copy-start = (f32[256,1024]{1,0:T(8,128)S(1)}, f32[256,1024]{1,0:T(8,128)}, u32[]{:S(2)}) copy-start(f32[256,1024]{1,0:T(8,128)} %weight.3) | copy-start | bytes 3145732
  74.0 11.4 %copy-start.2 = (f32[1024]{0:T(1024)S(1)}, f32[1024]{0:T(1024)}, u32[]{:S(2)}) copy-start(f32[1024]{0:T(1024)} %param.9) | copy-start | bytes 12292
  74.0 37.9 %copy-start.3 = (f32[256]{0:T(256)S(1)}, f32[256]{0:T(256)}, u32[]{:S(2)}) copy-start(f32[256]{0:T(256)} %param.8) | copy-start | bytes 3076

commit v10 on v9

--- a/solution.py
+++ b/solution.py
@@ -288,17 +288,18 @@
     place = jnp.stack([y, x, core, layer & 1])
     first = turn(place, exchange(pack(place, activations), CHIPS))
     second = next_layer(first)
-    line = join([out_grads] + [along(out_grads, k, 0) for k in range(1, SIDE)])
-    back, ahead = along(line, 1, 1), along(line, SIDE - 1, 1)
-    middle = 2 * TOKENS
-    far = [along(back[:middle], 1, 1), along(ahead[middle:], SIDE - 1, 1)]
-    whole = lambda operand: [(operand, i) for i in range(SIDE)]
+    line = [out_grads] + [along(out_grads, k, 0) for k in range(1, SIDE)]
+    low, high = join(line[:2]), join(line[2:])
+    back_low, ahead_high = along(low, 1, 1), along(high, SIDE - 1, 1)
+    far = [along(back_low, 1, 1), along(ahead_high, SIDE - 1, 1)]
+    back, ahead = [back_low, along(high, 1, 1)], [along(low, SIDE - 1, 1), ahead_high]
+    blocks = lambda operand: [(operand, 0), (operand, 1), (operand + 1, 0), (operand + 1, 1)]
     total = None
-    for group, lines in ((0, line), (1, back), (3, ahead)):
-        total = product(place, (first, first), [lines], [(group, True, whole(0))], total)
-    operands = [line, back, ahead] + far
-    parts = [(2, True, [(3, 0), (3, 1), (4, 0), (4, 1)]), (2, False, [(3, 0), (3, 1), (4, 0), (4, 1)])]
-    parts += [(group, False, whole(i)) for i, group in enumerate((0, 1, 3))]
+    for group, halves in ((0, [low, high]), (1, back), (3, ahead)):
+        total = product(place, (first, first), halves, [(group, True, blocks(0))], total)
+    operands = [low, high] + back + ahead + far
+    parts = [(2, True, blocks(6)), (2, False, blocks(6))]
+    parts += [(group, False, blocks(2 * i)) for i, group in enumerate((0, 1, 3))]
     theirs = product(place, (first, second), operands, parts, total, lambda core: 1 - core)
     received = lax.ppermute(theirs, "core", [(0, 1), (1, 0)])
     mine = product(place, (first, second), operands, parts, total, lambda core: core)

time: 127 us -> 126 us (level)
  starting transfers between devices: 44.8 us -> 47.6 us
  blocking collectives: 49 us -> 46.4 us
    ppermute x7 -> x9, starting transfers between devices: 23.4 us -> 27 us  [along(): return lax.ppermute(value, ROWS, pairs)]
    all_to_all x3, blocking collectives: 49 us -> 46.4 us  [exchange(): return lax.all_to_all(tiles, axes, 0, 0)]
    ppermute x7 -> x9, waiting for transfers between devices: 15.1 us -> 14.1 us  [along(): return lax.ppermute(value, ROWS, pairs)]
  transfers between devices with their start and end apart: 10 -> 12, of which waited for: 4 -> 5; matrix products, arithmetic and copies ran while one was open for 0% -> 0% of each run, Pallas kernels for 6% -> 6%
where the time goes in v10:
time: 126 us; the launch traced here: 125 us
  starting transfers between devices  47.6 us (38%)
  blocking collectives  46.4 us (37%)
  Pallas kernels  15.4 us (12%)
  waiting for transfers between devices  14.7 us (12%)
    all_to_all x3, blocking collectives, exchange(): return lax.all_to_all(tiles, axes, 0, 0)  46.4 us
    ppermute x9, starting transfers between devices, along(): return lax.ppermute(value, ROWS, pairs)  27 us
    ppermute x9, waiting for transfers between devices, along(): return lax.ppermute(value, ROWS, pairs)  14.1 us
    ppermute x1, starting transfers between devices, next_layer(): return lax.ppermute(value, ('core', 'z'), pairs)  11.1 us
    pallas_call x5, Pallas kernels, product(): pl.pallas_call(functools.partial(product_kernel, parts, which), out_shape...  8.34 us
    all_to_all x1, starting transfers between devices, exchange(): return lax.all_to_all(tiles, axes, 0, 0)  7.6 us
    pallas_call x1, Pallas kernels, pack(): pl.pallas_call(pack_kernel, out_shape=shape(COUNT, HALF, 2 * ROW_BLOCK, d...  2.9 us
  transfers between devices with their start and end apart: 12, of which 5 were waited for; matrix products, arithmetic and copies ran while one was open for 0% of the time, Pallas kernels for 6%

profile of v10, /device:TPU:1, one launch (start us, length us, event | category | flops | bytes accessed | tf_op | source)
XLA Modules:
  0.0 125.1 jit_solution(10132508998914864228)
XLA Ops:
  0.6 0.1 pad_add_fusion.place
  0.7 2.9 %shard_map.76 = bf16[16,64,512]{2,1,0:T(8,128)(2,1)} custom-call(s32[4]{0:T(128)S(1)} %pad_add_fusion.place, bf16[128,8192]{1,0:T(8,128)(2,1)} %source.1), custom_call_target="tpu_custom_call" | custom-call | bytes 2097152 | tf_op jit(solution)/shard_map/pallas_call | solution.py:85
  3.6 7.6 %all-to-all-start = ((bf16[16,64,512]{2,1,0:T(8,128)(2,1)}), bf16[16,64,512]{2,1,0:T(8,128)(2,1)S(1)}, u32[]{:S(2)}, u32[]{:S(2)}) async-start(bf16[16,64,512]{2,1,0:T(8,128)(2,1)} %shard_map.76), calls=%async_computation | async-start | bytes 2097152 | tf_op jit(solution)/shard_map/all_to_all | solution.py:69
  11.2 4.5 %collective-permute-start.3 = (bf16[128,1024]{1,0:T(8,128)(2,1)S(1)}, bf16[128,1024]{1,0:T(8,128)(2,1)S(1)}, u32[]{:S(2)}, u32[]{:S(2)}) collective-permute-start(bf16[128,1024]{1,0:T(8,128)(2,1)S(1)} %copy-done.1), channel_id=1, source_target_pairs={{0,96},{16,400},{32,0},{48,432},{64,32},{80,464},{96,64},{112,496}... | collective-permute-start | bytes 786440 | tf_op jit(solution)/shard_map/ppermute | solution.py:59
  15.7 2.5 %collective-permute-start.2 = (bf16[128,1024]{1,0:T(8,128)(2,1)S(1)}, bf16[128,1024]{1,0:T(8,128)(2,1)S(1)}, u32[]{:S(2)}, u32[]{:S(2)}) collective-permute-start(bf16[128,1024]{1,0:T(8,128)(2,1)S(1)} %copy-done.1), channel_id=1, source_target_pairs={{0,64},{16,272},{32,96},{48,304},{64,0},{80,336},{96,32},{112,368}... | collective-permute-start | bytes 786440 | tf_op jit(solution)/shard_map/ppermute | solution.py:59
  18.2 2.5 %collective-permute-start.1 = (bf16[128,1024]{1,0:T(8,128)(2,1)S(1)}, bf16[128,1024]{1,0:T(8,128)(2,1)S(1)}, u32[]{:S(2)}, u32[]{:S(2)}) collective-permute-start(bf16[128,1024]{1,0:T(8,128)(2,1)S(1)} %copy-done.1), channel_id=1, source_target_pairs={{0,32},{16,144},{32,64},{48,176},{64,96},{80,208},{96,0},{112,240}... | collective-permute-start | bytes 786440 | tf_op jit(solution)/shard_map/ppermute | solution.py:59
  20.7 7.8 %collective-permute-done.3.refs_1_ = bf16[128,1024]{1,0:T(8,128)(2,1)S(1)} collective-permute-done((bf16[128,1024]{1,0:T(8,128)(2,1)S(1)}, bf16[128,1024]{1,0:T(8,128)(2,1)S(1)}, u32[]{:S(2)}, u32[]{:S(2)}) %collective-permute-start.3) | collective-permute-done | bytes 262176 | tf_op jit(solution)/shard_map/ppermute | solution.py:59
  28.5 1.6 %collective-permute-done.2.refs_0_ = bf16[128,1024]{1,0:T(8,128)(2,1)S(1)} collective-permute-done((bf16[128,1024]{1,0:T(8,128)(2,1)S(1)}, bf16[128,1024]{1,0:T(8,128)(2,1)S(1)}, u32[]{:S(2)}, u32[]{:S(2)}) %collective-permute-start.2) | collective-permute-done | bytes 262176 | tf_op jit(solution)/shard_map/ppermute | solution.py:59
  30.1 3.8 %collective-permute-start.7 = (bf16[256,1024]{1,0:T(8,128)(2,1)S(1)}, bf16[256,1024]{1,0:T(8,128)(2,1)S(1)}, u32[]{:S(2)}, u32[]{:S(2)}) collective-permute-start(bf16[256,1024]{1,0:T(8,128)(2,1)S(1)} %shard_map.79.refs_1_), channel_id=1, source_target_pairs={{0,384},{16,112},{32,416},{48,16},{64,448},{80,48},{96,480},{112,8... | collective-permute-start | bytes 1572872 | tf_op jit(solution)/shard_map/ppermute | solution.py:59
  34.0 1.9 %collective-permute-start.4 = (bf16[256,1024]{1,0:T(8,128)(2,1)S(1)}, bf16[256,1024]{1,0:T(8,128)(2,1)S(1)}, u32[]{:S(2)}, u32[]{:S(2)}) collective-permute-start(bf16[256,1024]{1,0:T(8,128)(2,1)S(1)} %shard_map.78.refs_0_), channel_id=1, source_target_pairs={{0,128},{16,48},{32,160},{48,80},{64,192},{80,112},{96,224},{112,1... | collective-permute-start | bytes 1572872 | tf_op jit(solution)/shard_map/ppermute | solution.py:59
  36.0 0.9 shard_map.77.first.second
  36.9 11.1 %collective-permute-start = (bf16[512,1024]{1,0:T(8,128)(2,1)S(1)}, bf16[512,1024]{1,0:T(8,128)(2,1)S(1)}, u32[]{:S(2)}, u32[]{:S(2)}) collective-permute-start(bf16[512,1024]{1,0:T(8,128)(2,1)S(1)} %shard_map.77.first.second), channel_id=1, source_target_pairs={{0,1},{1,2},{2,3},{3,4},{4,5},{5,6},{6,7},{7,8},{8,9},{9,10},{10,1... | collective-permute-start | bytes 3145736 | tf_op jit(solution)/shard_map/ppermute | solution.py:65
  48.0 2.4 %collective-permute-start.5 = (bf16[256,1024]{1,0:T(8,128)(2,1)S(1)}, bf16[256,1024]{1,0:T(8,128)(2,1)S(1)}, u32[]{:S(2)}, u32[]{:S(2)}) collective-permute-start(bf16[256,1024]{1,0:T(8,128)(2,1)S(1)} %shard_map.79.refs_1_), channel_id=1, source_target_pairs={{0,128},{16,48},{32,160},{48,80},{64,192},{80,112},{96,224},{112,1... | collective-permute-start | bytes 1572872 | tf_op jit(solution)/shard_map/ppermute | solution.py:59
  50.4 4.1 %collective-permute-start.6 = (bf16[256,1024]{1,0:T(8,128)(2,1)S(1)}, bf16[256,1024]{1,0:T(8,128)(2,1)S(1)}, u32[]{:S(2)}, u32[]{:S(2)}) collective-permute-start(bf16[256,1024]{1,0:T(8,128)(2,1)S(1)} %shard_map.78.refs_0_), channel_id=1, source_target_pairs={{0,384},{16,112},{32,416},{48,16},{64,448},{80,48},{96,480},{112,8... | collective-permute-start | bytes 1572872 | tf_op jit(solution)/shard_map/ppermute | solution.py:59
  54.5 3.4 %collective-permute-start.9 = (bf16[256,1024]{1,0:T(8,128)(2,1)S(1)}, bf16[256,1024]{1,0:T(8,128)(2,1)S(1)}, u32[]{:S(2)}, u32[]{:S(2)}) collective-permute-start(bf16[256,1024]{1,0:T(8,128)(2,1)S(1)} %collective-permute-done.7.refs_1_.refs_5_), channel_id=1, source_target_pairs={{0,384},{16,112},{32,416},{48,16},{64,448},{80,48},{96,480},{112,8... | collective-permute-start | bytes 1572872 | tf_op jit(solution)/shard_map/ppermute | solution.py:59
  57.9 1.9 %collective-permute-start.8 = (bf16[256,1024]{1,0:T(8,128)(2,1)S(1)}, bf16[256,1024]{1,0:T(8,128)(2,1)S(1)}, u32[]{:S(2)}, u32[]{:S(2)}) collective-permute-start(bf16[256,1024]{1,0:T(8,128)(2,1)S(1)} %collective-permute-done.4.refs_0_.refs_2_), channel_id=1, source_target_pairs={{0,128},{16,48},{32,160},{48,80},{64,192},{80,112},{96,224},{112,1... | collective-permute-start | bytes 1572872 | tf_op jit(solution)/shard_map/ppermute | solution.py:59
  59.9 1.5 %shard_map.80.refs_2_ = f32[512,1024]{1,0:T(8,128)S(1)} custom-call(s32[4]{0:T(128)S(1)} %pad_add_fusion.place, bf16[512,1024]{1,0:T(8,128)(2,1)S(1)} %shard_map.77.first.second, bf16[512,1024]{1,0:T(8,128)(2,1)S(1)} %shard_map.77.first.second, bf16[256,1024]{1,0:T(8,128)(2,1)S(1)} %shard_map.78.refs_0_, bf16[256,1024]{1,0:T(8,128)(2,1)S(1)} %shard_map.79.refs_1_), custom_call_target="tpu_custom_call" | custom-call | flops 268435456 | bytes 1048576 | tf_op jit(solution)/shard_map/pallas_call | solution.py:165
  61.4 1.5 %shard_map.81.refs_2_ = f32[512,1024]{1,0:T(8,128)S(1)} custom-call(s32[4]{0:T(128)S(1)} %pad_add_fusion.place, bf16[512,1024]{1,0:T(8,128)(2,1)S(1)} %shard_map.77.first.second, bf16[512,1024]{1,0:T(8,128)(2,1)S(1)} %shard_map.77.first.second, bf16[256,1024]{1,0:T(8,128)(2,1)S(1)} %collective-permute-done.4.refs_0_.refs_2_, ...), custom_call_target="tpu_custom_call" | custom-call | flops 268435456 | bytes 1048576 | tf_op jit(solution)/shard_map/pallas_call | solution.py:165
  62.9 1.5 %shard_map.82.refs_8_ = f32[512,1024]{1,0:T(8,128)S(1)} custom-call(s32[4]{0:T(128)S(1)} %pad_add_fusion.place, bf16[512,1024]{1,0:T(8,128)(2,1)S(1)} %shard_map.77.first.second, bf16[512,1024]{1,0:T(8,128)(2,1)S(1)} %shard_map.77.first.second, bf16[256,1024]{1,0:T(8,128)(2,1)S(1)} %collective-permute-done.6.refs_0_.refs_4_, ...), custom_call_target="tpu_custom_call" | custom-call | flops 268435456 | bytes 1048576 | tf_op jit(solution)/shard_map/pallas_call | solution.py:165
  64.3 1.9 %collective-permute-done.9.refs_7_ = bf16[256,1024]{1,0:T(8,128)(2,1)S(1)} collective-permute-done((bf16[256,1024]{1,0:T(8,128)(2,1)S(1)}, bf16[256,1024]{1,0:T(8,128)(2,1)S(1)}, u32[]{:S(2)}, u32[]{:S(2)}) %collective-permute-start.9) | collective-permute-done | bytes 524320 | tf_op jit(solution)/shard_map/ppermute | solution.py:59
  66.3 2.8 %collective-permute-done.8.refs_6_ = bf16[256,1024]{1,0:T(8,128)(2,1)S(1)} collective-permute-done((bf16[256,1024]{1,0:T(8,128)(2,1)S(1)}, bf16[256,1024]{1,0:T(8,128)(2,1)S(1)}, u32[]{:S(2)}, u32[]{:S(2)}) %collective-permute-start.8) | collective-permute-done | bytes 524320 | tf_op jit(solution)/shard_map/ppermute | solution.py:59
  69.1 2.0 %shard_map.84 = f32[256,1024]{1,0:T(8,128)S(1)} custom-call(s32[4]{0:T(128)S(1)} %pad_add_fusion.place, bf16[512,1024]{1,0:T(8,128)(2,1)S(1)} %shard_map.77.first.second, bf16[512,1024]{1,0:T(8,128)(2,1)S(1)} %collective-permute-done.second, bf16[256,1024]{1,0:T(8,128)(2,1)S(1)} %shard_map.78.refs_0_, bf16[256,1024]{1,0:T(8,128)(2,1)S(1)} %shard_map.79.refs_1_, ...), custom_call_target="tpu_custom_call" | custom-call | flops 671088640 | bytes 1048576 | tf_op jit(solution)/shard_map/pallas_call | solution.py:165
  71.0 1.9 %collective-permute-start.10 = (f32[256,1024]{1,0:T(8,128)S(1)}, f32[256,1024]{1,0:T(8,128)S(1)}, u32[]{:S(2)}, u32[]{:S(2)}) collective-permute-start(f32[256,1024]{1,0:T(8,128)S(1)} %shard_map.84), channel_id=1, source_target_pairs={{0,16},{16,0},{1,17},{17,1},{2,18},{18,2},{3,19},{19,3},{4,20},{20... | collective-permute-start | bytes 3145736 | tf_op jit(solution)/shard_map/ppermute | solution.py:304
  73.0 1.9 %shard_map.83.mine = f32[256,1024]{1,0:T(8,128)S(1)} custom-call(s32[4]{0:T(128)S(1)} %pad_add_fusion.place, bf16[512,1024]{1,0:T(8,128)(2,1)S(1)} %shard_map.77.first.second, bf16[512,1024]{1,0:T(8,128)(2,1)S(1)} %collective-permute-done.second, bf16[256,1024]{1,0:T(8,128)(2,1)S(1)} %shard_map.78.refs_0_, bf16[256,1024]{1,0:T(8,128)(2,1)S(1)} %shard_map.79.refs_1_, ...), custom_call_target="tpu_custom_call" | custom-call | flops 671088640 | bytes 1048576 | tf_op jit(solution)/shard_map/pallas_call | solution.py:165
  75.0 0.6 collective-permute-done.10.theirs
  75.6 0.1 shard_map.85
  75.7 13.0 %all_to_all.20.received = f32[32,8,128]{2,1,0:T(8,128)S(1)} all-to-all(f32[32,8,128]{2,1,0:T(8,128)S(1)} %get-tuple-element.11), channel_id=1, replica_groups=mesh['y'=4,'x'=4,'core'=2,'z'=16] {'y','x','core'}, dimensions={0} | all-to-all | bytes 262144 | tf_op jit(solution)/shard_map/all_to_all | solution.py:69
  88.7 1.0 shard_map.86
  89.7 20.9 %all_to_all.21.received = f32[16,8,128]{2,1,0:T(8,128)S(1)} all-to-all(f32[16,8,128]{2,1,0:T(8,128)S(1)} %get-tuple-element.13), channel_id=1, replica_groups=mesh['y'=4,'x'=4,'core'=2,'z'=16] {'z'}, dimensions={0} | all-to-all | bytes 131072 | tf_op jit(solution)/shard_map/all_to_all | solution.py:69
  110.6 0.6 shard_map.87
  111.2 12.5 %all_to_all.22.received = f32[32,4,128]{2,1,0:T(4,128)S(1)} all-to-all(f32[32,4,128]{2,1,0:T(4,128)S(1)} %get-tuple-element.14), channel_id=1, replica_groups=mesh['y'=4,'x'=4,'core'=2,'z'=16] {'y','x','core'}, dimensions={0} | all-to-all | bytes 131072 | tf_op jit(solution)/shard_map/all_to_all | solution.py:69
  123.7 1.4 %shard_map.88 = f32[256,1024]{1,0:T(8,128)} custom-call(f32[32,4,128]{2,1,0:T(4,128)S(1)} %all_to_all.22.received, f32[2,128]{1,0:T(2,128)S(1)} %get-tuple-element.15.row_root, f32[8,128]{1,0:T(8,128)S(1)} %get-tuple-element.16.col_root, f32[256,1024]{1,0:T(8,128)S(1)} %get-tuple-element.12.grad, f32[256,1024]{1,0:T(8,128)S(1)} %copy-done), custom_call_target="tpu_custom_call" | custom-call | flops 1048576 | bytes 3145728 | tf_op jit(solution)/shard_map/pallas_call | solution.py:275
  (17 shorter events, 0.2 us)
Async XLA Ops:
  0.7 10.5 %copy-start.1 = (bf16[128,1024]{1,0:T(8,128)(2,1)S(1)}, bf16[128,1024]{1,0:T(8,128)(2,1)}, u32[]{:S(2)}) copy-start(bf16[128,1024]{1,0:T(8,128)(2,1)} %refs_0_.1) | copy-start | bytes 786436
  3.6 32.4 %all-to-all-start = ((bf16[16,64,512]{2,1,0:T(8,128)(2,1)}), bf16[16,64,512]{2,1,0:T(8,128)(2,1)S(1)}, u32[]{:S(2)}, u32[]{:S(2)}) async-start(bf16[16,64,512]{2,1,0:T(8,128)(2,1)} %shard_map.76), calls=%async_computation | async-start | bytes 2097152 | tf_op jit(solution)/shard_map/all_to_all | solution.py:69
  11.2 17.2 %collective-permute-start.3 = (bf16[128,1024]{1,0:T(8,128)(2,1)S(1)}, bf16[128,1024]{1,0:T(8,128)(2,1)S(1)}, u32[]{:S(2)}, u32[]{:S(2)}) collective-permute-start(bf16[128,1024]{1,0:T(8,128)(2,1)S(1)} %copy-done.1), channel_id=1, source_target_pairs={{0,96},{16,400},{32,0},{48,432},{64,32},{80,464},{96,64},{112,496}... | collective-permute-start | bytes 786440 | tf_op jit(solution)/shard_map/ppermute | solution.py:59
  15.7 14.3 %collective-permute-start.2 = (bf16[128,1024]{1,0:T(8,128)(2,1)S(1)}, bf16[128,1024]{1,0:T(8,128)(2,1)S(1)}, u32[]{:S(2)}, u32[]{:S(2)}) collective-permute-start(bf16[128,1024]{1,0:T(8,128)(2,1)S(1)} %copy-done.1), channel_id=1, source_target_pairs={{0,64},{16,272},{32,96},{48,304},{64,0},{80,336},{96,32},{112,368}... | collective-permute-start | bytes 786440 | tf_op jit(solution)/shard_map/ppermute | solution.py:59
  18.2 15.8 %collective-permute-start.1 = (bf16[128,1024]{1,0:T(8,128)(2,1)S(1)}, bf16[128,1024]{1,0:T(8,128)(2,1)S(1)}, u32[]{:S(2)}, u32[]{:S(2)}) collective-permute-start(bf16[128,1024]{1,0:T(8,128)(2,1)S(1)} %copy-done.1), channel_id=1, source_target_pairs={{0,32},{16,144},{32,64},{48,176},{64,96},{80,208},{96,0},{112,240}... | collective-permute-start | bytes 786440 | tf_op jit(solution)/shard_map/ppermute | solution.py:59
  30.1 24.4 %collective-permute-start.7 = (bf16[256,1024]{1,0:T(8,128)(2,1)S(1)}, bf16[256,1024]{1,0:T(8,128)(2,1)S(1)}, u32[]{:S(2)}, u32[]{:S(2)}) collective-permute-start(bf16[256,1024]{1,0:T(8,128)(2,1)S(1)} %shard_map.79.refs_1_), channel_id=1, source_target_pairs={{0,384},{16,112},{32,416},{48,16},{64,448},{80,48},{96,480},{112,8... | collective-permute-start | bytes 1572872 | tf_op jit(solution)/shard_map/ppermute | solution.py:59
  34.0 23.9 %collective-permute-start.4 = (bf16[256,1024]{1,0:T(8,128)(2,1)S(1)}, bf16[256,1024]{1,0:T(8,128)(2,1)S(1)}, u32[]{:S(2)}, u32[]{:S(2)}) collective-permute-start(bf16[256,1024]{1,0:T(8,128)(2,1)S(1)} %shard_map.78.refs_0_), channel_id=1, source_target_pairs={{0,128},{16,48},{32,160},{48,80},{64,192},{80,112},{96,224},{112,1... | collective-permute-start | bytes 1572872 | tf_op jit(solution)/shard_map/ppermute | solution.py:59
  36.9 32.2 %collective-permute-start = (bf16[512,1024]{1,0:T(8,128)(2,1)S(1)}, bf16[512,1024]{1,0:T(8,128)(2,1)S(1)}, u32[]{:S(2)}, u32[]{:S(2)}) collective-permute-start(bf16[512,1024]{1,0:T(8,128)(2,1)S(1)} %shard_map.77.first.second), channel_id=1, source_target_pairs={{0,1},{1,2},{2,3},{3,4},{4,5},{5,6},{6,7},{7,8},{8,9},{9,10},{10,1... | collective-permute-start | bytes 3145736 | tf_op jit(solution)/shard_map/ppermute | solution.py:65
  48.0 13.3 %collective-permute-start.5 = (bf16[256,1024]{1,0:T(8,128)(2,1)S(1)}, bf16[256,1024]{1,0:T(8,128)(2,1)S(1)}, u32[]{:S(2)}, u32[]{:S(2)}) collective-permute-start(bf16[256,1024]{1,0:T(8,128)(2,1)S(1)} %shard_map.79.refs_1_), channel_id=1, source_target_pairs={{0,128},{16,48},{32,160},{48,80},{64,192},{80,112},{96,224},{112,1... | collective-permute-start | bytes 1572872 | tf_op jit(solution)/shard_map/ppermute | solution.py:59
  50.4 12.4 %collective-permute-start.6 = (bf16[256,1024]{1,0:T(8,128)(2,1)S(1)}, bf16[256,1024]{1,0:T(8,128)(2,1)S(1)}, u32[]{:S(2)}, u32[]{:S(2)}) collective-permute-start(bf16[256,1024]{1,0:T(8,128)(2,1)S(1)} %shard_map.78.refs_0_), channel_id=1, source_target_pairs={{0,384},{16,112},{32,416},{48,16},{64,448},{80,48},{96,480},{112,8... | collective-permute-start | bytes 1572872 | tf_op jit(solution)/shard_map/ppermute | solution.py:59
  54.5 11.7 %collective-permute-start.9 = (bf16[256,1024]{1,0:T(8,128)(2,1)S(1)}, bf16[256,1024]{1,0:T(8,128)(2,1)S(1)}, u32[]{:S(2)}, u32[]{:S(2)}) collective-permute-start(bf16[256,1024]{1,0:T(8,128)(2,1)S(1)} %collective-permute-done.7.refs_1_.refs_5_), channel_id=1, source_target_pairs={{0,384},{16,112},{32,416},{48,16},{64,448},{80,48},{96,480},{112,8... | collective-permute-start | bytes 1572872 | tf_op jit(solution)/shard_map/ppermute | solution.py:59
  57.9 11.1 %collective-permute-start.8 = (bf16[256,1024]{1,0:T(8,128)(2,1)S(1)}, bf16[256,1024]{1,0:T(8,128)(2,1)S(1)}, u32[]{:S(2)}, u32[]{:S(2)}) collective-permute-start(bf16[256,1024]{1,0:T(8,128)(2,1)S(1)} %collective-permute-done.4.refs_0_.refs_2_), channel_id=1, source_target_pairs={{0,128},{16,48},{32,160},{48,80},{64,192},{80,112},{96,224},{112,1... | collective-permute-start | bytes 1572872 | tf_op jit(solution)/shard_map/ppermute | solution.py:59
  71.0 4.6 %collective-permute-start.10 = (f32[256,1024]{1,0:T(8,128)S(1)}, f32[256,1024]{1,0:T(8,128)S(1)}, u32[]{:S(2)}, u32[]{:S(2)}) collective-permute-start(f32[256,1024]{1,0:T(8,128)S(1)} %shard_map.84), channel_id=1, source_target_pairs={{0,16},{16,0},{1,17},{17,1},{2,18},{18,2},{3,19},{19,3},{4,20},{20... | collective-permute-start | bytes 3145736 | tf_op jit(solution)/shard_map/ppermute | solution.py:304
  74.9 13.8 %copy-start = (f32[256,1024]{1,0:T(8,128)S(1)}, f32[256,1024]{1,0:T(8,128)}, u32[]{:S(2)}) copy-start(f32[256,1024]{1,0:T(8,128)} %weight.3) | copy-start | bytes 3145732
  74.9 13.8 %copy-start.2 = (f32[1024]{0:T(1024)S(1)}, f32[1024]{0:T(1024)}, u32[]{:S(2)}) copy-start(f32[1024]{0:T(1024)} %param.9) | copy-start | bytes 12292
  74.9 35.7 %copy-start.3 = (f32[256]{0:T(256)S(1)}, f32[256]{0:T(256)}, u32[]{:S(2)}) copy-start(f32[256]{0:T(256)} %param.8) | copy-start | bytes 3076

commit v11 on v10

--- a/solution.py
+++ b/solution.py
@@ -286,9 +286,11 @@
 def shards(activations, out_grads, weight, row_moment, col_moment):
     y, x, core, layer = (lax.axis_index(name) for name in ("y", "x", "core", "z"))
     place = jnp.stack([y, x, core, layer & 1])
-    first = turn(place, exchange(pack(place, activations), CHIPS))
+    line = [out_grads] + [along(out_grads, k, 0) for k in range(1, SIDE)]
+    packed = pack(place, activations)
+    packed, *line[1:] = lax.optimization_barrier((packed, *line[1:]))
+    first = turn(place, exchange(packed, CHIPS))
     second = next_layer(first)
-    line = [out_grads] + [along(out_grads, k, 0) for k in range(1, SIDE)]
     low, high = join(line[:2]), join(line[2:])
     back_low, ahead_high = along(low, 1, 1), along(high, SIDE - 1, 1)
     far = [along(back_low, 1, 1), along(ahead_high, SIDE - 1, 1)]

time: 126 us -> 129 us (1.024)
  starting transfers between devices: 47.6 us -> 51 us
  blocking collectives: 46.4 us -> 48.9 us
  waiting for transfers between devices: 14.7 us -> 12.5 us
    ppermute x9, waiting for transfers between devices: 14.1 us -> 4.19 us  [along(): return lax.ppermute(value, ROWS, pairs)]
    all_to_all x1, waiting for transfers between devices: 0.01 us -> 8.03 us  [exchange(): return lax.all_to_all(tiles, axes, 0, 0)]
    ppermute x9, starting transfers between devices: 27 us -> 30.3 us  [along(): return lax.ppermute(value, ROWS, pairs)]
    all_to_all x3, blocking collectives: 46.4 us -> 48.9 us  [exchange(): return lax.all_to_all(tiles, axes, 0, 0)]
  transfers between devices with their start and end apart: 12 -> 12, of which waited for: 5 -> 5; matrix products, arithmetic and copies ran while one was open for 0% -> 0% of each run, Pallas kernels for 6% -> 8%
where the time goes in v11:
time: 129 us
  starting transfers between devices  51 us (40%)
  blocking collectives  48.9 us (38%)
  Pallas kernels  15.4 us (12%)
  waiting for transfers between devices  12.5 us (10%)
    all_to_all x3, blocking collectives, exchange(): return lax.all_to_all(tiles, axes, 0, 0)  48.9 us
    ppermute x9, starting transfers between devices, along(): return lax.ppermute(value, ROWS, pairs)  30.3 us
    ppermute x1, starting transfers between devices, next_layer(): return lax.ppermute(value, ('core', 'z'), pairs)  11.1 us
    pallas_call x5, Pallas kernels, product(): pl.pallas_call(functools.partial(product_kernel, parts, which), out_shape...  8.34 us
    all_to_all x1, waiting for transfers between devices, exchange(): return lax.all_to_all(tiles, axes, 0, 0)  8.03 us
    all_to_all x1, starting transfers between devices, exchange(): return lax.all_to_all(tiles, axes, 0, 0)  6.88 us
    ppermute x9, waiting for transfers between devices, along(): return lax.ppermute(value, ROWS, pairs)  4.19 us
    pallas_call x1, Pallas kernels, pack(): pl.pallas_call(pack_kernel, out_shape=shape(COUNT, HALF, 2 * ROW_BLOCK, d...  2.9 us
  transfers between devices with their start and end apart: 12, of which 5 were waited for; matrix products, arithmetic and copies ran while one was open for 0% of the time, Pallas kernels for 8%

profile of v11, /device:TPU:1, one launch (start us, length us, event | category | flops | bytes accessed | tf_op | source)
XLA Modules:
  0.0 128.8 jit_solution(7090142030492969768)
XLA Ops:
  0.6 5.7 %collective-permute-start.1 = (bf16[128,1024]{1,0:T(8,128)(2,1)}, bf16[128,1024]{1,0:T(8,128)(2,1)S(1)}, u32[]{:S(2)}, u32[]{:S(2)}) collective-permute-start(bf16[128,1024]{1,0:T(8,128)(2,1)} %refs_0_.1), channel_id=1, source_target_pairs={{0,64},{16,272},{32,96},{48,304},{64,0},{80,336},{96,32},{112,368}... | collective-permute-start | bytes 786440 | tf_op jit(solution)/shard_map/ppermute | solution.py:59
  6.3 2.3 %collective-permute-start = (bf16[128,1024]{1,0:T(8,128)(2,1)}, bf16[128,1024]{1,0:T(8,128)(2,1)S(1)}, u32[]{:S(2)}, u32[]{:S(2)}) collective-permute-start(bf16[128,1024]{1,0:T(8,128)(2,1)} %refs_0_.1), channel_id=1, source_target_pairs={{0,32},{16,144},{32,64},{48,176},{64,96},{80,208},{96,0},{112,240}... | collective-permute-start | bytes 786440 | tf_op jit(solution)/shard_map/ppermute | solution.py:59
  8.6 4.2 %collective-permute-start.2 = (bf16[128,1024]{1,0:T(8,128)(2,1)}, bf16[128,1024]{1,0:T(8,128)(2,1)S(1)}, u32[]{:S(2)}, u32[]{:S(2)}) collective-permute-start(bf16[128,1024]{1,0:T(8,128)(2,1)} %refs_0_.1), channel_id=1, source_target_pairs={{0,96},{16,400},{32,0},{48,432},{64,32},{80,464},{96,64},{112,496}... | collective-permute-start | bytes 786440 | tf_op jit(solution)/shard_map/ppermute | solution.py:59
  12.8 0.1 pad_add_fusion.place
  12.9 2.9 %shard_map.76 = bf16[16,64,512]{2,1,0:T(8,128)(2,1)} custom-call(s32[4]{0:T(128)S(1)} %pad_add_fusion.place, bf16[128,8192]{1,0:T(8,128)(2,1)} %source.1), custom_call_target="tpu_custom_call" | custom-call | bytes 2097152 | tf_op jit(solution)/shard_map/pallas_call | solution.py:85
  15.8 0.6 collective-permute-done.2.refs_1_
  16.4 6.9 %all-to-all-start = ((bf16[16,64,512]{2,1,0:T(8,128)(2,1)}), bf16[16,64,512]{2,1,0:T(8,128)(2,1)S(1)}, u32[]{:S(2)}, u32[]{:S(2)}) async-start(bf16[16,64,512]{2,1,0:T(8,128)(2,1)} %shard_map.76), calls=%async_computation | async-start | bytes 2097152 | tf_op jit(solution)/shard_map/all_to_all | solution.py:69
  23.4 4.5 %collective-permute-start.7 = (bf16[256,1024]{1,0:T(8,128)(2,1)S(1)}, bf16[256,1024]{1,0:T(8,128)(2,1)S(1)}, u32[]{:S(2)}, u32[]{:S(2)}) collective-permute-start(bf16[256,1024]{1,0:T(8,128)(2,1)S(1)} %shard_map.79.refs_1_), channel_id=1, source_target_pairs={{0,384},{16,112},{32,416},{48,16},{64,448},{80,48},{96,480},{112,8... | collective-permute-start | bytes 1572872 | tf_op jit(solution)/shard_map/ppermute | solution.py:59
  27.9 1.9 %collective-permute-start.4 = (bf16[256,1024]{1,0:T(8,128)(2,1)S(1)}, bf16[256,1024]{1,0:T(8,128)(2,1)S(1)}, u32[]{:S(2)}, u32[]{:S(2)}) collective-permute-start(bf16[256,1024]{1,0:T(8,128)(2,1)S(1)} %shard_map.78.refs_0_), channel_id=1, source_target_pairs={{0,128},{16,48},{32,160},{48,80},{64,192},{80,112},{96,224},{112,1... | collective-permute-start | bytes 1572872 | tf_op jit(solution)/shard_map/ppermute | solution.py:59
  29.9 8.0 %all-to-all-done.part = bf16[16,64,512]{2,1,0:T(8,128)(2,1)S(1)} async-done(((bf16[16,64,512]{2,1,0:T(8,128)(2,1)}), bf16[16,64,512]{2,1,0:T(8,128)(2,1)S(1)}, u32[]{:S(2)}, u32[]{:S(2)}) %all-to-all-start) | async-done | bytes 1048608 | tf_op jit(solution)/shard_map/all_to_all | solution.py:69
  37.9 0.9 shard_map.77.first.second
  38.8 11.1 %collective-permute-start.3 = (bf16[512,1024]{1,0:T(8,128)(2,1)S(1)}, bf16[512,1024]{1,0:T(8,128)(2,1)S(1)}, u32[]{:S(2)}, u32[]{:S(2)}) collective-permute-start(bf16[512,1024]{1,0:T(8,128)(2,1)S(1)} %shard_map.77.first.second), channel_id=1, source_target_pairs={{0,1},{1,2},{2,3},{3,4},{4,5},{5,6},{6,7},{7,8},{8,9},{9,10},{10,1... | collective-permute-start | bytes 3145736 | tf_op jit(solution)/shard_map/ppermute | solution.py:65
  49.9 2.2 %collective-permute-start.5 = (bf16[256,1024]{1,0:T(8,128)(2,1)S(1)}, bf16[256,1024]{1,0:T(8,128)(2,1)S(1)}, u32[]{:S(2)}, u32[]{:S(2)}) collective-permute-start(bf16[256,1024]{1,0:T(8,128)(2,1)S(1)} %shard_map.79.refs_1_), channel_id=1, source_target_pairs={{0,128},{16,48},{32,160},{48,80},{64,192},{80,112},{96,224},{112,1... | collective-permute-start | bytes 1572872 | tf_op jit(solution)/shard_map/ppermute | solution.py:59
  52.1 4.3 %collective-permute-start.6 = (bf16[256,1024]{1,0:T(8,128)(2,1)S(1)}, bf16[256,1024]{1,0:T(8,128)(2,1)S(1)}, u32[]{:S(2)}, u32[]{:S(2)}) collective-permute-start(bf16[256,1024]{1,0:T(8,128)(2,1)S(1)} %shard_map.78.refs_0_), channel_id=1, source_target_pairs={{0,384},{16,112},{32,416},{48,16},{64,448},{80,48},{96,480},{112,8... | collective-permute-start | bytes 1572872 | tf_op jit(solution)/shard_map/ppermute | solution.py:59
  56.5 1.9 %collective-permute-start.9 = (bf16[256,1024]{1,0:T(8,128)(2,1)S(1)}, bf16[256,1024]{1,0:T(8,128)(2,1)S(1)}, u32[]{:S(2)}, u32[]{:S(2)}) collective-permute-start(bf16[256,1024]{1,0:T(8,128)(2,1)S(1)} %collective-permute-done.7.refs_1_.refs_5_), channel_id=1, source_target_pairs={{0,384},{16,112},{32,416},{48,16},{64,448},{80,48},{96,480},{112,8... | collective-permute-start | bytes 1572872 | tf_op jit(solution)/shard_map/ppermute | solution.py:59
  58.4 3.4 %collective-permute-start.8 = (bf16[256,1024]{1,0:T(8,128)(2,1)S(1)}, bf16[256,1024]{1,0:T(8,128)(2,1)S(1)}, u32[]{:S(2)}, u32[]{:S(2)}) collective-permute-start(bf16[256,1024]{1,0:T(8,128)(2,1)S(1)} %collective-permute-done.4.refs_0_.refs_2_), channel_id=1, source_target_pairs={{0,128},{16,48},{32,160},{48,80},{64,192},{80,112},{96,224},{112,1... | collective-permute-start | bytes 1572872 | tf_op jit(solution)/shard_map/ppermute | solution.py:59
  61.8 1.5 %shard_map.80.refs_2_ = f32[512,1024]{1,0:T(8,128)S(1)} custom-call(s32[4]{0:T(128)S(1)} %pad_add_fusion.place, bf16[512,1024]{1,0:T(8,128)(2,1)S(1)} %shard_map.77.first.second, bf16[512,1024]{1,0:T(8,128)(2,1)S(1)} %shard_map.77.first.second, bf16[256,1024]{1,0:T(8,128)(2,1)S(1)} %shard_map.78.refs_0_, bf16[256,1024]{1,0:T(8,128)(2,1)S(1)} %shard_map.79.refs_1_), custom_call_target="tpu_custom_call" | custom-call | flops 268435456 | bytes 1048576 | tf_op jit(solution)/shard_map/pallas_call | solution.py:165
  63.3 1.5 %shard_map.81.refs_2_ = f32[512,1024]{1,0:T(8,128)S(1)} custom-call(s32[4]{0:T(128)S(1)} %pad_add_fusion.place, bf16[512,1024]{1,0:T(8,128)(2,1)S(1)} %shard_map.77.first.second, bf16[512,1024]{1,0:T(8,128)(2,1)S(1)} %shard_map.77.first.second, bf16[256,1024]{1,0:T(8,128)(2,1)S(1)} %collective-permute-done.4.refs_0_.refs_2_, ...), custom_call_target="tpu_custom_call" | custom-call | flops 268435456 | bytes 1048576 | tf_op jit(solution)/shard_map/pallas_call | solution.py:165
  64.8 1.5 %shard_map.82.refs_8_ = f32[512,1024]{1,0:T(8,128)S(1)} custom-call(s32[4]{0:T(128)S(1)} %pad_add_fusion.place, bf16[512,1024]{1,0:T(8,128)(2,1)S(1)} %shard_map.77.first.second, bf16[512,1024]{1,0:T(8,128)(2,1)S(1)} %shard_map.77.first.second, bf16[256,1024]{1,0:T(8,128)(2,1)S(1)} %collective-permute-done.6.refs_0_.refs_4_, ...), custom_call_target="tpu_custom_call" | custom-call | flops 268435456 | bytes 1048576 | tf_op jit(solution)/shard_map/pallas_call | solution.py:165
  66.2 1.9 %collective-permute-done.9.refs_7_ = bf16[256,1024]{1,0:T(8,128)(2,1)S(1)} collective-permute-done((bf16[256,1024]{1,0:T(8,128)(2,1)S(1)}, bf16[256,1024]{1,0:T(8,128)(2,1)S(1)}, u32[]{:S(2)}, u32[]{:S(2)}) %collective-permute-start.9) | collective-permute-done | bytes 524320 | tf_op jit(solution)/shard_map/ppermute | solution.py:59
  68.2 1.7 %collective-permute-done.8.refs_6_ = bf16[256,1024]{1,0:T(8,128)(2,1)S(1)} collective-permute-done((bf16[256,1024]{1,0:T(8,128)(2,1)S(1)}, bf16[256,1024]{1,0:T(8,128)(2,1)S(1)}, u32[]{:S(2)}, u32[]{:S(2)}) %collective-permute-start.8) | collective-permute-done | bytes 524320 | tf_op jit(solution)/shard_map/ppermute | solution.py:59
  69.8 1.9 %shard_map.84 = f32[256,1024]{1,0:T(8,128)S(1)} custom-call(s32[4]{0:T(128)S(1)} %pad_add_fusion.place, bf16[512,1024]{1,0:T(8,128)(2,1)S(1)} %shard_map.77.first.second, bf16[512,1024]{1,0:T(8,128)(2,1)S(1)} %collective-permute-done.3.second, bf16[256,1024]{1,0:T(8,128)(2,1)S(1)} %shard_map.78.refs_0_, bf16[256,1024]{1,0:T(8,128)(2,1)S(1)} %shard_map.79.refs_1_, ...), custom_call_target="tpu_custom_call" | custom-call | flops 671088640 | bytes 1048576 | tf_op jit(solution)/shard_map/pallas_call | solution.py:165
  71.8 2.7 %collective-permute-start.10 = (f32[256,1024]{1,0:T(8,128)S(1)}, f32[256,1024]{1,0:T(8,128)S(1)}, u32[]{:S(2)}, u32[]{:S(2)}) collective-permute-start(f32[256,1024]{1,0:T(8,128)S(1)} %shard_map.84), channel_id=1, source_target_pairs={{0,16},{16,0},{1,17},{17,1},{2,18},{18,2},{3,19},{19,3},{4,20},{20... | collective-permute-start | bytes 3145736 | tf_op jit(solution)/shard_map/ppermute | solution.py:306
  74.5 2.0 %shard_map.83.mine = f32[256,1024]{1,0:T(8,128)S(1)} custom-call(s32[4]{0:T(128)S(1)} %pad_add_fusion.place, bf16[512,1024]{1,0:T(8,128)(2,1)S(1)} %shard_map.77.first.second, bf16[512,1024]{1,0:T(8,128)(2,1)S(1)} %collective-permute-done.3.second, bf16[256,1024]{1,0:T(8,128)(2,1)S(1)} %shard_map.78.refs_0_, bf16[256,1024]{1,0:T(8,128)(2,1)S(1)} %shard_map.79.refs_1_, ...), custom_call_target="tpu_custom_call" | custom-call | flops 671088640 | bytes 1048576 | tf_op jit(solution)/shard_map/pallas_call | solution.py:165
  76.5 0.3 collective-permute-done.10.theirs
  76.7 0.1 shard_map.85
  76.9 11.7 %all_to_all.20.received = f32[32,8,128]{2,1,0:T(8,128)S(1)} all-to-all(f32[32,8,128]{2,1,0:T(8,128)S(1)} %get-tuple-element.19), channel_id=1, replica_groups=mesh['y'=4,'x'=4,'core'=2,'z'=16] {'y','x','core'}, dimensions={0} | all-to-all | bytes 262144 | tf_op jit(solution)/shard_map/all_to_all | solution.py:69
  88.6 1.0 shard_map.86
  89.5 24.7 %all_to_all.21.received = f32[16,8,128]{2,1,0:T(8,128)S(1)} all-to-all(f32[16,8,128]{2,1,0:T(8,128)S(1)} %get-tuple-element.21), channel_id=1, replica_groups=mesh['y'=4,'x'=4,'core'=2,'z'=16] {'z'}, dimensions={0} | all-to-all | bytes 131072 | tf_op jit(solution)/shard_map/all_to_all | solution.py:69
  114.2 0.6 shard_map.87
  114.8 12.5 %all_to_all.22.received = f32[32,4,128]{2,1,0:T(4,128)S(1)} all-to-all(f32[32,4,128]{2,1,0:T(4,128)S(1)} %get-tuple-element.22), channel_id=1, replica_groups=mesh['y'=4,'x'=4,'core'=2,'z'=16] {'y','x','core'}, dimensions={0} | all-to-all | bytes 131072 | tf_op jit(solution)/shard_map/all_to_all | solution.py:69
  127.3 1.4 %shard_map.88 = f32[256,1024]{1,0:T(8,128)} custom-call(f32[32,4,128]{2,1,0:T(4,128)S(1)} %all_to_all.22.received, f32[2,128]{1,0:T(2,128)S(1)} %get-tuple-element.23.row_root, f32[8,128]{1,0:T(8,128)S(1)} %get-tuple-element.24.col_root, f32[256,1024]{1,0:T(8,128)S(1)} %get-tuple-element.20.grad, f32[256,1024]{1,0:T(8,128)S(1)} %copy-done), custom_call_target="tpu_custom_call" | custom-call | flops 1048576 | bytes 3145728 | tf_op jit(solution)/shard_map/pallas_call | solution.py:275
  (17 shorter events, 0.2 us)
Async XLA Ops:
  0.6 15.2 %collective-permute-start.1 = (bf16[128,1024]{1,0:T(8,128)(2,1)}, bf16[128,1024]{1,0:T(8,128)(2,1)S(1)}, u32[]{:S(2)}, u32[]{:S(2)}) collective-permute-start(bf16[128,1024]{1,0:T(8,128)(2,1)} %refs_0_.1), channel_id=1, source_target_pairs={{0,64},{16,272},{32,96},{48,304},{64,0},{80,336},{96,32},{112,368}... | collective-permute-start | bytes 786440 | tf_op jit(solution)/shard_map/ppermute | solution.py:59
  6.3 9.5 %collective-permute-start = (bf16[128,1024]{1,0:T(8,128)(2,1)}, bf16[128,1024]{1,0:T(8,128)(2,1)S(1)}, u32[]{:S(2)}, u32[]{:S(2)}) collective-permute-start(bf16[128,1024]{1,0:T(8,128)(2,1)} %refs_0_.1), channel_id=1, source_target_pairs={{0,32},{16,144},{32,64},{48,176},{64,96},{80,208},{96,0},{112,240}... | collective-permute-start | bytes 786440 | tf_op jit(solution)/shard_map/ppermute | solution.py:59
  8.6 7.8 %collective-permute-start.2 = (bf16[128,1024]{1,0:T(8,128)(2,1)}, bf16[128,1024]{1,0:T(8,128)(2,1)S(1)}, u32[]{:S(2)}, u32[]{:S(2)}) collective-permute-start(bf16[128,1024]{1,0:T(8,128)(2,1)} %refs_0_.1), channel_id=1, source_target_pairs={{0,96},{16,400},{32,0},{48,432},{64,32},{80,464},{96,64},{112,496}... | collective-permute-start | bytes 786440 | tf_op jit(solution)/shard_map/ppermute | solution.py:59
  12.9 10.4 %copy-start.1 = (bf16[128,1024]{1,0:T(8,128)(2,1)S(1)}, bf16[128,1024]{1,0:T(8,128)(2,1)}, u32[]{:S(2)}) copy-start(bf16[128,1024]{1,0:T(8,128)(2,1)} %refs_0_.1) | copy-start | bytes 786436
  16.4 21.5 %all-to-all-start = ((bf16[16,64,512]{2,1,0:T(8,128)(2,1)}), bf16[16,64,512]{2,1,0:T(8,128)(2,1)S(1)}, u32[]{:S(2)}, u32[]{:S(2)}) async-start(bf16[16,64,512]{2,1,0:T(8,128)(2,1)} %shard_map.76), calls=%async_computation | async-start | bytes 2097152 | tf_op jit(solution)/shard_map/all_to_all | solution.py:69
  23.4 33.0 %collective-permute-start.7 = (bf16[256,1024]{1,0:T(8,128)(2,1)S(1)}, bf16[256,1024]{1,0:T(8,128)(2,1)S(1)}, u32[]{:S(2)}, u32[]{:S(2)}) collective-permute-start(bf16[256,1024]{1,0:T(8,128)(2,1)S(1)} %shard_map.79.refs_1_), channel_id=1, source_target_pairs={{0,384},{16,112},{32,416},{48,16},{64,448},{80,48},{96,480},{112,8... | collective-permute-start | bytes 1572872 | tf_op jit(solution)/shard_map/ppermute | solution.py:59
  27.9 30.4 %collective-permute-start.4 = (bf16[256,1024]{1,0:T(8,128)(2,1)S(1)}, bf16[256,1024]{1,0:T(8,128)(2,1)S(1)}, u32[]{:S(2)}, u32[]{:S(2)}) collective-permute-start(bf16[256,1024]{1,0:T(8,128)(2,1)S(1)} %shard_map.78.refs_0_), channel_id=1, source_target_pairs={{0,128},{16,48},{32,160},{48,80},{64,192},{80,112},{96,224},{112,1... | collective-permute-start | bytes 1572872 | tf_op jit(solution)/shard_map/ppermute | solution.py:59
  38.8 31.0 %collective-permute-start.3 = (bf16[512,1024]{1,0:T(8,128)(2,1)S(1)}, bf16[512,1024]{1,0:T(8,128)(2,1)S(1)}, u32[]{:S(2)}, u32[]{:S(2)}) collective-permute-start(bf16[512,1024]{1,0:T(8,128)(2,1)S(1)} %shard_map.77.first.second), channel_id=1, source_target_pairs={{0,1},{1,2},{2,3},{3,4},{4,5},{5,6},{6,7},{7,8},{8,9},{9,10},{10,1... | collective-permute-start | bytes 3145736 | tf_op jit(solution)/shard_map/ppermute | solution.py:65
  49.9 13.3 %collective-permute-start.5 = (bf16[256,1024]{1,0:T(8,128)(2,1)S(1)}, bf16[256,1024]{1,0:T(8,128)(2,1)S(1)}, u32[]{:S(2)}, u32[]{:S(2)}) collective-permute-start(bf16[256,1024]{1,0:T(8,128)(2,1)S(1)} %shard_map.79.refs_1_), channel_id=1, source_target_pairs={{0,128},{16,48},{32,160},{48,80},{64,192},{80,112},{96,224},{112,1... | collective-permute-start | bytes 1572872 | tf_op jit(solution)/shard_map/ppermute | solution.py:59
  52.1 12.6 %collective-permute-start.6 = (bf16[256,1024]{1,0:T(8,128)(2,1)S(1)}, bf16[256,1024]{1,0:T(8,128)(2,1)S(1)}, u32[]{:S(2)}, u32[]{:S(2)}) collective-permute-start(bf16[256,1024]{1,0:T(8,128)(2,1)S(1)} %shard_map.78.refs_0_), channel_id=1, source_target_pairs={{0,384},{16,112},{32,416},{48,16},{64,448},{80,48},{96,480},{112,8... | collective-permute-start | bytes 1572872 | tf_op jit(solution)/shard_map/ppermute | solution.py:59
  56.5 11.7 %collective-permute-start.9 = (bf16[256,1024]{1,0:T(8,128)(2,1)S(1)}, bf16[256,1024]{1,0:T(8,128)(2,1)S(1)}, u32[]{:S(2)}, u32[]{:S(2)}) collective-permute-start(bf16[256,1024]{1,0:T(8,128)(2,1)S(1)} %collective-permute-done.7.refs_1_.refs_5_), channel_id=1, source_target_pairs={{0,384},{16,112},{32,416},{48,16},{64,448},{80,48},{96,480},{112,8... | collective-permute-start | bytes 1572872 | tf_op jit(solution)/shard_map/ppermute | solution.py:59
  58.4 11.4 %collective-permute-start.8 = (bf16[256,1024]{1,0:T(8,128)(2,1)S(1)}, bf16[256,1024]{1,0:T(8,128)(2,1)S(1)}, u32[]{:S(2)}, u32[]{:S(2)}) collective-permute-start(bf16[256,1024]{1,0:T(8,128)(2,1)S(1)} %collective-permute-done.4.refs_0_.refs_2_), channel_id=1, source_target_pairs={{0,128},{16,48},{32,160},{48,80},{64,192},{80,112},{96,224},{112,1... | collective-permute-start | bytes 1572872 | tf_op jit(solution)/shard_map/ppermute | solution.py:59
  71.8 4.9 %collective-permute-start.10 = (f32[256,1024]{1,0:T(8,128)S(1)}, f32[256,1024]{1,0:T(8,128)S(1)}, u32[]{:S(2)}, u32[]{:S(2)}) collective-permute-start(f32[256,1024]{1,0:T(8,128)S(1)} %shard_map.84), channel_id=1, source_target_pairs={{0,16},{16,0},{1,17},{17,1},{2,18},{18,2},{3,19},{19,3},{4,20},{20... | collective-permute-start | bytes 3145736 | tf_op jit(solution)/shard_map/ppermute | solution.py:306
  76.4 12.1 %copy-start = (f32[256,1024]{1,0:T(8,128)S(1)}, f32[256,1024]{1,0:T(8,128)}, u32[]{:S(2)}) copy-start(f32[256,1024]{1,0:T(8,128)} %weight.3) | copy-start | bytes 3145732
  76.4 12.1 %copy-start.2 = (f32[1024]{0:T(1024)S(1)}, f32[1024]{0:T(1024)}, u32[]{:S(2)}) copy-start(f32[1024]{0:T(1024)} %param.9) | copy-start | bytes 12292
  76.5 37.8 %copy-start.3 = (f32[256]{0:T(256)S(1)}, f32[256]{0:T(256)}, u32[]{:S(2)}) copy-start(f32[256]{0:T(256)} %param.8) | copy-start | bytes 3076

commit v12 on v10

--- a/solution.py
+++ b/solution.py
@@ -84,7 +84,7 @@
 def pack(place, activations):
     return pl.pallas_call(
         pack_kernel,
-        out_shape=shape(COUNT, HALF, 2 * ROW_BLOCK, dtype=jnp.bfloat16),
+        out_shape=pltpu.VMEM((COUNT, HALF, 2 * ROW_BLOCK), jnp.bfloat16),
         in_specs=[SCALARS, ANYWHERE],
         out_specs=WHOLE,
         scratch_shapes=[pltpu.SemaphoreType.DMA((COUNT,))],
@@ -168,7 +168,7 @@
         in_specs=[SCALARS] + [WHOLE] * len(operands),
         out_specs=WHOLE,
         compiler_params=PARAMS,
-        cost_estimate=cost(2 * count * SIDE * HALF * WIDTH * len(parts), 2**20),
+        cost_estimate=cost(20 * count * SIDE * HALF * WIDTH * len(parts), 2**20),
     )(place, *operands)
 
 
@@ -294,15 +294,14 @@
     far = [along(back_low, 1, 1), along(ahead_high, SIDE - 1, 1)]
     back, ahead = [back_low, along(high, 1, 1)], [along(low, SIDE - 1, 1), ahead_high]
     blocks = lambda operand: [(operand, 0), (operand, 1), (operand + 1, 0), (operand + 1, 1)]
-    total = None
-    for group, halves in ((0, [low, high]), (1, back), (3, ahead)):
-        total = product(place, (first, first), halves, [(group, True, blocks(0))], total)
-    operands = [low, high] + back + ahead + far
-    parts = [(2, True, blocks(6)), (2, False, blocks(6))]
-    parts += [(group, False, blocks(2 * i)) for i, group in enumerate((0, 1, 3))]
-    theirs = product(place, (first, second), operands, parts, total, lambda core: 1 - core)
+    total = product(place, (first, first), [low, high], [(0, True, blocks(0))])
+    total = product(place, (first, first), back + ahead, [(1, True, blocks(0)), (3, True, blocks(2))], total)
+    parts = [(group, False, blocks(2 * i)) for i, group in enumerate((0, 1, 3))]
+    total = product(place, (second, second), [low, high] + back + ahead, parts, total)
+    parts = [(2, True, blocks(0)), (2, False, blocks(0))]
+    theirs = product(place, (first, second), far, parts, total, lambda core: 1 - core)
     received = lax.ppermute(theirs, "core", [(0, 1), (1, 0)])
-    mine = product(place, (first, second), operands, parts, total, lambda core: core)
+    mine = product(place, (first, second), far, parts, total, lambda core: core)
     weight_grad, tiles = columns(mine, received)
     new_cols, col_root, tiles = rows(exchange(tiles, ROWS), col_moment.reshape(TILE), weight_grad, weight)
     new_rows, row_root, tiles = scalars(exchange(tiles, "z"), row_moment.reshape(2, LANES))

time: 126 us -> 125 us (level)
  no operation moved by 1% of the time
where the time goes in v12:
time: 125 us
  starting transfers between devices  47.3 us (38%)
  blocking collectives  45.5 us (36%)
  waiting for transfers between devices  15.6 us (12%)
  Pallas kernels  15.3 us (12%)
    all_to_all x3, blocking collectives, exchange(): return lax.all_to_all(tiles, axes, 0, 0)  45.5 us
    ppermute x9, starting transfers between devices, along(): return lax.ppermute(value, ROWS, pairs)  27.4 us
    ppermute x9, waiting for transfers between devices, along(): return lax.ppermute(value, ROWS, pairs)  14.5 us
    ppermute x1, starting transfers between devices, next_layer(): return lax.ppermute(value, ('core', 'z'), pairs)  10.4 us
    pallas_call x5, Pallas kernels, product(): pl.pallas_call(functools.partial(product_kernel, parts, which), out_shape...  8.33 us
    all_to_all x1, starting transfers between devices, exchange(): return lax.all_to_all(tiles, axes, 0, 0)  7.6 us
    pallas_call x1, Pallas kernels, pack(): pl.pallas_call(pack_kernel, out_shape=pltpu.VMEM((COUNT, HALF, 2 * ROW_BL...  2.9 us
  transfers between devices with their start and end apart: 12, of which 5 were waited for; matrix products, arithmetic and copies ran while one was open for 0% of the time, Pallas kernels for 6%

profile of v12, /device:TPU:1, one launch (start us, length us, event | category | flops | bytes accessed | tf_op | source)
XLA Modules:
  0.0 124.7 jit_solution(6997203017365767514)
XLA Ops:
  0.6 0.1 pad_add_fusion.place
  0.7 2.9 %shard_map.76 = bf16[16,64,512]{2,1,0:T(8,128)(2,1)} custom-call(s32[4]{0:T(128)S(1)} %pad_add_fusion.place, bf16[128,8192]{1,0:T(8,128)(2,1)} %source.1), custom_call_target="tpu_custom_call" | custom-call | bytes 2097152 | tf_op jit(solution)/shard_map/pallas_call | solution.py:85
  3.6 7.6 %all-to-all-start = ((bf16[16,64,512]{2,1,0:T(8,128)(2,1)}), bf16[16,64,512]{2,1,0:T(8,128)(2,1)S(1)}, u32[]{:S(2)}, u32[]{:S(2)}) async-start(bf16[16,64,512]{2,1,0:T(8,128)(2,1)} %shard_map.76), calls=%async_computation | async-start | bytes 2097152 | tf_op jit(solution)/shard_map/all_to_all | solution.py:69
  11.2 4.8 %collective-permute-start.4 = (bf16[128,1024]{1,0:T(8,128)(2,1)S(1)}, bf16[128,1024]{1,0:T(8,128)(2,1)S(1)}, u32[]{:S(2)}, u32[]{:S(2)}) collective-permute-start(bf16[128,1024]{1,0:T(8,128)(2,1)S(1)} %copy-done.1), channel_id=1, source_target_pairs={{0,64},{16,272},{32,96},{48,304},{64,0},{80,336},{96,32},{112,368}... | collective-permute-start | bytes 786440 | tf_op jit(solution)/shard_map/ppermute | solution.py:59
  16.0 2.8 %collective-permute-start.5 = (bf16[128,1024]{1,0:T(8,128)(2,1)S(1)}, bf16[128,1024]{1,0:T(8,128)(2,1)S(1)}, u32[]{:S(2)}, u32[]{:S(2)}) collective-permute-start(bf16[128,1024]{1,0:T(8,128)(2,1)S(1)} %copy-done.1), channel_id=1, source_target_pairs={{0,96},{16,400},{32,0},{48,432},{64,32},{80,464},{96,64},{112,496}... | collective-permute-start | bytes 786440 | tf_op jit(solution)/shard_map/ppermute | solution.py:59
  18.8 2.5 %collective-permute-start.1 = (bf16[128,1024]{1,0:T(8,128)(2,1)S(1)}, bf16[128,1024]{1,0:T(8,128)(2,1)S(1)}, u32[]{:S(2)}, u32[]{:S(2)}) collective-permute-start(bf16[128,1024]{1,0:T(8,128)(2,1)S(1)} %copy-done.1), channel_id=1, source_target_pairs={{0,32},{16,144},{32,64},{48,176},{64,96},{80,208},{96,0},{112,240}... | collective-permute-start | bytes 786440 | tf_op jit(solution)/shard_map/ppermute | solution.py:59
  21.3 8.7 %collective-permute-done.4.refs_0_ = bf16[128,1024]{1,0:T(8,128)(2,1)S(1)} collective-permute-done((bf16[128,1024]{1,0:T(8,128)(2,1)S(1)}, bf16[128,1024]{1,0:T(8,128)(2,1)S(1)}, u32[]{:S(2)}, u32[]{:S(2)}) %collective-permute-start.4) | collective-permute-done | bytes 262176 | tf_op jit(solution)/shard_map/ppermute | solution.py:59
  30.0 2.0 %collective-permute-done.5.refs_1_ = bf16[128,1024]{1,0:T(8,128)(2,1)S(1)} collective-permute-done((bf16[128,1024]{1,0:T(8,128)(2,1)S(1)}, bf16[128,1024]{1,0:T(8,128)(2,1)S(1)}, u32[]{:S(2)}, u32[]{:S(2)}) %collective-permute-start.5) | collective-permute-done | bytes 262176 | tf_op jit(solution)/shard_map/ppermute | solution.py:59
  32.1 3.7 %collective-permute-start.6 = (bf16[256,1024]{1,0:T(8,128)(2,1)S(1)}, bf16[256,1024]{1,0:T(8,128)(2,1)S(1)}, u32[]{:S(2)}, u32[]{:S(2)}) collective-permute-start(bf16[256,1024]{1,0:T(8,128)(2,1)S(1)} %shard_map.79.refs_1_), channel_id=1, source_target_pairs={{0,384},{16,112},{32,416},{48,16},{64,448},{80,48},{96,480},{112,8... | collective-permute-start | bytes 1572872 | tf_op jit(solution)/shard_map/ppermute | solution.py:59
  35.8 1.9 %collective-permute-start.2 = (bf16[256,1024]{1,0:T(8,128)(2,1)S(1)}, bf16[256,1024]{1,0:T(8,128)(2,1)S(1)}, u32[]{:S(2)}, u32[]{:S(2)}) collective-permute-start(bf16[256,1024]{1,0:T(8,128)(2,1)S(1)} %shard_map.78.refs_0_), channel_id=1, source_target_pairs={{0,128},{16,48},{32,160},{48,80},{64,192},{80,112},{96,224},{112,1... | collective-permute-start | bytes 1572872 | tf_op jit(solution)/shard_map/ppermute | solution.py:59
  37.8 0.9 shard_map.77.first.second
  38.7 10.4 %collective-permute-start = (bf16[512,1024]{1,0:T(8,128)(2,1)S(1)}, bf16[512,1024]{1,0:T(8,128)(2,1)S(1)}, u32[]{:S(2)}, u32[]{:S(2)}) collective-permute-start(bf16[512,1024]{1,0:T(8,128)(2,1)S(1)} %shard_map.77.first.second), channel_id=1, source_target_pairs={{0,1},{1,2},{2,3},{3,4},{4,5},{5,6},{6,7},{7,8},{8,9},{9,10},{10,1... | collective-permute-start | bytes 3145736 | tf_op jit(solution)/shard_map/ppermute | solution.py:65
  49.0 2.4 %collective-permute-start.8 = (bf16[256,1024]{1,0:T(8,128)(2,1)S(1)}, bf16[256,1024]{1,0:T(8,128)(2,1)S(1)}, u32[]{:S(2)}, u32[]{:S(2)}) collective-permute-start(bf16[256,1024]{1,0:T(8,128)(2,1)S(1)} %shard_map.79.refs_1_), channel_id=1, source_target_pairs={{0,128},{16,48},{32,160},{48,80},{64,192},{80,112},{96,224},{112,1... | collective-permute-start | bytes 1572872 | tf_op jit(solution)/shard_map/ppermute | solution.py:59
  51.5 4.1 %collective-permute-start.9 = (bf16[256,1024]{1,0:T(8,128)(2,1)S(1)}, bf16[256,1024]{1,0:T(8,128)(2,1)S(1)}, u32[]{:S(2)}, u32[]{:S(2)}) collective-permute-start(bf16[256,1024]{1,0:T(8,128)(2,1)S(1)} %shard_map.78.refs_0_), channel_id=1, source_target_pairs={{0,384},{16,112},{32,416},{48,16},{64,448},{80,48},{96,480},{112,8... | collective-permute-start | bytes 1572872 | tf_op jit(solution)/shard_map/ppermute | solution.py:59
  55.6 3.4 %collective-permute-start.7 = (bf16[256,1024]{1,0:T(8,128)(2,1)S(1)}, bf16[256,1024]{1,0:T(8,128)(2,1)S(1)}, u32[]{:S(2)}, u32[]{:S(2)}) collective-permute-start(bf16[256,1024]{1,0:T(8,128)(2,1)S(1)} %collective-permute-done.6.refs_3_.refs_5_), channel_id=1, source_target_pairs={{0,384},{16,112},{32,416},{48,16},{64,448},{80,48},{96,480},{112,8... | collective-permute-start | bytes 1572872 | tf_op jit(solution)/shard_map/ppermute | solution.py:59
  58.9 1.9 %collective-permute-start.3 = (bf16[256,1024]{1,0:T(8,128)(2,1)S(1)}, bf16[256,1024]{1,0:T(8,128)(2,1)S(1)}, u32[]{:S(2)}, u32[]{:S(2)}) collective-permute-start(bf16[256,1024]{1,0:T(8,128)(2,1)S(1)} %collective-permute-done.2.refs_0_.refs_2_), channel_id=1, source_target_pairs={{0,128},{16,48},{32,160},{48,80},{64,192},{80,112},{96,224},{112,1... | collective-permute-start | bytes 1572872 | tf_op jit(solution)/shard_map/ppermute | solution.py:59
  60.9 1.5 %shard_map.80.refs_4_ = f32[512,1024]{1,0:T(8,128)S(1)} custom-call(s32[4]{0:T(128)S(1)} %pad_add_fusion.place, bf16[512,1024]{1,0:T(8,128)(2,1)S(1)} %shard_map.77.first.second, bf16[512,1024]{1,0:T(8,128)(2,1)S(1)} %shard_map.77.first.second, bf16[256,1024]{1,0:T(8,128)(2,1)S(1)} %shard_map.78.refs_0_, bf16[256,1024]{1,0:T(8,128)(2,1)S(1)} %shard_map.79.refs_1_), custom_call_target="tpu_custom_call" | custom-call | flops 2684354560 | bytes 1048576 | tf_op jit(solution)/shard_map/pallas_call | solution.py:165
  62.4 1.8 %shard_map.81.refs_6_ = f32[512,1024]{1,0:T(8,128)S(1)} custom-call(s32[4]{0:T(128)S(1)} %pad_add_fusion.place, bf16[512,1024]{1,0:T(8,128)(2,1)S(1)} %shard_map.77.first.second, bf16[512,1024]{1,0:T(8,128)(2,1)S(1)} %shard_map.77.first.second, bf16[256,1024]{1,0:T(8,128)(2,1)S(1)} %collective-permute-done.2.refs_0_.refs_2_, ...), custom_call_target="tpu_custom_call" | custom-call | flops 5368709120 | bytes 1048576 | tf_op jit(solution)/shard_map/pallas_call | solution.py:165
  64.2 2.1 %shard_map.82.refs_2_ = f32[512,1024]{1,0:T(8,128)S(1)} custom-call(s32[4]{0:T(128)S(1)} %pad_add_fusion.place, bf16[512,1024]{1,0:T(8,128)(2,1)S(1)} %collective-permute-done.first.second, bf16[512,1024]{1,0:T(8,128)(2,1)S(1)} %collective-permute-done.first.second, bf16[256,1024]{1,0:T(8,128)(2,1)S(1)} %shard_map.78.refs_0_, ...), custom_call_target="tpu_custom_call" | custom-call | flops 8053063680 | bytes 1048576 | tf_op jit(solution)/shard_map/pallas_call | solution.py:165
  66.3 1.0 collective-permute-done.7.refs_1_
  67.3 2.8 %collective-permute-done.3.refs_0_ = bf16[256,1024]{1,0:T(8,128)(2,1)S(1)} collective-permute-done((bf16[256,1024]{1,0:T(8,128)(2,1)S(1)}, bf16[256,1024]{1,0:T(8,128)(2,1)S(1)}, u32[]{:S(2)}, u32[]{:S(2)}) %collective-permute-start.3) | collective-permute-done | bytes 524320 | tf_op jit(solution)/shard_map/ppermute | solution.py:59
  70.1 1.5 %shard_map.84 = f32[256,1024]{1,0:T(8,128)S(1)} custom-call(s32[4]{0:T(128)S(1)} %pad_add_fusion.place, bf16[512,1024]{1,0:T(8,128)(2,1)S(1)} %shard_map.77.first.second, bf16[512,1024]{1,0:T(8,128)(2,1)S(1)} %collective-permute-done.first.second, bf16[256,1024]{1,0:T(8,128)(2,1)S(1)} %collective-permute-done.3.refs_0_, ...), custom_call_target="tpu_custom_call" | custom-call | flops 2684354560 | bytes 1048576 | tf_op jit(solution)/shard_map/pallas_call | solution.py:165
  71.6 1.9 %collective-permute-start.10 = (f32[256,1024]{1,0:T(8,128)S(1)}, f32[256,1024]{1,0:T(8,128)S(1)}, u32[]{:S(2)}, u32[]{:S(2)}) collective-permute-start(f32[256,1024]{1,0:T(8,128)S(1)} %shard_map.84), channel_id=1, source_target_pairs={{0,16},{16,0},{1,17},{17,1},{2,18},{18,2},{3,19},{19,3},{4,20},{20... | collective-permute-start | bytes 3145736 | tf_op jit(solution)/shard_map/ppermute | solution.py:303
  73.5 1.5 %shard_map.83.mine = f32[256,1024]{1,0:T(8,128)S(1)} custom-call(s32[4]{0:T(128)S(1)} %pad_add_fusion.place, bf16[512,1024]{1,0:T(8,128)(2,1)S(1)} %shard_map.77.first.second, bf16[512,1024]{1,0:T(8,128)(2,1)S(1)} %collective-permute-done.first.second, bf16[256,1024]{1,0:T(8,128)(2,1)S(1)} %collective-permute-done.3.refs_0_, ...), custom_call_target="tpu_custom_call" | custom-call | flops 2684354560 | bytes 1048576 | tf_op jit(solution)/shard_map/pallas_call | solution.py:165
  75.1 1.1 collective-permute-done.10.theirs
  76.1 0.1 shard_map.85
  76.3 11.8 %all_to_all.20.received = f32[32,8,128]{2,1,0:T(8,128)S(1)} all-to-all(f32[32,8,128]{2,1,0:T(8,128)S(1)} %get-tuple-element.11), channel_id=1, replica_groups=mesh['y'=4,'x'=4,'core'=2,'z'=16] {'y','x','core'}, dimensions={0} | all-to-all | bytes 262144 | tf_op jit(solution)/shard_map/all_to_all | solution.py:69
  88.1 1.0 shard_map.86
  89.0 21.2 %all_to_all.21.received = f32[16,8,128]{2,1,0:T(8,128)S(1)} all-to-all(f32[16,8,128]{2,1,0:T(8,128)S(1)} %get-tuple-element.13), channel_id=1, replica_groups=mesh['y'=4,'x'=4,'core'=2,'z'=16] {'z'}, dimensions={0} | all-to-all | bytes 131072 | tf_op jit(solution)/shard_map/all_to_all | solution.py:69
  110.2 0.6 shard_map.87
  110.8 12.5 %all_to_all.22.received = f32[32,4,128]{2,1,0:T(4,128)S(1)} all-to-all(f32[32,4,128]{2,1,0:T(4,128)S(1)} %get-tuple-element.14), channel_id=1, replica_groups=mesh['y'=4,'x'=4,'core'=2,'z'=16] {'y','x','core'}, dimensions={0} | all-to-all | bytes 131072 | tf_op jit(solution)/shard_map/all_to_all | solution.py:69
  123.3 1.4 %shard_map.88 = f32[256,1024]{1,0:T(8,128)} custom-call(f32[32,4,128]{2,1,0:T(4,128)S(1)} %all_to_all.22.received, f32[2,128]{1,0:T(2,128)S(1)} %get-tuple-element.15.row_root, f32[8,128]{1,0:T(8,128)S(1)} %get-tuple-element.16.col_root, f32[256,1024]{1,0:T(8,128)S(1)} %get-tuple-element.12.grad, f32[256,1024]{1,0:T(8,128)S(1)} %copy-done), custom_call_target="tpu_custom_call" | custom-call | flops 1048576 | bytes 3145728 | tf_op jit(solution)/shard_map/pallas_call | solution.py:275
  (17 shorter events, 0.2 us)
Async XLA Ops:
  0.7 10.5 %copy-start.1 = (bf16[128,1024]{1,0:T(8,128)(2,1)S(1)}, bf16[128,1024]{1,0:T(8,128)(2,1)}, u32[]{:S(2)}) copy-start(bf16[128,1024]{1,0:T(8,128)(2,1)} %refs_0_.1) | copy-start | bytes 786436
  3.6 34.1 %all-to-all-start = ((bf16[16,64,512]{2,1,0:T(8,128)(2,1)}), bf16[16,64,512]{2,1,0:T(8,128)(2,1)S(1)}, u32[]{:S(2)}, u32[]{:S(2)}) async-start(bf16[16,64,512]{2,1,0:T(8,128)(2,1)} %shard_map.76), calls=%async_computation | async-start | bytes 2097152 | tf_op jit(solution)/shard_map/all_to_all | solution.py:69
  11.2 18.7 %collective-permute-start.4 = (bf16[128,1024]{1,0:T(8,128)(2,1)S(1)}, bf16[128,1024]{1,0:T(8,128)(2,1)S(1)}, u32[]{:S(2)}, u32[]{:S(2)}) collective-permute-start(bf16[128,1024]{1,0:T(8,128)(2,1)S(1)} %copy-done.1), channel_id=1, source_target_pairs={{0,64},{16,272},{32,96},{48,304},{64,0},{80,336},{96,32},{112,368}... | collective-permute-start | bytes 786440 | tf_op jit(solution)/shard_map/ppermute | solution.py:59
  16.0 16.0 %collective-permute-start.5 = (bf16[128,1024]{1,0:T(8,128)(2,1)S(1)}, bf16[128,1024]{1,0:T(8,128)(2,1)S(1)}, u32[]{:S(2)}, u32[]{:S(2)}) collective-permute-start(bf16[128,1024]{1,0:T(8,128)(2,1)S(1)} %copy-done.1), channel_id=1, source_target_pairs={{0,96},{16,400},{32,0},{48,432},{64,32},{80,464},{96,64},{112,496}... | collective-permute-start | bytes 786440 | tf_op jit(solution)/shard_map/ppermute | solution.py:59
  18.8 16.9 %collective-permute-start.1 = (bf16[128,1024]{1,0:T(8,128)(2,1)S(1)}, bf16[128,1024]{1,0:T(8,128)(2,1)S(1)}, u32[]{:S(2)}, u32[]{:S(2)}) collective-permute-start(bf16[128,1024]{1,0:T(8,128)(2,1)S(1)} %copy-done.1), channel_id=1, source_target_pairs={{0,32},{16,144},{32,64},{48,176},{64,96},{80,208},{96,0},{112,240}... | collective-permute-start | bytes 786440 | tf_op jit(solution)/shard_map/ppermute | solution.py:59
  32.1 23.5 %collective-permute-start.6 = (bf16[256,1024]{1,0:T(8,128)(2,1)S(1)}, bf16[256,1024]{1,0:T(8,128)(2,1)S(1)}, u32[]{:S(2)}, u32[]{:S(2)}) collective-permute-start(bf16[256,1024]{1,0:T(8,128)(2,1)S(1)} %shard_map.79.refs_1_), channel_id=1, source_target_pairs={{0,384},{16,112},{32,416},{48,16},{64,448},{80,48},{96,480},{112,8... | collective-permute-start | bytes 1572872 | tf_op jit(solution)/shard_map/ppermute | solution.py:59
  35.8 23.1 %collective-permute-start.2 = (bf16[256,1024]{1,0:T(8,128)(2,1)S(1)}, bf16[256,1024]{1,0:T(8,128)(2,1)S(1)}, u32[]{:S(2)}, u32[]{:S(2)}) collective-permute-start(bf16[256,1024]{1,0:T(8,128)(2,1)S(1)} %shard_map.78.refs_0_), channel_id=1, source_target_pairs={{0,128},{16,48},{32,160},{48,80},{64,192},{80,112},{96,224},{112,1... | collective-permute-start | bytes 1572872 | tf_op jit(solution)/shard_map/ppermute | solution.py:59
  38.7 25.5 %collective-permute-start = (bf16[512,1024]{1,0:T(8,128)(2,1)S(1)}, bf16[512,1024]{1,0:T(8,128)(2,1)S(1)}, u32[]{:S(2)}, u32[]{:S(2)}) collective-permute-start(bf16[512,1024]{1,0:T(8,128)(2,1)S(1)} %shard_map.77.first.second), channel_id=1, source_target_pairs={{0,1},{1,2},{2,3},{3,4},{4,5},{5,6},{6,7},{7,8},{8,9},{9,10},{10,1... | collective-permute-start | bytes 3145736 | tf_op jit(solution)/shard_map/ppermute | solution.py:65
  49.0 13.3 %collective-permute-start.8 = (bf16[256,1024]{1,0:T(8,128)(2,1)S(1)}, bf16[256,1024]{1,0:T(8,128)(2,1)S(1)}, u32[]{:S(2)}, u32[]{:S(2)}) collective-permute-start(bf16[256,1024]{1,0:T(8,128)(2,1)S(1)} %shard_map.79.refs_1_), channel_id=1, source_target_pairs={{0,128},{16,48},{32,160},{48,80},{64,192},{80,112},{96,224},{112,1... | collective-permute-start | bytes 1572872 | tf_op jit(solution)/shard_map/ppermute | solution.py:59
  51.5 10.9 %collective-permute-start.9 = (bf16[256,1024]{1,0:T(8,128)(2,1)S(1)}, bf16[256,1024]{1,0:T(8,128)(2,1)S(1)}, u32[]{:S(2)}, u32[]{:S(2)}) collective-permute-start(bf16[256,1024]{1,0:T(8,128)(2,1)S(1)} %shard_map.78.refs_0_), channel_id=1, source_target_pairs={{0,384},{16,112},{32,416},{48,16},{64,448},{80,48},{96,480},{112,8... | collective-permute-start | bytes 1572872 | tf_op jit(solution)/shard_map/ppermute | solution.py:59
  55.6 11.7 %collective-permute-start.7 = (bf16[256,1024]{1,0:T(8,128)(2,1)S(1)}, bf16[256,1024]{1,0:T(8,128)(2,1)S(1)}, u32[]{:S(2)}, u32[]{:S(2)}) collective-permute-start(bf16[256,1024]{1,0:T(8,128)(2,1)S(1)} %collective-permute-done.6.refs_3_.refs_5_), channel_id=1, source_target_pairs={{0,384},{16,112},{32,416},{48,16},{64,448},{80,48},{96,480},{112,8... | collective-permute-start | bytes 1572872 | tf_op jit(solution)/shard_map/ppermute | solution.py:59
  58.9 11.1 %collective-permute-start.3 = (bf16[256,1024]{1,0:T(8,128)(2,1)S(1)}, bf16[256,1024]{1,0:T(8,128)(2,1)S(1)}, u32[]{:S(2)}, u32[]{:S(2)}) collective-permute-start(bf16[256,1024]{1,0:T(8,128)(2,1)S(1)} %collective-permute-done.2.refs_0_.refs_2_), channel_id=1, source_target_pairs={{0,128},{16,48},{32,160},{48,80},{64,192},{80,112},{96,224},{112,1... | collective-permute-start | bytes 1572872 | tf_op jit(solution)/shard_map/ppermute | solution.py:59
  71.6 4.6 %collective-permute-start.10 = (f32[256,1024]{1,0:T(8,128)S(1)}, f32[256,1024]{1,0:T(8,128)S(1)}, u32[]{:S(2)}, u32[]{:S(2)}) collective-permute-start(f32[256,1024]{1,0:T(8,128)S(1)} %shard_map.84), channel_id=1, source_target_pairs={{0,16},{16,0},{1,17},{17,1},{2,18},{18,2},{3,19},{19,3},{4,20},{20... | collective-permute-start | bytes 3145736 | tf_op jit(solution)/shard_map/ppermute | solution.py:303
  75.0 13.0 %copy-start = (f32[256,1024]{1,0:T(8,128)S(1)}, f32[256,1024]{1,0:T(8,128)}, u32[]{:S(2)}) copy-start(f32[256,1024]{1,0:T(8,128)} %weight.3) | copy-start | bytes 3145732
  75.0 13.0 %copy-start.2 = (f32[1024]{0:T(1024)S(1)}, f32[1024]{0:T(1024)}, u32[]{:S(2)}) copy-start(f32[1024]{0:T(1024)} %param.9) | copy-start | bytes 12292
  75.0 35.1 %copy-start.3 = (f32[256]{0:T(256)S(1)}, f32[256]{0:T(256)}, u32[]{:S(2)}) copy-start(f32[256]{0:T(256)} %param.8) | copy-start | bytes 3076

commit v13 on v12

--- a/solution.py
+++ b/solution.py
@@ -48,15 +48,20 @@
     return ((y % SIDE) * SIDE + x % SIDE) * 2 + core
 
 
-def along(value, step, stage):
+def along(value, step):
     pairs = []
     for y in range(SIDE):
         for x in range(SIDE):
-            for core in range(2):
-                on_x = core == stage
-                to = device(y, x + step, core) if on_x else device(y + step, x, core)
-                pairs.append((device(y, x, core), to))
+            pairs.append((device(y, x, 0), device(y + step, x, 0)))
+            pairs.append((device(y, x, 1), device(y, x + step, 1)))
     return lax.ppermute(value, ROWS, pairs)
+
+
+def gather_line(value):
+    groups = [[device(y, x, 0) for x in range(SIDE)] for y in range(SIDE)]
+    groups += [[device(y, x, 1) for y in range(SIDE)] for x in range(SIDE)]
+    sent = jnp.broadcast_to(value, (SIDE,) + value.shape)
+    return lax.all_to_all(sent, ROWS, 0, 0, axis_index_groups=groups)
 
 
 def next_layer(value):
@@ -93,36 +98,12 @@
     )(place, pltpu.with_memory_space_constraint(activations, pltpu.HBM))
 
 
-def join_kernel(*refs):
-    blocks, out, sems = refs[:-2], refs[-2], refs[-1]
-    copies = [
-        pltpu.make_async_copy(block, out.at[pl.ds(i * TOKENS, TOKENS)], sems.at[i]) for i, block in enumerate(blocks)
-    ]
-    for copy in copies:
-        copy.start()
-    for copy in copies:
-        copy.wait()
-
-
-def join(blocks):
-    return pl.pallas_call(
-        join_kernel,
-        out_shape=shape(len(blocks) * TOKENS, WIDTH, dtype=jnp.bfloat16),
-        in_specs=[ANYWHERE] * len(blocks),
-        out_specs=ANYWHERE,
-        scratch_shapes=[pltpu.SemaphoreType.DMA((len(blocks),))],
-        compiler_params=PARAMS,
-        cost_estimate=cost(0, 2**21),
-    )(*blocks)
-
-
 def turn_kernel(place, part, out):
     y, x, core = place[0], place[1], place[2]
 
     def block(i):
         j, k = i // SIDE, i % SIDE
-        dx, dy = jnp.where(core == 0, k, j), jnp.where(core == 0, j, k)
-        return part[((y - dy) & (SIDE - 1)) * SIDE + ((x - dx) & (SIDE - 1))]
+        return part[jnp.where(core == 0, ((y - j) & (SIDE - 1)) * SIDE + k, k * SIDE + ((x - j) & (SIDE - 1)))]
 
     for i in range(0, COUNT, 2):
         out[:, i * HALF : (i + 2) * HALF] = jnp.concatenate([block(i), block(i + 1)], axis=0).T
@@ -286,13 +267,14 @@
 def shards(activations, out_grads, weight, row_moment, col_moment):
     y, x, core, layer = (lax.axis_index(name) for name in ("y", "x", "core", "z"))
     place = jnp.stack([y, x, core, layer & 1])
-    first = turn(place, exchange(pack(place, activations), CHIPS))
+    line = gather_line(out_grads)
+    packed, line = lax.optimization_barrier((pack(place, activations), line))
+    first = turn(place, exchange(packed, CHIPS))
     second = next_layer(first)
-    line = [out_grads] + [along(out_grads, k, 0) for k in range(1, SIDE)]
-    low, high = join(line[:2]), join(line[2:])
-    back_low, ahead_high = along(low, 1, 1), along(high, SIDE - 1, 1)
-    far = [along(back_low, 1, 1), along(ahead_high, SIDE - 1, 1)]
-    back, ahead = [back_low, along(high, 1, 1)], [along(low, SIDE - 1, 1), ahead_high]
+    low, high = (line[i : i + 2].reshape(2 * TOKENS, WIDTH) for i in (0, 2))
+    back_low, ahead_high = along(low, 1), along(high, SIDE - 1)
+    far = [along(back_low, 1), along(ahead_high, SIDE - 1)]
+    back, ahead = [back_low, along(high, 1)], [along(low, SIDE - 1), ahead_high]
     blocks = lambda operand: [(operand, 0), (operand, 1), (operand + 1, 0), (operand + 1, 1)]
     total = product(place, (first, first), [low, high], [(0, True, blocks(0))])
     total = product(place, (first, first), back + ahead, [(1, True, blocks(0)), (3, True, blocks(2))], total)

time: 125 us -> 129 us (1.032)
  blocking collectives: 45.5 us -> 49.2 us
  local copies, waits for them, and re-layouts: 0.02 us -> 2.15 us
  waiting for transfers between devices: 15.6 us -> 14.3 us
    ppermute x9 -> x6, waiting for transfers between devices: 14.5 us -> 0.72 us  [along(): return lax.ppermute(value, ROWS, pairs)]
    ppermute x9 -> x6, starting transfers between devices: 27.4 us -> 19.5 us  [along(): return lax.ppermute(value, ROWS, pairs)]
    all_to_all x0 -> x1, waiting for transfers between devices: none -> 6.76 us  [gather_line(): return lax.all_to_all(sent, ROWS, 0, 0, axis_index_groups=groups)]
    all_to_all x1, waiting for transfers between devices: 0.01 us -> 6.06 us  [exchange(): return lax.all_to_all(tiles, axes, 0, 0)]
    all_to_all x0 -> x1, starting transfers between devices: none -> 5.01 us  [gather_line(): return lax.all_to_all(sent, ROWS, 0, 0, axis_index_groups=groups)]
    all_to_all x3, blocking collectives: 45.5 us -> 49.2 us  [exchange(): return lax.all_to_all(tiles, axes, 0, 0)]
    ppermute x1, starting transfers between devices: 10.4 us -> 13.3 us  [next_layer(): return lax.ppermute(value, ('core', 'z'), pairs)]
    all_to_all x1, starting transfers between devices: 7.6 us -> 4.76 us  [exchange(): return lax.all_to_all(tiles, axes, 0, 0)]
  transfers between devices with their start and end apart: 12 -> 10, of which waited for: 5 -> 4; matrix products, arithmetic and copies ran while one was open for 0% -> 0% of each run, Pallas kernels for 6% -> 8%
where the time goes in v13:
time: 129 us; the launch traced here: 128 us
  blocking collectives  49.2 us (38%)
  starting transfers between devices  46.6 us (36%)
  Pallas kernels  15.2 us (12%)
  waiting for transfers between devices  14.3 us (11%)
  local copies, waits for them, and re-layouts  2.15 us (2%)
    all_to_all x3, blocking collectives, exchange(): return lax.all_to_all(tiles, axes, 0, 0)  49.2 us
    ppermute x6, starting transfers between devices, along(): return lax.ppermute(value, ROWS, pairs)  19.5 us
    ppermute x1, starting transfers between devices, next_layer(): return lax.ppermute(value, ('core', 'z'), pairs)  13.3 us
    pallas_call x5, Pallas kernels, product(): pl.pallas_call(functools.partial(product_kernel, parts, which), out_shape...  8.34 us
    all_to_all x1, waiting for transfers between devices, gather_line(): return lax.all_to_all(sent, ROWS, 0, 0, axis_index_groups=groups)  6.76 us
    all_to_all x1, waiting for transfers between devices, exchange(): return lax.all_to_all(tiles, axes, 0, 0)  6.06 us
    all_to_all x1, starting transfers between devices, gather_line(): return lax.all_to_all(sent, ROWS, 0, 0, axis_index_groups=groups)  5.01 us
    all_to_all x1, starting transfers between devices, exchange(): return lax.all_to_all(tiles, axes, 0, 0)  4.76 us
  transfers between devices with their start and end apart: 10, of which 4 were waited for; matrix products, arithmetic and copies ran while one was open for 0% of the time, Pallas kernels for 8%

profile of v13, /device:TPU:1, one launch (start us, length us, event | category | flops | bytes accessed | tf_op | source)
XLA Modules:
  0.0 128.4 jit_solution(3710341881249830550)
XLA Ops:
  0.6 2.1 %broadcast_in_dim.3 = bf16[4,128,1024]{2,1,0:T(8,128)(2,1)} broadcast(bf16[128,1024]{1,0:T(8,128)(2,1)} %param.6), dimensions={1,2} | broadcast | bytes 1310720 | tf_op jit(solution)/shard_map/broadcast_in_dim | solution.py:63
  2.7 5.0 %all-to-all-start = ((bf16[4,128,1024]{2,1,0:T(8,128)(2,1)}), bf16[4,128,1024]{2,1,0:T(8,128)(2,1)S(1)}, u32[]{:S(2)}, u32[]{:S(2)}) async-start(bf16[4,128,1024]{2,1,0:T(8,128)(2,1)} %broadcast_in_dim.3), calls=%async_computation | async-start | bytes 2097152 | tf_op jit(solution)/shard_map/all_to_all | solution.py:64
  7.7 0.1 pad_add_fusion.place
  7.8 2.9 %shard_map.76 = bf16[16,64,512]{2,1,0:T(8,128)(2,1)} custom-call(s32[4]{0:T(128)S(1)} %pad_add_fusion.place, bf16[128,8192]{1,0:T(8,128)(2,1)} %source.1), custom_call_target="tpu_custom_call" | custom-call | bytes 2097152 | tf_op jit(solution)/shard_map/pallas_call | solution.py:90
  10.7 6.8 %all-to-all-done = bf16[4,128,1024]{2,1,0:T(8,128)(2,1)S(1)} async-done(((bf16[4,128,1024]{2,1,0:T(8,128)(2,1)}), bf16[4,128,1024]{2,1,0:T(8,128)(2,1)S(1)}, u32[]{:S(2)}, u32[]{:S(2)}) %all-to-all-start) | async-done | bytes 1048608 | tf_op jit(solution)/shard_map/all_to_all | solution.py:64
  17.4 4.8 %all-to-all-start.1 = ((bf16[16,64,512]{2,1,0:T(8,128)(2,1)}), bf16[16,64,512]{2,1,0:T(8,128)(2,1)S(1)}, u32[]{:S(2)}, u32[]{:S(2)}) async-start(bf16[16,64,512]{2,1,0:T(8,128)(2,1)} %shard_map.76), calls=%async_computation.1 | async-start | bytes 2097152 | tf_op jit(solution)/shard_map/all_to_all | solution.py:74
  22.2 0.1 fusion
  22.3 3.3 %collective-permute-start.1 = (bf16[256,1024]{1,0:T(8,128)(2,1)S(1)}, bf16[256,1024]{1,0:T(8,128)(2,1)S(1)}, u32[]{:S(2)}, u32[]{:S(2)}) collective-permute-start(bf16[256,1024]{1,0:T(8,128)(2,1)S(1)} %bitcast.14), channel_id=1, source_target_pairs={{0,128},{16,48},{32,160},{48,80},{64,192},{80,112},{96,224},{112,1... | collective-permute-start | bytes 1572872 | tf_op jit(solution)/shard_map/ppermute | solution.py:57
  25.6 3.2 %collective-permute-start.3 = (bf16[256,1024]{1,0:T(8,128)(2,1)S(1)}, bf16[256,1024]{1,0:T(8,128)(2,1)S(1)}, u32[]{:S(2)}, u32[]{:S(2)}) collective-permute-start(bf16[256,1024]{1,0:T(8,128)(2,1)S(1)} %bitcast.10), channel_id=1, source_target_pairs={{0,384},{16,112},{32,416},{48,16},{64,448},{80,48},{96,480},{112,8... | collective-permute-start | bytes 1572872 | tf_op jit(solution)/shard_map/ppermute | solution.py:57
  28.8 6.1 %all-to-all-done.1.part = bf16[16,64,512]{2,1,0:T(8,128)(2,1)S(1)} async-done(((bf16[16,64,512]{2,1,0:T(8,128)(2,1)}), bf16[16,64,512]{2,1,0:T(8,128)(2,1)S(1)}, u32[]{:S(2)}, u32[]{:S(2)}) %all-to-all-start.1) | async-done | bytes 1048608 | tf_op jit(solution)/shard_map/all_to_all | solution.py:74
  34.9 0.9 shard_map.77.first.second
  35.8 13.3 %collective-permute-start = (bf16[512,1024]{1,0:T(8,128)(2,1)S(1)}, bf16[512,1024]{1,0:T(8,128)(2,1)S(1)}, u32[]{:S(2)}, u32[]{:S(2)}) collective-permute-start(bf16[512,1024]{1,0:T(8,128)(2,1)S(1)} %shard_map.77.first.second), channel_id=1, source_target_pairs={{0,1},{1,2},{2,3},{3,4},{4,5},{5,6},{6,7},{7,8},{8,9},{9,10},{10,1... | collective-permute-start | bytes 3145736 | tf_op jit(solution)/shard_map/ppermute | solution.py:70
  49.1 2.2 %collective-permute-start.5 = (bf16[256,1024]{1,0:T(8,128)(2,1)S(1)}, bf16[256,1024]{1,0:T(8,128)(2,1)S(1)}, u32[]{:S(2)}, u32[]{:S(2)}) collective-permute-start(bf16[256,1024]{1,0:T(8,128)(2,1)S(1)} %bitcast.11), channel_id=1, source_target_pairs={{0,128},{16,48},{32,160},{48,80},{64,192},{80,112},{96,224},{112,1... | collective-permute-start | bytes 1572872 | tf_op jit(solution)/shard_map/ppermute | solution.py:57
  51.3 4.3 %collective-permute-start.6 = (bf16[256,1024]{1,0:T(8,128)(2,1)S(1)}, bf16[256,1024]{1,0:T(8,128)(2,1)S(1)}, u32[]{:S(2)}, u32[]{:S(2)}) collective-permute-start(bf16[256,1024]{1,0:T(8,128)(2,1)S(1)} %bitcast.15), channel_id=1, source_target_pairs={{0,384},{16,112},{32,416},{48,16},{64,448},{80,48},{96,480},{112,8... | collective-permute-start | bytes 1572872 | tf_op jit(solution)/shard_map/ppermute | solution.py:57
  55.6 1.9 %collective-permute-start.2 = (bf16[256,1024]{1,0:T(8,128)(2,1)S(1)}, bf16[256,1024]{1,0:T(8,128)(2,1)S(1)}, u32[]{:S(2)}, u32[]{:S(2)}) collective-permute-start(bf16[256,1024]{1,0:T(8,128)(2,1)S(1)} %collective-permute-done.1.refs_0_.refs_2_), channel_id=1, source_target_pairs={{0,128},{16,48},{32,160},{48,80},{64,192},{80,112},{96,224},{112,1... | collective-permute-start | bytes 1572872 | tf_op jit(solution)/shard_map/ppermute | solution.py:57
  57.6 4.6 %collective-permute-start.4 = (bf16[256,1024]{1,0:T(8,128)(2,1)S(1)}, bf16[256,1024]{1,0:T(8,128)(2,1)S(1)}, u32[]{:S(2)}, u32[]{:S(2)}) collective-permute-start(bf16[256,1024]{1,0:T(8,128)(2,1)S(1)} %collective-permute-done.3.refs_3_.refs_5_), channel_id=1, source_target_pairs={{0,384},{16,112},{32,416},{48,16},{64,448},{80,48},{96,480},{112,8... | collective-permute-start | bytes 1572872 | tf_op jit(solution)/shard_map/ppermute | solution.py:57
  62.1 1.5 %shard_map.78.refs_4_ = f32[512,1024]{1,0:T(8,128)S(1)} custom-call(s32[4]{0:T(128)S(1)} %pad_add_fusion.place, bf16[512,1024]{1,0:T(8,128)(2,1)S(1)} %shard_map.77.first.second, bf16[512,1024]{1,0:T(8,128)(2,1)S(1)} %shard_map.77.first.second, bf16[256,1024]{1,0:T(8,128)(2,1)S(1)} %bitcast.16, bf16[256,1024]{1,0:T(8,128)(2,1)S(1)} %bitcast.12), custom_call_target="tpu_custom_call" | custom-call | flops 2684354560 | bytes 1048576 | tf_op jit(solution)/shard_map/pallas_call | solution.py:146
  63.7 1.8 %shard_map.79.refs_6_ = f32[512,1024]{1,0:T(8,128)S(1)} custom-call(s32[4]{0:T(128)S(1)} %pad_add_fusion.place, bf16[512,1024]{1,0:T(8,128)(2,1)S(1)} %shard_map.77.first.second, bf16[512,1024]{1,0:T(8,128)(2,1)S(1)} %shard_map.77.first.second, bf16[256,1024]{1,0:T(8,128)(2,1)S(1)} %collective-permute-done.1.refs_0_.refs_2_, ...), custom_call_target="tpu_custom_call" | custom-call | flops 5368709120 | bytes 1048576 | tf_op jit(solution)/shard_map/pallas_call | solution.py:146
  65.5 2.1 %shard_map.80.refs_2_ = f32[512,1024]{1,0:T(8,128)S(1)} custom-call(s32[4]{0:T(128)S(1)} %pad_add_fusion.place, bf16[512,1024]{1,0:T(8,128)(2,1)S(1)} %collective-permute-done.first.second, bf16[512,1024]{1,0:T(8,128)(2,1)S(1)} %collective-permute-done.first.second, bf16[256,1024]{1,0:T(8,128)(2,1)S(1)} %bitcast.17, bf16[256,1024]{1,0:T(8,128)(2,1)S(1)} %bitcast.13, ...), custom_call_target="tpu_custom_call" | custom-call | flops 8053063680 | bytes 1048576 | tf_op jit(solution)/shard_map/pallas_call | solution.py:146
  67.5 0.7 collective-permute-done.4.refs_1_
  68.3 1.5 %shard_map.82 = f32[256,1024]{1,0:T(8,128)S(1)} custom-call(s32[4]{0:T(128)S(1)} %pad_add_fusion.place, bf16[512,1024]{1,0:T(8,128)(2,1)S(1)} %shard_map.77.first.second, bf16[512,1024]{1,0:T(8,128)(2,1)S(1)} %collective-permute-done.first.second, bf16[256,1024]{1,0:T(8,128)(2,1)S(1)} %collective-permute-done.2.refs_0_, ...), custom_call_target="tpu_custom_call" | custom-call | flops 2684354560 | bytes 1048576 | tf_op jit(solution)/shard_map/pallas_call | solution.py:146
  69.8 4.0 %collective-permute-start.7 = (f32[256,1024]{1,0:T(8,128)S(1)}, f32[256,1024]{1,0:T(8,128)S(1)}, u32[]{:S(2)}, u32[]{:S(2)}) collective-permute-start(f32[256,1024]{1,0:T(8,128)S(1)} %shard_map.82), channel_id=1, source_target_pairs={{0,16},{16,0},{1,17},{17,1},{2,18},{18,2},{3,19},{19,3},{4,20},{20... | collective-permute-start | bytes 3145736 | tf_op jit(solution)/shard_map/ppermute | solution.py:285
  73.8 1.5 %shard_map.81.mine = f32[256,1024]{1,0:T(8,128)S(1)} custom-call(s32[4]{0:T(128)S(1)} %pad_add_fusion.place, bf16[512,1024]{1,0:T(8,128)(2,1)S(1)} %shard_map.77.first.second, bf16[512,1024]{1,0:T(8,128)(2,1)S(1)} %collective-permute-done.first.second, bf16[256,1024]{1,0:T(8,128)(2,1)S(1)} %collective-permute-done.2.refs_0_, ...), custom_call_target="tpu_custom_call" | custom-call | flops 2684354560 | bytes 1048576 | tf_op jit(solution)/shard_map/pallas_call | solution.py:146
  75.3 0.0 copy-start.2
  75.3 0.7 collective-permute-done.7.theirs
  76.0 0.1 shard_map.83
  76.2 12.4 %all_to_all.25.received = f32[32,8,128]{2,1,0:T(8,128)S(1)} all-to-all(f32[32,8,128]{2,1,0:T(8,128)S(1)} %get-tuple-element.15), channel_id=1, replica_groups=mesh['y'=4,'x'=4,'core'=2,'z'=16] {'y','x','core'}, dimensions={0} | all-to-all | bytes 262144 | tf_op jit(solution)/shard_map/all_to_all | solution.py:74
  88.6 1.0 shard_map.84
  89.6 24.3 %all_to_all.26.received = f32[16,8,128]{2,1,0:T(8,128)S(1)} all-to-all(f32[16,8,128]{2,1,0:T(8,128)S(1)} %get-tuple-element.17), channel_id=1, replica_groups=mesh['y'=4,'x'=4,'core'=2,'z'=16] {'z'}, dimensions={0} | all-to-all | bytes 131072 | tf_op jit(solution)/shard_map/all_to_all | solution.py:74
  113.8 0.6 shard_map.85
  114.4 12.5 %all_to_all.27.received = f32[32,4,128]{2,1,0:T(4,128)S(1)} all-to-all(f32[32,4,128]{2,1,0:T(4,128)S(1)} %get-tuple-element.18), channel_id=1, replica_groups=mesh['y'=4,'x'=4,'core'=2,'z'=16] {'y','x','core'}, dimensions={0} | all-to-all | bytes 131072 | tf_op jit(solution)/shard_map/all_to_all | solution.py:74
  127.0 1.4 %shard_map.86 = f32[256,1024]{1,0:T(8,128)} custom-call(f32[32,4,128]{2,1,0:T(4,128)S(1)} %all_to_all.27.received, f32[2,128]{1,0:T(2,128)S(1)} %get-tuple-element.19.row_root, f32[8,128]{1,0:T(8,128)S(1)} %get-tuple-element.20.col_root, f32[256,1024]{1,0:T(8,128)S(1)} %get-tuple-element.16.grad, f32[256,1024]{1,0:T(8,128)S(1)} %copy-done), custom_call_target="tpu_custom_call" | custom-call | flops 1048576 | bytes 3145728 | tf_op jit(solution)/shard_map/pallas_call | solution.py:256
  (11 shorter events, 0.0 us)
Async XLA Ops:
  2.7 14.8 %all-to-all-start = ((bf16[4,128,1024]{2,1,0:T(8,128)(2,1)}), bf16[4,128,1024]{2,1,0:T(8,128)(2,1)S(1)}, u32[]{:S(2)}, u32[]{:S(2)}) async-start(bf16[4,128,1024]{2,1,0:T(8,128)(2,1)} %broadcast_in_dim.3), calls=%async_computation | async-start | bytes 2097152 | tf_op jit(solution)/shard_map/all_to_all | solution.py:64
  17.4 17.4 %all-to-all-start.1 = ((bf16[16,64,512]{2,1,0:T(8,128)(2,1)}), bf16[16,64,512]{2,1,0:T(8,128)(2,1)S(1)}, u32[]{:S(2)}, u32[]{:S(2)}) async-start(bf16[16,64,512]{2,1,0:T(8,128)(2,1)} %shard_map.76), calls=%async_computation.1 | async-start | bytes 2097152 | tf_op jit(solution)/shard_map/all_to_all | solution.py:74
  22.3 33.3 %collective-permute-start.1 = (bf16[256,1024]{1,0:T(8,128)(2,1)S(1)}, bf16[256,1024]{1,0:T(8,128)(2,1)S(1)}, u32[]{:S(2)}, u32[]{:S(2)}) collective-permute-start(bf16[256,1024]{1,0:T(8,128)(2,1)S(1)} %bitcast.14), channel_id=1, source_target_pairs={{0,128},{16,48},{32,160},{48,80},{64,192},{80,112},{96,224},{112,1... | collective-permute-start | bytes 1572872 | tf_op jit(solution)/shard_map/ppermute | solution.py:57
  25.6 32.0 %collective-permute-start.3 = (bf16[256,1024]{1,0:T(8,128)(2,1)S(1)}, bf16[256,1024]{1,0:T(8,128)(2,1)S(1)}, u32[]{:S(2)}, u32[]{:S(2)}) collective-permute-start(bf16[256,1024]{1,0:T(8,128)(2,1)S(1)} %bitcast.10), channel_id=1, source_target_pairs={{0,384},{16,112},{32,416},{48,16},{64,448},{80,48},{96,480},{112,8... | collective-permute-start | bytes 1572872 | tf_op jit(solution)/shard_map/ppermute | solution.py:57
  35.8 29.7 %collective-permute-start = (bf16[512,1024]{1,0:T(8,128)(2,1)S(1)}, bf16[512,1024]{1,0:T(8,128)(2,1)S(1)}, u32[]{:S(2)}, u32[]{:S(2)}) collective-permute-start(bf16[512,1024]{1,0:T(8,128)(2,1)S(1)} %shard_map.77.first.second), channel_id=1, source_target_pairs={{0,1},{1,2},{2,3},{3,4},{4,5},{5,6},{6,7},{7,8},{8,9},{9,10},{10,1... | collective-permute-start | bytes 3145736 | tf_op jit(solution)/shard_map/ppermute | solution.py:70
  49.1 14.5 %collective-permute-start.5 = (bf16[256,1024]{1,0:T(8,128)(2,1)S(1)}, bf16[256,1024]{1,0:T(8,128)(2,1)S(1)}, u32[]{:S(2)}, u32[]{:S(2)}) collective-permute-start(bf16[256,1024]{1,0:T(8,128)(2,1)S(1)} %bitcast.11), channel_id=1, source_target_pairs={{0,128},{16,48},{32,160},{48,80},{64,192},{80,112},{96,224},{112,1... | collective-permute-start | bytes 1572872 | tf_op jit(solution)/shard_map/ppermute | solution.py:57
  51.3 12.4 %collective-permute-start.6 = (bf16[256,1024]{1,0:T(8,128)(2,1)S(1)}, bf16[256,1024]{1,0:T(8,128)(2,1)S(1)}, u32[]{:S(2)}, u32[]{:S(2)}) collective-permute-start(bf16[256,1024]{1,0:T(8,128)(2,1)S(1)} %bitcast.15), channel_id=1, source_target_pairs={{0,384},{16,112},{32,416},{48,16},{64,448},{80,48},{96,480},{112,8... | collective-permute-start | bytes 1572872 | tf_op jit(solution)/shard_map/ppermute | solution.py:57
  55.6 11.9 %collective-permute-start.2 = (bf16[256,1024]{1,0:T(8,128)(2,1)S(1)}, bf16[256,1024]{1,0:T(8,128)(2,1)S(1)}, u32[]{:S(2)}, u32[]{:S(2)}) collective-permute-start(bf16[256,1024]{1,0:T(8,128)(2,1)S(1)} %collective-permute-done.1.refs_0_.refs_2_), channel_id=1, source_target_pairs={{0,128},{16,48},{32,160},{48,80},{64,192},{80,112},{96,224},{112,1... | collective-permute-start | bytes 1572872 | tf_op jit(solution)/shard_map/ppermute | solution.py:57
  57.6 10.7 %collective-permute-start.4 = (bf16[256,1024]{1,0:T(8,128)(2,1)S(1)}, bf16[256,1024]{1,0:T(8,128)(2,1)S(1)}, u32[]{:S(2)}, u32[]{:S(2)}) collective-permute-start(bf16[256,1024]{1,0:T(8,128)(2,1)S(1)} %collective-permute-done.3.refs_3_.refs_5_), channel_id=1, source_target_pairs={{0,384},{16,112},{32,416},{48,16},{64,448},{80,48},{96,480},{112,8... | collective-permute-start | bytes 1572872 | tf_op jit(solution)/shard_map/ppermute | solution.py:57
  69.8 6.3 %collective-permute-start.7 = (f32[256,1024]{1,0:T(8,128)S(1)}, f32[256,1024]{1,0:T(8,128)S(1)}, u32[]{:S(2)}, u32[]{:S(2)}) collective-permute-start(f32[256,1024]{1,0:T(8,128)S(1)} %shard_map.82), channel_id=1, source_target_pairs={{0,16},{16,0},{1,17},{17,1},{2,18},{18,2},{3,19},{19,3},{4,20},{20... | collective-permute-start | bytes 3145736 | tf_op jit(solution)/shard_map/ppermute | solution.py:285
  75.3 13.3 %copy-start = (f32[256,1024]{1,0:T(8,128)S(1)}, f32[256,1024]{1,0:T(8,128)}, u32[]{:S(2)}) copy-start(f32[256,1024]{1,0:T(8,128)} %weight.3) | copy-start | bytes 3145732
  75.3 13.3 %copy-start.1 = (f32[1024]{0:T(1024)S(1)}, f32[1024]{0:T(1024)}, u32[]{:S(2)}) copy-start(f32[1024]{0:T(1024)} %param.9) | copy-start | bytes 12292
  75.3 38.5 %copy-start.2 = (f32[256]{0:T(256)S(1)}, f32[256]{0:T(256)}, u32[]{:S(2)}) copy-start(f32[256]{0:T(256)} %param.8) | copy-start | bytes 3076

commit v14 on v13

--- a/solution.py
+++ b/solution.py
@@ -149,7 +149,7 @@
         in_specs=[SCALARS] + [WHOLE] * len(operands),
         out_specs=WHOLE,
         compiler_params=PARAMS,
-        cost_estimate=cost(20 * count * SIDE * HALF * WIDTH * len(parts), 2**20),
+        cost_estimate=cost(24 * count * SIDE * HALF * WIDTH * len(parts), 2**20),
     )(place, *operands)
 
 

time: 129 us -> 124 us (0.961)
  blocking collectives: 49.2 us -> 43.2 us
  waiting for transfers between devices: 14.3 us -> 8.73 us
  starting transfers between devices: 46.6 us -> 51.4 us
  Pallas kernels: 15.2 us -> 16.6 us
    all_to_all x1, waiting for transfers between devices: 6.06 us -> 0.01 us  [exchange(): return lax.all_to_all(tiles, axes, 0, 0)]
    all_to_all x3, blocking collectives: 49.2 us -> 43.2 us  [exchange(): return lax.all_to_all(tiles, axes, 0, 0)]
    ppermute x1, starting transfers between devices: 4.01 us -> 9.32 us  [shards(): received = lax.ppermute(theirs, 'core', [(0, 1), (1, 0)])]
    pallas_call x5, Pallas kernels: 8.34 us -> 9.67 us  [product(): pl.pallas_call(functools.partial(product_kernel, parts, which), out_shape...]
  transfers between devices with their start and end apart: 10 -> 10, of which waited for: 4 -> 3; matrix products, arithmetic and copies ran while one was open for 0% -> 0% of each run, Pallas kernels for 8% -> 10%
where the time goes in v14:
time: 124 us; the launch traced here: 123 us
  starting transfers between devices  51.4 us (41%)
  blocking collectives  43.2 us (35%)
  Pallas kernels  16.6 us (13%)
  waiting for transfers between devices  8.73 us (7%)
  local copies, waits for them, and re-layouts  2.15 us (2%)
    all_to_all x3, blocking collectives, exchange(): return lax.all_to_all(tiles, axes, 0, 0)  43.2 us
    ppermute x6, starting transfers between devices, along(): return lax.ppermute(value, ROWS, pairs)  19.5 us
    ppermute x1, starting transfers between devices, next_layer(): return lax.ppermute(value, ('core', 'z'), pairs)  12.9 us
    pallas_call x5, Pallas kernels, product(): pl.pallas_call(functools.partial(product_kernel, parts, which), out_shape...  9.67 us
    ppermute x1, starting transfers between devices, shards(): received = lax.ppermute(theirs, 'core', [(0, 1), (1, 0)])  9.32 us
    all_to_all x1, waiting for transfers between devices, gather_line(): return lax.all_to_all(sent, ROWS, 0, 0, axis_index_groups=groups)  6.76 us
    all_to_all x1, starting transfers between devices, gather_line(): return lax.all_to_all(sent, ROWS, 0, 0, axis_index_groups=groups)  5.01 us
    all_to_all x1, starting transfers between devices, exchange(): return lax.all_to_all(tiles, axes, 0, 0)  4.76 us
  transfers between devices with their start and end apart: 10, of which 3 were waited for; matrix products, arithmetic and copies ran while one was open for 0% of the time, Pallas kernels for 10%

profile of v14, /device:TPU:1, one launch (start us, length us, event | category | flops | bytes accessed | tf_op | source)
XLA Modules:
  0.0 123.0 jit_solution(8891503354148353662)
XLA Ops:
  0.6 2.1 %broadcast_in_dim.3 = bf16[4,128,1024]{2,1,0:T(8,128)(2,1)} broadcast(bf16[128,1024]{1,0:T(8,128)(2,1)} %param.6), dimensions={1,2} | broadcast | bytes 1310720 | tf_op jit(solution)/shard_map/broadcast_in_dim | solution.py:63
  2.7 5.0 %all-to-all-start = ((bf16[4,128,1024]{2,1,0:T(8,128)(2,1)}), bf16[4,128,1024]{2,1,0:T(8,128)(2,1)S(1)}, u32[]{:S(2)}, u32[]{:S(2)}) async-start(bf16[4,128,1024]{2,1,0:T(8,128)(2,1)} %broadcast_in_dim.3), calls=%async_computation | async-start | bytes 2097152 | tf_op jit(solution)/shard_map/all_to_all | solution.py:64
  7.7 0.1 pad_add_fusion.place
  7.8 2.9 %shard_map.76 = bf16[16,64,512]{2,1,0:T(8,128)(2,1)} custom-call(s32[4]{0:T(128)S(1)} %pad_add_fusion.place, bf16[128,8192]{1,0:T(8,128)(2,1)} %source.1), custom_call_target="tpu_custom_call" | custom-call | bytes 2097152 | tf_op jit(solution)/shard_map/pallas_call | solution.py:90
  10.7 6.8 %all-to-all-done = bf16[4,128,1024]{2,1,0:T(8,128)(2,1)S(1)} async-done(((bf16[4,128,1024]{2,1,0:T(8,128)(2,1)}), bf16[4,128,1024]{2,1,0:T(8,128)(2,1)S(1)}, u32[]{:S(2)}, u32[]{:S(2)}) %all-to-all-start) | async-done | bytes 1048608 | tf_op jit(solution)/shard_map/all_to_all | solution.py:64
  17.4 4.8 %all-to-all-start.1 = ((bf16[16,64,512]{2,1,0:T(8,128)(2,1)}), bf16[16,64,512]{2,1,0:T(8,128)(2,1)S(1)}, u32[]{:S(2)}, u32[]{:S(2)}) async-start(bf16[16,64,512]{2,1,0:T(8,128)(2,1)} %shard_map.76), calls=%async_computation.1 | async-start | bytes 2097152 | tf_op jit(solution)/shard_map/all_to_all | solution.py:74
  22.2 0.1 fusion
  22.3 3.3 %collective-permute-start.1 = (bf16[256,1024]{1,0:T(8,128)(2,1)S(1)}, bf16[256,1024]{1,0:T(8,128)(2,1)S(1)}, u32[]{:S(2)}, u32[]{:S(2)}) collective-permute-start(bf16[256,1024]{1,0:T(8,128)(2,1)S(1)} %bitcast.14), channel_id=1, source_target_pairs={{0,128},{16,48},{32,160},{48,80},{64,192},{80,112},{96,224},{112,1... | collective-permute-start | bytes 1572872 | tf_op jit(solution)/shard_map/ppermute | solution.py:57
  25.6 3.2 %collective-permute-start.3 = (bf16[256,1024]{1,0:T(8,128)(2,1)S(1)}, bf16[256,1024]{1,0:T(8,128)(2,1)S(1)}, u32[]{:S(2)}, u32[]{:S(2)}) collective-permute-start(bf16[256,1024]{1,0:T(8,128)(2,1)S(1)} %bitcast.10), channel_id=1, source_target_pairs={{0,384},{16,112},{32,416},{48,16},{64,448},{80,48},{96,480},{112,8... | collective-permute-start | bytes 1572872 | tf_op jit(solution)/shard_map/ppermute | solution.py:57
  28.8 2.1 %collective-permute-start.5 = (bf16[256,1024]{1,0:T(8,128)(2,1)S(1)}, bf16[256,1024]{1,0:T(8,128)(2,1)}, u32[]{:S(2)}, u32[]{:S(2)}) collective-permute-start(bf16[256,1024]{1,0:T(8,128)(2,1)S(1)} %bitcast.11), channel_id=1, source_target_pairs={{0,128},{16,48},{32,160},{48,80},{64,192},{80,112},{96,224},{112,1... | collective-permute-start | bytes 1572872 | tf_op jit(solution)/shard_map/ppermute | solution.py:57
  30.9 4.4 %collective-permute-start.6 = (bf16[256,1024]{1,0:T(8,128)(2,1)S(1)}, bf16[256,1024]{1,0:T(8,128)(2,1)}, u32[]{:S(2)}, u32[]{:S(2)}) collective-permute-start(bf16[256,1024]{1,0:T(8,128)(2,1)S(1)} %bitcast.15), channel_id=1, source_target_pairs={{0,384},{16,112},{32,416},{48,16},{64,448},{80,48},{96,480},{112,8... | collective-permute-start | bytes 1572872 | tf_op jit(solution)/shard_map/ppermute | solution.py:57
  35.3 0.9 shard_map.77.first.second
  36.2 12.9 %collective-permute-start = (bf16[512,1024]{1,0:T(8,128)(2,1)S(1)}, bf16[512,1024]{1,0:T(8,128)(2,1)S(1)}, u32[]{:S(2)}, u32[]{:S(2)}) collective-permute-start(bf16[512,1024]{1,0:T(8,128)(2,1)S(1)} %shard_map.77.first.second), channel_id=1, source_target_pairs={{0,1},{1,2},{2,3},{3,4},{4,5},{5,6},{6,7},{7,8},{8,9},{9,10},{10,1... | collective-permute-start | bytes 3145736 | tf_op jit(solution)/shard_map/ppermute | solution.py:70
  49.1 2.2 %collective-permute-start.2 = (bf16[256,1024]{1,0:T(8,128)(2,1)S(1)}, bf16[256,1024]{1,0:T(8,128)(2,1)S(1)}, u32[]{:S(2)}, u32[]{:S(2)}) collective-permute-start(bf16[256,1024]{1,0:T(8,128)(2,1)S(1)} %collective-permute-done.1.refs_0_.refs_2_), channel_id=1, source_target_pairs={{0,128},{16,48},{32,160},{48,80},{64,192},{80,112},{96,224},{112,1... | collective-permute-start | bytes 1572872 | tf_op jit(solution)/shard_map/ppermute | solution.py:57
  51.3 4.3 %collective-permute-start.4 = (bf16[256,1024]{1,0:T(8,128)(2,1)S(1)}, bf16[256,1024]{1,0:T(8,128)(2,1)S(1)}, u32[]{:S(2)}, u32[]{:S(2)}) collective-permute-start(bf16[256,1024]{1,0:T(8,128)(2,1)S(1)} %collective-permute-done.3.refs_3_.refs_5_), channel_id=1, source_target_pairs={{0,384},{16,112},{32,416},{48,16},{64,448},{80,48},{96,480},{112,8... | collective-permute-start | bytes 1572872 | tf_op jit(solution)/shard_map/ppermute | solution.py:57
  55.6 1.5 %shard_map.78.refs_4_ = f32[512,1024]{1,0:T(8,128)S(1)} custom-call(s32[4]{0:T(128)S(1)} %pad_add_fusion.place, bf16[512,1024]{1,0:T(8,128)(2,1)S(1)} %shard_map.77.first.second, bf16[512,1024]{1,0:T(8,128)(2,1)S(1)} %shard_map.77.first.second, bf16[256,1024]{1,0:T(8,128)(2,1)S(1)} %bitcast.16, bf16[256,1024]{1,0:T(8,128)(2,1)S(1)} %bitcast.12), custom_call_target="tpu_custom_call" | custom-call | flops 3221225472 | bytes 1048576 | tf_op jit(solution)/shard_map/pallas_call | solution.py:146
  57.1 2.4 %shard_map.79.refs_6_ = f32[512,1024]{1,0:T(8,128)S(1)} custom-call(s32[4]{0:T(128)S(1)} %pad_add_fusion.place, bf16[512,1024]{1,0:T(8,128)(2,1)S(1)} %shard_map.77.first.second, bf16[512,1024]{1,0:T(8,128)(2,1)S(1)} %shard_map.77.first.second, bf16[256,1024]{1,0:T(8,128)(2,1)S(1)} %collective-permute-done.1.refs_0_.refs_2_, ...), custom_call_target="tpu_custom_call" | custom-call | flops 6442450944 | bytes 1048576 | tf_op jit(solution)/shard_map/pallas_call | solution.py:146
  59.6 1.2 %collective-permute-done.first.second = bf16[512,1024]{1,0:T(8,128)(2,1)S(1)} collective-permute-done((bf16[512,1024]{1,0:T(8,128)(2,1)S(1)}, bf16[512,1024]{1,0:T(8,128)(2,1)S(1)}, u32[]{:S(2)}, u32[]{:S(2)}) %collective-permute-start) | collective-permute-done | bytes 1048608 | tf_op jit(solution)/shard_map/ppermute | solution.py:70
  60.8 2.7 %shard_map.80.refs_2_ = f32[512,1024]{1,0:T(8,128)S(1)} custom-call(s32[4]{0:T(128)S(1)} %pad_add_fusion.place, bf16[512,1024]{1,0:T(8,128)(2,1)S(1)} %collective-permute-done.first.second, bf16[512,1024]{1,0:T(8,128)(2,1)S(1)} %collective-permute-done.first.second, bf16[256,1024]{1,0:T(8,128)(2,1)S(1)} %bitcast.17, bf16[256,1024]{1,0:T(8,128)(2,1)S(1)} %bitcast.13, ...), custom_call_target="tpu_custom_call" | custom-call | flops 9663676416 | bytes 1048576 | tf_op jit(solution)/shard_map/pallas_call | solution.py:146
  63.6 1.5 %shard_map.82 = f32[256,1024]{1,0:T(8,128)S(1)} custom-call(s32[4]{0:T(128)S(1)} %pad_add_fusion.place, bf16[512,1024]{1,0:T(8,128)(2,1)S(1)} %shard_map.77.first.second, bf16[512,1024]{1,0:T(8,128)(2,1)S(1)} %collective-permute-done.first.second, bf16[256,1024]{1,0:T(8,128)(2,1)S(1)} %collective-permute-done.2.refs_0_, ...), custom_call_target="tpu_custom_call" | custom-call | flops 3221225472 | bytes 1048576 | tf_op jit(solution)/shard_map/pallas_call | solution.py:146
  65.1 9.3 %collective-permute-start.7 = (f32[256,1024]{1,0:T(8,128)S(1)}, f32[256,1024]{1,0:T(8,128)S(1)}, u32[]{:S(2)}, u32[]{:S(2)}) collective-permute-start(f32[256,1024]{1,0:T(8,128)S(1)} %shard_map.82), channel_id=1, source_target_pairs={{0,16},{16,0},{1,17},{17,1},{2,18},{18,2},{3,19},{19,3},{4,20},{20... | collective-permute-start | bytes 3145736 | tf_op jit(solution)/shard_map/ppermute | solution.py:285
  74.4 1.5 %shard_map.81.mine = f32[256,1024]{1,0:T(8,128)S(1)} custom-call(s32[4]{0:T(128)S(1)} %pad_add_fusion.place, bf16[512,1024]{1,0:T(8,128)(2,1)S(1)} %shard_map.77.first.second, bf16[512,1024]{1,0:T(8,128)(2,1)S(1)} %collective-permute-done.first.second, bf16[256,1024]{1,0:T(8,128)(2,1)S(1)} %collective-permute-done.2.refs_0_, ...), custom_call_target="tpu_custom_call" | custom-call | flops 3221225472 | bytes 1048576 | tf_op jit(solution)/shard_map/pallas_call | solution.py:146
  76.0 0.0 copy-start
  76.0 0.0 copy-start.2
  76.0 0.7 collective-permute-done.7.theirs
  76.7 0.1 shard_map.83
  76.8 10.7 %all_to_all.25.received = f32[32,8,128]{2,1,0:T(8,128)S(1)} all-to-all(f32[32,8,128]{2,1,0:T(8,128)S(1)} %get-tuple-element.15), channel_id=1, replica_groups=mesh['y'=4,'x'=4,'core'=2,'z'=16] {'y','x','core'}, dimensions={0} | all-to-all | bytes 262144 | tf_op jit(solution)/shard_map/all_to_all | solution.py:74
  87.6 1.0 shard_map.84
  88.5 20.0 %all_to_all.26.received = f32[16,8,128]{2,1,0:T(8,128)S(1)} all-to-all(f32[16,8,128]{2,1,0:T(8,128)S(1)} %get-tuple-element.17), channel_id=1, replica_groups=mesh['y'=4,'x'=4,'core'=2,'z'=16] {'z'}, dimensions={0} | all-to-all | bytes 131072 | tf_op jit(solution)/shard_map/all_to_all | solution.py:74
  108.6 0.6 shard_map.85
  109.1 12.5 %all_to_all.27.received = f32[32,4,128]{2,1,0:T(4,128)S(1)} all-to-all(f32[32,4,128]{2,1,0:T(4,128)S(1)} %get-tuple-element.18), channel_id=1, replica_groups=mesh['y'=4,'x'=4,'core'=2,'z'=16] {'y','x','core'}, dimensions={0} | all-to-all | bytes 131072 | tf_op jit(solution)/shard_map/all_to_all | solution.py:74
  121.6 1.4 %shard_map.86 = f32[256,1024]{1,0:T(8,128)} custom-call(f32[32,4,128]{2,1,0:T(4,128)S(1)} %all_to_all.27.received, f32[2,128]{1,0:T(2,128)S(1)} %get-tuple-element.19.row_root, f32[8,128]{1,0:T(8,128)S(1)} %get-tuple-element.20.col_root, f32[256,1024]{1,0:T(8,128)S(1)} %get-tuple-element.16.grad, f32[256,1024]{1,0:T(8,128)S(1)} %copy-done), custom_call_target="tpu_custom_call" | custom-call | flops 1048576 | bytes 3145728 | tf_op jit(solution)/shard_map/pallas_call | solution.py:256
  (11 shorter events, 0.0 us)
Async XLA Ops:
  2.7 14.8 %all-to-all-start = ((bf16[4,128,1024]{2,1,0:T(8,128)(2,1)}), bf16[4,128,1024]{2,1,0:T(8,128)(2,1)S(1)}, u32[]{:S(2)}, u32[]{:S(2)}) async-start(bf16[4,128,1024]{2,1,0:T(8,128)(2,1)} %broadcast_in_dim.3), calls=%async_computation | async-start | bytes 2097152 | tf_op jit(solution)/shard_map/all_to_all | solution.py:64
  17.4 17.9 %all-to-all-start.1 = ((bf16[16,64,512]{2,1,0:T(8,128)(2,1)}), bf16[16,64,512]{2,1,0:T(8,128)(2,1)S(1)}, u32[]{:S(2)}, u32[]{:S(2)}) async-start(bf16[16,64,512]{2,1,0:T(8,128)(2,1)} %shard_map.76), calls=%async_computation.1 | async-start | bytes 2097152 | tf_op jit(solution)/shard_map/all_to_all | solution.py:74
  22.3 26.8 %collective-permute-start.1 = (bf16[256,1024]{1,0:T(8,128)(2,1)S(1)}, bf16[256,1024]{1,0:T(8,128)(2,1)S(1)}, u32[]{:S(2)}, u32[]{:S(2)}) collective-permute-start(bf16[256,1024]{1,0:T(8,128)(2,1)S(1)} %bitcast.14), channel_id=1, source_target_pairs={{0,128},{16,48},{32,160},{48,80},{64,192},{80,112},{96,224},{112,1... | collective-permute-start | bytes 1572872 | tf_op jit(solution)/shard_map/ppermute | solution.py:57
  25.6 25.7 %collective-permute-start.3 = (bf16[256,1024]{1,0:T(8,128)(2,1)S(1)}, bf16[256,1024]{1,0:T(8,128)(2,1)S(1)}, u32[]{:S(2)}, u32[]{:S(2)}) collective-permute-start(bf16[256,1024]{1,0:T(8,128)(2,1)S(1)} %bitcast.10), channel_id=1, source_target_pairs={{0,384},{16,112},{32,416},{48,16},{64,448},{80,48},{96,480},{112,8... | collective-permute-start | bytes 1572872 | tf_op jit(solution)/shard_map/ppermute | solution.py:57
  28.8 28.3 %collective-permute-start.5 = (bf16[256,1024]{1,0:T(8,128)(2,1)S(1)}, bf16[256,1024]{1,0:T(8,128)(2,1)}, u32[]{:S(2)}, u32[]{:S(2)}) collective-permute-start(bf16[256,1024]{1,0:T(8,128)(2,1)S(1)} %bitcast.11), channel_id=1, source_target_pairs={{0,128},{16,48},{32,160},{48,80},{64,192},{80,112},{96,224},{112,1... | collective-permute-start | bytes 1572872 | tf_op jit(solution)/shard_map/ppermute | solution.py:57
  30.9 26.3 %collective-permute-start.6 = (bf16[256,1024]{1,0:T(8,128)(2,1)S(1)}, bf16[256,1024]{1,0:T(8,128)(2,1)}, u32[]{:S(2)}, u32[]{:S(2)}) collective-permute-start(bf16[256,1024]{1,0:T(8,128)(2,1)S(1)} %bitcast.15), channel_id=1, source_target_pairs={{0,384},{16,112},{32,416},{48,16},{64,448},{80,48},{96,480},{112,8... | collective-permute-start | bytes 1572872 | tf_op jit(solution)/shard_map/ppermute | solution.py:57
  36.2 24.6 %collective-permute-start = (bf16[512,1024]{1,0:T(8,128)(2,1)S(1)}, bf16[512,1024]{1,0:T(8,128)(2,1)S(1)}, u32[]{:S(2)}, u32[]{:S(2)}) collective-permute-start(bf16[512,1024]{1,0:T(8,128)(2,1)S(1)} %shard_map.77.first.second), channel_id=1, source_target_pairs={{0,1},{1,2},{2,3},{3,4},{4,5},{5,6},{6,7},{7,8},{8,9},{9,10},{10,1... | collective-permute-start | bytes 3145736 | tf_op jit(solution)/shard_map/ppermute | solution.py:70
  49.1 14.5 %collective-permute-start.2 = (bf16[256,1024]{1,0:T(8,128)(2,1)S(1)}, bf16[256,1024]{1,0:T(8,128)(2,1)S(1)}, u32[]{:S(2)}, u32[]{:S(2)}) collective-permute-start(bf16[256,1024]{1,0:T(8,128)(2,1)S(1)} %collective-permute-done.1.refs_0_.refs_2_), channel_id=1, source_target_pairs={{0,128},{16,48},{32,160},{48,80},{64,192},{80,112},{96,224},{112,1... | collective-permute-start | bytes 1572872 | tf_op jit(solution)/shard_map/ppermute | solution.py:57
  51.3 12.3 %collective-permute-start.4 = (bf16[256,1024]{1,0:T(8,128)(2,1)S(1)}, bf16[256,1024]{1,0:T(8,128)(2,1)S(1)}, u32[]{:S(2)}, u32[]{:S(2)}) collective-permute-start(bf16[256,1024]{1,0:T(8,128)(2,1)S(1)} %collective-permute-done.3.refs_3_.refs_5_), channel_id=1, source_target_pairs={{0,384},{16,112},{32,416},{48,16},{64,448},{80,48},{96,480},{112,8... | collective-permute-start | bytes 1572872 | tf_op jit(solution)/shard_map/ppermute | solution.py:57
  65.1 11.6 %collective-permute-start.7 = (f32[256,1024]{1,0:T(8,128)S(1)}, f32[256,1024]{1,0:T(8,128)S(1)}, u32[]{:S(2)}, u32[]{:S(2)}) collective-permute-start(f32[256,1024]{1,0:T(8,128)S(1)} %shard_map.82), channel_id=1, source_target_pairs={{0,16},{16,0},{1,17},{17,1},{2,18},{18,2},{3,19},{19,3},{4,20},{20... | collective-permute-start | bytes 3145736 | tf_op jit(solution)/shard_map/ppermute | solution.py:285
  76.0 11.6 %copy-start = (f32[256,1024]{1,0:T(8,128)S(1)}, f32[256,1024]{1,0:T(8,128)}, u32[]{:S(2)}) copy-start(f32[256,1024]{1,0:T(8,128)} %weight.3) | copy-start | bytes 3145732
  76.0 11.6 %copy-start.1 = (f32[1024]{0:T(1024)S(1)}, f32[1024]{0:T(1024)}, u32[]{:S(2)}) copy-start(f32[1024]{0:T(1024)} %param.9) | copy-start | bytes 12292
  76.0 32.6 %copy-start.2 = (f32[256]{0:T(256)S(1)}, f32[256]{0:T(256)}, u32[]{:S(2)}) copy-start(f32[256]{0:T(256)} %param.8) | copy-start | bytes 3076

commit v15 on v14

--- a/solution.py
+++ b/solution.py
@@ -278,12 +278,12 @@
     blocks = lambda operand: [(operand, 0), (operand, 1), (operand + 1, 0), (operand + 1, 1)]
     total = product(place, (first, first), [low, high], [(0, True, blocks(0))])
     total = product(place, (first, first), back + ahead, [(1, True, blocks(0)), (3, True, blocks(2))], total)
-    parts = [(group, False, blocks(2 * i)) for i, group in enumerate((0, 1, 3))]
-    total = product(place, (second, second), [low, high] + back + ahead, parts, total)
-    parts = [(2, True, blocks(0)), (2, False, blocks(0))]
-    theirs = product(place, (first, second), far, parts, total, lambda core: 1 - core)
+    operands = [low, high] + back + ahead + far
+    parts = [(2, True, blocks(6)), (2, False, blocks(6))]
+    parts += [(group, False, blocks(2 * i)) for i, group in enumerate((0, 1, 3))]
+    theirs = product(place, (first, second), operands, parts, total, lambda core: 1 - core)
     received = lax.ppermute(theirs, "core", [(0, 1), (1, 0)])
-    mine = product(place, (first, second), far, parts, total, lambda core: core)
+    mine = product(place, (first, second), operands, parts, total, lambda core: core)
     weight_grad, tiles = columns(mine, received)
     new_cols, col_root, tiles = rows(exchange(tiles, ROWS), col_moment.reshape(TILE), weight_grad, weight)
     new_rows, row_root, tiles = scalars(exchange(tiles, "z"), row_moment.reshape(2, LANES))

time: 124 us -> 123 us (level)
  starting transfers between devices: 51.4 us -> 49.8 us
    ppermute x6, waiting for transfers between devices: 0.02 us -> 2.16 us  [along(): return lax.ppermute(value, ROWS, pairs)]
    pallas_call x5 -> x4, Pallas kernels: 9.67 us -> 9.17 us  [product(): pl.pallas_call(functools.partial(product_kernel, parts, which), out_shape...]
  transfers between devices with their start and end apart: 10 -> 10, of which waited for: 3 -> 4; matrix products, arithmetic and copies ran while one was open for 0% -> 0% of each run, Pallas kernels for 10% -> 8%
where the time goes in v15:
time: 123 us
  starting transfers between devices  49.8 us (40%)
  blocking collectives  44.2 us (36%)
  Pallas kernels  16.1 us (13%)
  waiting for transfers between devices  9.69 us (8%)
  local copies, waits for them, and re-layouts  2.15 us (2%)
    all_to_all x3, blocking collectives, exchange(): return lax.all_to_all(tiles, axes, 0, 0)  44.2 us
    ppermute x6, starting transfers between devices, along(): return lax.ppermute(value, ROWS, pairs)  18.3 us
    ppermute x1, starting transfers between devices, next_layer(): return lax.ppermute(value, ('core', 'z'), pairs)  13.3 us
    pallas_call x4, Pallas kernels, product(): pl.pallas_call(functools.partial(product_kernel, parts, which), out_shape...  9.17 us
    ppermute x1, starting transfers between devices, shards(): received = lax.ppermute(theirs, 'core', [(0, 1), (1, 0)])  8.4 us
    all_to_all x1, waiting for transfers between devices, gather_line(): return lax.all_to_all(sent, ROWS, 0, 0, axis_index_groups=groups)  6.76 us
    all_to_all x1, starting transfers between devices, gather_line(): return lax.all_to_all(sent, ROWS, 0, 0, axis_index_groups=groups)  5.01 us
    all_to_all x1, starting transfers between devices, exchange(): return lax.all_to_all(tiles, axes, 0, 0)  4.76 us
  transfers between devices with their start and end apart: 10, of which 4 were waited for; matrix products, arithmetic and copies ran while one was open for 0% of the time, Pallas kernels for 8%

profile of v15, /device:TPU:1, one launch (start us, length us, event | category | flops | bytes accessed | tf_op | source)
XLA Modules:
  0.0 122.7 jit_solution(12728716927875813523)
XLA Ops:
  0.6 2.1 %broadcast_in_dim.3 = bf16[4,128,1024]{2,1,0:T(8,128)(2,1)} broadcast(bf16[128,1024]{1,0:T(8,128)(2,1)} %param.6), dimensions={1,2} | broadcast | bytes 1310720 | tf_op jit(solution)/shard_map/broadcast_in_dim | solution.py:63
  2.7 5.0 %all-to-all-start = ((bf16[4,128,1024]{2,1,0:T(8,128)(2,1)}), bf16[4,128,1024]{2,1,0:T(8,128)(2,1)S(1)}, u32[]{:S(2)}, u32[]{:S(2)}) async-start(bf16[4,128,1024]{2,1,0:T(8,128)(2,1)} %broadcast_in_dim.3), calls=%async_computation | async-start | bytes 2097152 | tf_op jit(solution)/shard_map/all_to_all | solution.py:64
  7.7 0.1 pad_add_fusion.place
  7.8 2.9 %shard_map.76 = bf16[16,64,512]{2,1,0:T(8,128)(2,1)} custom-call(s32[4]{0:T(128)S(1)} %pad_add_fusion.place, bf16[128,8192]{1,0:T(8,128)(2,1)} %source.1), custom_call_target="tpu_custom_call" | custom-call | bytes 2097152 | tf_op jit(solution)/shard_map/pallas_call | solution.py:90
  10.7 6.8 %all-to-all-done = bf16[4,128,1024]{2,1,0:T(8,128)(2,1)S(1)} async-done(((bf16[4,128,1024]{2,1,0:T(8,128)(2,1)}), bf16[4,128,1024]{2,1,0:T(8,128)(2,1)S(1)}, u32[]{:S(2)}, u32[]{:S(2)}) %all-to-all-start) | async-done | bytes 1048608 | tf_op jit(solution)/shard_map/all_to_all | solution.py:64
  17.4 4.8 %all-to-all-start.1 = ((bf16[16,64,512]{2,1,0:T(8,128)(2,1)}), bf16[16,64,512]{2,1,0:T(8,128)(2,1)S(1)}, u32[]{:S(2)}, u32[]{:S(2)}) async-start(bf16[16,64,512]{2,1,0:T(8,128)(2,1)} %shard_map.76), calls=%async_computation.1 | async-start | bytes 2097152 | tf_op jit(solution)/shard_map/all_to_all | solution.py:74
  22.2 0.1 fusion
  22.3 3.3 %collective-permute-start.1 = (bf16[256,1024]{1,0:T(8,128)(2,1)S(1)}, bf16[256,1024]{1,0:T(8,128)(2,1)S(1)}, u32[]{:S(2)}, u32[]{:S(2)}) collective-permute-start(bf16[256,1024]{1,0:T(8,128)(2,1)S(1)} %bitcast.15), channel_id=1, source_target_pairs={{0,128},{16,48},{32,160},{48,80},{64,192},{80,112},{96,224},{112,1... | collective-permute-start | bytes 1572872 | tf_op jit(solution)/shard_map/ppermute | solution.py:57
  25.6 3.2 %collective-permute-start.4 = (bf16[256,1024]{1,0:T(8,128)(2,1)S(1)}, bf16[256,1024]{1,0:T(8,128)(2,1)S(1)}, u32[]{:S(2)}, u32[]{:S(2)}) collective-permute-start(bf16[256,1024]{1,0:T(8,128)(2,1)S(1)} %bitcast.10), channel_id=1, source_target_pairs={{0,384},{16,112},{32,416},{48,16},{64,448},{80,48},{96,480},{112,8... | collective-permute-start | bytes 1572872 | tf_op jit(solution)/shard_map/ppermute | solution.py:57
  28.8 3.3 %collective-permute-start.3 = (bf16[256,1024]{1,0:T(8,128)(2,1)S(1)}, bf16[256,1024]{1,0:T(8,128)(2,1)}, u32[]{:S(2)}, u32[]{:S(2)}) collective-permute-start(bf16[256,1024]{1,0:T(8,128)(2,1)S(1)} %bitcast.16), channel_id=1, source_target_pairs={{0,384},{16,112},{32,416},{48,16},{64,448},{80,48},{96,480},{112,8... | collective-permute-start | bytes 1572872 | tf_op jit(solution)/shard_map/ppermute | solution.py:57
  32.1 2.0 %collective-permute-start.2 = (bf16[256,1024]{1,0:T(8,128)(2,1)S(1)}, bf16[256,1024]{1,0:T(8,128)(2,1)}, u32[]{:S(2)}, u32[]{:S(2)}) collective-permute-start(bf16[256,1024]{1,0:T(8,128)(2,1)S(1)} %bitcast.11), channel_id=1, source_target_pairs={{0,128},{16,48},{32,160},{48,80},{64,192},{80,112},{96,224},{112,1... | collective-permute-start | bytes 1572872 | tf_op jit(solution)/shard_map/ppermute | solution.py:57
  34.1 0.8 all-to-all-done.1.part
  34.9 0.9 shard_map.77.first.second
  35.8 13.3 %collective-permute-start = (bf16[512,1024]{1,0:T(8,128)(2,1)S(1)}, bf16[512,1024]{1,0:T(8,128)(2,1)S(1)}, u32[]{:S(2)}, u32[]{:S(2)}) collective-permute-start(bf16[512,1024]{1,0:T(8,128)(2,1)S(1)} %shard_map.77.first.second), channel_id=1, source_target_pairs={{0,1},{1,2},{2,3},{3,4},{4,5},{5,6},{6,7},{7,8},{8,9},{9,10},{10,1... | collective-permute-start | bytes 3145736 | tf_op jit(solution)/shard_map/ppermute | solution.py:70
  49.1 2.2 %collective-permute-start.5 = (bf16[256,1024]{1,0:T(8,128)(2,1)S(1)}, bf16[256,1024]{1,0:T(8,128)(2,1)S(1)}, u32[]{:S(2)}, u32[]{:S(2)}) collective-permute-start(bf16[256,1024]{1,0:T(8,128)(2,1)S(1)} %collective-permute-done.1.refs_0_.refs_2_), channel_id=1, source_target_pairs={{0,128},{16,48},{32,160},{48,80},{64,192},{80,112},{96,224},{112,1... | collective-permute-start | bytes 1572872 | tf_op jit(solution)/shard_map/ppermute | solution.py:57
  51.3 4.3 %collective-permute-start.6 = (bf16[256,1024]{1,0:T(8,128)(2,1)S(1)}, bf16[256,1024]{1,0:T(8,128)(2,1)S(1)}, u32[]{:S(2)}, u32[]{:S(2)}) collective-permute-start(bf16[256,1024]{1,0:T(8,128)(2,1)S(1)} %collective-permute-done.4.refs_3_.refs_5_), channel_id=1, source_target_pairs={{0,384},{16,112},{32,416},{48,16},{64,448},{80,48},{96,480},{112,8... | collective-permute-start | bytes 1572872 | tf_op jit(solution)/shard_map/ppermute | solution.py:57
  55.6 1.5 %shard_map.78.refs_4_ = f32[512,1024]{1,0:T(8,128)S(1)} custom-call(s32[4]{0:T(128)S(1)} %pad_add_fusion.place, bf16[512,1024]{1,0:T(8,128)(2,1)S(1)} %shard_map.77.first.second, bf16[512,1024]{1,0:T(8,128)(2,1)S(1)} %shard_map.77.first.second, bf16[256,1024]{1,0:T(8,128)(2,1)S(1)} %bitcast.17, bf16[256,1024]{1,0:T(8,128)(2,1)S(1)} %bitcast.12), custom_call_target="tpu_custom_call" | custom-call | flops 3221225472 | bytes 1048576 | tf_op jit(solution)/shard_map/pallas_call | solution.py:146
  57.1 2.4 %shard_map.79.refs_8_ = f32[512,1024]{1,0:T(8,128)S(1)} custom-call(s32[4]{0:T(128)S(1)} %pad_add_fusion.place, bf16[512,1024]{1,0:T(8,128)(2,1)S(1)} %shard_map.77.first.second, bf16[512,1024]{1,0:T(8,128)(2,1)S(1)} %shard_map.77.first.second, bf16[256,1024]{1,0:T(8,128)(2,1)S(1)} %collective-permute-done.1.refs_0_.refs_2_, ...), custom_call_target="tpu_custom_call" | custom-call | flops 6442450944 | bytes 1048576 | tf_op jit(solution)/shard_map/pallas_call | solution.py:146
  59.6 1.0 collective-permute-done.5.refs_6_
  60.5 1.2 collective-permute-done.6.refs_7_
  61.7 2.6 %shard_map.81 = f32[256,1024]{1,0:T(8,128)S(1)} custom-call(s32[4]{0:T(128)S(1)} %pad_add_fusion.place, bf16[512,1024]{1,0:T(8,128)(2,1)S(1)} %shard_map.77.first.second, bf16[512,1024]{1,0:T(8,128)(2,1)S(1)} %collective-permute-done.second, bf16[256,1024]{1,0:T(8,128)(2,1)S(1)} %bitcast.18, bf16[256,1024]{1,0:T(8,128)(2,1)S(1)} %bitcast.13, ...), custom_call_target="tpu_custom_call" | custom-call | flops 8053063680 | bytes 1048576 | tf_op jit(solution)/shard_map/pallas_call | solution.py:146
  64.4 8.4 %collective-permute-start.7 = (f32[256,1024]{1,0:T(8,128)S(1)}, f32[256,1024]{1,0:T(8,128)S(1)}, u32[]{:S(2)}, u32[]{:S(2)}) collective-permute-start(f32[256,1024]{1,0:T(8,128)S(1)} %shard_map.81), channel_id=1, source_target_pairs={{0,16},{16,0},{1,17},{17,1},{2,18},{18,2},{3,19},{19,3},{4,20},{20... | collective-permute-start | bytes 3145736 | tf_op jit(solution)/shard_map/ppermute | solution.py:285
  72.8 2.6 %shard_map.80.mine = f32[256,1024]{1,0:T(8,128)S(1)} custom-call(s32[4]{0:T(128)S(1)} %pad_add_fusion.place, bf16[512,1024]{1,0:T(8,128)(2,1)S(1)} %shard_map.77.first.second, bf16[512,1024]{1,0:T(8,128)(2,1)S(1)} %collective-permute-done.second, bf16[256,1024]{1,0:T(8,128)(2,1)S(1)} %bitcast.19, bf16[256,1024]{1,0:T(8,128)(2,1)S(1)} %bitcast.14, ...), custom_call_target="tpu_custom_call" | custom-call | flops 8053063680 | bytes 1048576 | tf_op jit(solution)/shard_map/pallas_call | solution.py:146
  75.4 0.0 copy-start
  75.4 0.0 copy-start.1
  75.5 0.1 shard_map.82
  75.6 10.6 %all_to_all.25.received = f32[32,8,128]{2,1,0:T(8,128)S(1)} all-to-all(f32[32,8,128]{2,1,0:T(8,128)S(1)} %get-tuple-element.15), channel_id=1, replica_groups=mesh['y'=4,'x'=4,'core'=2,'z'=16] {'y','x','core'}, dimensions={0} | all-to-all | bytes 262144 | tf_op jit(solution)/shard_map/all_to_all | solution.py:74
  86.2 1.0 shard_map.83
  87.1 21.1 %all_to_all.26.received = f32[16,8,128]{2,1,0:T(8,128)S(1)} all-to-all(f32[16,8,128]{2,1,0:T(8,128)S(1)} %get-tuple-element.17), channel_id=1, replica_groups=mesh['y'=4,'x'=4,'core'=2,'z'=16] {'z'}, dimensions={0} | all-to-all | bytes 131072 | tf_op jit(solution)/shard_map/all_to_all | solution.py:74
  108.2 0.6 shard_map.84
  108.8 12.5 %all_to_all.27.received = f32[32,4,128]{2,1,0:T(4,128)S(1)} all-to-all(f32[32,4,128]{2,1,0:T(4,128)S(1)} %get-tuple-element.18), channel_id=1, replica_groups=mesh['y'=4,'x'=4,'core'=2,'z'=16] {'y','x','core'}, dimensions={0} | all-to-all | bytes 131072 | tf_op jit(solution)/shard_map/all_to_all | solution.py:74
  121.3 1.4 %shard_map.85 = f32[256,1024]{1,0:T(8,128)} custom-call(f32[32,4,128]{2,1,0:T(4,128)S(1)} %all_to_all.27.received, f32[2,128]{1,0:T(2,128)S(1)} %get-tuple-element.19.row_root, f32[8,128]{1,0:T(8,128)S(1)} %get-tuple-element.20.col_root, f32[256,1024]{1,0:T(8,128)S(1)} %get-tuple-element.16.grad, f32[256,1024]{1,0:T(8,128)S(1)} %copy-done), custom_call_target="tpu_custom_call" | custom-call | flops 1048576 | bytes 3145728 | tf_op jit(solution)/shard_map/pallas_call | solution.py:256
  (10 shorter events, 0.0 us)
Async XLA Ops:
  2.7 14.8 %all-to-all-start = ((bf16[4,128,1024]{2,1,0:T(8,128)(2,1)}), bf16[4,128,1024]{2,1,0:T(8,128)(2,1)S(1)}, u32[]{:S(2)}, u32[]{:S(2)}) async-start(bf16[4,128,1024]{2,1,0:T(8,128)(2,1)} %broadcast_in_dim.3), calls=%async_computation | async-start | bytes 2097152 | tf_op jit(solution)/shard_map/all_to_all | solution.py:64
  17.4 17.4 %all-to-all-start.1 = ((bf16[16,64,512]{2,1,0:T(8,128)(2,1)}), bf16[16,64,512]{2,1,0:T(8,128)(2,1)S(1)}, u32[]{:S(2)}, u32[]{:S(2)}) async-start(bf16[16,64,512]{2,1,0:T(8,128)(2,1)} %shard_map.76), calls=%async_computation.1 | async-start | bytes 2097152 | tf_op jit(solution)/shard_map/all_to_all | solution.py:74
  22.3 26.8 %collective-permute-start.1 = (bf16[256,1024]{1,0:T(8,128)(2,1)S(1)}, bf16[256,1024]{1,0:T(8,128)(2,1)S(1)}, u32[]{:S(2)}, u32[]{:S(2)}) collective-permute-start(bf16[256,1024]{1,0:T(8,128)(2,1)S(1)} %bitcast.15), channel_id=1, source_target_pairs={{0,128},{16,48},{32,160},{48,80},{64,192},{80,112},{96,224},{112,1... | collective-permute-start | bytes 1572872 | tf_op jit(solution)/shard_map/ppermute | solution.py:57
  25.6 25.7 %collective-permute-start.4 = (bf16[256,1024]{1,0:T(8,128)(2,1)S(1)}, bf16[256,1024]{1,0:T(8,128)(2,1)S(1)}, u32[]{:S(2)}, u32[]{:S(2)}) collective-permute-start(bf16[256,1024]{1,0:T(8,128)(2,1)S(1)} %bitcast.10), channel_id=1, source_target_pairs={{0,384},{16,112},{32,416},{48,16},{64,448},{80,48},{96,480},{112,8... | collective-permute-start | bytes 1572872 | tf_op jit(solution)/shard_map/ppermute | solution.py:57
  28.8 28.3 %collective-permute-start.3 = (bf16[256,1024]{1,0:T(8,128)(2,1)S(1)}, bf16[256,1024]{1,0:T(8,128)(2,1)}, u32[]{:S(2)}, u32[]{:S(2)}) collective-permute-start(bf16[256,1024]{1,0:T(8,128)(2,1)S(1)} %bitcast.16), channel_id=1, source_target_pairs={{0,384},{16,112},{32,416},{48,16},{64,448},{80,48},{96,480},{112,8... | collective-permute-start | bytes 1572872 | tf_op jit(solution)/shard_map/ppermute | solution.py:57
  32.1 25.1 %collective-permute-start.2 = (bf16[256,1024]{1,0:T(8,128)(2,1)S(1)}, bf16[256,1024]{1,0:T(8,128)(2,1)}, u32[]{:S(2)}, u32[]{:S(2)}) collective-permute-start(bf16[256,1024]{1,0:T(8,128)(2,1)S(1)} %bitcast.11), channel_id=1, source_target_pairs={{0,128},{16,48},{32,160},{48,80},{64,192},{80,112},{96,224},{112,1... | collective-permute-start | bytes 1572872 | tf_op jit(solution)/shard_map/ppermute | solution.py:57
  35.8 26.0 %collective-permute-start = (bf16[512,1024]{1,0:T(8,128)(2,1)S(1)}, bf16[512,1024]{1,0:T(8,128)(2,1)S(1)}, u32[]{:S(2)}, u32[]{:S(2)}) collective-permute-start(bf16[512,1024]{1,0:T(8,128)(2,1)S(1)} %shard_map.77.first.second), channel_id=1, source_target_pairs={{0,1},{1,2},{2,3},{3,4},{4,5},{5,6},{6,7},{7,8},{8,9},{9,10},{10,1... | collective-permute-start | bytes 3145736 | tf_op jit(solution)/shard_map/ppermute | solution.py:70
  49.1 11.4 %collective-permute-start.5 = (bf16[256,1024]{1,0:T(8,128)(2,1)S(1)}, bf16[256,1024]{1,0:T(8,128)(2,1)S(1)}, u32[]{:S(2)}, u32[]{:S(2)}) collective-permute-start(bf16[256,1024]{1,0:T(8,128)(2,1)S(1)} %collective-permute-done.1.refs_0_.refs_2_), channel_id=1, source_target_pairs={{0,128},{16,48},{32,160},{48,80},{64,192},{80,112},{96,224},{112,1... | collective-permute-start | bytes 1572872 | tf_op jit(solution)/shard_map/ppermute | solution.py:57
  51.3 10.4 %collective-permute-start.6 = (bf16[256,1024]{1,0:T(8,128)(2,1)S(1)}, bf16[256,1024]{1,0:T(8,128)(2,1)S(1)}, u32[]{:S(2)}, u32[]{:S(2)}) collective-permute-start(bf16[256,1024]{1,0:T(8,128)(2,1)S(1)} %collective-permute-done.4.refs_3_.refs_5_), channel_id=1, source_target_pairs={{0,384},{16,112},{32,416},{48,16},{64,448},{80,48},{96,480},{112,8... | collective-permute-start | bytes 1572872 | tf_op jit(solution)/shard_map/ppermute | solution.py:57
  64.4 11.1 %collective-permute-start.7 = (f32[256,1024]{1,0:T(8,128)S(1)}, f32[256,1024]{1,0:T(8,128)S(1)}, u32[]{:S(2)}, u32[]{:S(2)}) collective-permute-start(f32[256,1024]{1,0:T(8,128)S(1)} %shard_map.81), channel_id=1, source_target_pairs={{0,16},{16,0},{1,17},{17,1},{2,18},{18,2},{3,19},{19,3},{4,20},{20... | collective-permute-start | bytes 3145736 | tf_op jit(solution)/shard_map/ppermute | solution.py:285
  75.4 10.8 %copy-start = (f32[256,1024]{1,0:T(8,128)S(1)}, f32[256,1024]{1,0:T(8,128)}, u32[]{:S(2)}) copy-start(f32[256,1024]{1,0:T(8,128)} %weight.3) | copy-start | bytes 3145732
  75.4 10.7 %copy-start.1 = (f32[1024]{0:T(1024)S(1)}, f32[1024]{0:T(1024)}, u32[]{:S(2)}) copy-start(f32[1024]{0:T(1024)} %param.9) | copy-start | bytes 12292
  75.4 32.8 %copy-start.2 = (f32[256]{0:T(256)S(1)}, f32[256]{0:T(256)}, u32[]{:S(2)}) copy-start(f32[256]{0:T(256)} %param.8) | copy-start | bytes 3076

commit v16 on v15

--- a/solution.py
+++ b/solution.py
@@ -131,7 +131,7 @@
         columns = pl.ds(pl.multiple_of(n * COLUMNS, COLUMNS), COLUMNS)
         value = None if total is None else total[rows, columns]
         for group, exchanged, blocks in parts:
-            depth = slice(group * SIDE * HALF, (group + 1) * SIDE * HALF)
+            depth = slice(group * SIDE * HALF, group * SIDE * HALF + len(blocks) * HALF)
             features, offset = (first, start) if exchanged else (second, HALF - start)
             offset = pl.multiple_of(offset, HALF)
             grads = [operands[index][pl.ds(i * TOKENS + offset, HALF), columns] for index, i in blocks]
@@ -148,8 +148,9 @@
         out_shape=shape(count, WIDTH),
         in_specs=[SCALARS] + [WHOLE] * len(operands),
         out_specs=WHOLE,
-        compiler_params=PARAMS,
-        cost_estimate=cost(24 * count * SIDE * HALF * WIDTH * len(parts), 2**20),
+        input_output_aliases={len(operands): 0} if total is not None and which is None else {},
+        compiler_params=PARAMS,
+        cost_estimate=cost(24 * count * HALF * WIDTH * sum(len(part[2]) for part in parts), 2**20),
     )(place, *operands)
 
 
@@ -277,10 +278,10 @@
     back, ahead = [back_low, along(high, 1)], [along(low, SIDE - 1), ahead_high]
     blocks = lambda operand: [(operand, 0), (operand, 1), (operand + 1, 0), (operand + 1, 1)]
     total = product(place, (first, first), [low, high], [(0, True, blocks(0))])
-    total = product(place, (first, first), back + ahead, [(1, True, blocks(0)), (3, True, blocks(2))], total)
-    operands = [low, high] + back + ahead + far
-    parts = [(2, True, blocks(6)), (2, False, blocks(6))]
-    parts += [(group, False, blocks(2 * i)) for i, group in enumerate((0, 1, 3))]
+    parts = [(1, True, blocks(0)), (3, True, blocks(2))]
+    total = product(place, (first, first), back + ahead, parts, total)
+    operands = [low, high] + back + far + ahead
+    parts = [(2, True, blocks(4)), (0, False, blocks(0) + blocks(2) + blocks(4) + blocks(6))]
     theirs = product(place, (first, second), operands, parts, total, lambda core: 1 - core)
     received = lax.ppermute(theirs, "core", [(0, 1), (1, 0)])
     mine = product(place, (first, second), operands, parts, total, lambda core: core)

time: 123 us -> 123 us (level)
  no operation moved by 1% of the time
where the time goes in v16:
time: 123 us
  starting transfers between devices  49.8 us (40%)
  blocking collectives  44.2 us (36%)
  Pallas kernels  16.1 us (13%)
  waiting for transfers between devices  9.63 us (8%)
  local copies, waits for them, and re-layouts  2.15 us (2%)
    all_to_all x3, blocking collectives, exchange(): return lax.all_to_all(tiles, axes, 0, 0)  44.2 us
    ppermute x6, starting transfers between devices, along(): return lax.ppermute(value, ROWS, pairs)  18.3 us
    ppermute x1, starting transfers between devices, next_layer(): return lax.ppermute(value, ('core', 'z'), pairs)  13.3 us
    pallas_call x4, Pallas kernels, product(): pl.pallas_call(functools.partial(product_kernel, parts, which), out_shape...  9.21 us
    ppermute x1, starting transfers between devices, shards(): received = lax.ppermute(theirs, 'core', [(0, 1), (1, 0)])  8.39 us
    all_to_all x1, waiting for transfers between devices, gather_line(): return lax.all_to_all(sent, ROWS, 0, 0, axis_index_groups=groups)  6.76 us
    all_to_all x1, starting transfers between devices, gather_line(): return lax.all_to_all(sent, ROWS, 0, 0, axis_index_groups=groups)  5.01 us
    all_to_all x1, starting transfers between devices, exchange(): return lax.all_to_all(tiles, axes, 0, 0)  4.76 us
  transfers between devices with their start and end apart: 10, of which 4 were waited for; matrix products, arithmetic and copies ran while one was open for 0% of the time, Pallas kernels for 8%

profile of v16, /device:TPU:1, one launch (start us, length us, event | category | flops | bytes accessed | tf_op | source)
XLA Modules:
  0.0 122.7 jit_solution(1628347565768564169)
XLA Ops:
  0.6 2.1 %broadcast_in_dim.3 = bf16[4,128,1024]{2,1,0:T(8,128)(2,1)} broadcast(bf16[128,1024]{1,0:T(8,128)(2,1)} %param.6), dimensions={1,2} | broadcast | bytes 1310720 | tf_op jit(solution)/shard_map/broadcast_in_dim | solution.py:63
  2.7 5.0 %all-to-all-start = ((bf16[4,128,1024]{2,1,0:T(8,128)(2,1)}), bf16[4,128,1024]{2,1,0:T(8,128)(2,1)S(1)}, u32[]{:S(2)}, u32[]{:S(2)}) async-start(bf16[4,128,1024]{2,1,0:T(8,128)(2,1)} %broadcast_in_dim.3), calls=%async_computation | async-start | bytes 2097152 | tf_op jit(solution)/shard_map/all_to_all | solution.py:64
  7.7 0.1 pad_add_fusion.place
  7.8 2.9 %shard_map.76 = bf16[16,64,512]{2,1,0:T(8,128)(2,1)} custom-call(s32[4]{0:T(128)S(1)} %pad_add_fusion.place, bf16[128,8192]{1,0:T(8,128)(2,1)} %source.1), custom_call_target="tpu_custom_call" | custom-call | bytes 2097152 | tf_op jit(solution)/shard_map/pallas_call | solution.py:90
  10.7 6.8 %all-to-all-done = bf16[4,128,1024]{2,1,0:T(8,128)(2,1)S(1)} async-done(((bf16[4,128,1024]{2,1,0:T(8,128)(2,1)}), bf16[4,128,1024]{2,1,0:T(8,128)(2,1)S(1)}, u32[]{:S(2)}, u32[]{:S(2)}) %all-to-all-start) | async-done | bytes 1048608 | tf_op jit(solution)/shard_map/all_to_all | solution.py:64
  17.4 4.8 %all-to-all-start.1 = ((bf16[16,64,512]{2,1,0:T(8,128)(2,1)}), bf16[16,64,512]{2,1,0:T(8,128)(2,1)S(1)}, u32[]{:S(2)}, u32[]{:S(2)}) async-start(bf16[16,64,512]{2,1,0:T(8,128)(2,1)} %shard_map.76), calls=%async_computation.1 | async-start | bytes 2097152 | tf_op jit(solution)/shard_map/all_to_all | solution.py:74
  22.2 0.1 fusion
  22.3 3.3 %collective-permute-start.1 = (bf16[256,1024]{1,0:T(8,128)(2,1)S(1)}, bf16[256,1024]{1,0:T(8,128)(2,1)S(1)}, u32[]{:S(2)}, u32[]{:S(2)}) collective-permute-start(bf16[256,1024]{1,0:T(8,128)(2,1)S(1)} %bitcast.15), channel_id=1, source_target_pairs={{0,128},{16,48},{32,160},{48,80},{64,192},{80,112},{96,224},{112,1... | collective-permute-start | bytes 1572872 | tf_op jit(solution)/shard_map/ppermute | solution.py:57
  25.6 3.2 %collective-permute-start.4 = (bf16[256,1024]{1,0:T(8,128)(2,1)S(1)}, bf16[256,1024]{1,0:T(8,128)(2,1)S(1)}, u32[]{:S(2)}, u32[]{:S(2)}) collective-permute-start(bf16[256,1024]{1,0:T(8,128)(2,1)S(1)} %bitcast.10), channel_id=1, source_target_pairs={{0,384},{16,112},{32,416},{48,16},{64,448},{80,48},{96,480},{112,8... | collective-permute-start | bytes 1572872 | tf_op jit(solution)/shard_map/ppermute | solution.py:57
  28.8 3.3 %collective-permute-start.6 = (bf16[256,1024]{1,0:T(8,128)(2,1)S(1)}, bf16[256,1024]{1,0:T(8,128)(2,1)}, u32[]{:S(2)}, u32[]{:S(2)}) collective-permute-start(bf16[256,1024]{1,0:T(8,128)(2,1)S(1)} %bitcast.16), channel_id=1, source_target_pairs={{0,384},{16,112},{32,416},{48,16},{64,448},{80,48},{96,480},{112,8... | collective-permute-start | bytes 1572872 | tf_op jit(solution)/shard_map/ppermute | solution.py:57
  32.1 2.0 %collective-permute-start.2 = (bf16[256,1024]{1,0:T(8,128)(2,1)S(1)}, bf16[256,1024]{1,0:T(8,128)(2,1)}, u32[]{:S(2)}, u32[]{:S(2)}) collective-permute-start(bf16[256,1024]{1,0:T(8,128)(2,1)S(1)} %bitcast.11), channel_id=1, source_target_pairs={{0,128},{16,48},{32,160},{48,80},{64,192},{80,112},{96,224},{112,1... | collective-permute-start | bytes 1572872 | tf_op jit(solution)/shard_map/ppermute | solution.py:57
  34.1 0.8 all-to-all-done.1.part
  34.9 0.9 shard_map.77.first.second
  35.8 13.3 %collective-permute-start = (bf16[512,1024]{1,0:T(8,128)(2,1)S(1)}, bf16[512,1024]{1,0:T(8,128)(2,1)S(1)}, u32[]{:S(2)}, u32[]{:S(2)}) collective-permute-start(bf16[512,1024]{1,0:T(8,128)(2,1)S(1)} %shard_map.77.first.second), channel_id=1, source_target_pairs={{0,1},{1,2},{2,3},{3,4},{4,5},{5,6},{6,7},{7,8},{8,9},{9,10},{10,1... | collective-permute-start | bytes 3145736 | tf_op jit(solution)/shard_map/ppermute | solution.py:70
  49.1 2.2 %collective-permute-start.3 = (bf16[256,1024]{1,0:T(8,128)(2,1)S(1)}, bf16[256,1024]{1,0:T(8,128)(2,1)S(1)}, u32[]{:S(2)}, u32[]{:S(2)}) collective-permute-start(bf16[256,1024]{1,0:T(8,128)(2,1)S(1)} %collective-permute-done.1.refs_0_.refs_2_), channel_id=1, source_target_pairs={{0,128},{16,48},{32,160},{48,80},{64,192},{80,112},{96,224},{112,1... | collective-permute-start | bytes 1572872 | tf_op jit(solution)/shard_map/ppermute | solution.py:57
  51.3 4.3 %collective-permute-start.5 = (bf16[256,1024]{1,0:T(8,128)(2,1)S(1)}, bf16[256,1024]{1,0:T(8,128)(2,1)S(1)}, u32[]{:S(2)}, u32[]{:S(2)}) collective-permute-start(bf16[256,1024]{1,0:T(8,128)(2,1)S(1)} %collective-permute-done.4.refs_3_.refs_7_), channel_id=1, source_target_pairs={{0,384},{16,112},{32,416},{48,16},{64,448},{80,48},{96,480},{112,8... | collective-permute-start | bytes 1572872 | tf_op jit(solution)/shard_map/ppermute | solution.py:57
  55.6 1.5 %shard_map.78.refs_4_ = f32[512,1024]{1,0:T(8,128)S(1)} custom-call(s32[4]{0:T(128)S(1)} %pad_add_fusion.place, bf16[512,1024]{1,0:T(8,128)(2,1)S(1)} %shard_map.77.first.second, bf16[512,1024]{1,0:T(8,128)(2,1)S(1)} %shard_map.77.first.second, bf16[256,1024]{1,0:T(8,128)(2,1)S(1)} %bitcast.17, bf16[256,1024]{1,0:T(8,128)(2,1)S(1)} %bitcast.12), custom_call_target="tpu_custom_call" | custom-call | flops 3221225472 | bytes 1048576 | tf_op jit(solution)/shard_map/pallas_call | solution.py:146
  57.1 2.5 %shard_map.79.refs_8_ = f32[512,1024]{1,0:T(8,128)S(1)} custom-call(s32[4]{0:T(128)S(1)} %pad_add_fusion.place, bf16[512,1024]{1,0:T(8,128)(2,1)S(1)} %shard_map.77.first.second, bf16[512,1024]{1,0:T(8,128)(2,1)S(1)} %shard_map.77.first.second, bf16[256,1024]{1,0:T(8,128)(2,1)S(1)} %collective-permute-done.1.refs_0_.refs_2_, ...), custom_call_target="tpu_custom_call", output_to_operand_aliasing={{}: (7, {})} | custom-call | flops 6442450944 | bytes 1048576 | tf_op jit(solution)/shard_map/pallas_call | solution.py:146
  59.7 0.9 collective-permute-done.3.refs_4_
  60.5 1.2 collective-permute-done.5.refs_5_
  61.7 2.6 %shard_map.81 = f32[256,1024]{1,0:T(8,128)S(1)} custom-call(s32[4]{0:T(128)S(1)} %pad_add_fusion.place, bf16[512,1024]{1,0:T(8,128)(2,1)S(1)} %shard_map.77.first.second, bf16[512,1024]{1,0:T(8,128)(2,1)S(1)} %collective-permute-done.second, bf16[256,1024]{1,0:T(8,128)(2,1)S(1)} %bitcast.18, bf16[256,1024]{1,0:T(8,128)(2,1)S(1)} %bitcast.13, ...), custom_call_target="tpu_custom_call" | custom-call | flops 8053063680 | bytes 1048576 | tf_op jit(solution)/shard_map/pallas_call | solution.py:146
  64.4 8.4 %collective-permute-start.7 = (f32[256,1024]{1,0:T(8,128)S(1)}, f32[256,1024]{1,0:T(8,128)S(1)}, u32[]{:S(2)}, u32[]{:S(2)}) collective-permute-start(f32[256,1024]{1,0:T(8,128)S(1)} %shard_map.81), channel_id=1, source_target_pairs={{0,16},{16,0},{1,17},{17,1},{2,18},{18,2},{3,19},{19,3},{4,20},{20... | collective-permute-start | bytes 3145736 | tf_op jit(solution)/shard_map/ppermute | solution.py:286
  72.8 2.6 %shard_map.80.mine = f32[256,1024]{1,0:T(8,128)S(1)} custom-call(s32[4]{0:T(128)S(1)} %pad_add_fusion.place, bf16[512,1024]{1,0:T(8,128)(2,1)S(1)} %shard_map.77.first.second, bf16[512,1024]{1,0:T(8,128)(2,1)S(1)} %collective-permute-done.second, bf16[256,1024]{1,0:T(8,128)(2,1)S(1)} %bitcast.19, bf16[256,1024]{1,0:T(8,128)(2,1)S(1)} %bitcast.14, ...), custom_call_target="tpu_custom_call" | custom-call | flops 8053063680 | bytes 1048576 | tf_op jit(solution)/shard_map/pallas_call | solution.py:146
  75.4 0.0 copy-start.1
  75.4 0.0 copy-start.2
  75.4 0.1 shard_map.82
  75.6 10.6 %all_to_all.25.received = f32[32,8,128]{2,1,0:T(8,128)S(1)} all-to-all(f32[32,8,128]{2,1,0:T(8,128)S(1)} %get-tuple-element.15), channel_id=1, replica_groups=mesh['y'=4,'x'=4,'core'=2,'z'=16] {'y','x','core'}, dimensions={0} | all-to-all | bytes 262144 | tf_op jit(solution)/shard_map/all_to_all | solution.py:74
  86.2 1.0 shard_map.83
  87.1 21.1 %all_to_all.26.received = f32[16,8,128]{2,1,0:T(8,128)S(1)} all-to-all(f32[16,8,128]{2,1,0:T(8,128)S(1)} %get-tuple-element.17), channel_id=1, replica_groups=mesh['y'=4,'x'=4,'core'=2,'z'=16] {'z'}, dimensions={0} | all-to-all | bytes 131072 | tf_op jit(solution)/shard_map/all_to_all | solution.py:74
  108.2 0.6 shard_map.84
  108.8 12.5 %all_to_all.27.received = f32[32,4,128]{2,1,0:T(4,128)S(1)} all-to-all(f32[32,4,128]{2,1,0:T(4,128)S(1)} %get-tuple-element.18), channel_id=1, replica_groups=mesh['y'=4,'x'=4,'core'=2,'z'=16] {'y','x','core'}, dimensions={0} | all-to-all | bytes 131072 | tf_op jit(solution)/shard_map/all_to_all | solution.py:74
  121.3 1.4 %shard_map.85 = f32[256,1024]{1,0:T(8,128)} custom-call(f32[32,4,128]{2,1,0:T(4,128)S(1)} %all_to_all.27.received, f32[2,128]{1,0:T(2,128)S(1)} %get-tuple-element.19.row_root, f32[8,128]{1,0:T(8,128)S(1)} %get-tuple-element.20.col_root, f32[256,1024]{1,0:T(8,128)S(1)} %get-tuple-element.16.grad, f32[256,1024]{1,0:T(8,128)S(1)} %copy-done), custom_call_target="tpu_custom_call" | custom-call | flops 1048576 | bytes 3145728 | tf_op jit(solution)/shard_map/pallas_call | solution.py:257
  (10 shorter events, 0.0 us)
Async XLA Ops:
  2.7 14.8 %all-to-all-start = ((bf16[4,128,1024]{2,1,0:T(8,128)(2,1)}), bf16[4,128,1024]{2,1,0:T(8,128)(2,1)S(1)}, u32[]{:S(2)}, u32[]{:S(2)}) async-start(bf16[4,128,1024]{2,1,0:T(8,128)(2,1)} %broadcast_in_dim.3), calls=%async_computation | async-start | bytes 2097152 | tf_op jit(solution)/shard_map/all_to_all | solution.py:64
  17.4 17.4 %all-to-all-start.1 = ((bf16[16,64,512]{2,1,0:T(8,128)(2,1)}), bf16[16,64,512]{2,1,0:T(8,128)(2,1)S(1)}, u32[]{:S(2)}, u32[]{:S(2)}) async-start(bf16[16,64,512]{2,1,0:T(8,128)(2,1)} %shard_map.76), calls=%async_computation.1 | async-start | bytes 2097152 | tf_op jit(solution)/shard_map/all_to_all | solution.py:74
  22.3 26.8 %collective-permute-start.1 = (bf16[256,1024]{1,0:T(8,128)(2,1)S(1)}, bf16[256,1024]{1,0:T(8,128)(2,1)S(1)}, u32[]{:S(2)}, u32[]{:S(2)}) collective-permute-start(bf16[256,1024]{1,0:T(8,128)(2,1)S(1)} %bitcast.15), channel_id=1, source_target_pairs={{0,128},{16,48},{32,160},{48,80},{64,192},{80,112},{96,224},{112,1... | collective-permute-start | bytes 1572872 | tf_op jit(solution)/shard_map/ppermute | solution.py:57
  25.6 25.7 %collective-permute-start.4 = (bf16[256,1024]{1,0:T(8,128)(2,1)S(1)}, bf16[256,1024]{1,0:T(8,128)(2,1)S(1)}, u32[]{:S(2)}, u32[]{:S(2)}) collective-permute-start(bf16[256,1024]{1,0:T(8,128)(2,1)S(1)} %bitcast.10), channel_id=1, source_target_pairs={{0,384},{16,112},{32,416},{48,16},{64,448},{80,48},{96,480},{112,8... | collective-permute-start | bytes 1572872 | tf_op jit(solution)/shard_map/ppermute | solution.py:57
  28.8 28.3 %collective-permute-start.6 = (bf16[256,1024]{1,0:T(8,128)(2,1)S(1)}, bf16[256,1024]{1,0:T(8,128)(2,1)}, u32[]{:S(2)}, u32[]{:S(2)}) collective-permute-start(bf16[256,1024]{1,0:T(8,128)(2,1)S(1)} %bitcast.16), channel_id=1, source_target_pairs={{0,384},{16,112},{32,416},{48,16},{64,448},{80,48},{96,480},{112,8... | collective-permute-start | bytes 1572872 | tf_op jit(solution)/shard_map/ppermute | solution.py:57
  32.1 25.1 %collective-permute-start.2 = (bf16[256,1024]{1,0:T(8,128)(2,1)S(1)}, bf16[256,1024]{1,0:T(8,128)(2,1)}, u32[]{:S(2)}, u32[]{:S(2)}) collective-permute-start(bf16[256,1024]{1,0:T(8,128)(2,1)S(1)} %bitcast.11), channel_id=1, source_target_pairs={{0,128},{16,48},{32,160},{48,80},{64,192},{80,112},{96,224},{112,1... | collective-permute-start | bytes 1572872 | tf_op jit(solution)/shard_map/ppermute | solution.py:57
  35.8 26.0 %collective-permute-start = (bf16[512,1024]{1,0:T(8,128)(2,1)S(1)}, bf16[512,1024]{1,0:T(8,128)(2,1)S(1)}, u32[]{:S(2)}, u32[]{:S(2)}) collective-permute-start(bf16[512,1024]{1,0:T(8,128)(2,1)S(1)} %shard_map.77.first.second), channel_id=1, source_target_pairs={{0,1},{1,2},{2,3},{3,4},{4,5},{5,6},{6,7},{7,8},{8,9},{9,10},{10,1... | collective-permute-start | bytes 3145736 | tf_op jit(solution)/shard_map/ppermute | solution.py:70
  49.1 11.4 %collective-permute-start.3 = (bf16[256,1024]{1,0:T(8,128)(2,1)S(1)}, bf16[256,1024]{1,0:T(8,128)(2,1)S(1)}, u32[]{:S(2)}, u32[]{:S(2)}) collective-permute-start(bf16[256,1024]{1,0:T(8,128)(2,1)S(1)} %collective-permute-done.1.refs_0_.refs_2_), channel_id=1, source_target_pairs={{0,128},{16,48},{32,160},{48,80},{64,192},{80,112},{96,224},{112,1... | collective-permute-start | bytes 1572872 | tf_op jit(solution)/shard_map/ppermute | solution.py:57
  51.3 10.4 %collective-permute-start.5 = (bf16[256,1024]{1,0:T(8,128)(2,1)S(1)}, bf16[256,1024]{1,0:T(8,128)(2,1)S(1)}, u32[]{:S(2)}, u32[]{:S(2)}) collective-permute-start(bf16[256,1024]{1,0:T(8,128)(2,1)S(1)} %collective-permute-done.4.refs_3_.refs_7_), channel_id=1, source_target_pairs={{0,384},{16,112},{32,416},{48,16},{64,448},{80,48},{96,480},{112,8... | collective-permute-start | bytes 1572872 | tf_op jit(solution)/shard_map/ppermute | solution.py:57
  64.4 11.0 %collective-permute-start.7 = (f32[256,1024]{1,0:T(8,128)S(1)}, f32[256,1024]{1,0:T(8,128)S(1)}, u32[]{:S(2)}, u32[]{:S(2)}) collective-permute-start(f32[256,1024]{1,0:T(8,128)S(1)} %shard_map.81), channel_id=1, source_target_pairs={{0,16},{16,0},{1,17},{17,1},{2,18},{18,2},{3,19},{19,3},{4,20},{20... | collective-permute-start | bytes 3145736 | tf_op jit(solution)/shard_map/ppermute | solution.py:286
  75.4 10.8 %copy-start = (f32[256,1024]{1,0:T(8,128)S(1)}, f32[256,1024]{1,0:T(8,128)}, u32[]{:S(2)}) copy-start(f32[256,1024]{1,0:T(8,128)} %weight.3) | copy-start | bytes 3145732
  75.4 10.8 %copy-start.1 = (f32[1024]{0:T(1024)S(1)}, f32[1024]{0:T(1024)}, u32[]{:S(2)}) copy-start(f32[1024]{0:T(1024)} %param.9) | copy-start | bytes 12292
  75.4 32.8 %copy-start.2 = (f32[256]{0:T(256)S(1)}, f32[256]{0:T(256)}, u32[]{:S(2)}) copy-start(f32[256]{0:T(256)} %param.8) | copy-start | bytes 3076

commit v17 on v16

--- a/solution.py
+++ b/solution.py
@@ -52,14 +52,14 @@
     pairs = []
     for y in range(SIDE):
         for x in range(SIDE):
-            pairs.append((device(y, x, 0), device(y + step, x, 0)))
-            pairs.append((device(y, x, 1), device(y, x + step, 1)))
+            pairs.append((device(y, x, 0), device(y, x + step, 0)))
+            pairs.append((device(y, x, 1), device(y + step, x, 1)))
     return lax.ppermute(value, ROWS, pairs)
 
 
 def gather_line(value):
-    groups = [[device(y, x, 0) for x in range(SIDE)] for y in range(SIDE)]
-    groups += [[device(y, x, 1) for y in range(SIDE)] for x in range(SIDE)]
+    groups = [[device(y, x, 0) for y in range(SIDE)] for x in range(SIDE)]
+    groups += [[device(y, x, 1) for x in range(SIDE)] for y in range(SIDE)]
     sent = jnp.broadcast_to(value, (SIDE,) + value.shape)
     return lax.all_to_all(sent, ROWS, 0, 0, axis_index_groups=groups)
 
@@ -103,7 +103,7 @@
 
     def block(i):
         j, k = i // SIDE, i % SIDE
-        return part[jnp.where(core == 0, ((y - j) & (SIDE - 1)) * SIDE + k, k * SIDE + ((x - j) & (SIDE - 1)))]
+        return part[jnp.where(core == 1, ((y - j) & (SIDE - 1)) * SIDE + k, k * SIDE + ((x - j) & (SIDE - 1)))]
 
     for i in range(0, COUNT, 2):
         out[:, i * HALF : (i + 2) * HALF] = jnp.concatenate([block(i), block(i + 1)], axis=0).T

time: 123 us -> 122 us (level)
  starting transfers between devices: 49.8 us -> 47.5 us
    ppermute x1, starting transfers between devices: 8.39 us -> 6.03 us  [shards(): received = lax.ppermute(theirs, 'core', [(0, 1), (1, 0)])]
  transfers between devices with their start and end apart: 10 -> 10, of which waited for: 4 -> 4; matrix products, arithmetic and copies ran while one was open for 0% -> 0% of each run, Pallas kernels for 8% -> 9%
where the time goes in v17:
time: 122 us
  starting transfers between devices  47.5 us (39%)
  blocking collectives  45.3 us (37%)
  Pallas kernels  16.1 us (13%)
  waiting for transfers between devices  9.71 us (8%)
  local copies, waits for them, and re-layouts  2.15 us (2%)
    all_to_all x3, blocking collectives, exchange(): return lax.all_to_all(tiles, axes, 0, 0)  45.3 us
    ppermute x6, starting transfers between devices, along(): return lax.ppermute(value, ROWS, pairs)  18.3 us
    ppermute x1, starting transfers between devices, next_layer(): return lax.ppermute(value, ('core', 'z'), pairs)  13.3 us
    pallas_call x4, Pallas kernels, product(): pl.pallas_call(functools.partial(product_kernel, parts, which), out_shape...  9.2 us
    all_to_all x1, waiting for transfers between devices, gather_line(): return lax.all_to_all(sent, ROWS, 0, 0, axis_index_groups=groups)  6.76 us
    ppermute x1, starting transfers between devices, shards(): received = lax.ppermute(theirs, 'core', [(0, 1), (1, 0)])  6.03 us
    all_to_all x1, starting transfers between devices, exchange(): return lax.all_to_all(tiles, axes, 0, 0)  5.01 us
    all_to_all x1, starting transfers between devices, gather_line(): return lax.all_to_all(sent, ROWS, 0, 0, axis_index_groups=groups)  4.84 us
  transfers between devices with their start and end apart: 10, of which 4 were waited for; matrix products, arithmetic and copies ran while one was open for 0% of the time, Pallas kernels for 9%

profile of v17, /device:TPU:1, one launch (start us, length us, event | category | flops | bytes accessed | tf_op | source)
XLA Modules:
  0.0 121.7 jit_solution(15759448351129598506)
XLA Ops:
  0.6 2.1 %broadcast_in_dim.3 = bf16[4,128,1024]{2,1,0:T(8,128)(2,1)} broadcast(bf16[128,1024]{1,0:T(8,128)(2,1)} %param.6), dimensions={1,2} | broadcast | bytes 1310720 | tf_op jit(solution)/shard_map/broadcast_in_dim | solution.py:63
  2.7 4.8 %all-to-all-start = ((bf16[4,128,1024]{2,1,0:T(8,128)(2,1)}), bf16[4,128,1024]{2,1,0:T(8,128)(2,1)S(1)}, u32[]{:S(2)}, u32[]{:S(2)}) async-start(bf16[4,128,1024]{2,1,0:T(8,128)(2,1)} %broadcast_in_dim.3), calls=%async_computation | async-start | bytes 2097152 | tf_op jit(solution)/shard_map/all_to_all | solution.py:64
  7.5 0.1 pad_add_fusion.place
  7.6 2.9 %shard_map.76 = bf16[16,64,512]{2,1,0:T(8,128)(2,1)} custom-call(s32[4]{0:T(128)S(1)} %pad_add_fusion.place, bf16[128,8192]{1,0:T(8,128)(2,1)} %source.1), custom_call_target="tpu_custom_call" | custom-call | bytes 2097152 | tf_op jit(solution)/shard_map/pallas_call | solution.py:90
  10.5 6.8 %all-to-all-done = bf16[4,128,1024]{2,1,0:T(8,128)(2,1)S(1)} async-done(((bf16[4,128,1024]{2,1,0:T(8,128)(2,1)}), bf16[4,128,1024]{2,1,0:T(8,128)(2,1)S(1)}, u32[]{:S(2)}, u32[]{:S(2)}) %all-to-all-start) | async-done | bytes 1048608 | tf_op jit(solution)/shard_map/all_to_all | solution.py:64
  17.3 5.0 %all-to-all-start.1 = ((bf16[16,64,512]{2,1,0:T(8,128)(2,1)}), bf16[16,64,512]{2,1,0:T(8,128)(2,1)S(1)}, u32[]{:S(2)}, u32[]{:S(2)}) async-start(bf16[16,64,512]{2,1,0:T(8,128)(2,1)} %shard_map.76), calls=%async_computation.1 | async-start | bytes 2097152 | tf_op jit(solution)/shard_map/all_to_all | solution.py:74
  22.3 0.1 fusion
  22.4 3.3 %collective-permute-start.1 = (bf16[256,1024]{1,0:T(8,128)(2,1)S(1)}, bf16[256,1024]{1,0:T(8,128)(2,1)S(1)}, u32[]{:S(2)}, u32[]{:S(2)}) collective-permute-start(bf16[256,1024]{1,0:T(8,128)(2,1)S(1)} %bitcast.15), channel_id=1, source_target_pairs={{0,32},{16,144},{32,64},{48,176},{64,96},{80,208},{96,0},{112,240}... | collective-permute-start | bytes 1572872 | tf_op jit(solution)/shard_map/ppermute | solution.py:57
  25.7 3.2 %collective-permute-start.4 = (bf16[256,1024]{1,0:T(8,128)(2,1)S(1)}, bf16[256,1024]{1,0:T(8,128)(2,1)S(1)}, u32[]{:S(2)}, u32[]{:S(2)}) collective-permute-start(bf16[256,1024]{1,0:T(8,128)(2,1)S(1)} %bitcast.10), channel_id=1, source_target_pairs={{0,96},{16,400},{32,0},{48,432},{64,32},{80,464},{96,64},{112,496}... | collective-permute-start | bytes 1572872 | tf_op jit(solution)/shard_map/ppermute | solution.py:57
  28.9 3.3 %collective-permute-start.6 = (bf16[256,1024]{1,0:T(8,128)(2,1)S(1)}, bf16[256,1024]{1,0:T(8,128)(2,1)}, u32[]{:S(2)}, u32[]{:S(2)}) collective-permute-start(bf16[256,1024]{1,0:T(8,128)(2,1)S(1)} %bitcast.16), channel_id=1, source_target_pairs={{0,96},{16,400},{32,0},{48,432},{64,32},{80,464},{96,64},{112,496}... | collective-permute-start | bytes 1572872 | tf_op jit(solution)/shard_map/ppermute | solution.py:57
  32.2 2.0 %collective-permute-start.2 = (bf16[256,1024]{1,0:T(8,128)(2,1)S(1)}, bf16[256,1024]{1,0:T(8,128)(2,1)}, u32[]{:S(2)}, u32[]{:S(2)}) collective-permute-start(bf16[256,1024]{1,0:T(8,128)(2,1)S(1)} %bitcast.11), channel_id=1, source_target_pairs={{0,32},{16,144},{32,64},{48,176},{64,96},{80,208},{96,0},{112,240}... | collective-permute-start | bytes 1572872 | tf_op jit(solution)/shard_map/ppermute | solution.py:57
  34.2 0.9 all-to-all-done.1.part
  35.0 0.9 shard_map.77.first.second
  36.0 13.3 %collective-permute-start = (bf16[512,1024]{1,0:T(8,128)(2,1)S(1)}, bf16[512,1024]{1,0:T(8,128)(2,1)S(1)}, u32[]{:S(2)}, u32[]{:S(2)}) collective-permute-start(bf16[512,1024]{1,0:T(8,128)(2,1)S(1)} %shard_map.77.first.second), channel_id=1, source_target_pairs={{0,1},{1,2},{2,3},{3,4},{4,5},{5,6},{6,7},{7,8},{8,9},{9,10},{10,1... | collective-permute-start | bytes 3145736 | tf_op jit(solution)/shard_map/ppermute | solution.py:70
  49.3 2.0 %collective-permute-start.3 = (bf16[256,1024]{1,0:T(8,128)(2,1)S(1)}, bf16[256,1024]{1,0:T(8,128)(2,1)S(1)}, u32[]{:S(2)}, u32[]{:S(2)}) collective-permute-start(bf16[256,1024]{1,0:T(8,128)(2,1)S(1)} %collective-permute-done.1.refs_0_.refs_2_), channel_id=1, source_target_pairs={{0,32},{16,144},{32,64},{48,176},{64,96},{80,208},{96,0},{112,240}... | collective-permute-start | bytes 1572872 | tf_op jit(solution)/shard_map/ppermute | solution.py:57
  51.3 4.5 %collective-permute-start.5 = (bf16[256,1024]{1,0:T(8,128)(2,1)S(1)}, bf16[256,1024]{1,0:T(8,128)(2,1)S(1)}, u32[]{:S(2)}, u32[]{:S(2)}) collective-permute-start(bf16[256,1024]{1,0:T(8,128)(2,1)S(1)} %collective-permute-done.4.refs_3_.refs_7_), channel_id=1, source_target_pairs={{0,96},{16,400},{32,0},{48,432},{64,32},{80,464},{96,64},{112,496}... | collective-permute-start | bytes 1572872 | tf_op jit(solution)/shard_map/ppermute | solution.py:57
  55.8 1.5 %shard_map.78.refs_4_ = f32[512,1024]{1,0:T(8,128)S(1)} custom-call(s32[4]{0:T(128)S(1)} %pad_add_fusion.place, bf16[512,1024]{1,0:T(8,128)(2,1)S(1)} %shard_map.77.first.second, bf16[512,1024]{1,0:T(8,128)(2,1)S(1)} %shard_map.77.first.second, bf16[256,1024]{1,0:T(8,128)(2,1)S(1)} %bitcast.17, bf16[256,1024]{1,0:T(8,128)(2,1)S(1)} %bitcast.12), custom_call_target="tpu_custom_call" | custom-call | flops 3221225472 | bytes 1048576 | tf_op jit(solution)/shard_map/pallas_call | solution.py:146
  57.3 2.5 %shard_map.79.refs_8_ = f32[512,1024]{1,0:T(8,128)S(1)} custom-call(s32[4]{0:T(128)S(1)} %pad_add_fusion.place, bf16[512,1024]{1,0:T(8,128)(2,1)S(1)} %shard_map.77.first.second, bf16[512,1024]{1,0:T(8,128)(2,1)S(1)} %shard_map.77.first.second, bf16[256,1024]{1,0:T(8,128)(2,1)S(1)} %collective-permute-done.1.refs_0_.refs_2_, ...), custom_call_target="tpu_custom_call", output_to_operand_aliasing={{}: (7, {})} | custom-call | flops 6442450944 | bytes 1048576 | tf_op jit(solution)/shard_map/pallas_call | solution.py:146
  59.8 0.9 collective-permute-done.3.refs_4_
  60.7 1.2 collective-permute-done.5.refs_5_
  61.9 2.6 %shard_map.81 = f32[256,1024]{1,0:T(8,128)S(1)} custom-call(s32[4]{0:T(128)S(1)} %pad_add_fusion.place, bf16[512,1024]{1,0:T(8,128)(2,1)S(1)} %shard_map.77.first.second, bf16[512,1024]{1,0:T(8,128)(2,1)S(1)} %collective-permute-done.second, bf16[256,1024]{1,0:T(8,128)(2,1)S(1)} %bitcast.18, bf16[256,1024]{1,0:T(8,128)(2,1)S(1)} %bitcast.13, ...), custom_call_target="tpu_custom_call" | custom-call | flops 8053063680 | bytes 1048576 | tf_op jit(solution)/shard_map/pallas_call | solution.py:146
  64.5 6.0 %collective-permute-start.7 = (f32[256,1024]{1,0:T(8,128)S(1)}, f32[256,1024]{1,0:T(8,128)S(1)}, u32[]{:S(2)}, u32[]{:S(2)}) collective-permute-start(f32[256,1024]{1,0:T(8,128)S(1)} %shard_map.81), channel_id=1, source_target_pairs={{0,16},{16,0},{1,17},{17,1},{2,18},{18,2},{3,19},{19,3},{4,20},{20... | collective-permute-start | bytes 3145736 | tf_op jit(solution)/shard_map/ppermute | solution.py:286
  70.6 2.6 %shard_map.80.mine = f32[256,1024]{1,0:T(8,128)S(1)} custom-call(s32[4]{0:T(128)S(1)} %pad_add_fusion.place, bf16[512,1024]{1,0:T(8,128)(2,1)S(1)} %shard_map.77.first.second, bf16[512,1024]{1,0:T(8,128)(2,1)S(1)} %collective-permute-done.second, bf16[256,1024]{1,0:T(8,128)(2,1)S(1)} %bitcast.19, bf16[256,1024]{1,0:T(8,128)(2,1)S(1)} %bitcast.14, ...), custom_call_target="tpu_custom_call" | custom-call | flops 8053063680 | bytes 1048576 | tf_op jit(solution)/shard_map/pallas_call | solution.py:146
  73.2 0.0 copy-start
  73.2 0.0 copy-start.2
  73.3 0.1 shard_map.82
  73.4 11.3 %all_to_all.25.received = f32[32,8,128]{2,1,0:T(8,128)S(1)} all-to-all(f32[32,8,128]{2,1,0:T(8,128)S(1)} %get-tuple-element.15), channel_id=1, replica_groups=mesh['y'=4,'x'=4,'core'=2,'z'=16] {'y','x','core'}, dimensions={0} | all-to-all | bytes 262144 | tf_op jit(solution)/shard_map/all_to_all | solution.py:74
  84.7 1.0 shard_map.83
  85.6 21.5 %all_to_all.26.received = f32[16,8,128]{2,1,0:T(8,128)S(1)} all-to-all(f32[16,8,128]{2,1,0:T(8,128)S(1)} %get-tuple-element.17), channel_id=1, replica_groups=mesh['y'=4,'x'=4,'core'=2,'z'=16] {'z'}, dimensions={0} | all-to-all | bytes 131072 | tf_op jit(solution)/shard_map/all_to_all | solution.py:74
  107.1 0.6 shard_map.84
  107.7 12.5 %all_to_all.27.received = f32[32,4,128]{2,1,0:T(4,128)S(1)} all-to-all(f32[32,4,128]{2,1,0:T(4,128)S(1)} %get-tuple-element.18), channel_id=1, replica_groups=mesh['y'=4,'x'=4,'core'=2,'z'=16] {'y','x','core'}, dimensions={0} | all-to-all | bytes 131072 | tf_op jit(solution)/shard_map/all_to_all | solution.py:74
  120.3 1.4 %shard_map.85 = f32[256,1024]{1,0:T(8,128)} custom-call(f32[32,4,128]{2,1,0:T(4,128)S(1)} %all_to_all.27.received, f32[2,128]{1,0:T(2,128)S(1)} %get-tuple-element.19.row_root, f32[8,128]{1,0:T(8,128)S(1)} %get-tuple-element.20.col_root, f32[256,1024]{1,0:T(8,128)S(1)} %get-tuple-element.16.grad, f32[256,1024]{1,0:T(8,128)S(1)} %copy-done), custom_call_target="tpu_custom_call" | custom-call | flops 1048576 | bytes 3145728 | tf_op jit(solution)/shard_map/pallas_call | solution.py:257
  (10 shorter events, 0.0 us)
Async XLA Ops:
  2.7 14.6 %all-to-all-start = ((bf16[4,128,1024]{2,1,0:T(8,128)(2,1)}), bf16[4,128,1024]{2,1,0:T(8,128)(2,1)S(1)}, u32[]{:S(2)}, u32[]{:S(2)}) async-start(bf16[4,128,1024]{2,1,0:T(8,128)(2,1)} %broadcast_in_dim.3), calls=%async_computation | async-start | bytes 2097152 | tf_op jit(solution)/shard_map/all_to_all | solution.py:64
  17.3 17.8 %all-to-all-start.1 = ((bf16[16,64,512]{2,1,0:T(8,128)(2,1)}), bf16[16,64,512]{2,1,0:T(8,128)(2,1)S(1)}, u32[]{:S(2)}, u32[]{:S(2)}) async-start(bf16[16,64,512]{2,1,0:T(8,128)(2,1)} %shard_map.76), calls=%async_computation.1 | async-start | bytes 2097152 | tf_op jit(solution)/shard_map/all_to_all | solution.py:74
  22.4 26.9 %collective-permute-start.1 = (bf16[256,1024]{1,0:T(8,128)(2,1)S(1)}, bf16[256,1024]{1,0:T(8,128)(2,1)S(1)}, u32[]{:S(2)}, u32[]{:S(2)}) collective-permute-start(bf16[256,1024]{1,0:T(8,128)(2,1)S(1)} %bitcast.15), channel_id=1, source_target_pairs={{0,32},{16,144},{32,64},{48,176},{64,96},{80,208},{96,0},{112,240}... | collective-permute-start | bytes 1572872 | tf_op jit(solution)/shard_map/ppermute | solution.py:57
  25.7 25.7 %collective-permute-start.4 = (bf16[256,1024]{1,0:T(8,128)(2,1)S(1)}, bf16[256,1024]{1,0:T(8,128)(2,1)S(1)}, u32[]{:S(2)}, u32[]{:S(2)}) collective-permute-start(bf16[256,1024]{1,0:T(8,128)(2,1)S(1)} %bitcast.10), channel_id=1, source_target_pairs={{0,96},{16,400},{32,0},{48,432},{64,32},{80,464},{96,64},{112,496}... | collective-permute-start | bytes 1572872 | tf_op jit(solution)/shard_map/ppermute | solution.py:57
  28.9 28.4 %collective-permute-start.6 = (bf16[256,1024]{1,0:T(8,128)(2,1)S(1)}, bf16[256,1024]{1,0:T(8,128)(2,1)}, u32[]{:S(2)}, u32[]{:S(2)}) collective-permute-start(bf16[256,1024]{1,0:T(8,128)(2,1)S(1)} %bitcast.16), channel_id=1, source_target_pairs={{0,96},{16,400},{32,0},{48,432},{64,32},{80,464},{96,64},{112,496}... | collective-permute-start | bytes 1572872 | tf_op jit(solution)/shard_map/ppermute | solution.py:57
  32.2 25.2 %collective-permute-start.2 = (bf16[256,1024]{1,0:T(8,128)(2,1)S(1)}, bf16[256,1024]{1,0:T(8,128)(2,1)}, u32[]{:S(2)}, u32[]{:S(2)}) collective-permute-start(bf16[256,1024]{1,0:T(8,128)(2,1)S(1)} %bitcast.11), channel_id=1, source_target_pairs={{0,32},{16,144},{32,64},{48,176},{64,96},{80,208},{96,0},{112,240}... | collective-permute-start | bytes 1572872 | tf_op jit(solution)/shard_map/ppermute | solution.py:57
  36.0 26.0 %collective-permute-start = (bf16[512,1024]{1,0:T(8,128)(2,1)S(1)}, bf16[512,1024]{1,0:T(8,128)(2,1)S(1)}, u32[]{:S(2)}, u32[]{:S(2)}) collective-permute-start(bf16[512,1024]{1,0:T(8,128)(2,1)S(1)} %shard_map.77.first.second), channel_id=1, source_target_pairs={{0,1},{1,2},{2,3},{3,4},{4,5},{5,6},{6,7},{7,8},{8,9},{9,10},{10,1... | collective-permute-start | bytes 3145736 | tf_op jit(solution)/shard_map/ppermute | solution.py:70
  49.3 11.4 %collective-permute-start.3 = (bf16[256,1024]{1,0:T(8,128)(2,1)S(1)}, bf16[256,1024]{1,0:T(8,128)(2,1)S(1)}, u32[]{:S(2)}, u32[]{:S(2)}) collective-permute-start(bf16[256,1024]{1,0:T(8,128)(2,1)S(1)} %collective-permute-done.1.refs_0_.refs_2_), channel_id=1, source_target_pairs={{0,32},{16,144},{32,64},{48,176},{64,96},{80,208},{96,0},{112,240}... | collective-permute-start | bytes 1572872 | tf_op jit(solution)/shard_map/ppermute | solution.py:57
  51.3 10.6 %collective-permute-start.5 = (bf16[256,1024]{1,0:T(8,128)(2,1)S(1)}, bf16[256,1024]{1,0:T(8,128)(2,1)S(1)}, u32[]{:S(2)}, u32[]{:S(2)}) collective-permute-start(bf16[256,1024]{1,0:T(8,128)(2,1)S(1)} %collective-permute-done.4.refs_3_.refs_7_), channel_id=1, source_target_pairs={{0,96},{16,400},{32,0},{48,432},{64,32},{80,464},{96,64},{112,496}... | collective-permute-start | bytes 1572872 | tf_op jit(solution)/shard_map/ppermute | solution.py:57
  64.5 8.7 %collective-permute-start.7 = (f32[256,1024]{1,0:T(8,128)S(1)}, f32[256,1024]{1,0:T(8,128)S(1)}, u32[]{:S(2)}, u32[]{:S(2)}) collective-permute-start(f32[256,1024]{1,0:T(8,128)S(1)} %shard_map.81), channel_id=1, source_target_pairs={{0,16},{16,0},{1,17},{17,1},{2,18},{18,2},{3,19},{19,3},{4,20},{20... | collective-permute-start | bytes 3145736 | tf_op jit(solution)/shard_map/ppermute | solution.py:286
  73.2 11.4 %copy-start = (f32[256,1024]{1,0:T(8,128)S(1)}, f32[256,1024]{1,0:T(8,128)}, u32[]{:S(2)}) copy-start(f32[256,1024]{1,0:T(8,128)} %weight.3) | copy-start | bytes 3145732
  73.2 11.4 %copy-start.1 = (f32[1024]{0:T(1024)S(1)}, f32[1024]{0:T(1024)}, u32[]{:S(2)}) copy-start(f32[1024]{0:T(1024)} %param.9) | copy-start | bytes 12292
  73.2 33.9 %copy-start.2 = (f32[256]{0:T(256)S(1)}, f32[256]{0:T(256)}, u32[]{:S(2)}) copy-start(f32[256]{0:T(256)} %param.8) | copy-start | bytes 3076

commit v18 on v17

--- a/solution.py
+++ b/solution.py
@@ -27,7 +27,7 @@
 ROW_BLOCK = 256
 WIDTH = 1024
 LANES = 128
-COLUMNS = 256
+COLUMNS = 512
 TILE = (8, LANES)
 
 ANYWHERE = pl.BlockSpec(memory_space=pl.ANY)
@@ -126,9 +126,8 @@
     start = place[3] * HALF
     rows = pl.ds(0 if which is None else pl.multiple_of(which(place[2]) * ROW_BLOCK, ROW_BLOCK), out.shape[0])
 
-    @pl.loop(0, WIDTH // COLUMNS)
-    def _(n):
-        columns = pl.ds(pl.multiple_of(n * COLUMNS, COLUMNS), COLUMNS)
+    for n in range(WIDTH // COLUMNS):
+        columns = slice(n * COLUMNS, (n + 1) * COLUMNS)
         value = None if total is None else total[rows, columns]
         for group, exchanged, blocks in parts:
             depth = slice(group * SIDE * HALF, group * SIDE * HALF + len(blocks) * HALF)
@@ -242,13 +241,15 @@
     decay = trust_ratio * WEIGHT_DECAY
     copies = []
     for half in range(2):
-        here = slice(half * LANES, (half + 1) * LANES)
-        scale = jnp.broadcast_to(by_row[half : half + 1, :], (LANES, LANES)).T
-        for i in range(WIDTH // LANES):
-            lanes = slice(i * LANES, (i + 1) * LANES)
-            done[here, lanes] = grad[here, lanes] * by_col[i : i + 1, :] * scale + decay * weight[here, lanes]
-        copies.append(pltpu.make_async_copy(done.at[here], out.at[here], sems.at[half]))
-        copies[-1].start()
+        scales = jnp.broadcast_to(by_row[half : half + 1, :], (LANES, LANES)).T
+        for part in range(2):
+            scale = scales[part * HALF : (part + 1) * HALF]
+            here = slice(half * LANES + part * HALF, half * LANES + (part + 1) * HALF)
+            for i in range(WIDTH // LANES):
+                lanes = slice(i * LANES, (i + 1) * LANES)
+                done[here, lanes] = grad[here, lanes] * by_col[i : i + 1, :] * scale + decay * weight[here, lanes]
+            copies.append(pltpu.make_async_copy(done.at[here], out.at[here], sems.at[len(copies)]))
+            copies[-1].start()
     for copy in copies:
         copy.wait()
 
@@ -259,7 +260,7 @@
         out_shape=shape(ROW_BLOCK, WIDTH),
         in_specs=[WHOLE] * 5,
         out_specs=ANYWHERE,
-        scratch_shapes=[pltpu.VMEM((ROW_BLOCK, WIDTH), jnp.float32), pltpu.SemaphoreType.DMA((2,))],
+        scratch_shapes=[pltpu.VMEM((ROW_BLOCK, WIDTH), jnp.float32), pltpu.SemaphoreType.DMA((4,))],
         compiler_params=PARAMS,
         cost_estimate=cost(2**20, 3 * 2**20),
     )(received, row_root, col_root, grad, weight)

time: 122 us -> 122 us (level)
  Pallas kernels: 16.1 us -> 14 us
    pallas_call x4, Pallas kernels: 9.2 us -> 7.18 us  [product(): pl.pallas_call(functools.partial(product_kernel, parts, which), out_shape...]
  transfers between devices with their start and end apart: 10 -> 10, of which waited for: 4 -> 5; matrix products, arithmetic and copies ran while one was open for 0% -> 0% of each run, Pallas kernels for 9% -> 7%
where the time goes in v18:
time: 122 us; the launch traced here: 121 us
  starting transfers between devices  47.5 us (39%)
  blocking collectives  45.4 us (37%)
  Pallas kernels  14 us (11%)
  waiting for transfers between devices  10.8 us (9%)
  local copies, waits for them, and re-layouts  2.15 us (2%)
    all_to_all x3, blocking collectives, exchange(): return lax.all_to_all(tiles, axes, 0, 0)  45.4 us
    ppermute x6, starting transfers between devices, along(): return lax.ppermute(value, ROWS, pairs)  18.3 us
    ppermute x1, starting transfers between devices, next_layer(): return lax.ppermute(value, ('core', 'z'), pairs)  13.3 us
    pallas_call x4, Pallas kernels, product(): pl.pallas_call(functools.partial(product_kernel, parts, which), out_shape...  7.18 us
    all_to_all x1, waiting for transfers between devices, gather_line(): return lax.all_to_all(sent, ROWS, 0, 0, axis_index_groups=groups)  6.76 us
    ppermute x1, starting transfers between devices, shards(): received = lax.ppermute(theirs, 'core', [(0, 1), (1, 0)])  6.02 us
    all_to_all x1, starting transfers between devices, exchange(): return lax.all_to_all(tiles, axes, 0, 0)  5.01 us
    all_to_all x1, starting transfers between devices, gather_line(): return lax.all_to_all(sent, ROWS, 0, 0, axis_index_groups=groups)  4.84 us
  transfers between devices with their start and end apart: 10, of which 5 were waited for; matrix products, arithmetic and copies ran while one was open for 0% of the time, Pallas kernels for 7%

profile of v18, /device:TPU:1, one launch (start us, length us, event | category | flops | bytes accessed | tf_op | source)
XLA Modules:
  0.0 120.8 jit_solution(5825217615417037088)
XLA Ops:
  0.6 2.1 %broadcast_in_dim.3 = bf16[4,128,1024]{2,1,0:T(8,128)(2,1)} broadcast(bf16[128,1024]{1,0:T(8,128)(2,1)} %param.6), dimensions={1,2} | broadcast | bytes 1310720 | tf_op jit(solution)/shard_map/broadcast_in_dim | solution.py:63
  2.7 4.8 %all-to-all-start = ((bf16[4,128,1024]{2,1,0:T(8,128)(2,1)}), bf16[4,128,1024]{2,1,0:T(8,128)(2,1)S(1)}, u32[]{:S(2)}, u32[]{:S(2)}) async-start(bf16[4,128,1024]{2,1,0:T(8,128)(2,1)} %broadcast_in_dim.3), calls=%async_computation | async-start | bytes 2097152 | tf_op jit(solution)/shard_map/all_to_all | solution.py:64
  7.5 0.1 pad_add_fusion.place
  7.6 2.9 %shard_map.76 = bf16[16,64,512]{2,1,0:T(8,128)(2,1)} custom-call(s32[4]{0:T(128)S(1)} %pad_add_fusion.place, bf16[128,8192]{1,0:T(8,128)(2,1)} %source.1), custom_call_target="tpu_custom_call" | custom-call | bytes 2097152 | tf_op jit(solution)/shard_map/pallas_call | solution.py:90
  10.5 6.8 %all-to-all-done = bf16[4,128,1024]{2,1,0:T(8,128)(2,1)S(1)} async-done(((bf16[4,128,1024]{2,1,0:T(8,128)(2,1)}), bf16[4,128,1024]{2,1,0:T(8,128)(2,1)S(1)}, u32[]{:S(2)}, u32[]{:S(2)}) %all-to-all-start) | async-done | bytes 1048608 | tf_op jit(solution)/shard_map/all_to_all | solution.py:64
  17.3 5.0 %all-to-all-start.1 = ((bf16[16,64,512]{2,1,0:T(8,128)(2,1)}), bf16[16,64,512]{2,1,0:T(8,128)(2,1)S(1)}, u32[]{:S(2)}, u32[]{:S(2)}) async-start(bf16[16,64,512]{2,1,0:T(8,128)(2,1)} %shard_map.76), calls=%async_computation.1 | async-start | bytes 2097152 | tf_op jit(solution)/shard_map/all_to_all | solution.py:74
  22.3 0.1 fusion
  22.4 3.3 %collective-permute-start.1 = (bf16[256,1024]{1,0:T(8,128)(2,1)S(1)}, bf16[256,1024]{1,0:T(8,128)(2,1)S(1)}, u32[]{:S(2)}, u32[]{:S(2)}) collective-permute-start(bf16[256,1024]{1,0:T(8,128)(2,1)S(1)} %bitcast.15), channel_id=1, source_target_pairs={{0,32},{16,144},{32,64},{48,176},{64,96},{80,208},{96,0},{112,240}... | collective-permute-start | bytes 1572872 | tf_op jit(solution)/shard_map/ppermute | solution.py:57
  25.7 3.2 %collective-permute-start.4 = (bf16[256,1024]{1,0:T(8,128)(2,1)S(1)}, bf16[256,1024]{1,0:T(8,128)(2,1)S(1)}, u32[]{:S(2)}, u32[]{:S(2)}) collective-permute-start(bf16[256,1024]{1,0:T(8,128)(2,1)S(1)} %bitcast.10), channel_id=1, source_target_pairs={{0,96},{16,400},{32,0},{48,432},{64,32},{80,464},{96,64},{112,496}... | collective-permute-start | bytes 1572872 | tf_op jit(solution)/shard_map/ppermute | solution.py:57
  28.9 3.3 %collective-permute-start.6 = (bf16[256,1024]{1,0:T(8,128)(2,1)S(1)}, bf16[256,1024]{1,0:T(8,128)(2,1)}, u32[]{:S(2)}, u32[]{:S(2)}) collective-permute-start(bf16[256,1024]{1,0:T(8,128)(2,1)S(1)} %bitcast.16), channel_id=1, source_target_pairs={{0,96},{16,400},{32,0},{48,432},{64,32},{80,464},{96,64},{112,496}... | collective-permute-start | bytes 1572872 | tf_op jit(solution)/shard_map/ppermute | solution.py:57
  32.2 2.0 %collective-permute-start.2 = (bf16[256,1024]{1,0:T(8,128)(2,1)S(1)}, bf16[256,1024]{1,0:T(8,128)(2,1)}, u32[]{:S(2)}, u32[]{:S(2)}) collective-permute-start(bf16[256,1024]{1,0:T(8,128)(2,1)S(1)} %bitcast.11), channel_id=1, source_target_pairs={{0,32},{16,144},{32,64},{48,176},{64,96},{80,208},{96,0},{112,240}... | collective-permute-start | bytes 1572872 | tf_op jit(solution)/shard_map/ppermute | solution.py:57
  34.2 0.9 all-to-all-done.1.part
  35.0 0.9 shard_map.77.first.second
  36.0 13.3 %collective-permute-start = (bf16[512,1024]{1,0:T(8,128)(2,1)S(1)}, bf16[512,1024]{1,0:T(8,128)(2,1)S(1)}, u32[]{:S(2)}, u32[]{:S(2)}) collective-permute-start(bf16[512,1024]{1,0:T(8,128)(2,1)S(1)} %shard_map.77.first.second), channel_id=1, source_target_pairs={{0,1},{1,2},{2,3},{3,4},{4,5},{5,6},{6,7},{7,8},{8,9},{9,10},{10,1... | collective-permute-start | bytes 3145736 | tf_op jit(solution)/shard_map/ppermute | solution.py:70
  49.3 2.0 %collective-permute-start.3 = (bf16[256,1024]{1,0:T(8,128)(2,1)S(1)}, bf16[256,1024]{1,0:T(8,128)(2,1)S(1)}, u32[]{:S(2)}, u32[]{:S(2)}) collective-permute-start(bf16[256,1024]{1,0:T(8,128)(2,1)S(1)} %collective-permute-done.1.refs_0_.refs_2_), channel_id=1, source_target_pairs={{0,32},{16,144},{32,64},{48,176},{64,96},{80,208},{96,0},{112,240}... | collective-permute-start | bytes 1572872 | tf_op jit(solution)/shard_map/ppermute | solution.py:57
  51.3 4.5 %collective-permute-start.5 = (bf16[256,1024]{1,0:T(8,128)(2,1)S(1)}, bf16[256,1024]{1,0:T(8,128)(2,1)S(1)}, u32[]{:S(2)}, u32[]{:S(2)}) collective-permute-start(bf16[256,1024]{1,0:T(8,128)(2,1)S(1)} %collective-permute-done.4.refs_3_.refs_7_), channel_id=1, source_target_pairs={{0,96},{16,400},{32,0},{48,432},{64,32},{80,464},{96,64},{112,496}... | collective-permute-start | bytes 1572872 | tf_op jit(solution)/shard_map/ppermute | solution.py:57
  55.8 1.0 shard_map.78.refs_4_
  56.8 2.1 %shard_map.79.refs_8_ = f32[512,1024]{1,0:T(8,128)S(1)} custom-call(s32[4]{0:T(128)S(1)} %pad_add_fusion.place, bf16[512,1024]{1,0:T(8,128)(2,1)S(1)} %shard_map.77.first.second, bf16[512,1024]{1,0:T(8,128)(2,1)S(1)} %shard_map.77.first.second, bf16[256,1024]{1,0:T(8,128)(2,1)S(1)} %collective-permute-done.1.refs_0_.refs_2_, ...), custom_call_target="tpu_custom_call", output_to_operand_aliasing={{}: (7, {})} | custom-call | flops 6442450944 | bytes 1048576 | tf_op jit(solution)/shard_map/pallas_call | solution.py:145
  58.9 1.8 %collective-permute-done.3.refs_4_ = bf16[256,1024]{1,0:T(8,128)(2,1)S(1)} collective-permute-done((bf16[256,1024]{1,0:T(8,128)(2,1)S(1)}, bf16[256,1024]{1,0:T(8,128)(2,1)S(1)}, u32[]{:S(2)}, u32[]{:S(2)}) %collective-permute-start.3) | collective-permute-done | bytes 524320 | tf_op jit(solution)/shard_map/ppermute | solution.py:57
  60.7 1.2 collective-permute-done.5.refs_5_
  61.9 2.1 %shard_map.81 = f32[256,1024]{1,0:T(8,128)S(1)} custom-call(s32[4]{0:T(128)S(1)} %pad_add_fusion.place, bf16[512,1024]{1,0:T(8,128)(2,1)S(1)} %shard_map.77.first.second, bf16[512,1024]{1,0:T(8,128)(2,1)S(1)} %collective-permute-done.second, bf16[256,1024]{1,0:T(8,128)(2,1)S(1)} %bitcast.18, bf16[256,1024]{1,0:T(8,128)(2,1)S(1)} %bitcast.13, ...), custom_call_target="tpu_custom_call" | custom-call | flops 8053063680 | bytes 1048576 | tf_op jit(solution)/shard_map/pallas_call | solution.py:145
  64.0 6.0 %collective-permute-start.7 = (f32[256,1024]{1,0:T(8,128)S(1)}, f32[256,1024]{1,0:T(8,128)S(1)}, u32[]{:S(2)}, u32[]{:S(2)}) collective-permute-start(f32[256,1024]{1,0:T(8,128)S(1)} %shard_map.81), channel_id=1, source_target_pairs={{0,16},{16,0},{1,17},{17,1},{2,18},{18,2},{3,19},{19,3},{4,20},{20... | collective-permute-start | bytes 3145736 | tf_op jit(solution)/shard_map/ppermute | solution.py:287
  70.0 2.1 %shard_map.80.mine = f32[256,1024]{1,0:T(8,128)S(1)} custom-call(s32[4]{0:T(128)S(1)} %pad_add_fusion.place, bf16[512,1024]{1,0:T(8,128)(2,1)S(1)} %shard_map.77.first.second, bf16[512,1024]{1,0:T(8,128)(2,1)S(1)} %collective-permute-done.second, bf16[256,1024]{1,0:T(8,128)(2,1)S(1)} %bitcast.19, bf16[256,1024]{1,0:T(8,128)(2,1)S(1)} %bitcast.14, ...), custom_call_target="tpu_custom_call" | custom-call | flops 8053063680 | bytes 1048576 | tf_op jit(solution)/shard_map/pallas_call | solution.py:145
  72.1 0.0 copy-start
  72.1 0.2 collective-permute-done.7.theirs
  72.3 0.1 shard_map.82
  72.4 11.4 %all_to_all.25.received = f32[32,8,128]{2,1,0:T(8,128)S(1)} all-to-all(f32[32,8,128]{2,1,0:T(8,128)S(1)} %get-tuple-element.15), channel_id=1, replica_groups=mesh['y'=4,'x'=4,'core'=2,'z'=16] {'y','x','core'}, dimensions={0} | all-to-all | bytes 262144 | tf_op jit(solution)/shard_map/all_to_all | solution.py:74
  83.8 1.0 shard_map.83
  84.8 21.5 %all_to_all.26.received = f32[16,8,128]{2,1,0:T(8,128)S(1)} all-to-all(f32[16,8,128]{2,1,0:T(8,128)S(1)} %get-tuple-element.17), channel_id=1, replica_groups=mesh['y'=4,'x'=4,'core'=2,'z'=16] {'z'}, dimensions={0} | all-to-all | bytes 131072 | tf_op jit(solution)/shard_map/all_to_all | solution.py:74
  106.3 0.6 shard_map.84
  106.9 12.5 %all_to_all.27.received = f32[32,4,128]{2,1,0:T(4,128)S(1)} all-to-all(f32[32,4,128]{2,1,0:T(4,128)S(1)} %get-tuple-element.18), channel_id=1, replica_groups=mesh['y'=4,'x'=4,'core'=2,'z'=16] {'y','x','core'}, dimensions={0} | all-to-all | bytes 131072 | tf_op jit(solution)/shard_map/all_to_all | solution.py:74
  119.4 1.4 %shard_map.85 = f32[256,1024]{1,0:T(8,128)} custom-call(f32[32,4,128]{2,1,0:T(4,128)S(1)} %all_to_all.27.received, f32[2,128]{1,0:T(2,128)S(1)} %get-tuple-element.19.row_root, f32[8,128]{1,0:T(8,128)S(1)} %get-tuple-element.20.col_root, f32[256,1024]{1,0:T(8,128)S(1)} %get-tuple-element.16.grad, f32[256,1024]{1,0:T(8,128)S(1)} %copy-done), custom_call_target="tpu_custom_call" | custom-call | flops 1048576 | bytes 3145728 | tf_op jit(solution)/shard_map/pallas_call | solution.py:258
  (10 shorter events, 0.0 us)
Async XLA Ops:
  2.7 14.6 %all-to-all-start = ((bf16[4,128,1024]{2,1,0:T(8,128)(2,1)}), bf16[4,128,1024]{2,1,0:T(8,128)(2,1)S(1)}, u32[]{:S(2)}, u32[]{:S(2)}) async-start(bf16[4,128,1024]{2,1,0:T(8,128)(2,1)} %broadcast_in_dim.3), calls=%async_computation | async-start | bytes 2097152 | tf_op jit(solution)/shard_map/all_to_all | solution.py:64
  17.3 17.8 %all-to-all-start.1 = ((bf16[16,64,512]{2,1,0:T(8,128)(2,1)}), bf16[16,64,512]{2,1,0:T(8,128)(2,1)S(1)}, u32[]{:S(2)}, u32[]{:S(2)}) async-start(bf16[16,64,512]{2,1,0:T(8,128)(2,1)} %shard_map.76), calls=%async_computation.1 | async-start | bytes 2097152 | tf_op jit(solution)/shard_map/all_to_all | solution.py:74
  22.4 26.9 %collective-permute-start.1 = (bf16[256,1024]{1,0:T(8,128)(2,1)S(1)}, bf16[256,1024]{1,0:T(8,128)(2,1)S(1)}, u32[]{:S(2)}, u32[]{:S(2)}) collective-permute-start(bf16[256,1024]{1,0:T(8,128)(2,1)S(1)} %bitcast.15), channel_id=1, source_target_pairs={{0,32},{16,144},{32,64},{48,176},{64,96},{80,208},{96,0},{112,240}... | collective-permute-start | bytes 1572872 | tf_op jit(solution)/shard_map/ppermute | solution.py:57
  25.7 25.7 %collective-permute-start.4 = (bf16[256,1024]{1,0:T(8,128)(2,1)S(1)}, bf16[256,1024]{1,0:T(8,128)(2,1)S(1)}, u32[]{:S(2)}, u32[]{:S(2)}) collective-permute-start(bf16[256,1024]{1,0:T(8,128)(2,1)S(1)} %bitcast.10), channel_id=1, source_target_pairs={{0,96},{16,400},{32,0},{48,432},{64,32},{80,464},{96,64},{112,496}... | collective-permute-start | bytes 1572872 | tf_op jit(solution)/shard_map/ppermute | solution.py:57
  28.9 27.9 %collective-permute-start.6 = (bf16[256,1024]{1,0:T(8,128)(2,1)S(1)}, bf16[256,1024]{1,0:T(8,128)(2,1)}, u32[]{:S(2)}, u32[]{:S(2)}) collective-permute-start(bf16[256,1024]{1,0:T(8,128)(2,1)S(1)} %bitcast.16), channel_id=1, source_target_pairs={{0,96},{16,400},{32,0},{48,432},{64,32},{80,464},{96,64},{112,496}... | collective-permute-start | bytes 1572872 | tf_op jit(solution)/shard_map/ppermute | solution.py:57
  32.2 24.7 %collective-permute-start.2 = (bf16[256,1024]{1,0:T(8,128)(2,1)S(1)}, bf16[256,1024]{1,0:T(8,128)(2,1)}, u32[]{:S(2)}, u32[]{:S(2)}) collective-permute-start(bf16[256,1024]{1,0:T(8,128)(2,1)S(1)} %bitcast.11), channel_id=1, source_target_pairs={{0,32},{16,144},{32,64},{48,176},{64,96},{80,208},{96,0},{112,240}... | collective-permute-start | bytes 1572872 | tf_op jit(solution)/shard_map/ppermute | solution.py:57
  36.0 26.0 %collective-permute-start = (bf16[512,1024]{1,0:T(8,128)(2,1)S(1)}, bf16[512,1024]{1,0:T(8,128)(2,1)S(1)}, u32[]{:S(2)}, u32[]{:S(2)}) collective-permute-start(bf16[512,1024]{1,0:T(8,128)(2,1)S(1)} %shard_map.77.first.second), channel_id=1, source_target_pairs={{0,1},{1,2},{2,3},{3,4},{4,5},{5,6},{6,7},{7,8},{8,9},{9,10},{10,1... | collective-permute-start | bytes 3145736 | tf_op jit(solution)/shard_map/ppermute | solution.py:70
  49.3 11.4 %collective-permute-start.3 = (bf16[256,1024]{1,0:T(8,128)(2,1)S(1)}, bf16[256,1024]{1,0:T(8,128)(2,1)S(1)}, u32[]{:S(2)}, u32[]{:S(2)}) collective-permute-start(bf16[256,1024]{1,0:T(8,128)(2,1)S(1)} %collective-permute-done.1.refs_0_.refs_2_), channel_id=1, source_target_pairs={{0,32},{16,144},{32,64},{48,176},{64,96},{80,208},{96,0},{112,240}... | collective-permute-start | bytes 1572872 | tf_op jit(solution)/shard_map/ppermute | solution.py:57
  51.3 10.6 %collective-permute-start.5 = (bf16[256,1024]{1,0:T(8,128)(2,1)S(1)}, bf16[256,1024]{1,0:T(8,128)(2,1)S(1)}, u32[]{:S(2)}, u32[]{:S(2)}) collective-permute-start(bf16[256,1024]{1,0:T(8,128)(2,1)S(1)} %collective-permute-done.4.refs_3_.refs_7_), channel_id=1, source_target_pairs={{0,96},{16,400},{32,0},{48,432},{64,32},{80,464},{96,64},{112,496}... | collective-permute-start | bytes 1572872 | tf_op jit(solution)/shard_map/ppermute | solution.py:57
  64.0 8.3 %collective-permute-start.7 = (f32[256,1024]{1,0:T(8,128)S(1)}, f32[256,1024]{1,0:T(8,128)S(1)}, u32[]{:S(2)}, u32[]{:S(2)}) collective-permute-start(f32[256,1024]{1,0:T(8,128)S(1)} %shard_map.81), channel_id=1, source_target_pairs={{0,16},{16,0},{1,17},{17,1},{2,18},{18,2},{3,19},{19,3},{4,20},{20... | collective-permute-start | bytes 3145736 | tf_op jit(solution)/shard_map/ppermute | solution.py:287
  72.1 11.7 %copy-start = (f32[256,1024]{1,0:T(8,128)S(1)}, f32[256,1024]{1,0:T(8,128)}, u32[]{:S(2)}) copy-start(f32[256,1024]{1,0:T(8,128)} %weight.3) | copy-start | bytes 3145732
  72.1 11.7 %copy-start.1 = (f32[1024]{0:T(1024)S(1)}, f32[1024]{0:T(1024)}, u32[]{:S(2)}) copy-start(f32[1024]{0:T(1024)} %param.9) | copy-start | bytes 12292
  72.1 34.2 %copy-start.2 = (f32[256]{0:T(256)S(1)}, f32[256]{0:T(256)}, u32[]{:S(2)}) copy-start(f32[256]{0:T(256)} %param.8) | copy-start | bytes 3076

commit v19 on v18

--- a/solution.py
+++ b/solution.py
@@ -271,8 +271,8 @@
     place = jnp.stack([y, x, core, layer & 1])
     line = gather_line(out_grads)
     packed, line = lax.optimization_barrier((pack(place, activations), line))
-    first = turn(place, exchange(packed, CHIPS))
-    second = next_layer(first)
+    first = exchange(packed, CHIPS)
+    first, second = turn(place, first), turn(place, next_layer(first))
     low, high = (line[i : i + 2].reshape(2 * TOKENS, WIDTH) for i in (0, 2))
     back_low, ahead_high = along(low, 1), along(high, SIDE - 1)
     far = [along(back_low, 1), along(ahead_high, SIDE - 1)]

time: 122 us -> 122 us (level)
  waiting for transfers between devices: 10.8 us -> 8.97 us
    ppermute x6, waiting for transfers between devices: 3.03 us -> 0.02 us  [along(): return lax.ppermute(value, ROWS, pairs)]
  transfers between devices with their start and end apart: 10 -> 10, of which waited for: 5 -> 4; matrix products, arithmetic and copies ran while one was open for 0% -> 0% of each run, Pallas kernels for 7% -> 8%
where the time goes in v19:
time: 122 us; the launch traced here: 121 us
  starting transfers between devices  48.4 us (40%)
  blocking collectives  45.4 us (37%)
  Pallas kernels  14.9 us (12%)
  waiting for transfers between devices  8.97 us (7%)
  local copies, waits for them, and re-layouts  2.15 us (2%)
    all_to_all x3, blocking collectives, exchange(): return lax.all_to_all(tiles, axes, 0, 0)  45.4 us
    ppermute x6, starting transfers between devices, along(): return lax.ppermute(value, ROWS, pairs)  18.3 us
    ppermute x1, starting transfers between devices, next_layer(): return lax.ppermute(value, ('core', 'z'), pairs)  13.3 us
    pallas_call x4, Pallas kernels, product(): pl.pallas_call(functools.partial(product_kernel, parts, which), out_shape...  7.19 us
    ppermute x1, starting transfers between devices, shards(): received = lax.ppermute(theirs, 'core', [(0, 1), (1, 0)])  6.94 us
    all_to_all x1, waiting for transfers between devices, gather_line(): return lax.all_to_all(sent, ROWS, 0, 0, axis_index_groups=groups)  6.76 us
    all_to_all x1, starting transfers between devices, exchange(): return lax.all_to_all(tiles, axes, 0, 0)  5.01 us
    all_to_all x1, starting transfers between devices, gather_line(): return lax.all_to_all(sent, ROWS, 0, 0, axis_index_groups=groups)  4.84 us
  transfers between devices with their start and end apart: 10, of which 4 were waited for; matrix products, arithmetic and copies ran while one was open for 0% of the time, Pallas kernels for 8%

profile of v19, /device:TPU:1, one launch (start us, length us, event | category | flops | bytes accessed | tf_op | source)
XLA Modules:
  0.0 120.8 jit_solution(6548809617331176581)
XLA Ops:
  0.6 2.1 %broadcast_in_dim.3 = bf16[4,128,1024]{2,1,0:T(8,128)(2,1)} broadcast(bf16[128,1024]{1,0:T(8,128)(2,1)} %param.6), dimensions={1,2} | broadcast | bytes 1310720 | tf_op jit(solution)/shard_map/broadcast_in_dim | solution.py:63
  2.7 4.8 %all-to-all-start = ((bf16[4,128,1024]{2,1,0:T(8,128)(2,1)}), bf16[4,128,1024]{2,1,0:T(8,128)(2,1)S(1)}, u32[]{:S(2)}, u32[]{:S(2)}) async-start(bf16[4,128,1024]{2,1,0:T(8,128)(2,1)} %broadcast_in_dim.3), calls=%async_computation | async-start | bytes 2097152 | tf_op jit(solution)/shard_map/all_to_all | solution.py:64
  7.5 0.1 pad_add_fusion.place
  7.6 2.9 %shard_map.76 = bf16[16,64,512]{2,1,0:T(8,128)(2,1)} custom-call(s32[4]{0:T(128)S(1)} %pad_add_fusion.place, bf16[128,8192]{1,0:T(8,128)(2,1)} %source.1), custom_call_target="tpu_custom_call" | custom-call | bytes 2097152 | tf_op jit(solution)/shard_map/pallas_call | solution.py:90
  10.5 6.8 %all-to-all-done = bf16[4,128,1024]{2,1,0:T(8,128)(2,1)S(1)} async-done(((bf16[4,128,1024]{2,1,0:T(8,128)(2,1)}), bf16[4,128,1024]{2,1,0:T(8,128)(2,1)S(1)}, u32[]{:S(2)}, u32[]{:S(2)}) %all-to-all-start) | async-done | bytes 1048608 | tf_op jit(solution)/shard_map/all_to_all | solution.py:64
  17.3 5.0 %all-to-all-start.1 = ((bf16[16,64,512]{2,1,0:T(8,128)(2,1)}), bf16[16,64,512]{2,1,0:T(8,128)(2,1)S(1)}, u32[]{:S(2)}, u32[]{:S(2)}) async-start(bf16[16,64,512]{2,1,0:T(8,128)(2,1)} %shard_map.76), calls=%async_computation.1 | async-start | bytes 2097152 | tf_op jit(solution)/shard_map/all_to_all | solution.py:74
  22.3 0.1 fusion
  22.4 3.3 %collective-permute-start.1 = (bf16[256,1024]{1,0:T(8,128)(2,1)S(1)}, bf16[256,1024]{1,0:T(8,128)(2,1)S(1)}, u32[]{:S(2)}, u32[]{:S(2)}) collective-permute-start(bf16[256,1024]{1,0:T(8,128)(2,1)S(1)} %bitcast.15), channel_id=1, source_target_pairs={{0,32},{16,144},{32,64},{48,176},{64,96},{80,208},{96,0},{112,240}... | collective-permute-start | bytes 1572872 | tf_op jit(solution)/shard_map/ppermute | solution.py:57
  25.7 3.2 %collective-permute-start.4 = (bf16[256,1024]{1,0:T(8,128)(2,1)S(1)}, bf16[256,1024]{1,0:T(8,128)(2,1)S(1)}, u32[]{:S(2)}, u32[]{:S(2)}) collective-permute-start(bf16[256,1024]{1,0:T(8,128)(2,1)S(1)} %bitcast.10), channel_id=1, source_target_pairs={{0,96},{16,400},{32,0},{48,432},{64,32},{80,464},{96,64},{112,496}... | collective-permute-start | bytes 1572872 | tf_op jit(solution)/shard_map/ppermute | solution.py:57
  28.9 3.3 %collective-permute-start.6 = (bf16[256,1024]{1,0:T(8,128)(2,1)S(1)}, bf16[256,1024]{1,0:T(8,128)(2,1)}, u32[]{:S(2)}, u32[]{:S(2)}) collective-permute-start(bf16[256,1024]{1,0:T(8,128)(2,1)S(1)} %bitcast.16), channel_id=1, source_target_pairs={{0,96},{16,400},{32,0},{48,432},{64,32},{80,464},{96,64},{112,496}... | collective-permute-start | bytes 1572872 | tf_op jit(solution)/shard_map/ppermute | solution.py:57
  32.2 2.0 %collective-permute-start.2 = (bf16[256,1024]{1,0:T(8,128)(2,1)S(1)}, bf16[256,1024]{1,0:T(8,128)(2,1)}, u32[]{:S(2)}, u32[]{:S(2)}) collective-permute-start(bf16[256,1024]{1,0:T(8,128)(2,1)S(1)} %bitcast.11), channel_id=1, source_target_pairs={{0,32},{16,144},{32,64},{48,176},{64,96},{80,208},{96,0},{112,240}... | collective-permute-start | bytes 1572872 | tf_op jit(solution)/shard_map/ppermute | solution.py:57
  34.2 0.9 all-to-all-done.1.part
  35.0 13.3 %collective-permute-start = (bf16[16,64,512]{2,1,0:T(8,128)(2,1)S(1)}, bf16[16,64,512]{2,1,0:T(8,128)(2,1)S(1)}, u32[]{:S(2)}, u32[]{:S(2)}) collective-permute-start(bf16[16,64,512]{2,1,0:T(8,128)(2,1)S(1)} %all-to-all-done.1.part), channel_id=1, source_target_pairs={{0,1},{1,2},{2,3},{3,4},{4,5},{5,6},{6,7},{7,8},{8,9},{9,10},{10,1... | collective-permute-start | bytes 3145736 | tf_op jit(solution)/shard_map/ppermute | solution.py:70
  48.4 2.0 %collective-permute-start.3 = (bf16[256,1024]{1,0:T(8,128)(2,1)S(1)}, bf16[256,1024]{1,0:T(8,128)(2,1)S(1)}, u32[]{:S(2)}, u32[]{:S(2)}) collective-permute-start(bf16[256,1024]{1,0:T(8,128)(2,1)S(1)} %collective-permute-done.1.refs_0_.refs_2_), channel_id=1, source_target_pairs={{0,32},{16,144},{32,64},{48,176},{64,96},{80,208},{96,0},{112,240}... | collective-permute-start | bytes 1572872 | tf_op jit(solution)/shard_map/ppermute | solution.py:57
  50.4 4.5 %collective-permute-start.5 = (bf16[256,1024]{1,0:T(8,128)(2,1)S(1)}, bf16[256,1024]{1,0:T(8,128)(2,1)S(1)}, u32[]{:S(2)}, u32[]{:S(2)}) collective-permute-start(bf16[256,1024]{1,0:T(8,128)(2,1)S(1)} %collective-permute-done.4.refs_3_.refs_7_), channel_id=1, source_target_pairs={{0,96},{16,400},{32,0},{48,432},{64,32},{80,464},{96,64},{112,496}... | collective-permute-start | bytes 1572872 | tf_op jit(solution)/shard_map/ppermute | solution.py:57
  54.9 0.9 shard_map.77.first.second
  55.8 1.0 shard_map.79.refs_4_
  56.8 2.1 %shard_map.80.refs_8_ = f32[512,1024]{1,0:T(8,128)S(1)} custom-call(s32[4]{0:T(128)S(1)} %pad_add_fusion.place, bf16[512,1024]{1,0:T(8,128)(2,1)S(1)} %shard_map.77.first.second, bf16[512,1024]{1,0:T(8,128)(2,1)S(1)} %shard_map.77.first.second, bf16[256,1024]{1,0:T(8,128)(2,1)S(1)} %collective-permute-done.1.refs_0_.refs_2_, ...), custom_call_target="tpu_custom_call", output_to_operand_aliasing={{}: (7, {})} | custom-call | flops 6442450944 | bytes 1048576 | tf_op jit(solution)/shard_map/pallas_call | solution.py:145
  58.9 1.2 collective-permute-done.part
  60.1 0.9 shard_map.78.second
  61.0 2.1 %shard_map.82 = f32[256,1024]{1,0:T(8,128)S(1)} custom-call(s32[4]{0:T(128)S(1)} %pad_add_fusion.place, bf16[512,1024]{1,0:T(8,128)(2,1)S(1)} %shard_map.77.first.second, bf16[512,1024]{1,0:T(8,128)(2,1)S(1)} %shard_map.78.second, bf16[256,1024]{1,0:T(8,128)(2,1)S(1)} %bitcast.18, bf16[256,1024]{1,0:T(8,128)(2,1)S(1)} %bitcast.13, ...), custom_call_target="tpu_custom_call" | custom-call | flops 8053063680 | bytes 1048576 | tf_op jit(solution)/shard_map/pallas_call | solution.py:145
  63.1 6.9 %collective-permute-start.7 = (f32[256,1024]{1,0:T(8,128)S(1)}, f32[256,1024]{1,0:T(8,128)S(1)}, u32[]{:S(2)}, u32[]{:S(2)}) collective-permute-start(f32[256,1024]{1,0:T(8,128)S(1)} %shard_map.82), channel_id=1, source_target_pairs={{0,16},{16,0},{1,17},{17,1},{2,18},{18,2},{3,19},{19,3},{4,20},{20... | collective-permute-start | bytes 3145736 | tf_op jit(solution)/shard_map/ppermute | solution.py:287
  70.0 2.1 %shard_map.81.mine = f32[256,1024]{1,0:T(8,128)S(1)} custom-call(s32[4]{0:T(128)S(1)} %pad_add_fusion.place, bf16[512,1024]{1,0:T(8,128)(2,1)S(1)} %shard_map.77.first.second, bf16[512,1024]{1,0:T(8,128)(2,1)S(1)} %shard_map.78.second, bf16[256,1024]{1,0:T(8,128)(2,1)S(1)} %bitcast.19, bf16[256,1024]{1,0:T(8,128)(2,1)S(1)} %bitcast.14, ...), custom_call_target="tpu_custom_call" | custom-call | flops 8053063680 | bytes 1048576 | tf_op jit(solution)/shard_map/pallas_call | solution.py:145
  72.1 0.0 copy-start.1
  72.2 0.2 collective-permute-done.7.theirs
  72.3 0.1 shard_map.83
  72.4 11.4 %all_to_all.25.received = f32[32,8,128]{2,1,0:T(8,128)S(1)} all-to-all(f32[32,8,128]{2,1,0:T(8,128)S(1)} %get-tuple-element.15), channel_id=1, replica_groups=mesh['y'=4,'x'=4,'core'=2,'z'=16] {'y','x','core'}, dimensions={0} | all-to-all | bytes 262144 | tf_op jit(solution)/shard_map/all_to_all | solution.py:74
  83.9 1.0 shard_map.84
  84.8 21.5 %all_to_all.26.received = f32[16,8,128]{2,1,0:T(8,128)S(1)} all-to-all(f32[16,8,128]{2,1,0:T(8,128)S(1)} %get-tuple-element.17), channel_id=1, replica_groups=mesh['y'=4,'x'=4,'core'=2,'z'=16] {'z'}, dimensions={0} | all-to-all | bytes 131072 | tf_op jit(solution)/shard_map/all_to_all | solution.py:74
  106.3 0.6 shard_map.85
  106.9 12.5 %all_to_all.27.received = f32[32,4,128]{2,1,0:T(4,128)S(1)} all-to-all(f32[32,4,128]{2,1,0:T(4,128)S(1)} %get-tuple-element.18), channel_id=1, replica_groups=mesh['y'=4,'x'=4,'core'=2,'z'=16] {'y','x','core'}, dimensions={0} | all-to-all | bytes 131072 | tf_op jit(solution)/shard_map/all_to_all | solution.py:74
  119.4 1.4 %shard_map.86 = f32[256,1024]{1,0:T(8,128)} custom-call(f32[32,4,128]{2,1,0:T(4,128)S(1)} %all_to_all.27.received, f32[2,128]{1,0:T(2,128)S(1)} %get-tuple-element.19.row_root, f32[8,128]{1,0:T(8,128)S(1)} %get-tuple-element.20.col_root, f32[256,1024]{1,0:T(8,128)S(1)} %get-tuple-element.16.grad, f32[256,1024]{1,0:T(8,128)S(1)} %copy-done), custom_call_target="tpu_custom_call" | custom-call | flops 1048576 | bytes 3145728 | tf_op jit(solution)/shard_map/pallas_call | solution.py:258
  (11 shorter events, 0.0 us)
Async XLA Ops:
  2.7 14.6 %all-to-all-start = ((bf16[4,128,1024]{2,1,0:T(8,128)(2,1)}), bf16[4,128,1024]{2,1,0:T(8,128)(2,1)S(1)}, u32[]{:S(2)}, u32[]{:S(2)}) async-start(bf16[4,128,1024]{2,1,0:T(8,128)(2,1)} %broadcast_in_dim.3), calls=%async_computation | async-start | bytes 2097152 | tf_op jit(solution)/shard_map/all_to_all | solution.py:64
  17.3 17.8 %all-to-all-start.1 = ((bf16[16,64,512]{2,1,0:T(8,128)(2,1)}), bf16[16,64,512]{2,1,0:T(8,128)(2,1)S(1)}, u32[]{:S(2)}, u32[]{:S(2)}) async-start(bf16[16,64,512]{2,1,0:T(8,128)(2,1)} %shard_map.76), calls=%async_computation.1 | async-start | bytes 2097152 | tf_op jit(solution)/shard_map/all_to_all | solution.py:74
  22.4 26.0 %collective-permute-start.1 = (bf16[256,1024]{1,0:T(8,128)(2,1)S(1)}, bf16[256,1024]{1,0:T(8,128)(2,1)S(1)}, u32[]{:S(2)}, u32[]{:S(2)}) collective-permute-start(bf16[256,1024]{1,0:T(8,128)(2,1)S(1)} %bitcast.15), channel_id=1, source_target_pairs={{0,32},{16,144},{32,64},{48,176},{64,96},{80,208},{96,0},{112,240}... | collective-permute-start | bytes 1572872 | tf_op jit(solution)/shard_map/ppermute | solution.py:57
  25.7 24.7 %collective-permute-start.4 = (bf16[256,1024]{1,0:T(8,128)(2,1)S(1)}, bf16[256,1024]{1,0:T(8,128)(2,1)S(1)}, u32[]{:S(2)}, u32[]{:S(2)}) collective-permute-start(bf16[256,1024]{1,0:T(8,128)(2,1)S(1)} %bitcast.10), channel_id=1, source_target_pairs={{0,96},{16,400},{32,0},{48,432},{64,32},{80,464},{96,64},{112,496}... | collective-permute-start | bytes 1572872 | tf_op jit(solution)/shard_map/ppermute | solution.py:57
  28.9 27.9 %collective-permute-start.6 = (bf16[256,1024]{1,0:T(8,128)(2,1)S(1)}, bf16[256,1024]{1,0:T(8,128)(2,1)}, u32[]{:S(2)}, u32[]{:S(2)}) collective-permute-start(bf16[256,1024]{1,0:T(8,128)(2,1)S(1)} %bitcast.16), channel_id=1, source_target_pairs={{0,96},{16,400},{32,0},{48,432},{64,32},{80,464},{96,64},{112,496}... | collective-permute-start | bytes 1572872 | tf_op jit(solution)/shard_map/ppermute | solution.py:57
  32.2 24.6 %collective-permute-start.2 = (bf16[256,1024]{1,0:T(8,128)(2,1)S(1)}, bf16[256,1024]{1,0:T(8,128)(2,1)}, u32[]{:S(2)}, u32[]{:S(2)}) collective-permute-start(bf16[256,1024]{1,0:T(8,128)(2,1)S(1)} %bitcast.11), channel_id=1, source_target_pairs={{0,32},{16,144},{32,64},{48,176},{64,96},{80,208},{96,0},{112,240}... | collective-permute-start | bytes 1572872 | tf_op jit(solution)/shard_map/ppermute | solution.py:57
  35.0 25.1 %collective-permute-start = (bf16[16,64,512]{2,1,0:T(8,128)(2,1)S(1)}, bf16[16,64,512]{2,1,0:T(8,128)(2,1)S(1)}, u32[]{:S(2)}, u32[]{:S(2)}) collective-permute-start(bf16[16,64,512]{2,1,0:T(8,128)(2,1)S(1)} %all-to-all-done.1.part), channel_id=1, source_target_pairs={{0,1},{1,2},{2,3},{3,4},{4,5},{5,6},{6,7},{7,8},{8,9},{9,10},{10,1... | collective-permute-start | bytes 3145736 | tf_op jit(solution)/shard_map/ppermute | solution.py:70
  48.4 12.6 %collective-permute-start.3 = (bf16[256,1024]{1,0:T(8,128)(2,1)S(1)}, bf16[256,1024]{1,0:T(8,128)(2,1)S(1)}, u32[]{:S(2)}, u32[]{:S(2)}) collective-permute-start(bf16[256,1024]{1,0:T(8,128)(2,1)S(1)} %collective-permute-done.1.refs_0_.refs_2_), channel_id=1, source_target_pairs={{0,32},{16,144},{32,64},{48,176},{64,96},{80,208},{96,0},{112,240}... | collective-permute-start | bytes 1572872 | tf_op jit(solution)/shard_map/ppermute | solution.py:57
  50.4 10.6 %collective-permute-start.5 = (bf16[256,1024]{1,0:T(8,128)(2,1)S(1)}, bf16[256,1024]{1,0:T(8,128)(2,1)S(1)}, u32[]{:S(2)}, u32[]{:S(2)}) collective-permute-start(bf16[256,1024]{1,0:T(8,128)(2,1)S(1)} %collective-permute-done.4.refs_3_.refs_7_), channel_id=1, source_target_pairs={{0,96},{16,400},{32,0},{48,432},{64,32},{80,464},{96,64},{112,496}... | collective-permute-start | bytes 1572872 | tf_op jit(solution)/shard_map/ppermute | solution.py:57
  63.1 9.2 %collective-permute-start.7 = (f32[256,1024]{1,0:T(8,128)S(1)}, f32[256,1024]{1,0:T(8,128)S(1)}, u32[]{:S(2)}, u32[]{:S(2)}) collective-permute-start(f32[256,1024]{1,0:T(8,128)S(1)} %shard_map.82), channel_id=1, source_target_pairs={{0,16},{16,0},{1,17},{17,1},{2,18},{18,2},{3,19},{19,3},{4,20},{20... | collective-permute-start | bytes 3145736 | tf_op jit(solution)/shard_map/ppermute | solution.py:287
  72.1 11.7 %copy-start = (f32[256,1024]{1,0:T(8,128)S(1)}, f32[256,1024]{1,0:T(8,128)}, u32[]{:S(2)}) copy-start(f32[256,1024]{1,0:T(8,128)} %weight.3) | copy-start | bytes 3145732
  72.1 11.7 %copy-start.1 = (f32[1024]{0:T(1024)S(1)}, f32[1024]{0:T(1024)}, u32[]{:S(2)}) copy-start(f32[1024]{0:T(1024)} %param.9) | copy-start | bytes 12292
  72.1 34.1 %copy-start.2 = (f32[256]{0:T(256)S(1)}, f32[256]{0:T(256)}, u32[]{:S(2)}) copy-start(f32[256]{0:T(256)} %param.8) | copy-start | bytes 3076

commit v20 on v19

--- a/solution.py
+++ b/solution.py
@@ -27,6 +27,7 @@
 ROW_BLOCK = 256
 WIDTH = 1024
 LANES = 128
+GROUPS = (0, 2, 1, 3)
 COLUMNS = 512
 TILE = (8, LANES)
 
@@ -102,7 +103,7 @@
     y, x, core = place[0], place[1], place[2]
 
     def block(i):
-        j, k = i // SIDE, i % SIDE
+        j, k = GROUPS[i // SIDE], i % SIDE
         return part[jnp.where(core == 1, ((y - j) & (SIDE - 1)) * SIDE + k, k * SIDE + ((x - j) & (SIDE - 1)))]
 
     for i in range(0, COUNT, 2):
@@ -120,15 +121,20 @@
     )(place, part)
 
 
-def product_kernel(parts, which, place, first, second, *refs):
-    operands, out = refs[:-1], refs[-1]
+def product_kernel(parts, which, late, place, first, second, *refs):
+    if late:
+        refs, held, sems = refs[:-2], refs[-2], refs[-1]
+    operands, out = list(refs[:-1]), refs[-1]
     total = operands[-1] if len(operands) > 1 + max(index for *_, blocks in parts for index, _ in blocks) else None
+    copies = []
+    for i, index in enumerate(late):
+        copies.append(pltpu.make_async_copy(operands[index], held.at[i], sems.at[i]))
+        copies[-1].start()
+        operands[index] = held.at[i]
     start = place[3] * HALF
     rows = pl.ds(0 if which is None else pl.multiple_of(which(place[2]) * ROW_BLOCK, ROW_BLOCK), out.shape[0])
 
-    for n in range(WIDTH // COLUMNS):
-        columns = slice(n * COLUMNS, (n + 1) * COLUMNS)
-        value = None if total is None else total[rows, columns]
+    def add(parts, columns, value):
         for group, exchanged, blocks in parts:
             depth = slice(group * SIDE * HALF, group * SIDE * HALF + len(blocks) * HALF)
             features, offset = (first, start) if exchanged else (second, HALF - start)
@@ -136,21 +142,38 @@
             grads = [operands[index][pl.ds(i * TOKENS + offset, HALF), columns] for index, i in blocks]
             term = jnp.dot(features[rows, depth], jnp.concatenate(grads, axis=0), preferred_element_type=jnp.float32)
             value = term if value is None else value + term
-        out[:, columns] = value
-
-
-def product(place, features, operands, parts, total=None, which=None):
+        return value
+
+    waits = lambda part: any(index in late for index, _ in part[2])
+    tiles = [slice(n * COLUMNS, (n + 1) * COLUMNS) for n in range(WIDTH // COLUMNS)]
+    for columns in tiles:
+        held_total = None if total is None else total[rows, columns]
+        out[:, columns] = add([part for part in parts if not waits(part)], columns, held_total)
+    if late:
+        for copy in copies:
+            copy.wait()
+        for columns in tiles:
+            out[:, columns] = add([part for part in parts if waits(part)], columns, out[:, columns])
+
+
+def product(place, features, operands, parts, total=None, which=None, late=()):
     count = 2 * ROW_BLOCK if which is None else ROW_BLOCK
-    operands = [*features, *operands] + ([] if total is None else [total])
-    return pl.pallas_call(
-        functools.partial(product_kernel, parts, which),
+    specs = [WHOLE] * 2 + [ANYWHERE if i in late else WHOLE for i in range(len(operands))]
+    scratch = []
+    if late:
+        scratch = [pltpu.VMEM((len(late), 2 * TOKENS, WIDTH), jnp.bfloat16), pltpu.SemaphoreType.DMA((len(late),))]
+    if total is not None:
+        operands, specs = operands + [total], specs + [WHOLE]
+    return pl.pallas_call(
+        functools.partial(product_kernel, parts, which, late),
         out_shape=shape(count, WIDTH),
-        in_specs=[SCALARS] + [WHOLE] * len(operands),
+        in_specs=[SCALARS] + specs,
         out_specs=WHOLE,
-        input_output_aliases={len(operands): 0} if total is not None and which is None else {},
+        scratch_shapes=scratch,
+        input_output_aliases={2 + len(operands): 0} if total is not None and which is None else {},
         compiler_params=PARAMS,
         cost_estimate=cost(24 * count * HALF * WIDTH * sum(len(part[2]) for part in parts), 2**20),
-    )(place, *operands)
+    )(place, *features, *operands)
 
 
 def columns_kernel(mine, theirs, grad, sent):
@@ -279,13 +302,12 @@
     back, ahead = [back_low, along(high, 1)], [along(low, SIDE - 1), ahead_high]
     blocks = lambda operand: [(operand, 0), (operand, 1), (operand + 1, 0), (operand + 1, 1)]
     total = product(place, (first, first), [low, high], [(0, True, blocks(0))])
-    parts = [(1, True, blocks(0)), (3, True, blocks(2))]
-    total = product(place, (first, first), back + ahead, parts, total)
-    operands = [low, high] + back + far + ahead
-    parts = [(2, True, blocks(4)), (0, False, blocks(0) + blocks(2) + blocks(4) + blocks(6))]
-    theirs = product(place, (first, second), operands, parts, total, lambda core: 1 - core)
+    total = product(place, (first, first), back + ahead, [(2, True, blocks(0) + blocks(2))], total)
+    operands = [low, high] + far + back + ahead
+    parts = [(1, True, blocks(2)), (0, False, blocks(0) + blocks(2)), (2, False, blocks(4) + blocks(6))]
+    theirs = product(place, (first, second), operands, parts, total, lambda core: 1 - core, (5, 6))
     received = lax.ppermute(theirs, "core", [(0, 1), (1, 0)])
-    mine = product(place, (first, second), operands, parts, total, lambda core: core)
+    mine = product(place, (first, second), operands, parts, total, lambda core: core, (5, 6))
     weight_grad, tiles = columns(mine, received)
     new_cols, col_root, tiles = rows(exchange(tiles, ROWS), col_moment.reshape(TILE), weight_grad, weight)
     new_rows, row_root, tiles = scalars(exchange(tiles, "z"), row_moment.reshape(2, LANES))

time: 122 us -> 122 us (level)
  transfers between devices with their start and end apart: 10 -> 10, of which waited for: 4 -> 3; matrix products, arithmetic and copies ran while one was open for 0% -> 0% of each run, Pallas kernels for 8% -> 8%
where the time goes in v20:
time: 122 us; the launch traced here: 121 us
  starting transfers between devices  48.4 us (40%)
  blocking collectives  45.3 us (37%)
  Pallas kernels  15.7 us (13%)
  waiting for transfers between devices  8.82 us (7%)
  local copies, waits for them, and re-layouts  2.15 us (2%)
    all_to_all x3, blocking collectives, exchange(): return lax.all_to_all(tiles, axes, 0, 0)  45.3 us
    ppermute x6, starting transfers between devices, along(): return lax.ppermute(value, ROWS, pairs)  18.3 us
    ppermute x1, starting transfers between devices, next_layer(): return lax.ppermute(value, ('core', 'z'), pairs)  13.3 us
    pallas_call x4, Pallas kernels, product(): pl.pallas_call(functools.partial(product_kernel, parts, which, late), out...  7.97 us
    ppermute x1, starting transfers between devices, shards(): received = lax.ppermute(theirs, 'core', [(0, 1), (1, 0)])  6.94 us
    all_to_all x1, waiting for transfers between devices, gather_line(): return lax.all_to_all(sent, ROWS, 0, 0, axis_index_groups=groups)  6.76 us
    all_to_all x1, starting transfers between devices, exchange(): return lax.all_to_all(tiles, axes, 0, 0)  5.01 us
    all_to_all x1, starting transfers between devices, gather_line(): return lax.all_to_all(sent, ROWS, 0, 0, axis_index_groups=groups)  4.84 us
  transfers between devices with their start and end apart: 10, of which 3 were waited for; matrix products, arithmetic and copies ran while one was open for 0% of the time, Pallas kernels for 8%

profile of v20, /device:TPU:1, one launch (start us, length us, event | category | flops | bytes accessed | tf_op | source)
XLA Modules:
  0.0 121.3 jit_solution(17596055307797270511)
XLA Ops:
  0.6 2.1 %broadcast_in_dim.3 = bf16[4,128,1024]{2,1,0:T(8,128)(2,1)} broadcast(bf16[128,1024]{1,0:T(8,128)(2,1)} %param.6), dimensions={1,2} | broadcast | bytes 1310720 | tf_op jit(solution)/shard_map/broadcast_in_dim | solution.py:64
  2.7 4.8 %all-to-all-start = ((bf16[4,128,1024]{2,1,0:T(8,128)(2,1)}), bf16[4,128,1024]{2,1,0:T(8,128)(2,1)S(1)}, u32[]{:S(2)}, u32[]{:S(2)}) async-start(bf16[4,128,1024]{2,1,0:T(8,128)(2,1)} %broadcast_in_dim.3), calls=%async_computation | async-start | bytes 2097152 | tf_op jit(solution)/shard_map/all_to_all | solution.py:65
  7.5 0.1 pad_add_fusion.place
  7.6 2.9 %shard_map.76 = bf16[16,64,512]{2,1,0:T(8,128)(2,1)} custom-call(s32[4]{0:T(128)S(1)} %pad_add_fusion.place, bf16[128,8192]{1,0:T(8,128)(2,1)} %source.1), custom_call_target="tpu_custom_call" | custom-call | bytes 2097152 | tf_op jit(solution)/shard_map/pallas_call | solution.py:91
  10.5 6.8 %all-to-all-done = bf16[4,128,1024]{2,1,0:T(8,128)(2,1)S(1)} async-done(((bf16[4,128,1024]{2,1,0:T(8,128)(2,1)}), bf16[4,128,1024]{2,1,0:T(8,128)(2,1)S(1)}, u32[]{:S(2)}, u32[]{:S(2)}) %all-to-all-start) | async-done | bytes 1048608 | tf_op jit(solution)/shard_map/all_to_all | solution.py:65
  17.3 5.0 %all-to-all-start.1 = ((bf16[16,64,512]{2,1,0:T(8,128)(2,1)}), bf16[16,64,512]{2,1,0:T(8,128)(2,1)S(1)}, u32[]{:S(2)}, u32[]{:S(2)}) async-start(bf16[16,64,512]{2,1,0:T(8,128)(2,1)} %shard_map.76), calls=%async_computation.1 | async-start | bytes 2097152 | tf_op jit(solution)/shard_map/all_to_all | solution.py:75
  22.3 0.1 fusion
  22.4 3.3 %collective-permute-start.1 = (bf16[256,1024]{1,0:T(8,128)(2,1)S(1)}, bf16[256,1024]{1,0:T(8,128)(2,1)S(1)}, u32[]{:S(2)}, u32[]{:S(2)}) collective-permute-start(bf16[256,1024]{1,0:T(8,128)(2,1)S(1)} %bitcast.15), channel_id=1, source_target_pairs={{0,32},{16,144},{32,64},{48,176},{64,96},{80,208},{96,0},{112,240}... | collective-permute-start | bytes 1572872 | tf_op jit(solution)/shard_map/ppermute | solution.py:58
  25.7 3.2 %collective-permute-start.3 = (bf16[256,1024]{1,0:T(8,128)(2,1)S(1)}, bf16[256,1024]{1,0:T(8,128)(2,1)S(1)}, u32[]{:S(2)}, u32[]{:S(2)}) collective-permute-start(bf16[256,1024]{1,0:T(8,128)(2,1)S(1)} %bitcast.10), channel_id=1, source_target_pairs={{0,96},{16,400},{32,0},{48,432},{64,32},{80,464},{96,64},{112,496}... | collective-permute-start | bytes 1572872 | tf_op jit(solution)/shard_map/ppermute | solution.py:58
  28.9 3.3 %collective-permute-start.6 = (bf16[256,1024]{1,0:T(8,128)(2,1)S(1)}, bf16[256,1024]{1,0:T(8,128)(2,1)}, u32[]{:S(2)}, u32[]{:S(2)}) collective-permute-start(bf16[256,1024]{1,0:T(8,128)(2,1)S(1)} %bitcast.16), channel_id=1, source_target_pairs={{0,96},{16,400},{32,0},{48,432},{64,32},{80,464},{96,64},{112,496}... | collective-permute-start | bytes 1572872 | tf_op jit(solution)/shard_map/ppermute | solution.py:58
  32.2 2.0 %collective-permute-start.5 = (bf16[256,1024]{1,0:T(8,128)(2,1)S(1)}, bf16[256,1024]{1,0:T(8,128)(2,1)}, u32[]{:S(2)}, u32[]{:S(2)}) collective-permute-start(bf16[256,1024]{1,0:T(8,128)(2,1)S(1)} %bitcast.11), channel_id=1, source_target_pairs={{0,32},{16,144},{32,64},{48,176},{64,96},{80,208},{96,0},{112,240}... | collective-permute-start | bytes 1572872 | tf_op jit(solution)/shard_map/ppermute | solution.py:58
  34.2 0.9 all-to-all-done.1.part
  35.0 13.3 %collective-permute-start = (bf16[16,64,512]{2,1,0:T(8,128)(2,1)S(1)}, bf16[16,64,512]{2,1,0:T(8,128)(2,1)S(1)}, u32[]{:S(2)}, u32[]{:S(2)}) collective-permute-start(bf16[16,64,512]{2,1,0:T(8,128)(2,1)S(1)} %all-to-all-done.1.part), channel_id=1, source_target_pairs={{0,1},{1,2},{2,3},{3,4},{4,5},{5,6},{6,7},{7,8},{8,9},{9,10},{10,1... | collective-permute-start | bytes 3145736 | tf_op jit(solution)/shard_map/ppermute | solution.py:71
  48.4 2.0 %collective-permute-start.2 = (bf16[256,1024]{1,0:T(8,128)(2,1)S(1)}, bf16[256,1024]{1,0:T(8,128)(2,1)S(1)}, u32[]{:S(2)}, u32[]{:S(2)}) collective-permute-start(bf16[256,1024]{1,0:T(8,128)(2,1)S(1)} %collective-permute-done.1.refs_0_.refs_4_), channel_id=1, source_target_pairs={{0,32},{16,144},{32,64},{48,176},{64,96},{80,208},{96,0},{112,240}... | collective-permute-start | bytes 1572872 | tf_op jit(solution)/shard_map/ppermute | solution.py:58
  50.4 4.5 %collective-permute-start.4 = (bf16[256,1024]{1,0:T(8,128)(2,1)S(1)}, bf16[256,1024]{1,0:T(8,128)(2,1)S(1)}, u32[]{:S(2)}, u32[]{:S(2)}) collective-permute-start(bf16[256,1024]{1,0:T(8,128)(2,1)S(1)} %collective-permute-done.3.refs_3_.refs_7_), channel_id=1, source_target_pairs={{0,96},{16,400},{32,0},{48,432},{64,32},{80,464},{96,64},{112,496}... | collective-permute-start | bytes 1572872 | tf_op jit(solution)/shard_map/ppermute | solution.py:58
  54.9 0.9 shard_map.77.first.second
  55.8 1.0 shard_map.79.refs_4_
  56.8 2.1 %shard_map.80.refs_8_ = f32[512,1024]{1,0:T(8,128)S(1)} custom-call(s32[4]{0:T(128)S(1)} %pad_add_fusion.place, bf16[512,1024]{1,0:T(8,128)(2,1)S(1)} %shard_map.77.first.second, bf16[512,1024]{1,0:T(8,128)(2,1)S(1)} %shard_map.77.first.second, bf16[256,1024]{1,0:T(8,128)(2,1)S(1)} %collective-permute-done.1.refs_0_.refs_4_, ...), custom_call_target="tpu_custom_call", output_to_operand_aliasing={{}: (7, {})} | custom-call | flops 6442450944 | bytes 1048576 | tf_op jit(solution)/shard_map/pallas_call | solution.py:167
  58.9 1.2 collective-permute-done.part
  60.1 0.9 shard_map.78.second
  61.0 2.5 %shard_map.82 = f32[256,1024]{1,0:T(8,128)S(1)} custom-call(s32[4]{0:T(128)S(1)} %pad_add_fusion.place, bf16[512,1024]{1,0:T(8,128)(2,1)S(1)} %shard_map.77.first.second, bf16[512,1024]{1,0:T(8,128)(2,1)S(1)} %shard_map.78.second, bf16[256,1024]{1,0:T(8,128)(2,1)S(1)} %bitcast.18, bf16[256,1024]{1,0:T(8,128)(2,1)S(1)} %bitcast.13, ...), custom_call_target="tpu_custom_call" | custom-call | flops 8053063680 | bytes 1048576 | tf_op jit(solution)/shard_map/pallas_call | solution.py:167
  63.5 6.9 %collective-permute-start.7 = (f32[256,1024]{1,0:T(8,128)S(1)}, f32[256,1024]{1,0:T(8,128)S(1)}, u32[]{:S(2)}, u32[]{:S(2)}) collective-permute-start(f32[256,1024]{1,0:T(8,128)S(1)} %shard_map.82), channel_id=1, source_target_pairs={{0,16},{16,0},{1,17},{17,1},{2,18},{18,2},{3,19},{19,3},{4,20},{20... | collective-permute-start | bytes 3145736 | tf_op jit(solution)/shard_map/ppermute | solution.py:309
  70.4 2.4 %shard_map.81.mine = f32[256,1024]{1,0:T(8,128)S(1)} custom-call(s32[4]{0:T(128)S(1)} %pad_add_fusion.place, bf16[512,1024]{1,0:T(8,128)(2,1)S(1)} %shard_map.77.first.second, bf16[512,1024]{1,0:T(8,128)(2,1)S(1)} %shard_map.78.second, bf16[256,1024]{1,0:T(8,128)(2,1)S(1)} %bitcast.19, bf16[256,1024]{1,0:T(8,128)(2,1)S(1)} %bitcast.14, ...), custom_call_target="tpu_custom_call" | custom-call | flops 8053063680 | bytes 1048576 | tf_op jit(solution)/shard_map/pallas_call | solution.py:167
  72.9 0.0 copy-start.1
  72.9 0.0 copy-start.2
  72.9 0.1 shard_map.83
  73.1 11.3 %all_to_all.25.received = f32[32,8,128]{2,1,0:T(8,128)S(1)} all-to-all(f32[32,8,128]{2,1,0:T(8,128)S(1)} %get-tuple-element.15), channel_id=1, replica_groups=mesh['y'=4,'x'=4,'core'=2,'z'=16] {'y','x','core'}, dimensions={0} | all-to-all | bytes 262144 | tf_op jit(solution)/shard_map/all_to_all | solution.py:75
  84.4 1.0 shard_map.84
  85.4 21.5 %all_to_all.26.received = f32[16,8,128]{2,1,0:T(8,128)S(1)} all-to-all(f32[16,8,128]{2,1,0:T(8,128)S(1)} %get-tuple-element.17), channel_id=1, replica_groups=mesh['y'=4,'x'=4,'core'=2,'z'=16] {'z'}, dimensions={0} | all-to-all | bytes 131072 | tf_op jit(solution)/shard_map/all_to_all | solution.py:75
  106.8 0.6 shard_map.85
  107.4 12.5 %all_to_all.27.received = f32[32,4,128]{2,1,0:T(4,128)S(1)} all-to-all(f32[32,4,128]{2,1,0:T(4,128)S(1)} %get-tuple-element.18), channel_id=1, replica_groups=mesh['y'=4,'x'=4,'core'=2,'z'=16] {'y','x','core'}, dimensions={0} | all-to-all | bytes 131072 | tf_op jit(solution)/shard_map/all_to_all | solution.py:75
  119.9 1.4 %shard_map.86 = f32[256,1024]{1,0:T(8,128)} custom-call(f32[32,4,128]{2,1,0:T(4,128)S(1)} %all_to_all.27.received, f32[2,128]{1,0:T(2,128)S(1)} %get-tuple-element.19.row_root, f32[8,128]{1,0:T(8,128)S(1)} %get-tuple-element.20.col_root, f32[256,1024]{1,0:T(8,128)S(1)} %get-tuple-element.16.grad, f32[256,1024]{1,0:T(8,128)S(1)} %copy-done), custom_call_target="tpu_custom_call" | custom-call | flops 1048576 | bytes 3145728 | tf_op jit(solution)/shard_map/pallas_call | solution.py:281
  (11 shorter events, 0.0 us)
Async XLA Ops:
  2.7 14.6 %all-to-all-start = ((bf16[4,128,1024]{2,1,0:T(8,128)(2,1)}), bf16[4,128,1024]{2,1,0:T(8,128)(2,1)S(1)}, u32[]{:S(2)}, u32[]{:S(2)}) async-start(bf16[4,128,1024]{2,1,0:T(8,128)(2,1)} %broadcast_in_dim.3), calls=%async_computation | async-start | bytes 2097152 | tf_op jit(solution)/shard_map/all_to_all | solution.py:65
  17.3 17.8 %all-to-all-start.1 = ((bf16[16,64,512]{2,1,0:T(8,128)(2,1)}), bf16[16,64,512]{2,1,0:T(8,128)(2,1)S(1)}, u32[]{:S(2)}, u32[]{:S(2)}) async-start(bf16[16,64,512]{2,1,0:T(8,128)(2,1)} %shard_map.76), calls=%async_computation.1 | async-start | bytes 2097152 | tf_op jit(solution)/shard_map/all_to_all | solution.py:75
  22.4 26.0 %collective-permute-start.1 = (bf16[256,1024]{1,0:T(8,128)(2,1)S(1)}, bf16[256,1024]{1,0:T(8,128)(2,1)S(1)}, u32[]{:S(2)}, u32[]{:S(2)}) collective-permute-start(bf16[256,1024]{1,0:T(8,128)(2,1)S(1)} %bitcast.15), channel_id=1, source_target_pairs={{0,32},{16,144},{32,64},{48,176},{64,96},{80,208},{96,0},{112,240}... | collective-permute-start | bytes 1572872 | tf_op jit(solution)/shard_map/ppermute | solution.py:58
  25.7 24.7 %collective-permute-start.3 = (bf16[256,1024]{1,0:T(8,128)(2,1)S(1)}, bf16[256,1024]{1,0:T(8,128)(2,1)S(1)}, u32[]{:S(2)}, u32[]{:S(2)}) collective-permute-start(bf16[256,1024]{1,0:T(8,128)(2,1)S(1)} %bitcast.10), channel_id=1, source_target_pairs={{0,96},{16,400},{32,0},{48,432},{64,32},{80,464},{96,64},{112,496}... | collective-permute-start | bytes 1572872 | tf_op jit(solution)/shard_map/ppermute | solution.py:58
  28.9 27.9 %collective-permute-start.6 = (bf16[256,1024]{1,0:T(8,128)(2,1)S(1)}, bf16[256,1024]{1,0:T(8,128)(2,1)}, u32[]{:S(2)}, u32[]{:S(2)}) collective-permute-start(bf16[256,1024]{1,0:T(8,128)(2,1)S(1)} %bitcast.16), channel_id=1, source_target_pairs={{0,96},{16,400},{32,0},{48,432},{64,32},{80,464},{96,64},{112,496}... | collective-permute-start | bytes 1572872 | tf_op jit(solution)/shard_map/ppermute | solution.py:58
  32.2 24.6 %collective-permute-start.5 = (bf16[256,1024]{1,0:T(8,128)(2,1)S(1)}, bf16[256,1024]{1,0:T(8,128)(2,1)}, u32[]{:S(2)}, u32[]{:S(2)}) collective-permute-start(bf16[256,1024]{1,0:T(8,128)(2,1)S(1)} %bitcast.11), channel_id=1, source_target_pairs={{0,32},{16,144},{32,64},{48,176},{64,96},{80,208},{96,0},{112,240}... | collective-permute-start | bytes 1572872 | tf_op jit(solution)/shard_map/ppermute | solution.py:58
  35.0 25.1 %collective-permute-start = (bf16[16,64,512]{2,1,0:T(8,128)(2,1)S(1)}, bf16[16,64,512]{2,1,0:T(8,128)(2,1)S(1)}, u32[]{:S(2)}, u32[]{:S(2)}) collective-permute-start(bf16[16,64,512]{2,1,0:T(8,128)(2,1)S(1)} %all-to-all-done.1.part), channel_id=1, source_target_pairs={{0,1},{1,2},{2,3},{3,4},{4,5},{5,6},{6,7},{7,8},{8,9},{9,10},{10,1... | collective-permute-start | bytes 3145736 | tf_op jit(solution)/shard_map/ppermute | solution.py:71
  48.4 12.6 %collective-permute-start.2 = (bf16[256,1024]{1,0:T(8,128)(2,1)S(1)}, bf16[256,1024]{1,0:T(8,128)(2,1)S(1)}, u32[]{:S(2)}, u32[]{:S(2)}) collective-permute-start(bf16[256,1024]{1,0:T(8,128)(2,1)S(1)} %collective-permute-done.1.refs_0_.refs_4_), channel_id=1, source_target_pairs={{0,32},{16,144},{32,64},{48,176},{64,96},{80,208},{96,0},{112,240}... | collective-permute-start | bytes 1572872 | tf_op jit(solution)/shard_map/ppermute | solution.py:58
  50.4 10.6 %collective-permute-start.4 = (bf16[256,1024]{1,0:T(8,128)(2,1)S(1)}, bf16[256,1024]{1,0:T(8,128)(2,1)S(1)}, u32[]{:S(2)}, u32[]{:S(2)}) collective-permute-start(bf16[256,1024]{1,0:T(8,128)(2,1)S(1)} %collective-permute-done.3.refs_3_.refs_7_), channel_id=1, source_target_pairs={{0,96},{16,400},{32,0},{48,432},{64,32},{80,464},{96,64},{112,496}... | collective-permute-start | bytes 1572872 | tf_op jit(solution)/shard_map/ppermute | solution.py:58
  63.5 9.4 %collective-permute-start.7 = (f32[256,1024]{1,0:T(8,128)S(1)}, f32[256,1024]{1,0:T(8,128)S(1)}, u32[]{:S(2)}, u32[]{:S(2)}) collective-permute-start(f32[256,1024]{1,0:T(8,128)S(1)} %shard_map.82), channel_id=1, source_target_pairs={{0,16},{16,0},{1,17},{17,1},{2,18},{18,2},{3,19},{19,3},{4,20},{20... | collective-permute-start | bytes 3145736 | tf_op jit(solution)/shard_map/ppermute | solution.py:309
  72.9 11.5 %copy-start = (f32[256,1024]{1,0:T(8,128)S(1)}, f32[256,1024]{1,0:T(8,128)}, u32[]{:S(2)}) copy-start(f32[256,1024]{1,0:T(8,128)} %weight.3) | copy-start | bytes 3145732
  72.9 11.5 %copy-start.1 = (f32[1024]{0:T(1024)S(1)}, f32[1024]{0:T(1024)}, u32[]{:S(2)}) copy-start(f32[1024]{0:T(1024)} %param.9) | copy-start | bytes 12292
  72.9 33.9 %copy-start.2 = (f32[256]{0:T(256)S(1)}, f32[256]{0:T(256)}, u32[]{:S(2)}) copy-start(f32[256]{0:T(256)} %param.8) | copy-start | bytes 3076

commit v21 on v19

--- a/solution.py
+++ b/solution.py
@@ -120,9 +120,12 @@
     )(place, part)
 
 
-def product_kernel(parts, which, place, first, second, *refs):
-    operands, out = refs[:-1], refs[-1]
+def product_kernel(parts, which, kept, place, first, second, *refs):
+    split = len(refs) - 1 - len(kept)
+    operands, out, copies = refs[:split], refs[split], refs[split + 1 :]
     total = operands[-1] if len(operands) > 1 + max(index for *_, blocks in parts for index, _ in blocks) else None
+    for index, copy in zip(kept, copies):
+        copy[...] = operands[index][...]
     start = place[3] * HALF
     rows = pl.ds(0 if which is None else pl.multiple_of(which(place[2]) * ROW_BLOCK, ROW_BLOCK), out.shape[0])
 
@@ -139,18 +142,20 @@
         out[:, columns] = value
 
 
-def product(place, features, operands, parts, total=None, which=None):
+def product(place, features, operands, parts, total=None, which=None, kept=()):
     count = 2 * ROW_BLOCK if which is None else ROW_BLOCK
     operands = [*features, *operands] + ([] if total is None else [total])
-    return pl.pallas_call(
-        functools.partial(product_kernel, parts, which),
-        out_shape=shape(count, WIDTH),
+    out_shape = (shape(count, WIDTH),) + (shape(2 * TOKENS, WIDTH, dtype=jnp.bfloat16),) * len(kept)
+    out = pl.pallas_call(
+        functools.partial(product_kernel, parts, which, kept),
+        out_shape=out_shape,
         in_specs=[SCALARS] + [WHOLE] * len(operands),
-        out_specs=WHOLE,
+        out_specs=(WHOLE,) * len(out_shape),
         input_output_aliases={len(operands): 0} if total is not None and which is None else {},
         compiler_params=PARAMS,
         cost_estimate=cost(24 * count * HALF * WIDTH * sum(len(part[2]) for part in parts), 2**20),
     )(place, *operands)
+    return out if kept else out[0]
 
 
 def columns_kernel(mine, theirs, grad, sent):
@@ -280,7 +285,7 @@
     blocks = lambda operand: [(operand, 0), (operand, 1), (operand + 1, 0), (operand + 1, 1)]
     total = product(place, (first, first), [low, high], [(0, True, blocks(0))])
     parts = [(1, True, blocks(0)), (3, True, blocks(2))]
-    total = product(place, (first, first), back + ahead, parts, total)
+    total, back[1], ahead[0] = product(place, (first, first), back + ahead, parts, total, kept=(1, 2))
     operands = [low, high] + back + far + ahead
     parts = [(2, True, blocks(4)), (0, False, blocks(0) + blocks(2) + blocks(4) + blocks(6))]
     theirs = product(place, (first, second), operands, parts, total, lambda core: 1 - core)

time: 122 us -> 121 us (level)
    pallas_call x4, Pallas kernels: 7.19 us -> 5.89 us  [product(): pl.pallas_call(functools.partial(product_kernel, parts, which, kept), out...]
  transfers between devices with their start and end apart: 10 -> 10, of which waited for: 4 -> 3; matrix products, arithmetic and copies ran while one was open for 0% -> 0% of each run, Pallas kernels for 8% -> 8%
where the time goes in v21:
time: 121 us; the launch traced here: 120 us
  starting transfers between devices  49.2 us (41%)
  blocking collectives  45.4 us (38%)
  Pallas kernels  13.7 us (11%)
  waiting for transfers between devices  8.74 us (7%)
  local copies, waits for them, and re-layouts  2.15 us (2%)
    all_to_all x3, blocking collectives, exchange(): return lax.all_to_all(tiles, axes, 0, 0)  45.4 us
    ppermute x6, starting transfers between devices, along(): return lax.ppermute(value, ROWS, pairs)  19.5 us
    ppermute x1, starting transfers between devices, next_layer(): return lax.ppermute(value, ('core', 'z'), pairs)  13 us
    ppermute x1, starting transfers between devices, shards(): received = lax.ppermute(theirs, 'core', [(0, 1), (1, 0)])  6.94 us
    all_to_all x1, waiting for transfers between devices, gather_line(): return lax.all_to_all(sent, ROWS, 0, 0, axis_index_groups=groups)  6.76 us
    pallas_call x4, Pallas kernels, product(): pl.pallas_call(functools.partial(product_kernel, parts, which, kept), out...  5.89 us
    all_to_all x1, starting transfers between devices, exchange(): return lax.all_to_all(tiles, axes, 0, 0)  5.01 us
    all_to_all x1, starting transfers between devices, gather_line(): return lax.all_to_all(sent, ROWS, 0, 0, axis_index_groups=groups)  4.84 us
  transfers between devices with their start and end apart: 10, of which 3 were waited for; matrix products, arithmetic and copies ran while one was open for 0% of the time, Pallas kernels for 8%

profile of v21, /device:TPU:1, one launch (start us, length us, event | category | flops | bytes accessed | tf_op | source)
XLA Modules:
  0.0 120.1 jit_solution(9670321158274677074)
XLA Ops:
  0.6 2.1 %broadcast_in_dim.3 = bf16[4,128,1024]{2,1,0:T(8,128)(2,1)} broadcast(bf16[128,1024]{1,0:T(8,128)(2,1)} %param.6), dimensions={1,2} | broadcast | bytes 1310720 | tf_op jit(solution)/shard_map/broadcast_in_dim | solution.py:63
  2.7 4.8 %all-to-all-start = ((bf16[4,128,1024]{2,1,0:T(8,128)(2,1)}), bf16[4,128,1024]{2,1,0:T(8,128)(2,1)S(1)}, u32[]{:S(2)}, u32[]{:S(2)}) async-start(bf16[4,128,1024]{2,1,0:T(8,128)(2,1)} %broadcast_in_dim.3), calls=%async_computation | async-start | bytes 2097152 | tf_op jit(solution)/shard_map/all_to_all | solution.py:64
  7.5 0.1 pad_add_fusion.place
  7.6 2.9 %shard_map.76 = bf16[16,64,512]{2,1,0:T(8,128)(2,1)} custom-call(s32[4]{0:T(128)S(1)} %pad_add_fusion.place, bf16[128,8192]{1,0:T(8,128)(2,1)} %source.1), custom_call_target="tpu_custom_call" | custom-call | bytes 2097152 | tf_op jit(solution)/shard_map/pallas_call | solution.py:90
  10.5 6.8 %all-to-all-done = bf16[4,128,1024]{2,1,0:T(8,128)(2,1)S(1)} async-done(((bf16[4,128,1024]{2,1,0:T(8,128)(2,1)}), bf16[4,128,1024]{2,1,0:T(8,128)(2,1)S(1)}, u32[]{:S(2)}, u32[]{:S(2)}) %all-to-all-start) | async-done | bytes 1048608 | tf_op jit(solution)/shard_map/all_to_all | solution.py:64
  17.3 5.0 %all-to-all-start.1 = ((bf16[16,64,512]{2,1,0:T(8,128)(2,1)}), bf16[16,64,512]{2,1,0:T(8,128)(2,1)S(1)}, u32[]{:S(2)}, u32[]{:S(2)}) async-start(bf16[16,64,512]{2,1,0:T(8,128)(2,1)} %shard_map.76), calls=%async_computation.1 | async-start | bytes 2097152 | tf_op jit(solution)/shard_map/all_to_all | solution.py:74
  22.3 0.1 fusion
  22.4 3.3 %collective-permute-start.1 = (bf16[256,1024]{1,0:T(8,128)(2,1)S(1)}, bf16[256,1024]{1,0:T(8,128)(2,1)S(1)}, u32[]{:S(2)}, u32[]{:S(2)}) collective-permute-start(bf16[256,1024]{1,0:T(8,128)(2,1)S(1)} %bitcast.15), channel_id=1, source_target_pairs={{0,32},{16,144},{32,64},{48,176},{64,96},{80,208},{96,0},{112,240}... | collective-permute-start | bytes 1572872 | tf_op jit(solution)/shard_map/ppermute | solution.py:57
  25.7 3.2 %collective-permute-start.4 = (bf16[256,1024]{1,0:T(8,128)(2,1)S(1)}, bf16[256,1024]{1,0:T(8,128)(2,1)S(1)}, u32[]{:S(2)}, u32[]{:S(2)}) collective-permute-start(bf16[256,1024]{1,0:T(8,128)(2,1)S(1)} %bitcast.10), channel_id=1, source_target_pairs={{0,96},{16,400},{32,0},{48,432},{64,32},{80,464},{96,64},{112,496}... | collective-permute-start | bytes 1572872 | tf_op jit(solution)/shard_map/ppermute | solution.py:57
  28.9 2.1 %collective-permute-start.2 = (bf16[256,1024]{1,0:T(8,128)(2,1)S(1)}, bf16[256,1024]{1,0:T(8,128)(2,1)}, u32[]{:S(2)}, u32[]{:S(2)}) collective-permute-start(bf16[256,1024]{1,0:T(8,128)(2,1)S(1)} %bitcast.11), channel_id=1, source_target_pairs={{0,32},{16,144},{32,64},{48,176},{64,96},{80,208},{96,0},{112,240}... | collective-permute-start | bytes 1572872 | tf_op jit(solution)/shard_map/ppermute | solution.py:57
  31.0 4.4 %collective-permute-start.3 = (bf16[256,1024]{1,0:T(8,128)(2,1)S(1)}, bf16[256,1024]{1,0:T(8,128)(2,1)}, u32[]{:S(2)}, u32[]{:S(2)}) collective-permute-start(bf16[256,1024]{1,0:T(8,128)(2,1)S(1)} %bitcast.16), channel_id=1, source_target_pairs={{0,96},{16,400},{32,0},{48,432},{64,32},{80,464},{96,64},{112,496}... | collective-permute-start | bytes 1572872 | tf_op jit(solution)/shard_map/ppermute | solution.py:57
  35.4 13.0 %collective-permute-start = (bf16[16,64,512]{2,1,0:T(8,128)(2,1)S(1)}, bf16[16,64,512]{2,1,0:T(8,128)(2,1)S(1)}, u32[]{:S(2)}, u32[]{:S(2)}) collective-permute-start(bf16[16,64,512]{2,1,0:T(8,128)(2,1)S(1)} %all-to-all-done.1.part), channel_id=1, source_target_pairs={{0,1},{1,2},{2,3},{3,4},{4,5},{5,6},{6,7},{7,8},{8,9},{9,10},{10,1... | collective-permute-start | bytes 3145736 | tf_op jit(solution)/shard_map/ppermute | solution.py:70
  48.4 2.0 %collective-permute-start.5 = (bf16[256,1024]{1,0:T(8,128)(2,1)S(1)}, bf16[256,1024]{1,0:T(8,128)(2,1)S(1)}, u32[]{:S(2)}, u32[]{:S(2)}) collective-permute-start(bf16[256,1024]{1,0:T(8,128)(2,1)S(1)} %collective-permute-done.1.refs_0_.refs_2_), channel_id=1, source_target_pairs={{0,32},{16,144},{32,64},{48,176},{64,96},{80,208},{96,0},{112,240}... | collective-permute-start | bytes 1572872 | tf_op jit(solution)/shard_map/ppermute | solution.py:57
  50.4 4.5 %collective-permute-start.6 = (bf16[256,1024]{1,0:T(8,128)(2,1)S(1)}, bf16[256,1024]{1,0:T(8,128)(2,1)S(1)}, u32[]{:S(2)}, u32[]{:S(2)}) collective-permute-start(bf16[256,1024]{1,0:T(8,128)(2,1)S(1)} %collective-permute-done.4.refs_3_.refs_7_), channel_id=1, source_target_pairs={{0,96},{16,400},{32,0},{48,432},{64,32},{80,464},{96,64},{112,496}... | collective-permute-start | bytes 1572872 | tf_op jit(solution)/shard_map/ppermute | solution.py:57
  54.9 0.9 shard_map.77.first.second
  55.8 1.0 shard_map.79.refs_4_
  56.8 2.1 %shard_map.80 = (f32[512,1024]{1,0:T(8,128)S(1)}, bf16[256,1024]{1,0:T(8,128)(2,1)S(1)}, bf16[256,1024]{1,0:T(8,128)(2,1)S(1)}) custom-call(s32[4]{0:T(128)S(1)} %pad_add_fusion.place, bf16[512,1024]{1,0:T(8,128)(2,1)S(1)} %shard_map.77.first.second, bf16[512,1024]{1,0:T(8,128)(2,1)S(1)} %shard_map.77.first.second, ...), custom_call_target="tpu_custom_call", output_to_operand_aliasing={{0}: (7, {})} | custom-call | flops 6442450944 | bytes 1048576 | tf_op jit(solution)/shard_map/pallas_call | solution.py:149
  59.0 1.1 collective-permute-done.part
  60.1 0.9 shard_map.78.second
  61.0 1.4 %shard_map.82 = f32[256,1024]{1,0:T(8,128)S(1)} custom-call(s32[4]{0:T(128)S(1)} %pad_add_fusion.place, bf16[512,1024]{1,0:T(8,128)(2,1)S(1)} %shard_map.77.first.second, bf16[512,1024]{1,0:T(8,128)(2,1)S(1)} %shard_map.78.second, bf16[256,1024]{1,0:T(8,128)(2,1)S(1)} %bitcast.18, bf16[256,1024]{1,0:T(8,128)(2,1)S(1)} %bitcast.13, ...), custom_call_target="tpu_custom_call" | custom-call | flops 8053063680 | bytes 1048576 | tf_op jit(solution)/shard_map/pallas_call | solution.py:149
  62.4 6.9 %collective-permute-start.7 = (f32[256,1024]{1,0:T(8,128)S(1)}, f32[256,1024]{1,0:T(8,128)S(1)}, u32[]{:S(2)}, u32[]{:S(2)}) collective-permute-start(f32[256,1024]{1,0:T(8,128)S(1)} %shard_map.82), channel_id=1, source_target_pairs={{0,16},{16,0},{1,17},{17,1},{2,18},{18,2},{3,19},{19,3},{4,20},{20... | collective-permute-start | bytes 3145736 | tf_op jit(solution)/shard_map/ppermute | solution.py:292
  69.4 1.4 %shard_map.81.mine = f32[256,1024]{1,0:T(8,128)S(1)} custom-call(s32[4]{0:T(128)S(1)} %pad_add_fusion.place, bf16[512,1024]{1,0:T(8,128)(2,1)S(1)} %shard_map.77.first.second, bf16[512,1024]{1,0:T(8,128)(2,1)S(1)} %shard_map.78.second, bf16[256,1024]{1,0:T(8,128)(2,1)S(1)} %bitcast.19, bf16[256,1024]{1,0:T(8,128)(2,1)S(1)} %bitcast.14, ...), custom_call_target="tpu_custom_call" | custom-call | flops 8053063680 | bytes 1048576 | tf_op jit(solution)/shard_map/pallas_call | solution.py:149
  70.8 0.0 copy-start
  70.8 0.0 copy-start.1
  70.8 0.8 collective-permute-done.7.theirs
  71.6 0.1 shard_map.83
  71.8 10.9 %all_to_all.25.received = f32[32,8,128]{2,1,0:T(8,128)S(1)} all-to-all(f32[32,8,128]{2,1,0:T(8,128)S(1)} %get-tuple-element.21), channel_id=1, replica_groups=mesh['y'=4,'x'=4,'core'=2,'z'=16] {'y','x','core'}, dimensions={0} | all-to-all | bytes 262144 | tf_op jit(solution)/shard_map/all_to_all | solution.py:74
  82.7 1.0 shard_map.84
  83.6 22.0 %all_to_all.26.received = f32[16,8,128]{2,1,0:T(8,128)S(1)} all-to-all(f32[16,8,128]{2,1,0:T(8,128)S(1)} %get-tuple-element.23), channel_id=1, replica_groups=mesh['y'=4,'x'=4,'core'=2,'z'=16] {'z'}, dimensions={0} | all-to-all | bytes 131072 | tf_op jit(solution)/shard_map/all_to_all | solution.py:74
  105.6 0.6 shard_map.85
  106.2 12.5 %all_to_all.27.received = f32[32,4,128]{2,1,0:T(4,128)S(1)} all-to-all(f32[32,4,128]{2,1,0:T(4,128)S(1)} %get-tuple-element.24), channel_id=1, replica_groups=mesh['y'=4,'x'=4,'core'=2,'z'=16] {'y','x','core'}, dimensions={0} | all-to-all | bytes 131072 | tf_op jit(solution)/shard_map/all_to_all | solution.py:74
  118.7 1.4 %shard_map.86 = f32[256,1024]{1,0:T(8,128)} custom-call(f32[32,4,128]{2,1,0:T(4,128)S(1)} %all_to_all.27.received, f32[2,128]{1,0:T(2,128)S(1)} %get-tuple-element.25.row_root, f32[8,128]{1,0:T(8,128)S(1)} %get-tuple-element.26.col_root, f32[256,1024]{1,0:T(8,128)S(1)} %get-tuple-element.22.grad, f32[256,1024]{1,0:T(8,128)S(1)} %copy-done), custom_call_target="tpu_custom_call" | custom-call | flops 1048576 | bytes 3145728 | tf_op jit(solution)/shard_map/pallas_call | solution.py:263
  (11 shorter events, 0.0 us)
Async XLA Ops:
  2.7 14.6 %all-to-all-start = ((bf16[4,128,1024]{2,1,0:T(8,128)(2,1)}), bf16[4,128,1024]{2,1,0:T(8,128)(2,1)S(1)}, u32[]{:S(2)}, u32[]{:S(2)}) async-start(bf16[4,128,1024]{2,1,0:T(8,128)(2,1)} %broadcast_in_dim.3), calls=%async_computation | async-start | bytes 2097152 | tf_op jit(solution)/shard_map/all_to_all | solution.py:64
  17.3 18.1 %all-to-all-start.1 = ((bf16[16,64,512]{2,1,0:T(8,128)(2,1)}), bf16[16,64,512]{2,1,0:T(8,128)(2,1)S(1)}, u32[]{:S(2)}, u32[]{:S(2)}) async-start(bf16[16,64,512]{2,1,0:T(8,128)(2,1)} %shard_map.76), calls=%async_computation.1 | async-start | bytes 2097152 | tf_op jit(solution)/shard_map/all_to_all | solution.py:74
  22.4 26.0 %collective-permute-start.1 = (bf16[256,1024]{1,0:T(8,128)(2,1)S(1)}, bf16[256,1024]{1,0:T(8,128)(2,1)S(1)}, u32[]{:S(2)}, u32[]{:S(2)}) collective-permute-start(bf16[256,1024]{1,0:T(8,128)(2,1)S(1)} %bitcast.15), channel_id=1, source_target_pairs={{0,32},{16,144},{32,64},{48,176},{64,96},{80,208},{96,0},{112,240}... | collective-permute-start | bytes 1572872 | tf_op jit(solution)/shard_map/ppermute | solution.py:57
  25.7 24.7 %collective-permute-start.4 = (bf16[256,1024]{1,0:T(8,128)(2,1)S(1)}, bf16[256,1024]{1,0:T(8,128)(2,1)S(1)}, u32[]{:S(2)}, u32[]{:S(2)}) collective-permute-start(bf16[256,1024]{1,0:T(8,128)(2,1)S(1)} %bitcast.10), channel_id=1, source_target_pairs={{0,96},{16,400},{32,0},{48,432},{64,32},{80,464},{96,64},{112,496}... | collective-permute-start | bytes 1572872 | tf_op jit(solution)/shard_map/ppermute | solution.py:57
  28.9 27.9 %collective-permute-start.2 = (bf16[256,1024]{1,0:T(8,128)(2,1)S(1)}, bf16[256,1024]{1,0:T(8,128)(2,1)}, u32[]{:S(2)}, u32[]{:S(2)}) collective-permute-start(bf16[256,1024]{1,0:T(8,128)(2,1)S(1)} %bitcast.11), channel_id=1, source_target_pairs={{0,32},{16,144},{32,64},{48,176},{64,96},{80,208},{96,0},{112,240}... | collective-permute-start | bytes 1572872 | tf_op jit(solution)/shard_map/ppermute | solution.py:57
  31.0 25.9 %collective-permute-start.3 = (bf16[256,1024]{1,0:T(8,128)(2,1)S(1)}, bf16[256,1024]{1,0:T(8,128)(2,1)}, u32[]{:S(2)}, u32[]{:S(2)}) collective-permute-start(bf16[256,1024]{1,0:T(8,128)(2,1)S(1)} %bitcast.16), channel_id=1, source_target_pairs={{0,96},{16,400},{32,0},{48,432},{64,32},{80,464},{96,64},{112,496}... | collective-permute-start | bytes 1572872 | tf_op jit(solution)/shard_map/ppermute | solution.py:57
  35.4 24.7 %collective-permute-start = (bf16[16,64,512]{2,1,0:T(8,128)(2,1)S(1)}, bf16[16,64,512]{2,1,0:T(8,128)(2,1)S(1)}, u32[]{:S(2)}, u32[]{:S(2)}) collective-permute-start(bf16[16,64,512]{2,1,0:T(8,128)(2,1)S(1)} %all-to-all-done.1.part), channel_id=1, source_target_pairs={{0,1},{1,2},{2,3},{3,4},{4,5},{5,6},{6,7},{7,8},{8,9},{9,10},{10,1... | collective-permute-start | bytes 3145736 | tf_op jit(solution)/shard_map/ppermute | solution.py:70
  48.4 12.6 %collective-permute-start.5 = (bf16[256,1024]{1,0:T(8,128)(2,1)S(1)}, bf16[256,1024]{1,0:T(8,128)(2,1)S(1)}, u32[]{:S(2)}, u32[]{:S(2)}) collective-permute-start(bf16[256,1024]{1,0:T(8,128)(2,1)S(1)} %collective-permute-done.1.refs_0_.refs_2_), channel_id=1, source_target_pairs={{0,32},{16,144},{32,64},{48,176},{64,96},{80,208},{96,0},{112,240}... | collective-permute-start | bytes 1572872 | tf_op jit(solution)/shard_map/ppermute | solution.py:57
  50.4 10.6 %collective-permute-start.6 = (bf16[256,1024]{1,0:T(8,128)(2,1)S(1)}, bf16[256,1024]{1,0:T(8,128)(2,1)S(1)}, u32[]{:S(2)}, u32[]{:S(2)}) collective-permute-start(bf16[256,1024]{1,0:T(8,128)(2,1)S(1)} %collective-permute-done.4.refs_3_.refs_7_), channel_id=1, source_target_pairs={{0,96},{16,400},{32,0},{48,432},{64,32},{80,464},{96,64},{112,496}... | collective-permute-start | bytes 1572872 | tf_op jit(solution)/shard_map/ppermute | solution.py:57
  62.4 9.2 %collective-permute-start.7 = (f32[256,1024]{1,0:T(8,128)S(1)}, f32[256,1024]{1,0:T(8,128)S(1)}, u32[]{:S(2)}, u32[]{:S(2)}) collective-permute-start(f32[256,1024]{1,0:T(8,128)S(1)} %shard_map.82), channel_id=1, source_target_pairs={{0,16},{16,0},{1,17},{17,1},{2,18},{18,2},{3,19},{19,3},{4,20},{20... | collective-permute-start | bytes 3145736 | tf_op jit(solution)/shard_map/ppermute | solution.py:292
  70.8 11.9 %copy-start = (f32[256,1024]{1,0:T(8,128)S(1)}, f32[256,1024]{1,0:T(8,128)}, u32[]{:S(2)}) copy-start(f32[256,1024]{1,0:T(8,128)} %weight.3) | copy-start | bytes 3145732
  70.8 11.9 %copy-start.1 = (f32[1024]{0:T(1024)S(1)}, f32[1024]{0:T(1024)}, u32[]{:S(2)}) copy-start(f32[1024]{0:T(1024)} %param.9) | copy-start | bytes 12292
  70.8 34.8 %copy-start.2 = (f32[256]{0:T(256)S(1)}, f32[256]{0:T(256)}, u32[]{:S(2)}) copy-start(f32[256]{0:T(256)} %param.8) | copy-start | bytes 3076

commit v22 on v21

--- a/solution.py
+++ b/solution.py
@@ -178,36 +178,56 @@
     )(mine, theirs)
 
 
-def rows_kernel(received, moment, grad, weight, cols, col_root, sent):
+def by_rows(value):
+    halves = (value[:LANES], value[LANES:])
+    return jnp.concatenate([jnp.sum(half.T, axis=0, keepdims=True) for half in halves], axis=0)
+
+
+def weights_kernel(weight, out):
+    value = jnp.zeros((ROW_BLOCK, LANES), jnp.float32)
+    for i in range(WIDTH // LANES):
+        held = weight[:, i * LANES : (i + 1) * LANES]
+        value += held * held
+    out[...] = by_rows(value)
+
+
+def weights(weight):
+    return pl.pallas_call(
+        weights_kernel,
+        out_shape=shape(2, LANES),
+        in_specs=[WHOLE],
+        out_specs=WHOLE,
+        compiler_params=PARAMS,
+        cost_estimate=cost(2**19, 2**20),
+    )(weight)
+
+
+def rows_kernel(received, moment, grad, weight, weight_rows, cols, col_root, sent):
     new = BETA_TWO * moment[...] + (1.0 - BETA_TWO) * (jnp.sum(received[...], axis=0) / D)
     cols[...] = new
     root = lax.rsqrt(new)
     col_root[...] = root
-    sums = [jnp.zeros((ROW_BLOCK, LANES), jnp.float32)] * 4
+    sums = [jnp.zeros((ROW_BLOCK, LANES), jnp.float32)] * 3
     for i in range(WIDTH // LANES):
         lanes = slice(i * LANES, (i + 1) * LANES)
         value, held = grad[:, lanes], weight[:, lanes]
         by_cols = value * root[i : i + 1, :]
-        terms = (value * value, by_cols * by_cols, by_cols * held, held * held)
+        terms = (value * value, by_cols * by_cols, by_cols * held)
         sums = [a + b for a, b in zip(sums, terms)]
-    parts = []
-    for value in sums:
-        for row in range(0, ROW_BLOCK, LANES):
-            parts.append(jnp.sum(value[row : row + LANES, :].T, axis=0, keepdims=True))
-    tile = jnp.concatenate(parts, axis=0)
+    tile = jnp.concatenate([by_rows(value) for value in sums] + [weight_rows[...]], axis=0)
     for i in range(LAYERS):
         sent[i] = tile
 
 
-def rows(received, moment, grad, weight):
+def rows(received, moment, grad, weight, weight_rows):
     return pl.pallas_call(
         rows_kernel,
         out_shape=(shape(*TILE), shape(*TILE), shape(LAYERS, *TILE)),
-        in_specs=[WHOLE] * 4,
+        in_specs=[WHOLE] * 5,
         out_specs=(WHOLE, WHOLE, WHOLE),
         compiler_params=PARAMS,
         cost_estimate=cost(2**21, 2**21),
-    )(received, moment, grad, weight)
+    )(received, moment, grad, weight, weight_rows)
 
 
 def scalars_kernel(received, moment, rows_out, row_root, sent):
@@ -284,6 +304,8 @@
     back, ahead = [back_low, along(high, 1)], [along(low, SIDE - 1), ahead_high]
     blocks = lambda operand: [(operand, 0), (operand, 1), (operand + 1, 0), (operand + 1, 1)]
     total = product(place, (first, first), [low, high], [(0, True, blocks(0))])
+    total, held = lax.optimization_barrier((total, weight))
+    total, weight_rows = lax.optimization_barrier((total, weights(held)))
     parts = [(1, True, blocks(0)), (3, True, blocks(2))]
     total, back[1], ahead[0] = product(place, (first, first), back + ahead, parts, total, kept=(1, 2))
     operands = [low, high] + back + far + ahead
@@ -292,7 +314,7 @@
     received = lax.ppermute(theirs, "core", [(0, 1), (1, 0)])
     mine = product(place, (first, second), operands, parts, total, lambda core: core)
     weight_grad, tiles = columns(mine, received)
-    new_cols, col_root, tiles = rows(exchange(tiles, ROWS), col_moment.reshape(TILE), weight_grad, weight)
+    new_cols, col_root, tiles = rows(exchange(tiles, ROWS), col_moment.reshape(TILE), weight_grad, weight, weight_rows)
     new_rows, row_root, tiles = scalars(exchange(tiles, "z"), row_moment.reshape(2, LANES))
     out = update(exchange(tiles, ROWS), row_root, col_root, weight_grad, weight)
     return (out, new_rows.reshape(-1), new_cols.reshape(-1))

time: 121 us -> 121 us (level)
  no operation moved by 1% of the time
where the time goes in v22:
time: 121 us; the launch traced here: 120 us
  starting transfers between devices  49.2 us (41%)
  blocking collectives  45.4 us (38%)
  Pallas kernels  13.8 us (11%)
  waiting for transfers between devices  8.37 us (7%)
  local copies, waits for them, and re-layouts  2.38 us (2%)
    all_to_all x3, blocking collectives, exchange(): return lax.all_to_all(tiles, axes, 0, 0)  45.4 us
    ppermute x6, starting transfers between devices, along(): return lax.ppermute(value, ROWS, pairs)  19.5 us
    ppermute x1, starting transfers between devices, next_layer(): return lax.ppermute(value, ('core', 'z'), pairs)  13 us
    ppermute x1, starting transfers between devices, shards(): received = lax.ppermute(theirs, 'core', [(0, 1), (1, 0)])  6.94 us
    all_to_all x1, waiting for transfers between devices, gather_line(): return lax.all_to_all(sent, ROWS, 0, 0, axis_index_groups=groups)  6.76 us
    pallas_call x4, Pallas kernels, product(): pl.pallas_call(functools.partial(product_kernel, parts, which, kept), out...  5.89 us
    all_to_all x1, starting transfers between devices, exchange(): return lax.all_to_all(tiles, axes, 0, 0)  5.01 us
    all_to_all x1, starting transfers between devices, gather_line(): return lax.all_to_all(sent, ROWS, 0, 0, axis_index_groups=groups)  4.84 us
  transfers between devices with their start and end apart: 10, of which 3 were waited for; matrix products, arithmetic and copies ran while one was open for 0% of the time, Pallas kernels for 8%

profile of v22, /device:TPU:1, one launch (start us, length us, event | category | flops | bytes accessed | tf_op | source)
XLA Modules:
  0.0 120.1 jit_solution(3333073894565534624)
XLA Ops:
  0.6 2.1 %broadcast_in_dim.3 = bf16[4,128,1024]{2,1,0:T(8,128)(2,1)} broadcast(bf16[128,1024]{1,0:T(8,128)(2,1)} %param.6), dimensions={1,2} | broadcast | bytes 1310720 | tf_op jit(solution)/shard_map/broadcast_in_dim | solution.py:63
  2.7 4.8 %all-to-all-start = ((bf16[4,128,1024]{2,1,0:T(8,128)(2,1)}), bf16[4,128,1024]{2,1,0:T(8,128)(2,1)S(1)}, u32[]{:S(2)}, u32[]{:S(2)}) async-start(bf16[4,128,1024]{2,1,0:T(8,128)(2,1)} %broadcast_in_dim.3), calls=%async_computation | async-start | bytes 2097152 | tf_op jit(solution)/shard_map/all_to_all | solution.py:64
  7.5 0.1 pad_add_fusion.place
  7.6 2.9 %shard_map.76 = bf16[16,64,512]{2,1,0:T(8,128)(2,1)} custom-call(s32[4]{0:T(128)S(1)} %pad_add_fusion.place, bf16[128,8192]{1,0:T(8,128)(2,1)} %source.1), custom_call_target="tpu_custom_call" | custom-call | bytes 2097152 | tf_op jit(solution)/shard_map/pallas_call | solution.py:90
  10.5 6.8 %all-to-all-done = bf16[4,128,1024]{2,1,0:T(8,128)(2,1)S(1)} async-done(((bf16[4,128,1024]{2,1,0:T(8,128)(2,1)}), bf16[4,128,1024]{2,1,0:T(8,128)(2,1)S(1)}, u32[]{:S(2)}, u32[]{:S(2)}) %all-to-all-start) | async-done | bytes 1048608 | tf_op jit(solution)/shard_map/all_to_all | solution.py:64
  17.3 5.0 %all-to-all-start.1 = ((bf16[16,64,512]{2,1,0:T(8,128)(2,1)}), bf16[16,64,512]{2,1,0:T(8,128)(2,1)S(1)}, u32[]{:S(2)}, u32[]{:S(2)}) async-start(bf16[16,64,512]{2,1,0:T(8,128)(2,1)} %shard_map.76), calls=%async_computation.1 | async-start | bytes 2097152 | tf_op jit(solution)/shard_map/all_to_all | solution.py:74
  22.3 0.1 fusion
  22.4 3.3 %collective-permute-start.1 = (bf16[256,1024]{1,0:T(8,128)(2,1)S(1)}, bf16[256,1024]{1,0:T(8,128)(2,1)S(1)}, u32[]{:S(2)}, u32[]{:S(2)}) collective-permute-start(bf16[256,1024]{1,0:T(8,128)(2,1)S(1)} %bitcast.15), channel_id=1, source_target_pairs={{0,32},{16,144},{32,64},{48,176},{64,96},{80,208},{96,0},{112,240}... | collective-permute-start | bytes 1572872 | tf_op jit(solution)/shard_map/ppermute | solution.py:57
  25.7 3.2 %collective-permute-start.4 = (bf16[256,1024]{1,0:T(8,128)(2,1)S(1)}, bf16[256,1024]{1,0:T(8,128)(2,1)S(1)}, u32[]{:S(2)}, u32[]{:S(2)}) collective-permute-start(bf16[256,1024]{1,0:T(8,128)(2,1)S(1)} %bitcast.10), channel_id=1, source_target_pairs={{0,96},{16,400},{32,0},{48,432},{64,32},{80,464},{96,64},{112,496}... | collective-permute-start | bytes 1572872 | tf_op jit(solution)/shard_map/ppermute | solution.py:57
  28.9 2.1 %collective-permute-start.2 = (bf16[256,1024]{1,0:T(8,128)(2,1)S(1)}, bf16[256,1024]{1,0:T(8,128)(2,1)}, u32[]{:S(2)}, u32[]{:S(2)}) collective-permute-start(bf16[256,1024]{1,0:T(8,128)(2,1)S(1)} %bitcast.11), channel_id=1, source_target_pairs={{0,32},{16,144},{32,64},{48,176},{64,96},{80,208},{96,0},{112,240}... | collective-permute-start | bytes 1572872 | tf_op jit(solution)/shard_map/ppermute | solution.py:57
  31.0 4.4 %collective-permute-start.3 = (bf16[256,1024]{1,0:T(8,128)(2,1)S(1)}, bf16[256,1024]{1,0:T(8,128)(2,1)}, u32[]{:S(2)}, u32[]{:S(2)}) collective-permute-start(bf16[256,1024]{1,0:T(8,128)(2,1)S(1)} %bitcast.16), channel_id=1, source_target_pairs={{0,96},{16,400},{32,0},{48,432},{64,32},{80,464},{96,64},{112,496}... | collective-permute-start | bytes 1572872 | tf_op jit(solution)/shard_map/ppermute | solution.py:57
  35.4 13.0 %collective-permute-start = (bf16[16,64,512]{2,1,0:T(8,128)(2,1)S(1)}, bf16[16,64,512]{2,1,0:T(8,128)(2,1)S(1)}, u32[]{:S(2)}, u32[]{:S(2)}) collective-permute-start(bf16[16,64,512]{2,1,0:T(8,128)(2,1)S(1)} %all-to-all-done.1.part), channel_id=1, source_target_pairs={{0,1},{1,2},{2,3},{3,4},{4,5},{5,6},{6,7},{7,8},{8,9},{9,10},{10,1... | collective-permute-start | bytes 3145736 | tf_op jit(solution)/shard_map/ppermute | solution.py:70
  48.4 2.0 %collective-permute-start.5 = (bf16[256,1024]{1,0:T(8,128)(2,1)S(1)}, bf16[256,1024]{1,0:T(8,128)(2,1)S(1)}, u32[]{:S(2)}, u32[]{:S(2)}) collective-permute-start(bf16[256,1024]{1,0:T(8,128)(2,1)S(1)} %collective-permute-done.1.refs_0_.refs_2_), channel_id=1, source_target_pairs={{0,32},{16,144},{32,64},{48,176},{64,96},{80,208},{96,0},{112,240}... | collective-permute-start | bytes 1572872 | tf_op jit(solution)/shard_map/ppermute | solution.py:57
  50.4 4.5 %collective-permute-start.6 = (bf16[256,1024]{1,0:T(8,128)(2,1)S(1)}, bf16[256,1024]{1,0:T(8,128)(2,1)S(1)}, u32[]{:S(2)}, u32[]{:S(2)}) collective-permute-start(bf16[256,1024]{1,0:T(8,128)(2,1)S(1)} %collective-permute-done.4.refs_3_.refs_7_), channel_id=1, source_target_pairs={{0,96},{16,400},{32,0},{48,432},{64,32},{80,464},{96,64},{112,496}... | collective-permute-start | bytes 1572872 | tf_op jit(solution)/shard_map/ppermute | solution.py:57
  54.9 0.9 shard_map.77.first.second
  55.8 1.0 shard_map.79.refs_4_
  56.8 0.2 copy-done
  57.0 0.1 shard_map.80.weight_rows
  57.2 2.1 %shard_map.81 = (f32[512,1024]{1,0:T(8,128)S(1)}, bf16[256,1024]{1,0:T(8,128)(2,1)S(1)}, bf16[256,1024]{1,0:T(8,128)(2,1)S(1)}) custom-call(s32[4]{0:T(128)S(1)} %pad_add_fusion.place, bf16[512,1024]{1,0:T(8,128)(2,1)S(1)} %shard_map.77.first.second, bf16[512,1024]{1,0:T(8,128)(2,1)S(1)} %shard_map.77.first.second, ...), custom_call_target="tpu_custom_call", output_to_operand_aliasing={{0}: (7, {})} | custom-call | flops 6442450944 | bytes 1048576 | tf_op jit(solution)/shard_map/pallas_call | solution.py:149
  59.3 0.7 collective-permute-done.part
  60.1 0.9 shard_map.78.second
  61.0 1.4 %shard_map.83 = f32[256,1024]{1,0:T(8,128)S(1)} custom-call(s32[4]{0:T(128)S(1)} %pad_add_fusion.place, bf16[512,1024]{1,0:T(8,128)(2,1)S(1)} %shard_map.77.first.second, bf16[512,1024]{1,0:T(8,128)(2,1)S(1)} %shard_map.78.second, bf16[256,1024]{1,0:T(8,128)(2,1)S(1)} %bitcast.18, bf16[256,1024]{1,0:T(8,128)(2,1)S(1)} %bitcast.13, ...), custom_call_target="tpu_custom_call" | custom-call | flops 8053063680 | bytes 1048576 | tf_op jit(solution)/shard_map/pallas_call | solution.py:149
  62.4 6.9 %collective-permute-start.7 = (f32[256,1024]{1,0:T(8,128)S(1)}, f32[256,1024]{1,0:T(8,128)S(1)}, u32[]{:S(2)}, u32[]{:S(2)}) collective-permute-start(f32[256,1024]{1,0:T(8,128)S(1)} %shard_map.83), channel_id=1, source_target_pairs={{0,16},{16,0},{1,17},{17,1},{2,18},{18,2},{3,19},{19,3},{4,20},{20... | collective-permute-start | bytes 3145736 | tf_op jit(solution)/shard_map/ppermute | solution.py:314
  69.4 1.4 %shard_map.82.mine = f32[256,1024]{1,0:T(8,128)S(1)} custom-call(s32[4]{0:T(128)S(1)} %pad_add_fusion.place, bf16[512,1024]{1,0:T(8,128)(2,1)S(1)} %shard_map.77.first.second, bf16[512,1024]{1,0:T(8,128)(2,1)S(1)} %shard_map.78.second, bf16[256,1024]{1,0:T(8,128)(2,1)S(1)} %bitcast.19, bf16[256,1024]{1,0:T(8,128)(2,1)S(1)} %bitcast.14, ...), custom_call_target="tpu_custom_call" | custom-call | flops 8053063680 | bytes 1048576 | tf_op jit(solution)/shard_map/pallas_call | solution.py:149
  70.8 0.8 collective-permute-done.7.theirs
  71.6 0.1 shard_map.84
  71.8 10.9 %all_to_all.25.received = f32[32,8,128]{2,1,0:T(8,128)S(1)} all-to-all(f32[32,8,128]{2,1,0:T(8,128)S(1)} %get-tuple-element.28), channel_id=1, replica_groups=mesh['y'=4,'x'=4,'core'=2,'z'=16] {'y','x','core'}, dimensions={0} | all-to-all | bytes 262144 | tf_op jit(solution)/shard_map/all_to_all | solution.py:74
  82.6 0.9 shard_map.85
  83.6 22.0 %all_to_all.26.received = f32[16,8,128]{2,1,0:T(8,128)S(1)} all-to-all(f32[16,8,128]{2,1,0:T(8,128)S(1)} %get-tuple-element.31), channel_id=1, replica_groups=mesh['y'=4,'x'=4,'core'=2,'z'=16] {'z'}, dimensions={0} | all-to-all | bytes 131072 | tf_op jit(solution)/shard_map/all_to_all | solution.py:74
  105.6 0.6 shard_map.86
  106.1 12.5 %all_to_all.27.received = f32[32,4,128]{2,1,0:T(4,128)S(1)} all-to-all(f32[32,4,128]{2,1,0:T(4,128)S(1)} %get-tuple-element.32), channel_id=1, replica_groups=mesh['y'=4,'x'=4,'core'=2,'z'=16] {'y','x','core'}, dimensions={0} | all-to-all | bytes 131072 | tf_op jit(solution)/shard_map/all_to_all | solution.py:74
  118.7 1.4 %shard_map.87 = f32[256,1024]{1,0:T(8,128)} custom-call(f32[32,4,128]{2,1,0:T(4,128)S(1)} %all_to_all.27.received, f32[2,128]{1,0:T(2,128)S(1)} %get-tuple-element.33.row_root, f32[8,128]{1,0:T(8,128)S(1)} %get-tuple-element.34.col_root, f32[256,1024]{1,0:T(8,128)S(1)} %get-tuple-element.29.grad, f32[256,1024]{1,0:T(8,128)S(1)} %copy-done), custom_call_target="tpu_custom_call" | custom-call | flops 1048576 | bytes 3145728 | tf_op jit(solution)/shard_map/pallas_call | solution.py:283
  (12 shorter events, 0.0 us)
Async XLA Ops:
  2.7 14.6 %all-to-all-start = ((bf16[4,128,1024]{2,1,0:T(8,128)(2,1)}), bf16[4,128,1024]{2,1,0:T(8,128)(2,1)S(1)}, u32[]{:S(2)}, u32[]{:S(2)}) async-start(bf16[4,128,1024]{2,1,0:T(8,128)(2,1)} %broadcast_in_dim.3), calls=%async_computation | async-start | bytes 2097152 | tf_op jit(solution)/shard_map/all_to_all | solution.py:64
  17.3 18.1 %all-to-all-start.1 = ((bf16[16,64,512]{2,1,0:T(8,128)(2,1)}), bf16[16,64,512]{2,1,0:T(8,128)(2,1)S(1)}, u32[]{:S(2)}, u32[]{:S(2)}) async-start(bf16[16,64,512]{2,1,0:T(8,128)(2,1)} %shard_map.76), calls=%async_computation.1 | async-start | bytes 2097152 | tf_op jit(solution)/shard_map/all_to_all | solution.py:74
  22.4 26.0 %collective-permute-start.1 = (bf16[256,1024]{1,0:T(8,128)(2,1)S(1)}, bf16[256,1024]{1,0:T(8,128)(2,1)S(1)}, u32[]{:S(2)}, u32[]{:S(2)}) collective-permute-start(bf16[256,1024]{1,0:T(8,128)(2,1)S(1)} %bitcast.15), channel_id=1, source_target_pairs={{0,32},{16,144},{32,64},{48,176},{64,96},{80,208},{96,0},{112,240}... | collective-permute-start | bytes 1572872 | tf_op jit(solution)/shard_map/ppermute | solution.py:57
  25.7 24.7 %collective-permute-start.4 = (bf16[256,1024]{1,0:T(8,128)(2,1)S(1)}, bf16[256,1024]{1,0:T(8,128)(2,1)S(1)}, u32[]{:S(2)}, u32[]{:S(2)}) collective-permute-start(bf16[256,1024]{1,0:T(8,128)(2,1)S(1)} %bitcast.10), channel_id=1, source_target_pairs={{0,96},{16,400},{32,0},{48,432},{64,32},{80,464},{96,64},{112,496}... | collective-permute-start | bytes 1572872 | tf_op jit(solution)/shard_map/ppermute | solution.py:57
  28.9 28.3 %collective-permute-start.2 = (bf16[256,1024]{1,0:T(8,128)(2,1)S(1)}, bf16[256,1024]{1,0:T(8,128)(2,1)}, u32[]{:S(2)}, u32[]{:S(2)}) collective-permute-start(bf16[256,1024]{1,0:T(8,128)(2,1)S(1)} %bitcast.11), channel_id=1, source_target_pairs={{0,32},{16,144},{32,64},{48,176},{64,96},{80,208},{96,0},{112,240}... | collective-permute-start | bytes 1572872 | tf_op jit(solution)/shard_map/ppermute | solution.py:57
  31.0 26.2 %collective-permute-start.3 = (bf16[256,1024]{1,0:T(8,128)(2,1)S(1)}, bf16[256,1024]{1,0:T(8,128)(2,1)}, u32[]{:S(2)}, u32[]{:S(2)}) collective-permute-start(bf16[256,1024]{1,0:T(8,128)(2,1)S(1)} %bitcast.16), channel_id=1, source_target_pairs={{0,96},{16,400},{32,0},{48,432},{64,32},{80,464},{96,64},{112,496}... | collective-permute-start | bytes 1572872 | tf_op jit(solution)/shard_map/ppermute | solution.py:57
  35.4 24.7 %collective-permute-start = (bf16[16,64,512]{2,1,0:T(8,128)(2,1)S(1)}, bf16[16,64,512]{2,1,0:T(8,128)(2,1)S(1)}, u32[]{:S(2)}, u32[]{:S(2)}) collective-permute-start(bf16[16,64,512]{2,1,0:T(8,128)(2,1)S(1)} %all-to-all-done.1.part), channel_id=1, source_target_pairs={{0,1},{1,2},{2,3},{3,4},{4,5},{5,6},{6,7},{7,8},{8,9},{9,10},{10,1... | collective-permute-start | bytes 3145736 | tf_op jit(solution)/shard_map/ppermute | solution.py:70
  48.4 12.6 %collective-permute-start.5 = (bf16[256,1024]{1,0:T(8,128)(2,1)S(1)}, bf16[256,1024]{1,0:T(8,128)(2,1)S(1)}, u32[]{:S(2)}, u32[]{:S(2)}) collective-permute-start(bf16[256,1024]{1,0:T(8,128)(2,1)S(1)} %collective-permute-done.1.refs_0_.refs_2_), channel_id=1, source_target_pairs={{0,32},{16,144},{32,64},{48,176},{64,96},{80,208},{96,0},{112,240}... | collective-permute-start | bytes 1572872 | tf_op jit(solution)/shard_map/ppermute | solution.py:57
  50.4 10.6 %collective-permute-start.6 = (bf16[256,1024]{1,0:T(8,128)(2,1)S(1)}, bf16[256,1024]{1,0:T(8,128)(2,1)S(1)}, u32[]{:S(2)}, u32[]{:S(2)}) collective-permute-start(bf16[256,1024]{1,0:T(8,128)(2,1)S(1)} %collective-permute-done.4.refs_3_.refs_7_), channel_id=1, source_target_pairs={{0,96},{16,400},{32,0},{48,432},{64,32},{80,464},{96,64},{112,496}... | collective-permute-start | bytes 1572872 | tf_op jit(solution)/shard_map/ppermute | solution.py:57
  55.8 1.2 %copy-start = (f32[256,1024]{1,0:T(8,128)S(1)}, f32[256,1024]{1,0:T(8,128)}, u32[]{:S(2)}) copy-start(f32[256,1024]{1,0:T(8,128)} %weight.4) | copy-start | bytes 3145732
  62.4 9.2 %collective-permute-start.7 = (f32[256,1024]{1,0:T(8,128)S(1)}, f32[256,1024]{1,0:T(8,128)S(1)}, u32[]{:S(2)}, u32[]{:S(2)}) collective-permute-start(f32[256,1024]{1,0:T(8,128)S(1)} %shard_map.83), channel_id=1, source_target_pairs={{0,16},{16,0},{1,17},{17,1},{2,18},{18,2},{3,19},{19,3},{4,20},{20... | collective-permute-start | bytes 3145736 | tf_op jit(solution)/shard_map/ppermute | solution.py:314
  70.8 11.9 %copy-start.1 = (f32[1024]{0:T(1024)S(1)}, f32[1024]{0:T(1024)}, u32[]{:S(2)}) copy-start(f32[1024]{0:T(1024)} %param.9) | copy-start | bytes 12292
  70.8 34.8 %copy-start.2 = (f32[256]{0:T(256)S(1)}, f32[256]{0:T(256)}, u32[]{:S(2)}) copy-start(f32[256]{0:T(256)} %param.8) | copy-start | bytes 3076

commit v23 on v21

--- a/solution.py
+++ b/solution.py
@@ -65,8 +65,8 @@
 
 
 def next_layer(value):
-    pairs = [(i, (i + 1) % LAYERS) for i in range(LAYERS)]
-    pairs += [(LAYERS + i, LAYERS + (i - 1) % LAYERS) for i in range(LAYERS)]
+    pairs = [(i, (i - 1) % LAYERS) for i in range(LAYERS)]
+    pairs += [(LAYERS + i, LAYERS + (i + 1) % LAYERS) for i in range(LAYERS)]
     return lax.ppermute(value, ("core", "z"), pairs)
 
 

time: 121 us -> 121 us (level)
  waiting for transfers between devices: 8.74 us -> 17.1 us
  starting transfers between devices: 49.2 us -> 41 us
    ppermute x1, starting transfers between devices: 13 us -> 5.38 us  [next_layer(): return lax.ppermute(value, ('core', 'z'), pairs)]
    ppermute x1, waiting for transfers between devices: 1.13 us -> 6.63 us  [next_layer(): return lax.ppermute(value, ('core', 'z'), pairs)]
    ppermute x6, waiting for transfers between devices: 0.02 us -> 2.85 us  [along(): return lax.ppermute(value, ROWS, pairs)]
  transfers between devices with their start and end apart: 10 -> 10, of which waited for: 3 -> 4; matrix products, arithmetic and copies ran while one was open for 0% -> 0% of each run, Pallas kernels for 8% -> 8%
where the time goes in v23:
time: 121 us; the launch traced here: 120 us
  blocking collectives  45.3 us (37%)
  starting transfers between devices  41 us (34%)
  waiting for transfers between devices  17.1 us (14%)
  Pallas kernels  13.7 us (11%)
  local copies, waits for them, and re-layouts  2.15 us (2%)
    all_to_all x3, blocking collectives, exchange(): return lax.all_to_all(tiles, axes, 0, 0)  45.3 us
    ppermute x6, starting transfers between devices, along(): return lax.ppermute(value, ROWS, pairs)  19.5 us
    all_to_all x1, waiting for transfers between devices, gather_line(): return lax.all_to_all(sent, ROWS, 0, 0, axis_index_groups=groups)  6.76 us
    ppermute x1, waiting for transfers between devices, next_layer(): return lax.ppermute(value, ('core', 'z'), pairs)  6.63 us
    ppermute x1, starting transfers between devices, shards(): received = lax.ppermute(theirs, 'core', [(0, 1), (1, 0)])  6.26 us
    pallas_call x4, Pallas kernels, product(): pl.pallas_call(functools.partial(product_kernel, parts, which, kept), out...  5.9 us
    ppermute x1, starting transfers between devices, next_layer(): return lax.ppermute(value, ('core', 'z'), pairs)  5.38 us
    all_to_all x1, starting transfers between devices, exchange(): return lax.all_to_all(tiles, axes, 0, 0)  5.01 us
  transfers between devices with their start and end apart: 10, of which 4 were waited for; matrix products, arithmetic and copies ran while one was open for 0% of the time, Pallas kernels for 8%

profile of v23, /device:TPU:1, one launch (start us, length us, event | category | flops | bytes accessed | tf_op | source)
XLA Modules:
  0.0 120.1 jit_solution(1812403349952189500)
XLA Ops:
  0.6 2.1 %broadcast_in_dim.3 = bf16[4,128,1024]{2,1,0:T(8,128)(2,1)} broadcast(bf16[128,1024]{1,0:T(8,128)(2,1)} %param.6), dimensions={1,2} | broadcast | bytes 1310720 | tf_op jit(solution)/shard_map/broadcast_in_dim | solution.py:63
  2.7 4.8 %all-to-all-start = ((bf16[4,128,1024]{2,1,0:T(8,128)(2,1)}), bf16[4,128,1024]{2,1,0:T(8,128)(2,1)S(1)}, u32[]{:S(2)}, u32[]{:S(2)}) async-start(bf16[4,128,1024]{2,1,0:T(8,128)(2,1)} %broadcast_in_dim.3), calls=%async_computation | async-start | bytes 2097152 | tf_op jit(solution)/shard_map/all_to_all | solution.py:64
  7.5 0.1 pad_add_fusion.place
  7.6 2.9 %shard_map.76 = bf16[16,64,512]{2,1,0:T(8,128)(2,1)} custom-call(s32[4]{0:T(128)S(1)} %pad_add_fusion.place, bf16[128,8192]{1,0:T(8,128)(2,1)} %source.1), custom_call_target="tpu_custom_call" | custom-call | bytes 2097152 | tf_op jit(solution)/shard_map/pallas_call | solution.py:90
  10.5 6.8 %all-to-all-done = bf16[4,128,1024]{2,1,0:T(8,128)(2,1)S(1)} async-done(((bf16[4,128,1024]{2,1,0:T(8,128)(2,1)}), bf16[4,128,1024]{2,1,0:T(8,128)(2,1)S(1)}, u32[]{:S(2)}, u32[]{:S(2)}) %all-to-all-start) | async-done | bytes 1048608 | tf_op jit(solution)/shard_map/all_to_all | solution.py:64
  17.3 5.0 %all-to-all-start.1 = ((bf16[16,64,512]{2,1,0:T(8,128)(2,1)}), bf16[16,64,512]{2,1,0:T(8,128)(2,1)S(1)}, u32[]{:S(2)}, u32[]{:S(2)}) async-start(bf16[16,64,512]{2,1,0:T(8,128)(2,1)} %shard_map.76), calls=%async_computation.1 | async-start | bytes 2097152 | tf_op jit(solution)/shard_map/all_to_all | solution.py:74
  22.3 0.1 fusion
  22.4 3.3 %collective-permute-start.1 = (bf16[256,1024]{1,0:T(8,128)(2,1)S(1)}, bf16[256,1024]{1,0:T(8,128)(2,1)S(1)}, u32[]{:S(2)}, u32[]{:S(2)}) collective-permute-start(bf16[256,1024]{1,0:T(8,128)(2,1)S(1)} %bitcast.15), channel_id=1, source_target_pairs={{0,32},{16,144},{32,64},{48,176},{64,96},{80,208},{96,0},{112,240}... | collective-permute-start | bytes 1572872 | tf_op jit(solution)/shard_map/ppermute | solution.py:57
  25.7 3.2 %collective-permute-start.4 = (bf16[256,1024]{1,0:T(8,128)(2,1)S(1)}, bf16[256,1024]{1,0:T(8,128)(2,1)S(1)}, u32[]{:S(2)}, u32[]{:S(2)}) collective-permute-start(bf16[256,1024]{1,0:T(8,128)(2,1)S(1)} %bitcast.10), channel_id=1, source_target_pairs={{0,96},{16,400},{32,0},{48,432},{64,32},{80,464},{96,64},{112,496}... | collective-permute-start | bytes 1572872 | tf_op jit(solution)/shard_map/ppermute | solution.py:57
  28.9 2.1 %collective-permute-start.2 = (bf16[256,1024]{1,0:T(8,128)(2,1)S(1)}, bf16[256,1024]{1,0:T(8,128)(2,1)}, u32[]{:S(2)}, u32[]{:S(2)}) collective-permute-start(bf16[256,1024]{1,0:T(8,128)(2,1)S(1)} %bitcast.11), channel_id=1, source_target_pairs={{0,32},{16,144},{32,64},{48,176},{64,96},{80,208},{96,0},{112,240}... | collective-permute-start | bytes 1572872 | tf_op jit(solution)/shard_map/ppermute | solution.py:57
  31.0 4.4 %collective-permute-start.3 = (bf16[256,1024]{1,0:T(8,128)(2,1)S(1)}, bf16[256,1024]{1,0:T(8,128)(2,1)}, u32[]{:S(2)}, u32[]{:S(2)}) collective-permute-start(bf16[256,1024]{1,0:T(8,128)(2,1)S(1)} %bitcast.16), channel_id=1, source_target_pairs={{0,96},{16,400},{32,0},{48,432},{64,32},{80,464},{96,64},{112,496}... | collective-permute-start | bytes 1572872 | tf_op jit(solution)/shard_map/ppermute | solution.py:57
  35.4 5.4 %collective-permute-start = (bf16[16,64,512]{2,1,0:T(8,128)(2,1)S(1)}, bf16[16,64,512]{2,1,0:T(8,128)(2,1)S(1)}, u32[]{:S(2)}, u32[]{:S(2)}) collective-permute-start(bf16[16,64,512]{2,1,0:T(8,128)(2,1)S(1)} %all-to-all-done.1.part), channel_id=1, source_target_pairs={{0,15},{1,0},{2,1},{3,2},{4,3},{5,4},{6,5},{7,6},{8,7},{9,8},{10,9... | collective-permute-start | bytes 3145736 | tf_op jit(solution)/shard_map/ppermute | solution.py:70
  40.8 2.8 %collective-permute-done.1.refs_0_.refs_2_ = bf16[256,1024]{1,0:T(8,128)(2,1)S(1)} collective-permute-done((bf16[256,1024]{1,0:T(8,128)(2,1)S(1)}, bf16[256,1024]{1,0:T(8,128)(2,1)S(1)}, u32[]{:S(2)}, u32[]{:S(2)}) %collective-permute-start.1) | collective-permute-done | bytes 524320 | tf_op jit(solution)/shard_map/ppermute | solution.py:57
  43.6 1.9 %collective-permute-start.5 = (bf16[256,1024]{1,0:T(8,128)(2,1)S(1)}, bf16[256,1024]{1,0:T(8,128)(2,1)S(1)}, u32[]{:S(2)}, u32[]{:S(2)}) collective-permute-start(bf16[256,1024]{1,0:T(8,128)(2,1)S(1)} %collective-permute-done.1.refs_0_.refs_2_), channel_id=1, source_target_pairs={{0,32},{16,144},{32,64},{48,176},{64,96},{80,208},{96,0},{112,240}... | collective-permute-start | bytes 1572872 | tf_op jit(solution)/shard_map/ppermute | solution.py:57
  45.6 4.6 %collective-permute-start.6 = (bf16[256,1024]{1,0:T(8,128)(2,1)S(1)}, bf16[256,1024]{1,0:T(8,128)(2,1)S(1)}, u32[]{:S(2)}, u32[]{:S(2)}) collective-permute-start(bf16[256,1024]{1,0:T(8,128)(2,1)S(1)} %collective-permute-done.4.refs_3_.refs_7_), channel_id=1, source_target_pairs={{0,96},{16,400},{32,0},{48,432},{64,32},{80,464},{96,64},{112,496}... | collective-permute-start | bytes 1572872 | tf_op jit(solution)/shard_map/ppermute | solution.py:57
  50.1 0.9 shard_map.77.first.second
  51.1 1.0 shard_map.79.refs_4_
  52.1 2.1 %shard_map.80 = (f32[512,1024]{1,0:T(8,128)S(1)}, bf16[256,1024]{1,0:T(8,128)(2,1)S(1)}, bf16[256,1024]{1,0:T(8,128)(2,1)S(1)}) custom-call(s32[4]{0:T(128)S(1)} %pad_add_fusion.place, bf16[512,1024]{1,0:T(8,128)(2,1)S(1)} %shard_map.77.first.second, bf16[512,1024]{1,0:T(8,128)(2,1)S(1)} %shard_map.77.first.second, ...), custom_call_target="tpu_custom_call", output_to_operand_aliasing={{0}: (7, {})} | custom-call | flops 6442450944 | bytes 1048576 | tf_op jit(solution)/shard_map/pallas_call | solution.py:149
  54.2 6.6 %collective-permute-done.part = bf16[16,64,512]{2,1,0:T(8,128)(2,1)S(1)} collective-permute-done((bf16[16,64,512]{2,1,0:T(8,128)(2,1)S(1)}, bf16[16,64,512]{2,1,0:T(8,128)(2,1)S(1)}, u32[]{:S(2)}, u32[]{:S(2)}) %collective-permute-start) | collective-permute-done | bytes 1048608 | tf_op jit(solution)/shard_map/ppermute | solution.py:70
  60.8 0.9 shard_map.78.second
  61.8 1.4 %shard_map.82 = f32[256,1024]{1,0:T(8,128)S(1)} custom-call(s32[4]{0:T(128)S(1)} %pad_add_fusion.place, bf16[512,1024]{1,0:T(8,128)(2,1)S(1)} %shard_map.77.first.second, bf16[512,1024]{1,0:T(8,128)(2,1)S(1)} %shard_map.78.second, bf16[256,1024]{1,0:T(8,128)(2,1)S(1)} %bitcast.18, bf16[256,1024]{1,0:T(8,128)(2,1)S(1)} %bitcast.13, ...), custom_call_target="tpu_custom_call" | custom-call | flops 8053063680 | bytes 1048576 | tf_op jit(solution)/shard_map/pallas_call | solution.py:149
  63.2 6.3 %collective-permute-start.7 = (f32[256,1024]{1,0:T(8,128)S(1)}, f32[256,1024]{1,0:T(8,128)S(1)}, u32[]{:S(2)}, u32[]{:S(2)}) collective-permute-start(f32[256,1024]{1,0:T(8,128)S(1)} %shard_map.82), channel_id=1, source_target_pairs={{0,16},{16,0},{1,17},{17,1},{2,18},{18,2},{3,19},{19,3},{4,20},{20... | collective-permute-start | bytes 3145736 | tf_op jit(solution)/shard_map/ppermute | solution.py:292
  69.4 1.4 %shard_map.81.mine = f32[256,1024]{1,0:T(8,128)S(1)} custom-call(s32[4]{0:T(128)S(1)} %pad_add_fusion.place, bf16[512,1024]{1,0:T(8,128)(2,1)S(1)} %shard_map.77.first.second, bf16[512,1024]{1,0:T(8,128)(2,1)S(1)} %shard_map.78.second, bf16[256,1024]{1,0:T(8,128)(2,1)S(1)} %bitcast.19, bf16[256,1024]{1,0:T(8,128)(2,1)S(1)} %bitcast.14, ...), custom_call_target="tpu_custom_call" | custom-call | flops 8053063680 | bytes 1048576 | tf_op jit(solution)/shard_map/pallas_call | solution.py:149
  70.8 0.0 copy-start
  70.9 0.8 collective-permute-done.7.theirs
  71.7 0.1 shard_map.83
  71.8 13.6 %all_to_all.25.received = f32[32,8,128]{2,1,0:T(8,128)S(1)} all-to-all(f32[32,8,128]{2,1,0:T(8,128)S(1)} %get-tuple-element.21), channel_id=1, replica_groups=mesh['y'=4,'x'=4,'core'=2,'z'=16] {'y','x','core'}, dimensions={0} | all-to-all | bytes 262144 | tf_op jit(solution)/shard_map/all_to_all | solution.py:74
  85.5 1.0 shard_map.84
  86.4 19.2 %all_to_all.26.received = f32[16,8,128]{2,1,0:T(8,128)S(1)} all-to-all(f32[16,8,128]{2,1,0:T(8,128)S(1)} %get-tuple-element.23), channel_id=1, replica_groups=mesh['y'=4,'x'=4,'core'=2,'z'=16] {'z'}, dimensions={0} | all-to-all | bytes 131072 | tf_op jit(solution)/shard_map/all_to_all | solution.py:74
  105.6 0.6 shard_map.85
  106.2 12.5 %all_to_all.27.received = f32[32,4,128]{2,1,0:T(4,128)S(1)} all-to-all(f32[32,4,128]{2,1,0:T(4,128)S(1)} %get-tuple-element.24), channel_id=1, replica_groups=mesh['y'=4,'x'=4,'core'=2,'z'=16] {'y','x','core'}, dimensions={0} | all-to-all | bytes 131072 | tf_op jit(solution)/shard_map/all_to_all | solution.py:74
  118.7 1.4 %shard_map.86 = f32[256,1024]{1,0:T(8,128)} custom-call(f32[32,4,128]{2,1,0:T(4,128)S(1)} %all_to_all.27.received, f32[2,128]{1,0:T(2,128)S(1)} %get-tuple-element.25.row_root, f32[8,128]{1,0:T(8,128)S(1)} %get-tuple-element.26.col_root, f32[256,1024]{1,0:T(8,128)S(1)} %get-tuple-element.22.grad, f32[256,1024]{1,0:T(8,128)S(1)} %copy-done), custom_call_target="tpu_custom_call" | custom-call | flops 1048576 | bytes 3145728 | tf_op jit(solution)/shard_map/pallas_call | solution.py:263
  (11 shorter events, 0.0 us)
Async XLA Ops:
  2.7 14.6 %all-to-all-start = ((bf16[4,128,1024]{2,1,0:T(8,128)(2,1)}), bf16[4,128,1024]{2,1,0:T(8,128)(2,1)S(1)}, u32[]{:S(2)}, u32[]{:S(2)}) async-start(bf16[4,128,1024]{2,1,0:T(8,128)(2,1)} %broadcast_in_dim.3), calls=%async_computation | async-start | bytes 2097152 | tf_op jit(solution)/shard_map/all_to_all | solution.py:64
  17.3 18.1 %all-to-all-start.1 = ((bf16[16,64,512]{2,1,0:T(8,128)(2,1)}), bf16[16,64,512]{2,1,0:T(8,128)(2,1)S(1)}, u32[]{:S(2)}, u32[]{:S(2)}) async-start(bf16[16,64,512]{2,1,0:T(8,128)(2,1)} %shard_map.76), calls=%async_computation.1 | async-start | bytes 2097152 | tf_op jit(solution)/shard_map/all_to_all | solution.py:74
  22.4 21.3 %collective-permute-start.1 = (bf16[256,1024]{1,0:T(8,128)(2,1)S(1)}, bf16[256,1024]{1,0:T(8,128)(2,1)S(1)}, u32[]{:S(2)}, u32[]{:S(2)}) collective-permute-start(bf16[256,1024]{1,0:T(8,128)(2,1)S(1)} %bitcast.15), channel_id=1, source_target_pairs={{0,32},{16,144},{32,64},{48,176},{64,96},{80,208},{96,0},{112,240}... | collective-permute-start | bytes 1572872 | tf_op jit(solution)/shard_map/ppermute | solution.py:57
  25.7 19.9 %collective-permute-start.4 = (bf16[256,1024]{1,0:T(8,128)(2,1)S(1)}, bf16[256,1024]{1,0:T(8,128)(2,1)S(1)}, u32[]{:S(2)}, u32[]{:S(2)}) collective-permute-start(bf16[256,1024]{1,0:T(8,128)(2,1)S(1)} %bitcast.10), channel_id=1, source_target_pairs={{0,96},{16,400},{32,0},{48,432},{64,32},{80,464},{96,64},{112,496}... | collective-permute-start | bytes 1572872 | tf_op jit(solution)/shard_map/ppermute | solution.py:57
  28.9 23.2 %collective-permute-start.2 = (bf16[256,1024]{1,0:T(8,128)(2,1)S(1)}, bf16[256,1024]{1,0:T(8,128)(2,1)}, u32[]{:S(2)}, u32[]{:S(2)}) collective-permute-start(bf16[256,1024]{1,0:T(8,128)(2,1)S(1)} %bitcast.11), channel_id=1, source_target_pairs={{0,32},{16,144},{32,64},{48,176},{64,96},{80,208},{96,0},{112,240}... | collective-permute-start | bytes 1572872 | tf_op jit(solution)/shard_map/ppermute | solution.py:57
  31.0 21.1 %collective-permute-start.3 = (bf16[256,1024]{1,0:T(8,128)(2,1)S(1)}, bf16[256,1024]{1,0:T(8,128)(2,1)}, u32[]{:S(2)}, u32[]{:S(2)}) collective-permute-start(bf16[256,1024]{1,0:T(8,128)(2,1)S(1)} %bitcast.16), channel_id=1, source_target_pairs={{0,96},{16,400},{32,0},{48,432},{64,32},{80,464},{96,64},{112,496}... | collective-permute-start | bytes 1572872 | tf_op jit(solution)/shard_map/ppermute | solution.py:57
  35.4 25.4 %collective-permute-start = (bf16[16,64,512]{2,1,0:T(8,128)(2,1)S(1)}, bf16[16,64,512]{2,1,0:T(8,128)(2,1)S(1)}, u32[]{:S(2)}, u32[]{:S(2)}) collective-permute-start(bf16[16,64,512]{2,1,0:T(8,128)(2,1)S(1)} %all-to-all-done.1.part), channel_id=1, source_target_pairs={{0,15},{1,0},{2,1},{3,2},{4,3},{5,4},{6,5},{7,6},{8,7},{9,8},{10,9... | collective-permute-start | bytes 3145736 | tf_op jit(solution)/shard_map/ppermute | solution.py:70
  43.6 18.1 %collective-permute-start.5 = (bf16[256,1024]{1,0:T(8,128)(2,1)S(1)}, bf16[256,1024]{1,0:T(8,128)(2,1)S(1)}, u32[]{:S(2)}, u32[]{:S(2)}) collective-permute-start(bf16[256,1024]{1,0:T(8,128)(2,1)S(1)} %collective-permute-done.1.refs_0_.refs_2_), channel_id=1, source_target_pairs={{0,32},{16,144},{32,64},{48,176},{64,96},{80,208},{96,0},{112,240}... | collective-permute-start | bytes 1572872 | tf_op jit(solution)/shard_map/ppermute | solution.py:57
  45.6 16.2 %collective-permute-start.6 = (bf16[256,1024]{1,0:T(8,128)(2,1)S(1)}, bf16[256,1024]{1,0:T(8,128)(2,1)S(1)}, u32[]{:S(2)}, u32[]{:S(2)}) collective-permute-start(bf16[256,1024]{1,0:T(8,128)(2,1)S(1)} %collective-permute-done.4.refs_3_.refs_7_), channel_id=1, source_target_pairs={{0,96},{16,400},{32,0},{48,432},{64,32},{80,464},{96,64},{112,496}... | collective-permute-start | bytes 1572872 | tf_op jit(solution)/shard_map/ppermute | solution.py:57
  63.2 8.5 %collective-permute-start.7 = (f32[256,1024]{1,0:T(8,128)S(1)}, f32[256,1024]{1,0:T(8,128)S(1)}, u32[]{:S(2)}, u32[]{:S(2)}) collective-permute-start(f32[256,1024]{1,0:T(8,128)S(1)} %shard_map.82), channel_id=1, source_target_pairs={{0,16},{16,0},{1,17},{17,1},{2,18},{18,2},{3,19},{19,3},{4,20},{20... | collective-permute-start | bytes 3145736 | tf_op jit(solution)/shard_map/ppermute | solution.py:292
  70.8 14.6 %copy-start = (f32[256,1024]{1,0:T(8,128)S(1)}, f32[256,1024]{1,0:T(8,128)}, u32[]{:S(2)}) copy-start(f32[256,1024]{1,0:T(8,128)} %weight.3) | copy-start | bytes 3145732
  70.8 14.6 %copy-start.1 = (f32[1024]{0:T(1024)S(1)}, f32[1024]{0:T(1024)}, u32[]{:S(2)}) copy-start(f32[1024]{0:T(1024)} %param.9) | copy-start | bytes 12292
  70.9 34.8 %copy-start.2 = (f32[256]{0:T(256)S(1)}, f32[256]{0:T(256)}, u32[]{:S(2)}) copy-start(f32[256]{0:T(256)} %param.8) | copy-start | bytes 3076
